TPU v7x, 32 devices: a whole 2x2x4 slice. The times are simulated.
32 devices in a mesh: req: 8 (over y, x, core), wgt: 4 (over z).
Axes of the slice: x: 2, y: 2, z: 4, core: 2. Of those that a mesh axis runs over, the one named last changes fastest.
Arguments:
- arrivals: bfloat16 [32, 48, 6144], P('req', None, 'wgt'), may hold values from -6 to 6
- group_of: int32 [32], replicated, may hold values from 0 to 7, as said below
- lengths: int32 [32], P('req'), may hold values from 1 to 2048, as said below
- page_table: int32 [32, 16], P('req'), may hold values from 0 to 39, as said below
- ln_gain: bfloat16 [6144], replicated, may hold values from 0.25 to 1.75
- ln_bias: bfloat16 [6144], replicated, may hold values from -1.5 to 1.5
- w_qkv: bfloat16 [6144, 9216], P('req', 'wgt'), may hold values from -0.078125 to 0.078125
- qkv_bias: bfloat16 [9216], P('wgt'), may hold values from -4.5 to 4.5
- key_pool: bfloat16 [320, 128, 3072], P('req', None, 'wgt'), may hold values from -8 to 8
- value_pool: bfloat16 [320, 128, 3072], P('req', None, 'wgt'), may hold values from -6 to 6
Outputs:
- attended: bfloat16 [32, 48, 3072], P('req', None, 'wgt')
- new_keys: bfloat16 [32, 48, 3072], P('req', None, 'wgt')
- new_values: bfloat16 [32, 48, 3072], P('req', None, 'wgt')
Inputs may be any that keep to these rules, and one draw needn't show every extreme that they name: `group_of`: every group number is named by exactly 4 requests; the requests that arrive at one group (consecutive blocks of 4 in arrival order) name different groups. `lengths`: in each group at most one request has more than 1024 cached tokens; some request has exactly 2048. `page_table`: entries name pages of the request's group's own pool of 40; the pages that hold cached tokens of one group's requests are all different.
All inputs are finite; a program needn't handle non-finite values.
Results may differ from a plain program's by a relative error of at most 0.0066.
Values may be sent and summed in bfloat16 or wider, within the bound.
No kernel may reach another device: no remote copies, remote signals or barrier semaphores. Data moves between devices by JAX's collectives and lax.ppermute only.
A program may use at most 128 MiB of HBM per device.

v0:
```python
import functools
import math

import jax
import jax.numpy as jnp
import numpy as np
from jax import lax
from jax.experimental import pallas as pl
from jax.experimental.pallas import tpu as pltpu
from jax.sharding import PartitionSpec as P

HEAD = 96
ROT = 24
EPS = 1e-05
LANES = 128
WINDOW = 2 * LANES
CHUNK_PAGES = 4
VMEM_LIMIT = 58 * 1024 * 1024

SMEM = pl.BlockSpec(memory_space=pltpu.SMEM)
VMEM = pl.BlockSpec(memory_space=pltpu.VMEM)
HBM = pl.BlockSpec(memory_space=pltpu.HBM)


def plan_kernel(req_count, place, group_of, arrivals, slots, sources, picks, stats, *refs):
    order, slot_of, color, filled = refs
    everyone = group_of.shape[0]
    groups = everyone // req_count
    half = req_count // 2
    me = place[0]

    def clear(group, carry):
        filled[group] = 0
        return carry

    lax.fori_loop(0, groups, clear, 0)

    def rank(item, carry):
        group = group_of[item]
        slot = group * req_count + filled[group]
        filled[group] = filled[group] + 1
        slot_of[item] = slot
        order[slot] = item
        color[item] = -1
        return carry

    lax.fori_loop(0, everyone, rank, 0)

    shift = req_count.bit_length() - 1

    def note(item, shade):
        color[item] = shade
        slot = slot_of[item]
        to = (shade * groups + (slot >> shift)) * half + ((slot & (req_count - 1)) >> 1)
        origin = item >> shift
        row = ((origin & 1) ^ (me & 1)) * (groups // 2) + (origin >> 1)
        sources[to] = row * half + ((item & (req_count - 1)) >> 1)
        return slot

    def walk(pair, carry):
        def body(state):
            note(state[0], 0)
            following = order[note(state[0] ^ 1, 1) ^ 1]
            return following, color[following]

        lax.while_loop(lambda state: state[1] < 0, body, (2 * pair, color[2 * pair]))
        return carry

    lax.fori_loop(0, everyone // 2, walk, 0)

    for pair in range(half):
        first = color[me * req_count + 2 * pair]
        for part in range(2):
            picks[part * half + pair] = 2 * pair + (first ^ part)
        first = color[order[me * req_count + 2 * pair]]
        for part in range(2):
            slots[part * half + pair] = 2 * pair + (first ^ part)

    fresh_len, width = arrivals.shape[1:]

    def measure(index, carry):
        value = arrivals[index].astype(jnp.float32)
        center = jnp.sum(value, axis=-1, keepdims=True) / width
        square = jnp.sum(jnp.square(value - center), axis=-1, keepdims=True)
        lane = lax.broadcasted_iota(jnp.int32, (fresh_len, LANES), 1)
        stats[index] = jnp.where(lane == 0, center, jnp.where(lane == 1, square, 0.0))
        return carry

    lax.fori_loop(0, req_count, measure, 0)


def norm_kernel(picks, arrivals, gain, bias, *refs):
    stats, outs = refs[:-2], refs[-2:]
    depth = len(stats)
    width = arrivals.shape[2]
    blocks, rows, block = outs[0].shape
    fresh_len = arrivals.shape[1]
    held_count = rows // fresh_len
    for part, out in enumerate(outs):
        for item in range(held_count):
            index = picks[part * held_count + item]
            pairs = [ref[index] for ref in stats]
            center = sum(pair[:, 0:1] for pair in pairs) / depth
            square = sum(
                pair[:, 1:2] + width * jnp.square(pair[:, 0:1] - center) for pair in pairs
            )
            scale = lax.rsqrt(square / (depth * width) + EPS)
            value = (arrivals[index].astype(jnp.float32) - center) * scale
            value = (value * gain[...] + bias[...]).astype(jnp.bfloat16)
            for place in range(blocks):
                out[place, item * fresh_len : (item + 1) * fresh_len, :] = value[
                    :, place * block : (place + 1) * block
                ]


def project_kernel(fresh_len, held_count, part, place, source, *refs):
    groups = len(refs) - 10
    tokens = refs[:groups]
    own_rows, other_rows = refs[groups : groups + 2]
    out, held, weights, picked, ready, sems, weight_sems, out_sems = refs[groups + 2 :]
    core, begin = place[0], place[1]
    depth = own_rows.shape[0]
    copies = [
        pltpu.make_async_copy(
            own_rows,
            weights.at[pl.ds(pl.multiple_of(core * depth, 16), depth)],
            weight_sems.at[0],
        ),
        pltpu.make_async_copy(
            other_rows,
            weights.at[pl.ds(pl.multiple_of((1 - core) * depth, 16), depth)],
            weight_sems.at[1],
        ),
    ]
    chips = groups // 2
    copies += [
        pltpu.make_async_copy(
            token,
            held.at[
                pl.ds(
                    (index // chips * chips + (index % chips ^ begin)) * held_count, held_count
                )
            ],
            sems.at[index],
        )
        for index, token in enumerate(tokens)
    ]
    for copy in copies:
        copy.start()
    for copy in copies:
        copy.wait()
    rows = held_count * fresh_len
    together = min(groups, 4)
    for first in range(0, groups, together):
        for item in range(together * held_count):
            picked[item * fresh_len : (item + 1) * fresh_len, :] = held[
                source[(part * groups + first) * held_count + item]
            ]
        result = jnp.dot(picked[...], weights[...], preferred_element_type=jnp.float32).astype(
            jnp.bfloat16
        )
        for index in range(together):
            ready[first + index] = result[index * rows : (index + 1) * rows]
        targets = pl.ds(first, together)
        copies.append(
            pltpu.make_async_copy(
                ready.at[targets], out.at[targets], out_sems.at[first // together]
            )
        )
        copies[-1].start()
    for copy in copies[groups + 2 :]:
        copy.wait()


def attend_kernel(shape, slots, all_lengths, table, *refs):
    groups, held_count, fresh_len, page, heads, part = shape
    parts, bias, cosine, sine_up, sine_down, key_pool, value_pool = refs[:7]
    before = refs[7:-6]
    outs = refs[-6:-3]
    keys, values, sems = refs[-3:]
    chunk = CHUNK_PAGES * page
    pairs = heads // 2

    slot = [slots[part * held_count + index] for index in range(held_count)]
    lengths = [all_lengths[slot[index]] for index in range(held_count)]
    counts = [pl.cdiv(lengths[index], chunk) for index in range(held_count)]
    bases = [jnp.int32(0)]
    for count in counts[:-1]:
        bases.append(bases[-1] + count * CHUNK_PAGES)

    def copies(index, entry):
        number = table[slot[index], entry]
        to = bases[index] + entry
        return (
            pltpu.make_async_copy(key_pool.at[number], keys.at[to], sems.at[index]),
            pltpu.make_async_copy(value_pool.at[number], values.at[to], sems.at[index]),
        )

    for index in range(held_count):

        def start(entry, carry, index=index):
            for copy in copies(index, entry):
                copy.start()
            return carry

        lax.fori_loop(0, counts[index] * CHUNK_PAGES, start, 0)

    def cached(pages, index, part, pair):
        held = pages[
            pl.ds(bases[index] + part * CHUNK_PAGES, CHUNK_PAGES),
            :,
            starts[pair] : starts[pair] + WINDOW,
        ]
        return held.reshape(chunk, WINDOW)

    halves = [
        sum(parts[index].astype(jnp.float32) for index in range(side, groups, 2))
        for side in range(2)
    ]
    halves = [
        half + bias[:, side * half.shape[1] : (side + 1) * half.shape[1]]
        for side, half in enumerate(halves)
    ]

    def kind(which):
        pieces = []
        for head in range(heads):
            half = halves[head // pairs]
            begin = (head % pairs) * 3 * HEAD + which * HEAD
            pieces.append(half[:, begin : begin + HEAD])
        return jnp.concatenate(pieces, axis=1)

    width = heads * HEAD

    def rows_of(ref):
        return jnp.concatenate([ref[slot[index]] for index in range(held_count)], axis=0)

    cosine, sine_up, sine_down = rows_of(cosine), rows_of(sine_up), rows_of(sine_down)

    def turn(block):
        half_rot = ROT // 2
        return (
            block * cosine
            + pltpu.roll(block, width - half_rot, 1) * sine_up
            + pltpu.roll(block, half_rot, 1) * sine_down
        )

    queries = turn(kind(0)).astype(jnp.bfloat16)
    turned = turn(kind(1)).astype(jnp.bfloat16)
    plain = kind(2).astype(jnp.bfloat16)

    def put(which, index, value):
        outs[which][slot[index] if before else index] = value

    for which, held in enumerate(before):
        for index in range(held_count):
            outs[which][slots[index]] = held[index]
    for index in range(held_count):
        rows = slice(index * fresh_len, (index + 1) * fresh_len)
        put(1, index, turned[rows])
        put(2, index, plain[rows])

    factor = 1.0 / math.sqrt(HEAD) / math.log(2.0)
    starts = [(2 * HEAD * pair) // LANES * LANES for pair in range(pairs)]
    lane = lax.broadcasted_iota(jnp.int32, (fresh_len, WINDOW), 1)

    def owned(pair, member):
        begin = (2 * pair + member) * HEAD - starts[pair]
        return (lane >= begin) & (lane < begin + HEAD)

    def contract(left, right):
        return lax.dot_general(
            left, right, (((1,), (1,)), ((), ())), preferred_element_type=jnp.float32
        )

    zero = jnp.zeros((fresh_len, WINDOW), jnp.bfloat16)
    spread_rows = heads * fresh_len
    row = lax.broadcasted_iota(jnp.int32, (2 * fresh_len, fresh_len), 0)
    causal_pair = lax.rem(row, fresh_len) >= lax.broadcasted_iota(
        jnp.int32, (2 * fresh_len, fresh_len), 1
    )
    for index in range(held_count):
        rows = slice(index * fresh_len, (index + 1) * fresh_len)
        spread = []
        for pair in range(pairs):
            window = queries[rows, starts[pair] : starts[pair] + WINDOW]
            spread.append(
                jnp.concatenate(
                    [jnp.where(owned(pair, member), window, zero) for member in range(2)], axis=0
                )
            )
        scores = jnp.concatenate(
            [
                jnp.where(
                    causal_pair,
                    contract(spread[pair], turned[rows, starts[pair] : starts[pair] + WINDOW]),
                    -1e30,
                )
                for pair in range(pairs)
            ],
            axis=0,
        )
        peak = jnp.max(scores, axis=1, keepdims=True)
        weight = jnp.exp2((scores - peak) * factor)
        denom = jnp.sum(weight, axis=1, keepdims=True)
        weight = weight.astype(jnp.bfloat16)
        mixed = jnp.concatenate(
            [
                jnp.dot(
                    weight[pair * 2 * fresh_len : (pair + 1) * 2 * fresh_len],
                    plain[rows, starts[pair] : starts[pair] + WINDOW],
                    preferred_element_type=jnp.float32,
                )
                for pair in range(pairs)
            ],
            axis=0,
        )

        def finish(entry, carry, index=index):
            for copy in copies(index, entry):
                copy.wait()
            return carry

        lax.fori_loop(0, counts[index] * CHUNK_PAGES, finish, 0)

        def step(part, carry, index=index, spread=spread):
            peak, denom, mixed = carry
            scores = jnp.concatenate(
                [
                    contract(spread[pair], cached(keys, index, part, pair))
                    for pair in range(pairs)
                ],
                axis=0,
            )
            position = part * chunk + lax.broadcasted_iota(jnp.int32, (spread_rows, chunk), 1)
            scores = jnp.where(position < lengths[index], scores, -1e30)
            higher = jnp.maximum(peak, jnp.max(scores, axis=1, keepdims=True))
            shrink = jnp.exp2((peak - higher) * factor)
            weight = jnp.exp2((scores - higher) * factor)
            denom = denom * shrink + jnp.sum(weight, axis=1, keepdims=True)
            weight = weight.astype(jnp.bfloat16)
            added = jnp.concatenate(
                [
                    jnp.dot(
                        weight[pair * 2 * fresh_len : (pair + 1) * 2 * fresh_len],
                        cached(values, index, part, pair),
                        preferred_element_type=jnp.float32,
                    )
                    for pair in range(pairs)
                ],
                axis=0,
            )
            return higher, denom, mixed * shrink + added

        peak, denom, mixed = lax.fori_loop(0, counts[index], step, (peak, denom, mixed))
        mixed = mixed / denom
        tiles = [None] * (width // LANES)
        for pair in range(pairs):
            for member in range(2):
                begin = (2 * pair + member) * fresh_len
                part = jnp.where(owned(pair, member), mixed[begin : begin + fresh_len], 0.0)
                for side in range(2):
                    place_at = starts[pair] // LANES + side
                    tile = part[:, side * LANES : (side + 1) * LANES]
                    tiles[place_at] = tile if tiles[place_at] is None else tiles[place_at] + tile
        put(0, index, jnp.concatenate(tiles, axis=1).astype(jnp.bfloat16))


def per_device(
    req_size,
    wgt_size,
    arrivals,
    group_of,
    lengths,
    page_table,
    ln_gain,
    ln_bias,
    w_qkv,
    qkv_bias,
    key_pool,
    value_pool,
):
    req_count, fresh_len, width = arrivals.shape
    rows = req_count * fresh_len
    depth, local_cols = w_qkv.shape
    half_cols = local_cols // 2
    heads = local_cols // (3 * HEAD)
    page = key_pool.shape[1]
    chips = req_size // 2
    block = 2 * depth
    everyone = group_of.shape[0]
    me = lax.axis_index("req")
    layer = lax.axis_index("wgt")
    core = me & 1
    chip = me >> 1

    def swap(value, distance):
        return lax.ppermute(
            value, "req", [(device, device ^ distance) for device in range(req_size)]
        )

    def after(value, others):
        return lax.optimization_barrier((value, others))[0]

    half = req_count // 2
    slots, sources, picks, stats = pl.pallas_call(
        functools.partial(plan_kernel, req_count),
        out_shape=[
            jax.ShapeDtypeStruct((2 * half,), jnp.int32),
            jax.ShapeDtypeStruct((2 * req_size * half,), jnp.int32),
            jax.ShapeDtypeStruct((2 * half,), jnp.int32),
            jax.ShapeDtypeStruct((req_count, fresh_len, LANES), jnp.float32),
        ],
        in_specs=[SMEM, SMEM, VMEM],
        out_specs=[SMEM, SMEM, SMEM, VMEM],
        scratch_shapes=[
            pltpu.SMEM((everyone,), jnp.int32),
            pltpu.SMEM((everyone,), jnp.int32),
            pltpu.SMEM((everyone,), jnp.int32),
            pltpu.SMEM((req_size,), jnp.int32),
        ],
        name="plan",
    )(jnp.stack([me]).astype(jnp.int32), group_of, arrivals)

    lane = np.arange(heads * HEAD) % HEAD
    half_rot = ROT // 2
    inverse = jnp.power(10000.0, -jnp.asarray(lane % half_rot, jnp.float32) * 2.0 / ROT)
    positions = (
        lengths[:, None] + jnp.arange(fresh_len, dtype=jnp.int32)[None, :]
    ).astype(jnp.float32)
    angles = positions.reshape(rows, 1) * inverse[None, :]
    turns = jnp.asarray(lane < ROT)[None, :]
    cosine = jnp.where(turns, jnp.cos(angles), 1.0)
    sine = jnp.sin(angles)
    sine_up = jnp.where(jnp.asarray(lane < half_rot)[None, :], -sine, 0.0)
    sine_down = jnp.where(turns & jnp.asarray(lane >= half_rot)[None, :], sine, 0.0)

    tables = [
        value.reshape(req_count, fresh_len, heads * HEAD)
        for value in (cosine, sine_up, sine_down)
    ]
    layer = lax.axis_index("wgt")
    per = chips // wgt_size
    gain, shift = (
        lax.dynamic_slice_in_dim(value, layer * width, width).astype(jnp.float32).reshape(1, width)
        for value in (ln_gain, ln_bias)
    )
    bias = qkv_bias.astype(jnp.float32).reshape(1, local_cols)
    place = jnp.stack([core, layer * per + chip % per]).astype(jnp.int32)
    chunk_rows = half * fresh_len
    span = page_table.shape[1]
    pages = span + (half - 1) * (span // 2)

    measured = [stats] + [
        lax.ppermute(stats, "wgt", [(at, at ^ distance) for at in range(wgt_size)])
        for distance in range(1, wgt_size)
    ]
    normed = pl.pallas_call(
        norm_kernel,
        out_shape=[jax.ShapeDtypeStruct((per, chunk_rows, block), jnp.bfloat16)] * 2,
        in_specs=[SMEM] + [VMEM] * (3 + wgt_size),
        out_specs=[VMEM] * 2,
        compiler_params=pltpu.CompilerParams(vmem_limit_bytes=VMEM_LIMIT),
        name="norm",
    )(picks, arrivals, gain, shift, *measured)

    def route(value, turn):
        pairs = []
        for device in range(req_size):
            for at in range(wgt_size):
                to = device // 2
                origin = turn ^ (at * per + to % per)
                pairs.append(
                    ((2 * origin + device % 2) * wgt_size + to // per, device * wgt_size + at)
                )
        return lax.ppermute(value, ("req", "wgt"), pairs)

    pieces = []
    for part in range(2):
        received = []
        for turn in range(chips):
            sent = normed[part]
            sent = sent[0] if per == 1 else lax.dynamic_index_in_dim(
                sent, (chip ^ turn) % per, 0, False
            )
            if part:
                sent = after(sent, pieces[0][turn])
            received.append(route(sent, turn))
        pieces.append(received)

    rows_held = after(w_qkv, stats)
    own_rows = lax.dynamic_slice_in_dim(rows_held, core * half_cols, half_cols, 1)
    other_rows = swap(
        lax.dynamic_slice_in_dim(rows_held, (1 - core) * half_cols, half_cols, 1), 1
    )

    projected = []
    for part in range(2):
        tokens = pieces[part] + [swap(piece, 1) for piece in pieces[part]]

        partial = pl.pallas_call(
            functools.partial(project_kernel, fresh_len, half, part),
            out_shape=jax.ShapeDtypeStruct((req_size, chunk_rows, half_cols), jnp.bfloat16),
            in_specs=[SMEM] * 2 + [HBM] * (req_size + 2),
            out_specs=HBM,
            scratch_shapes=[
                pltpu.VMEM((req_size * half, fresh_len, block), jnp.bfloat16),
                pltpu.VMEM((block, half_cols), jnp.bfloat16),
                pltpu.VMEM((min(req_size, 4) * chunk_rows, block), jnp.bfloat16),
                pltpu.VMEM((req_size, chunk_rows, half_cols), jnp.bfloat16),
                pltpu.SemaphoreType.DMA((req_size,)),
                pltpu.SemaphoreType.DMA((2,)),
                pltpu.SemaphoreType.DMA((req_size // min(req_size, 4),)),
            ],
            compiler_params=pltpu.CompilerParams(vmem_limit_bytes=VMEM_LIMIT),
            name="project",
        )(
            place,
            sources,
            *[token.reshape(half, fresh_len, block) for token in tokens],
            own_rows,
            other_rows,
        )

        projected.append(partial)

    results = []
    for part in range(2):
        parts = lax.all_to_all(projected[part], "req", 0, 0, tiled=True)
        if part == 0:
            parts = after(parts, projected[1])

        operands = [
            slots, lengths, page_table, parts, bias, *tables, key_pool, value_pool
        ]
        specs = [SMEM] * 3 + [VMEM] * 5 + [HBM] * 2
        count = half if part == 0 else req_count
        out = jax.ShapeDtypeStruct((count, fresh_len, heads * HEAD), jnp.bfloat16)
        results = pl.pallas_call(
            functools.partial(
                attend_kernel, (req_size, half, fresh_len, page, heads, part)
            ),
            out_shape=[out] * 3,
            in_specs=specs + [VMEM] * len(results),
            out_specs=[VMEM] * 3,
            scratch_shapes=[
                pltpu.VMEM((pages, page, heads * HEAD), jnp.bfloat16),
                pltpu.VMEM((pages, page, heads * HEAD), jnp.bfloat16),
                pltpu.SemaphoreType.DMA((half,)),
            ],
            compiler_params=pltpu.CompilerParams(vmem_limit_bytes=VMEM_LIMIT),
            name="attend",
        )(*operands, *results)
    return results


def solution(mesh):
    in_specs = (
        P("req", None, "wgt"),
        P(),
        P("req"),
        P("req", None),
        P(),
        P(),
        P("req", "wgt"),
        P("wgt"),
        P("req", None, "wgt"),
        P("req", None, "wgt"),
    )
    out_specs = (P("req", None, "wgt"), P("req", None, "wgt"), P("req", None, "wgt"))
    return jax.shard_map(
        functools.partial(per_device, mesh.shape["req"], mesh.shape["wgt"]),
        mesh=mesh,
        in_specs=in_specs,
        out_specs=out_specs,
        check_vma=False,
    )
```

profile of v0, /device:TPU:0, one launch (start us, length us, event | category | flops | bytes accessed | tf_op | source)
XLA Modules:
  0.0 156.8 jit_solution(6893607983522592319)
XLA Ops:
  0.6 3.6 %plan.1 = (s32[4]{0:T(128)}, s32[32]{0:T(128)}, s32[4]{0:T(128)}, f32[4,48,128]{2,1,0:T(8,128)}) custom-call(s32[1]{0:T(128)} %bitcast.place, s32[32]{0:T(128)} %group_of.1, bf16[4,48,1536]{2,1,0:T(8,128)(2,1)} %arrivals.3), custom_call_target="tpu_custom_call" | custom-call | tf_op jit(solution)/shard_map/plan/pallas_call | solution.py:406
  4.3 3.6 %constant_dynamic-slice_fusion = (bf16[768,1152]{1,0:T(8,128)(2,1)S(1)}, bf16[768,1152]{1,0:T(8,128)(2,1)}) fusion(bf16[768,2304]{1,0:T(8,128)(2,1)} %param.20, s32[]{:T(128)S(6)} %select_n.30, s32[]{:T(128)S(6)} %select_n.29), kind=kLoop, calls=%fused_computation.10 | loop fusion | bytes 7077896 | tf_op jit(solution)/shard_map/dynamic_slice | solution.py:494
  7.8 0.5 collective-permute-start.15
  8.3 2.6 %collective-permute-start = (f32[4,48,128]{2,1,0:T(8,128)}, f32[4,48,128]{2,1,0:T(8,128)}, u32[]{:S(2)}, u32[]{:S(2)}) collective-permute-start(f32[4,48,128]{2,1,0:T(8,128)} %get-tuple-element.21.refs_0_), channel_id=1, source_target_pairs={{0,1},{1,0},{2,3},{3,2},{4,5},{5,4},{6,7},{7,6},{8,9},{9,8},{10,11... | collective-permute-start | bytes 294920 | tf_op jit(solution)/shard_map/ppermute | solution.py:455
  10.8 2.6 %collective-permute-start.1 = (f32[4,48,128]{2,1,0:T(8,128)}, f32[4,48,128]{2,1,0:T(8,128)}, u32[]{:S(2)}, u32[]{:S(2)}) collective-permute-start(f32[4,48,128]{2,1,0:T(8,128)} %get-tuple-element.21.refs_0_), channel_id=1, source_target_pairs={{0,2},{1,3},{2,0},{3,1},{4,6},{5,7},{6,4},{7,5},{8,10},{9,11},{10,... | collective-permute-start | bytes 294920 | tf_op jit(solution)/shard_map/ppermute | solution.py:455
  13.4 0.0 collective-permute-start.2
  13.4 0.8 dynamic-slice_convert_fusion
  14.2 0.6 reshape.157.gain
  14.8 0.6 reshape.159.bias
  15.4 0.0 collective-permute-done.refs_1_
  15.4 6.5 %collective-permute-done.1.refs_2_ = f32[4,48,128]{2,1,0:T(8,128)} collective-permute-done((f32[4,48,128]{2,1,0:T(8,128)}, f32[4,48,128]{2,1,0:T(8,128)}, u32[]{:S(2)}, u32[]{:S(2)}) %collective-permute-start.1) | collective-permute-done | bytes 98336 | tf_op jit(solution)/shard_map/ppermute | solution.py:455
  21.9 0.0 collective-permute-done.2.refs_3_
  21.9 2.4 %norm.1 = (bf16[1,96,1536]{2,1,0:T(8,128)(2,1)}, bf16[1,96,1536]{2,1,0:T(8,128)(2,1)}) custom-call(s32[4]{0:T(128)} %get-tuple-element.20.picks, bf16[4,48,1536]{2,1,0:T(8,128)(2,1)} %arrivals.3, f32[1,1536]{1,0:T(1,128)} %reshape.157.gain, f32[1,1536]{1,0:T(1,128)} %reshape.159.bias, f32[4,48,128]{2,1,0:T(8,128)} %get-tuple-element.21.refs_0_, ...), custom_call_target="tpu_custom_call" | custom-call | tf_op jit(solution)/shard_map/norm/pallas_call | solution.py:458
  24.3 1.6 %collective-permute-start.3 = (bf16[96,1536]{1,0:T(8,128)(2,1)}, bf16[96,1536]{1,0:T(8,128)(2,1)S(1)}, u32[]{:S(2)}, u32[]{:S(2)}) collective-permute-start(bf16[96,1536]{1,0:T(8,128)(2,1)} %bitcast.41), channel_id=1, source_target_pairs={{0,0},{8,1},{16,2},{24,3},{4,4},{12,5},{20,6},{28,7},{1,8},{9,9},{... | collective-permute-start | bytes 884744 | tf_op jit(solution)/shard_map/ppermute | solution.py:476
  25.9 3.3 %collective-permute-start.5 = (bf16[96,1536]{1,0:T(8,128)(2,1)}, bf16[96,1536]{1,0:T(8,128)(2,1)S(1)}, u32[]{:S(2)}, u32[]{:S(2)}) collective-permute-start(bf16[96,1536]{1,0:T(8,128)(2,1)} %bitcast.42), channel_id=1, source_target_pairs={{8,0},{0,1},{24,2},{16,3},{12,4},{4,5},{28,6},{20,7},{9,8},{1,9},{... | collective-permute-start | bytes 884744 | tf_op jit(solution)/shard_map/ppermute | solution.py:476
  29.2 3.9 %collective-permute-start.7 = (bf16[96,1536]{1,0:T(8,128)(2,1)}, bf16[96,1536]{1,0:T(8,128)(2,1)S(1)}, u32[]{:S(2)}, u32[]{:S(2)}) collective-permute-start(bf16[96,1536]{1,0:T(8,128)(2,1)} %bitcast.43), channel_id=1, source_target_pairs={{16,0},{24,1},{0,2},{8,3},{20,4},{28,5},{4,6},{12,7},{17,8},{25,9}... | collective-permute-start | bytes 884744 | tf_op jit(solution)/shard_map/ppermute | solution.py:476
  33.1 0.4 collective-permute-start.9
  33.5 0.0 collective-permute-done.3
  33.5 0.0 collective-permute-start.16
  33.5 3.1 %collective-permute-done.5 = bf16[96,1536]{1,0:T(8,128)(2,1)S(1)} collective-permute-done((bf16[96,1536]{1,0:T(8,128)(2,1)}, bf16[96,1536]{1,0:T(8,128)(2,1)S(1)}, u32[]{:S(2)}, u32[]{:S(2)}) %collective-permute-start.5) | collective-permute-done | bytes 294944 | tf_op jit(solution)/shard_map/ppermute | solution.py:476
  36.7 0.0 collective-permute-start.17
  36.7 8.8 %collective-permute-done.7 = bf16[96,1536]{1,0:T(8,128)(2,1)S(1)} collective-permute-done((bf16[96,1536]{1,0:T(8,128)(2,1)}, bf16[96,1536]{1,0:T(8,128)(2,1)S(1)}, u32[]{:S(2)}, u32[]{:S(2)}) %collective-permute-start.7) | collective-permute-done | bytes 294944 | tf_op jit(solution)/shard_map/ppermute | solution.py:476
  45.5 1.8 %collective-permute-done.9 = bf16[96,1536]{1,0:T(8,128)(2,1)S(1)} collective-permute-done((bf16[96,1536]{1,0:T(8,128)(2,1)}, bf16[96,1536]{1,0:T(8,128)(2,1)S(1)}, u32[]{:S(2)}, u32[]{:S(2)}) %collective-permute-start.9) | collective-permute-done | bytes 294944 | tf_op jit(solution)/shard_map/ppermute | solution.py:476
  47.2 0.7 pad_add_fusion.place
  47.9 0.0 collective-permute-done.17
  48.0 0.9 collective-permute-done.19
  48.8 0.0 collective-permute-done.15.refs_9_
  48.9 0.6 copy-done.17
  49.5 0.6 copy-done.2
  50.1 7.7 %project.3 = bf16[8,96,1152]{2,1,0:T(8,128)(2,1)} custom-call(s32[2]{0:T(128)} %pad_add_fusion.place, s32[32]{0:T(128)} %get-tuple-element.19.source, bf16[2,48,1536]{2,1,0:T(8,128)(2,1)} %bitcast.21, bf16[2,48,1536]{2,1,0:T(8,128)(2,1)} %bitcast.22, bf16[2,48,1536]{2,1,0:T(8,128)(2,1)} %bitcast.24, bf16[2,48,1536]{2,1,0:T(8,128)(2,1)} %bitcast.26, ...), custom_call_target="tpu_custom_call" | custom-call | tf_op jit(solution)/shard_map/project/pallas_call | solution.py:501
  57.8 0.0 copy-start.22
  57.8 16.2 %all-to-all-start.1 = ((bf16[8,96,1152]{2,1,0:T(8,128)(2,1)}), bf16[8,96,1152]{2,1,0:T(8,128)(2,1)S(1)}, u32[]{:S(2)}, u32[]{:S(2)}) async-start(bf16[8,96,1152]{2,1,0:T(8,128)(2,1)} %project.3), calls=%async_computation.1 | async-start | bytes 3538944 | tf_op jit(solution)/shard_map/all_to_all | solution.py:529
  74.1 0.1 collective-permute-start.8
  74.1 3.4 %collective-permute-start.10 = (bf16[96,1536]{1,0:T(8,128)(2,1)S(1)}, bf16[96,1536]{1,0:T(8,128)(2,1)S(1)}, u32[]{:S(2)}, u32[]{:S(2)}) collective-permute-start(bf16[96,1536]{1,0:T(8,128)(2,1)S(1)} %bitcast.38), channel_id=1, source_target_pairs={{24,0},{16,1},{8,2},{0,3},{28,4},{20,5},{12,6},{4,7},{25,8},{17,9}... | collective-permute-start | bytes 884744 | tf_op jit(solution)/shard_map/ppermute | solution.py:476
  77.5 3.1 %collective-permute-start.6 = (bf16[96,1536]{1,0:T(8,128)(2,1)S(1)}, bf16[96,1536]{1,0:T(8,128)(2,1)S(1)}, u32[]{:S(2)}, u32[]{:S(2)}) collective-permute-start(bf16[96,1536]{1,0:T(8,128)(2,1)S(1)} %bitcast.39), channel_id=1, source_target_pairs={{8,0},{0,1},{24,2},{16,3},{12,4},{4,5},{28,6},{20,7},{9,8},{1,9},{... | collective-permute-start | bytes 884744 | tf_op jit(solution)/shard_map/ppermute | solution.py:476
  80.6 0.7 collective-permute-start.4
  81.3 23.1 %collective-permute-done.8 = bf16[96,1536]{1,0:T(8,128)(2,1)S(1)} collective-permute-done((bf16[96,1536]{1,0:T(8,128)(2,1)S(1)}, bf16[96,1536]{1,0:T(8,128)(2,1)S(1)}, u32[]{:S(2)}, u32[]{:S(2)}) %collective-permute-start.8) | collective-permute-done | bytes 294944 | tf_op jit(solution)/shard_map/ppermute | solution.py:476
  104.4 0.0 collective-permute-start.13
  104.4 5.5 %collective-permute-done.10 = bf16[96,1536]{1,0:T(8,128)(2,1)S(1)} collective-permute-done((bf16[96,1536]{1,0:T(8,128)(2,1)S(1)}, bf16[96,1536]{1,0:T(8,128)(2,1)S(1)}, u32[]{:S(2)}, u32[]{:S(2)}) %collective-permute-start.10) | collective-permute-done | bytes 294944 | tf_op jit(solution)/shard_map/ppermute | solution.py:476
  109.9 0.0 collective-permute-start.14
  109.9 0.0 collective-permute-done.6
  109.9 0.0 copy-start.9
  109.9 0.5 collective-permute-start.12
  110.4 0.0 collective-permute-done.4
  110.4 0.1 collective-permute-start.11
  110.5 0.0 collective-permute-done.13
  110.5 1.0 collective-permute-done.14
  111.5 0.4 collective-permute-done.12
  111.9 0.4 collective-permute-done.11
  112.4 0.3 copy-done.16
  112.7 0.4 copy-done.18
  113.1 7.7 %project.2 = bf16[8,96,1152]{2,1,0:T(8,128)(2,1)} custom-call(s32[2]{0:T(128)} %pad_add_fusion.place, s32[32]{0:T(128)} %get-tuple-element.19.source, bf16[2,48,1536]{2,1,0:T(8,128)(2,1)} %bitcast.28, bf16[2,48,1536]{2,1,0:T(8,128)(2,1)} %bitcast.27, bf16[2,48,1536]{2,1,0:T(8,128)(2,1)} %bitcast.23, bf16[2,48,1536]{2,1,0:T(8,128)(2,1)} %bitcast.25, ...), custom_call_target="tpu_custom_call" | custom-call | tf_op jit(solution)/shard_map/project/pallas_call | solution.py:501
  120.8 0.0 copy-start.19
  120.8 0.0 copy-start.20
  120.8 0.0 copy-start.21
  120.9 1.3 copy-done
  122.1 3.6 %all-to-all-start = ((bf16[8,96,1152]{2,1,0:T(8,128)(2,1)}), bf16[8,96,1152]{2,1,0:T(8,128)(2,1)S(1)}, u32[]{:S(2)}, u32[]{:S(2)}) async-start(bf16[8,96,1152]{2,1,0:T(8,128)(2,1)} %project.2), calls=%async_computation | async-start | bytes 3538944 | tf_op jit(solution)/shard_map/all_to_all | solution.py:529
  125.7 0.6 reshape.161.refs_1_
  126.3 0.1 add_convert_fusion
  126.4 4.1 %fusion = (f32[4,48,768]{2,1,0:T(8,128)}, f32[4,48,768]{2,1,0:T(8,128)}, f32[4,48,768]{2,1,0:T(8,128)}) fusion(f32[768]{0:T(1024)S(1)} %copy-done.21, f32[4,48]{1,0:T(4,128)S(1)} %add_convert_fusion, pred[768]{0:T(1024)(128)(4,1)} %constant.60, pred[768]{0:T(1024)(128)(4,1)} %constant.52.clone, pred[768]{0:T(1024)(128)(4,1)} %constant.51.clone), kind=kLoop, calls=%fused_computation.2 | loop fusion | flops 737280 | bytes 1775616 | tf_op jit(solution)/shard_map/jit(_where)/select_n | solution.py:436
  130.5 11.2 %attend.2 = (bf16[2,48,768]{2,1,0:T(8,128)(2,1)}, bf16[2,48,768]{2,1,0:T(8,128)(2,1)}, bf16[2,48,768]{2,1,0:T(8,128)(2,1)}) custom-call(s32[4]{0:T(128)} %get-tuple-element.18.slots, s32[4]{0:T(128)} %all_lengths.3, s32[4,16]{1,0:T(4,128)} %table.3, bf16[8,96,1152]{2,1,0:T(8,128)(2,1)} %copy-done, f32[1,2304]{1,0:T(1,128)} %reshape.161.refs_1_, ...), custom_call_target="tpu_custom_call" | custom-call | tf_op jit(solution)/shard_map/attend/pallas_call | solution.py:539
  141.7 7.1 %all-to-all-done.refs_0_ = bf16[8,96,1152]{2,1,0:T(8,128)(2,1)S(1)} async-done(((bf16[8,96,1152]{2,1,0:T(8,128)(2,1)}), bf16[8,96,1152]{2,1,0:T(8,128)(2,1)S(1)}, u32[]{:S(2)}, u32[]{:S(2)}) %all-to-all-start) | async-done | bytes 1769504 | tf_op jit(solution)/shard_map/all_to_all | solution.py:529
  148.8 1.3 copy-done.1
  150.0 6.7 %attend.3 = (bf16[4,48,768]{2,1,0:T(8,128)(2,1)}, bf16[4,48,768]{2,1,0:T(8,128)(2,1)}, bf16[4,48,768]{2,1,0:T(8,128)(2,1)}) custom-call(s32[4]{0:T(128)} %get-tuple-element.18.slots, s32[4]{0:T(128)} %all_lengths.3, s32[4,16]{1,0:T(4,128)} %table.3, bf16[8,96,1152]{2,1,0:T(8,128)(2,1)} %copy-done.1, f32[1,2304]{1,0:T(1,128)} %reshape.161.refs_1_, ...), custom_call_target="tpu_custom_call" | custom-call | tf_op jit(solution)/shard_map/attend/pallas_call | solution.py:539
  (40 shorter events, 0.1 us)
Async XLA Ops:
  7.8 41.0 %collective-permute-start.15 = (bf16[768,1152]{1,0:T(8,128)(2,1)S(1)}, bf16[768,1152]{1,0:T(8,128)(2,1)S(1)}, u32[]{:S(2)}, u32[]{:S(2)}) collective-permute-start(bf16[768,1152]{1,0:T(8,128)(2,1)S(1)} %get-tuple-element.33), channel_id=1, source_target_pairs={{0,4},{4,0},{8,12},{12,8},{16,20},{20,16},{24,28},{28,24},{1,5},{5... | collective-permute-start | bytes 5308424 | tf_op jit(solution)/shard_map/ppermute | solution.py:398
  8.3 7.1 %collective-permute-start = (f32[4,48,128]{2,1,0:T(8,128)}, f32[4,48,128]{2,1,0:T(8,128)}, u32[]{:S(2)}, u32[]{:S(2)}) collective-permute-start(f32[4,48,128]{2,1,0:T(8,128)} %get-tuple-element.21.refs_0_), channel_id=1, source_target_pairs={{0,1},{1,0},{2,3},{3,2},{4,5},{5,4},{6,7},{7,6},{8,9},{9,8},{10,11... | collective-permute-start | bytes 294920 | tf_op jit(solution)/shard_map/ppermute | solution.py:455
  10.8 11.1 %collective-permute-start.1 = (f32[4,48,128]{2,1,0:T(8,128)}, f32[4,48,128]{2,1,0:T(8,128)}, u32[]{:S(2)}, u32[]{:S(2)}) collective-permute-start(f32[4,48,128]{2,1,0:T(8,128)} %get-tuple-element.21.refs_0_), channel_id=1, source_target_pairs={{0,2},{1,3},{2,0},{3,1},{4,6},{5,7},{6,4},{7,5},{8,10},{9,11},{10,... | collective-permute-start | bytes 294920 | tf_op jit(solution)/shard_map/ppermute | solution.py:455
  13.4 8.5 %collective-permute-start.2 = (f32[4,48,128]{2,1,0:T(8,128)}, f32[4,48,128]{2,1,0:T(8,128)}, u32[]{:S(2)}, u32[]{:S(2)}) collective-permute-start(f32[4,48,128]{2,1,0:T(8,128)} %get-tuple-element.21.refs_0_), channel_id=1, source_target_pairs={{0,3},{1,2},{2,1},{3,0},{4,7},{5,6},{6,5},{7,4},{8,11},{9,10},{10,... | collective-permute-start | bytes 294920 | tf_op jit(solution)/shard_map/ppermute | solution.py:455
  24.3 9.2 %collective-permute-start.3 = (bf16[96,1536]{1,0:T(8,128)(2,1)}, bf16[96,1536]{1,0:T(8,128)(2,1)S(1)}, u32[]{:S(2)}, u32[]{:S(2)}) collective-permute-start(bf16[96,1536]{1,0:T(8,128)(2,1)} %bitcast.41), channel_id=1, source_target_pairs={{0,0},{8,1},{16,2},{24,3},{4,4},{12,5},{20,6},{28,7},{1,8},{9,9},{... | collective-permute-start | bytes 884744 | tf_op jit(solution)/shard_map/ppermute | solution.py:476
  25.9 10.8 %collective-permute-start.5 = (bf16[96,1536]{1,0:T(8,128)(2,1)}, bf16[96,1536]{1,0:T(8,128)(2,1)S(1)}, u32[]{:S(2)}, u32[]{:S(2)}) collective-permute-start(bf16[96,1536]{1,0:T(8,128)(2,1)} %bitcast.42), channel_id=1, source_target_pairs={{8,0},{0,1},{24,2},{16,3},{12,4},{4,5},{28,6},{20,7},{9,8},{1,9},{... | collective-permute-start | bytes 884744 | tf_op jit(solution)/shard_map/ppermute | solution.py:476
  29.2 16.3 %collective-permute-start.7 = (bf16[96,1536]{1,0:T(8,128)(2,1)}, bf16[96,1536]{1,0:T(8,128)(2,1)S(1)}, u32[]{:S(2)}, u32[]{:S(2)}) collective-permute-start(bf16[96,1536]{1,0:T(8,128)(2,1)} %bitcast.43), channel_id=1, source_target_pairs={{16,0},{24,1},{0,2},{8,3},{20,4},{28,5},{4,6},{12,7},{17,8},{25,9}... | collective-permute-start | bytes 884744 | tf_op jit(solution)/shard_map/ppermute | solution.py:476
  33.1 14.1 %collective-permute-start.9 = (bf16[96,1536]{1,0:T(8,128)(2,1)}, bf16[96,1536]{1,0:T(8,128)(2,1)S(1)}, u32[]{:S(2)}, u32[]{:S(2)}) collective-permute-start(bf16[96,1536]{1,0:T(8,128)(2,1)} %bitcast.44), channel_id=1, source_target_pairs={{24,0},{16,1},{8,2},{0,3},{28,4},{20,5},{12,6},{4,7},{25,8},{17,9}... | collective-permute-start | bytes 884744 | tf_op jit(solution)/shard_map/ppermute | solution.py:476
  33.5 15.3 %copy-start.3 = (bf16[96,1536]{1,0:T(8,128)(2,1)}, bf16[96,1536]{1,0:T(8,128)(2,1)S(1)}, u32[]{:S(2)}) copy-start(bf16[96,1536]{1,0:T(8,128)(2,1)S(1)} %collective-permute-done.3) | copy-start | bytes 884740
  33.5 14.4 %collective-permute-start.16 = (bf16[96,1536]{1,0:T(8,128)(2,1)S(1)}, bf16[96,1536]{1,0:T(8,128)(2,1)S(1)}, u32[]{:S(2)}, u32[]{:S(2)}) collective-permute-start(bf16[96,1536]{1,0:T(8,128)(2,1)S(1)} %collective-permute-done.3), channel_id=1, source_target_pairs={{0,4},{4,0},{8,12},{12,8},{16,20},{20,16},{24,28},{28,24},{1,5},{5... | collective-permute-start | bytes 884744 | tf_op jit(solution)/shard_map/ppermute | solution.py:398
  36.7 12.2 %copy-start.4 = (bf16[96,1536]{1,0:T(8,128)(2,1)}, bf16[96,1536]{1,0:T(8,128)(2,1)S(1)}, u32[]{:S(2)}) copy-start(bf16[96,1536]{1,0:T(8,128)(2,1)S(1)} %collective-permute-done.5) | copy-start | bytes 884740
  36.7 11.3 %collective-permute-start.17 = (bf16[96,1536]{1,0:T(8,128)(2,1)S(1)}, bf16[96,1536]{1,0:T(8,128)(2,1)S(1)}, u32[]{:S(2)}, u32[]{:S(2)}) collective-permute-start(bf16[96,1536]{1,0:T(8,128)(2,1)S(1)} %collective-permute-done.5), channel_id=1, source_target_pairs={{0,4},{4,0},{8,12},{12,8},{16,20},{20,16},{24,28},{28,24},{1,5},{5... | collective-permute-start | bytes 884744 | tf_op jit(solution)/shard_map/ppermute | solution.py:398
  45.5 3.4 %copy-start.6 = (bf16[96,1536]{1,0:T(8,128)(2,1)}, bf16[96,1536]{1,0:T(8,128)(2,1)S(1)}, u32[]{:S(2)}) copy-start(bf16[96,1536]{1,0:T(8,128)(2,1)S(1)} %collective-permute-done.7) | copy-start | bytes 884740
  45.5 2.5 %collective-permute-start.18 = (bf16[96,1536]{1,0:T(8,128)(2,1)S(1)}, bf16[96,1536]{1,0:T(8,128)(2,1)S(1)}, u32[]{:S(2)}, u32[]{:S(2)}) collective-permute-start(bf16[96,1536]{1,0:T(8,128)(2,1)S(1)} %collective-permute-done.7), channel_id=1, source_target_pairs={{0,4},{4,0},{8,12},{12,8},{16,20},{20,16},{24,28},{28,24},{1,5},{5... | collective-permute-start | bytes 884744 | tf_op jit(solution)/shard_map/ppermute | solution.py:398
  47.2 1.6 %copy-start.8 = (bf16[96,1536]{1,0:T(8,128)(2,1)}, bf16[96,1536]{1,0:T(8,128)(2,1)S(1)}, u32[]{:S(2)}) copy-start(bf16[96,1536]{1,0:T(8,128)(2,1)S(1)} %collective-permute-done.9) | copy-start | bytes 884740
  47.2 1.6 %collective-permute-start.19 = (bf16[96,1536]{1,0:T(8,128)(2,1)S(1)}, bf16[96,1536]{1,0:T(8,128)(2,1)S(1)}, u32[]{:S(2)}, u32[]{:S(2)}) collective-permute-start(bf16[96,1536]{1,0:T(8,128)(2,1)S(1)} %collective-permute-done.9), channel_id=1, source_target_pairs={{0,4},{4,0},{8,12},{12,8},{16,20},{20,16},{24,28},{28,24},{1,5},{5... | collective-permute-start | bytes 884744 | tf_op jit(solution)/shard_map/ppermute | solution.py:398
  47.9 0.9 copy-start.11
  47.9 1.0 copy-start.13
  48.0 0.9 copy-start.15
  48.8 0.7 copy-start.17
  48.8 1.3 copy-start.2
  57.8 16.3 %copy-start.22 = (bf16[1,96,1536]{2,1,0:T(8,128)(2,1)S(1)}, bf16[1,96,1536]{2,1,0:T(8,128)(2,1)}, u32[]{:S(2)}) copy-start(bf16[1,96,1536]{2,1,0:T(8,128)(2,1)} %get-tuple-element.22) | copy-start | bytes 884740
  57.8 63.0 %all-to-all-start.1 = ((bf16[8,96,1152]{2,1,0:T(8,128)(2,1)}), bf16[8,96,1152]{2,1,0:T(8,128)(2,1)S(1)}, u32[]{:S(2)}, u32[]{:S(2)}) async-start(bf16[8,96,1152]{2,1,0:T(8,128)(2,1)} %project.3), calls=%async_computation.1 | async-start | bytes 3538944 | tf_op jit(solution)/shard_map/all_to_all | solution.py:529
  74.1 30.3 %collective-permute-start.8 = (bf16[96,1536]{1,0:T(8,128)(2,1)S(1)}, bf16[96,1536]{1,0:T(8,128)(2,1)S(1)}, u32[]{:S(2)}, u32[]{:S(2)}) collective-permute-start(bf16[96,1536]{1,0:T(8,128)(2,1)S(1)} %bitcast.37), channel_id=1, source_target_pairs={{16,0},{24,1},{0,2},{8,3},{20,4},{28,5},{4,6},{12,7},{17,8},{25,9}... | collective-permute-start | bytes 884744 | tf_op jit(solution)/shard_map/ppermute | solution.py:476
  74.1 35.7 %collective-permute-start.10 = (bf16[96,1536]{1,0:T(8,128)(2,1)S(1)}, bf16[96,1536]{1,0:T(8,128)(2,1)S(1)}, u32[]{:S(2)}, u32[]{:S(2)}) collective-permute-start(bf16[96,1536]{1,0:T(8,128)(2,1)S(1)} %bitcast.38), channel_id=1, source_target_pairs={{24,0},{16,1},{8,2},{0,3},{28,4},{20,5},{12,6},{4,7},{25,8},{17,9}... | collective-permute-start | bytes 884744 | tf_op jit(solution)/shard_map/ppermute | solution.py:476
  77.5 32.4 %collective-permute-start.6 = (bf16[96,1536]{1,0:T(8,128)(2,1)S(1)}, bf16[96,1536]{1,0:T(8,128)(2,1)S(1)}, u32[]{:S(2)}, u32[]{:S(2)}) collective-permute-start(bf16[96,1536]{1,0:T(8,128)(2,1)S(1)} %bitcast.39), channel_id=1, source_target_pairs={{8,0},{0,1},{24,2},{16,3},{12,4},{4,5},{28,6},{20,7},{9,8},{1,9},{... | collective-permute-start | bytes 884744 | tf_op jit(solution)/shard_map/ppermute | solution.py:476
  80.6 29.8 %collective-permute-start.4 = (bf16[96,1536]{1,0:T(8,128)(2,1)S(1)}, bf16[96,1536]{1,0:T(8,128)(2,1)S(1)}, u32[]{:S(2)}, u32[]{:S(2)}) collective-permute-start(bf16[96,1536]{1,0:T(8,128)(2,1)S(1)} %bitcast.40), channel_id=1, source_target_pairs={{0,0},{8,1},{16,2},{24,3},{4,4},{12,5},{20,6},{28,7},{1,8},{9,9},{... | collective-permute-start | bytes 884744 | tf_op jit(solution)/shard_map/ppermute | solution.py:476
  104.4 8.0 %copy-start.5 = (bf16[96,1536]{1,0:T(8,128)(2,1)}, bf16[96,1536]{1,0:T(8,128)(2,1)S(1)}, u32[]{:S(2)}) copy-start(bf16[96,1536]{1,0:T(8,128)(2,1)S(1)} %collective-permute-done.8) | copy-start | bytes 884740
  104.4 6.1 %collective-permute-start.13 = (bf16[96,1536]{1,0:T(8,128)(2,1)S(1)}, bf16[96,1536]{1,0:T(8,128)(2,1)S(1)}, u32[]{:S(2)}, u32[]{:S(2)}) collective-permute-start(bf16[96,1536]{1,0:T(8,128)(2,1)S(1)} %collective-permute-done.8), channel_id=1, source_target_pairs={{0,4},{4,0},{8,12},{12,8},{16,20},{20,16},{24,28},{28,24},{1,5},{5... | collective-permute-start | bytes 884744 | tf_op jit(solution)/shard_map/ppermute | solution.py:398
  109.9 2.4 %copy-start.7 = (bf16[96,1536]{1,0:T(8,128)(2,1)}, bf16[96,1536]{1,0:T(8,128)(2,1)S(1)}, u32[]{:S(2)}) copy-start(bf16[96,1536]{1,0:T(8,128)(2,1)S(1)} %collective-permute-done.10) | copy-start | bytes 884740
  109.9 1.6 %collective-permute-start.14 = (bf16[96,1536]{1,0:T(8,128)(2,1)S(1)}, bf16[96,1536]{1,0:T(8,128)(2,1)S(1)}, u32[]{:S(2)}, u32[]{:S(2)}) collective-permute-start(bf16[96,1536]{1,0:T(8,128)(2,1)S(1)} %collective-permute-done.10), channel_id=1, source_target_pairs={{0,4},{4,0},{8,12},{12,8},{16,20},{20,16},{24,28},{28,24},{1,5},{5... | collective-permute-start | bytes 884744 | tf_op jit(solution)/shard_map/ppermute | solution.py:398
  109.9 2.4 %copy-start.9 = (bf16[96,1536]{1,0:T(8,128)(2,1)}, bf16[96,1536]{1,0:T(8,128)(2,1)S(1)}, u32[]{:S(2)}) copy-start(bf16[96,1536]{1,0:T(8,128)(2,1)S(1)} %collective-permute-done.6) | copy-start | bytes 884740
  109.9 2.0 %collective-permute-start.12 = (bf16[96,1536]{1,0:T(8,128)(2,1)S(1)}, bf16[96,1536]{1,0:T(8,128)(2,1)S(1)}, u32[]{:S(2)}, u32[]{:S(2)}) collective-permute-start(bf16[96,1536]{1,0:T(8,128)(2,1)S(1)} %collective-permute-done.6), channel_id=1, source_target_pairs={{0,4},{4,0},{8,12},{12,8},{16,20},{20,16},{24,28},{28,24},{1,5},{5... | collective-permute-start | bytes 884744 | tf_op jit(solution)/shard_map/ppermute | solution.py:398
  110.4 1.9 %copy-start.10 = (bf16[96,1536]{1,0:T(8,128)(2,1)}, bf16[96,1536]{1,0:T(8,128)(2,1)S(1)}, u32[]{:S(2)}) copy-start(bf16[96,1536]{1,0:T(8,128)(2,1)S(1)} %collective-permute-done.4) | copy-start | bytes 884740
  110.4 1.9 %collective-permute-start.11 = (bf16[96,1536]{1,0:T(8,128)(2,1)S(1)}, bf16[96,1536]{1,0:T(8,128)(2,1)S(1)}, u32[]{:S(2)}, u32[]{:S(2)}) collective-permute-start(bf16[96,1536]{1,0:T(8,128)(2,1)S(1)} %collective-permute-done.4), channel_id=1, source_target_pairs={{0,4},{4,0},{8,12},{12,8},{16,20},{20,16},{24,28},{28,24},{1,5},{5... | collective-permute-start | bytes 884744 | tf_op jit(solution)/shard_map/ppermute | solution.py:398
  110.5 1.8 %copy-start.12 = (bf16[96,1536]{1,0:T(8,128)(2,1)}, bf16[96,1536]{1,0:T(8,128)(2,1)S(1)}, u32[]{:S(2)}) copy-start(bf16[96,1536]{1,0:T(8,128)(2,1)S(1)} %collective-permute-done.13) | copy-start | bytes 884740
  111.5 0.9 copy-start.14
  111.9 0.8 copy-start.16
  112.3 0.8 copy-start.18
  120.8 4.9 %copy-start.19 = (bf16[2304]{0:T(1024)(128)(2,1)S(1)}, bf16[2304]{0:T(1024)(128)(2,1)}, u32[]{:S(2)}) copy-start(bf16[2304]{0:T(1024)(128)(2,1)} %param.21) | copy-start | bytes 13828
  120.8 5.5 %copy-start.20 = (s32[4]{0:T(128)S(1)}, s32[4]{0:T(128)}, u32[]{:S(2)}) copy-start(s32[4]{0:T(128)} %all_lengths.3) | copy-start | bytes 52
  120.8 5.6 %copy-start.21 = (f32[768]{0:T(1024)S(1)}, f32[768]{0:T(1024)}, u32[]{:S(2)}) copy-start(f32[768]{0:T(1024)} %constant.59) | copy-start | bytes 9220
  120.9 1.3 copy-start
  122.1 26.7 %all-to-all-start = ((bf16[8,96,1152]{2,1,0:T(8,128)(2,1)}), bf16[8,96,1152]{2,1,0:T(8,128)(2,1)S(1)}, u32[]{:S(2)}, u32[]{:S(2)}) async-start(bf16[8,96,1152]{2,1,0:T(8,128)(2,1)} %project.2), calls=%async_computation | async-start | bytes 3538944 | tf_op jit(solution)/shard_map/all_to_all | solution.py:529
  148.8 1.3 copy-start.1
where the time goes:
time: 160 us; the launch traced here: 157 us
  waiting for transfers between devices  58.6 us (37%)
  starting transfers between devices  42.5 us (27%)
  Pallas kernels  39.3 us (25%)
  local copies, waits for them, and re-layouts  9.89 us (6%)
  other arithmetic  5.62 us (4%)
    ppermute x8, waiting for transfers between devices, route(): return lax.ppermute(value, ('req', 'wgt'), pairs)  42.3 us
    all_to_all x2, starting transfers between devices, per_device(): parts = lax.all_to_all(projected[part], 'req', 0, 0, tiled=True)  19.8 us
    pallas_call x2, Pallas kernels, per_device(): pl.pallas_call(functools.partial(attend_kernel, (req_size, half, fresh_le...  17.9 us
    ppermute x8, starting transfers between devices, route(): return lax.ppermute(value, ('req', 'wgt'), pairs)  16.4 us
    pallas_call x2, Pallas kernels, per_device(): pl.pallas_call(functools.partial(project_kernel, fresh_len, half, part),...  15.4 us
    all_to_all x2, waiting for transfers between devices, per_device(): parts = lax.all_to_all(projected[part], 'req', 0, 0, tiled=True)  7.12 us
    ppermute x3, waiting for transfers between devices, per_device(): lax.ppermute(stats, 'wgt', [(at, at ^ distance) for at in range(wgt_size)])  6.49 us
    ppermute x3, starting transfers between devices, per_device(): lax.ppermute(stats, 'wgt', [(at, at ^ distance) for at in range(wgt_size)])  5.17 us
  transfers between devices with their start and end apart: 22, of which 11 were waited for; matrix products, arithmetic and copies ran while one was open for 5% of the time, Pallas kernels for 14%

commit v1 on v0

--- a/solution.py
+++ b/solution.py
@@ -22,105 +22,28 @@
 HBM = pl.BlockSpec(memory_space=pltpu.HBM)
 
 
-def plan_kernel(req_count, place, group_of, arrivals, slots, sources, picks, stats, *refs):
-    order, slot_of, color, filled = refs
-    everyone = group_of.shape[0]
-    groups = everyone // req_count
-    half = req_count // 2
-    me = place[0]
-
-    def clear(group, carry):
-        filled[group] = 0
-        return carry
-
-    lax.fori_loop(0, groups, clear, 0)
-
-    def rank(item, carry):
-        group = group_of[item]
-        slot = group * req_count + filled[group]
-        filled[group] = filled[group] + 1
-        slot_of[item] = slot
-        order[slot] = item
-        color[item] = -1
-        return carry
-
-    lax.fori_loop(0, everyone, rank, 0)
-
-    shift = req_count.bit_length() - 1
-
-    def note(item, shade):
-        color[item] = shade
-        slot = slot_of[item]
-        to = (shade * groups + (slot >> shift)) * half + ((slot & (req_count - 1)) >> 1)
-        origin = item >> shift
-        row = ((origin & 1) ^ (me & 1)) * (groups // 2) + (origin >> 1)
-        sources[to] = row * half + ((item & (req_count - 1)) >> 1)
-        return slot
-
-    def walk(pair, carry):
-        def body(state):
-            note(state[0], 0)
-            following = order[note(state[0] ^ 1, 1) ^ 1]
-            return following, color[following]
-
-        lax.while_loop(lambda state: state[1] < 0, body, (2 * pair, color[2 * pair]))
-        return carry
-
-    lax.fori_loop(0, everyone // 2, walk, 0)
-
-    for pair in range(half):
-        first = color[me * req_count + 2 * pair]
-        for part in range(2):
-            picks[part * half + pair] = 2 * pair + (first ^ part)
-        first = color[order[me * req_count + 2 * pair]]
-        for part in range(2):
-            slots[part * half + pair] = 2 * pair + (first ^ part)
-
-    fresh_len, width = arrivals.shape[1:]
-
-    def measure(index, carry):
-        value = arrivals[index].astype(jnp.float32)
-        center = jnp.sum(value, axis=-1, keepdims=True) / width
-        square = jnp.sum(jnp.square(value - center), axis=-1, keepdims=True)
-        lane = lax.broadcasted_iota(jnp.int32, (fresh_len, LANES), 1)
-        stats[index] = jnp.where(lane == 0, center, jnp.where(lane == 1, square, 0.0))
-        return carry
-
-    lax.fori_loop(0, req_count, measure, 0)
-
-
-def norm_kernel(picks, arrivals, gain, bias, *refs):
-    stats, outs = refs[:-2], refs[-2:]
-    depth = len(stats)
-    width = arrivals.shape[2]
-    blocks, rows, block = outs[0].shape
-    fresh_len = arrivals.shape[1]
-    held_count = rows // fresh_len
-    for part, out in enumerate(outs):
-        for item in range(held_count):
-            index = picks[part * held_count + item]
-            pairs = [ref[index] for ref in stats]
-            center = sum(pair[:, 0:1] for pair in pairs) / depth
-            square = sum(
-                pair[:, 1:2] + width * jnp.square(pair[:, 0:1] - center) for pair in pairs
-            )
-            scale = lax.rsqrt(square / (depth * width) + EPS)
-            value = (arrivals[index].astype(jnp.float32) - center) * scale
-            value = (value * gain[...] + bias[...]).astype(jnp.bfloat16)
-            for place in range(blocks):
-                out[place, item * fresh_len : (item + 1) * fresh_len, :] = value[
-                    :, place * block : (place + 1) * block
-                ]
-
-
-def project_kernel(fresh_len, held_count, part, place, source, *refs):
-    groups = len(refs) - 10
+def project_kernel(part, place, source, *refs):
+    groups = len(refs) - 14
     tokens = refs[:groups]
-    own_rows, other_rows = refs[groups : groups + 2]
-    out, held, weights, picked, ready, sems, weight_sems, out_sems = refs[groups + 2 :]
+    center, scale, gain, bias, own_rows, other_rows = refs[groups : groups + 6]
+    out, held, weights, picked, ready, sems, weight_sems, out_sems = refs[groups + 6 :]
     core, begin = place[0], place[1]
     depth = own_rows.shape[0]
+    chips = groups // 2
+    req_count, fresh_len = tokens[0].shape[:2]
+    rows = out.shape[1]
+    held_count = rows // fresh_len
     copies = [
+        pltpu.make_async_copy(
+            token,
+            held.at[
+                pl.ds((index // chips * chips + (index % chips ^ begin)) * req_count, req_count)
+            ],
+            sems.at[index],
+        )
+        for index, token in enumerate(tokens)
+    ]
+    copies += [
         pltpu.make_async_copy(
             own_rows,
             weights.at[pl.ds(pl.multiple_of(core * depth, 16), depth)],
@@ -132,47 +55,36 @@
             weight_sems.at[1],
         ),
     ]
-    chips = groups // 2
-    copies += [
-        pltpu.make_async_copy(
-            token,
-            held.at[
-                pl.ds(
-                    (index // chips * chips + (index % chips ^ begin)) * held_count, held_count
-                )
-            ],
-            sems.at[index],
-        )
-        for index, token in enumerate(tokens)
-    ]
     for copy in copies:
         copy.start()
     for copy in copies:
         copy.wait()
-    rows = held_count * fresh_len
     together = min(groups, 4)
+    sent = []
     for first in range(0, groups, together):
         for item in range(together * held_count):
-            picked[item * fresh_len : (item + 1) * fresh_len, :] = held[
-                source[(part * groups + first) * held_count + item]
-            ]
+            row = source[(part * groups + first) * held_count + item]
+            value = held[row].astype(jnp.float32)
+            value = (value - center[row][:, 0:1]) * scale[row][:, 0:1]
+            value = value * gain[...] + bias[...]
+            picked[item * fresh_len : (item + 1) * fresh_len, :] = value.astype(jnp.bfloat16)
         result = jnp.dot(picked[...], weights[...], preferred_element_type=jnp.float32).astype(
             jnp.bfloat16
         )
         for index in range(together):
             ready[first + index] = result[index * rows : (index + 1) * rows]
         targets = pl.ds(first, together)
-        copies.append(
+        sent.append(
             pltpu.make_async_copy(
                 ready.at[targets], out.at[targets], out_sems.at[first // together]
             )
         )
-        copies[-1].start()
-    for copy in copies[groups + 2 :]:
+        sent[-1].start()
+    for copy in sent:
         copy.wait()
 
 
-def attend_kernel(shape, slots, all_lengths, table, *refs):
+def attend_kernel(shape, all_lengths, table, *refs):
     groups, held_count, fresh_len, page, heads, part = shape
     parts, bias, cosine, sine_up, sine_down, key_pool, value_pool = refs[:7]
     before = refs[7:-6]
@@ -181,7 +93,7 @@
     chunk = CHUNK_PAGES * page
     pairs = heads // 2
 
-    slot = [slots[part * held_count + index] for index in range(held_count)]
+    slot = [part * held_count + index for index in range(held_count)]
     lengths = [all_lengths[slot[index]] for index in range(held_count)]
     counts = [pl.cdiv(lengths[index], chunk) for index in range(held_count)]
     bases = [jnp.int32(0)]
@@ -254,7 +166,7 @@
 
     for which, held in enumerate(before):
         for index in range(held_count):
-            outs[which][slots[index]] = held[index]
+            outs[which][index] = held[index]
     for index in range(held_count):
         rows = slice(index * fresh_len, (index + 1) * fresh_len)
         put(1, index, turned[rows])
@@ -403,24 +315,52 @@
         return lax.optimization_barrier((value, others))[0]
 
     half = req_count // 2
-    slots, sources, picks, stats = pl.pallas_call(
-        functools.partial(plan_kernel, req_count),
-        out_shape=[
-            jax.ShapeDtypeStruct((2 * half,), jnp.int32),
-            jax.ShapeDtypeStruct((2 * req_size * half,), jnp.int32),
-            jax.ShapeDtypeStruct((2 * half,), jnp.int32),
-            jax.ShapeDtypeStruct((req_count, fresh_len, LANES), jnp.float32),
-        ],
-        in_specs=[SMEM, SMEM, VMEM],
-        out_specs=[SMEM, SMEM, SMEM, VMEM],
-        scratch_shapes=[
-            pltpu.SMEM((everyone,), jnp.int32),
-            pltpu.SMEM((everyone,), jnp.int32),
-            pltpu.SMEM((everyone,), jnp.int32),
-            pltpu.SMEM((req_size,), jnp.int32),
-        ],
-        name="plan",
-    )(jnp.stack([me]).astype(jnp.int32), group_of, arrivals)
+    layer = lax.axis_index("wgt")
+    per = chips // wgt_size
+    tokens = arrivals.reshape(rows, per, block) if per > 1 else arrivals.reshape(rows, width)
+
+    def route(turn):
+        pairs = []
+        for device in range(req_size):
+            for at in range(wgt_size):
+                to = device // 2
+                origin = turn ^ (at * per + to % per)
+                pairs.append(
+                    ((2 * origin + device % 2) * wgt_size + to // per, device * wgt_size + at)
+                )
+        value = tokens
+        if per > 1:
+            value = lax.dynamic_index_in_dim(tokens, (chip ^ turn) % per, 1, False)
+        return lax.ppermute(value, ("req", "wgt"), pairs)
+
+    received = [route(turn) for turn in range(chips)]
+
+    widened = arrivals.reshape(rows, width).astype(jnp.float32)
+    middle = jnp.mean(widened, axis=-1)
+    square = jnp.sum(jnp.square(widened - middle[:, None]), axis=-1)
+    stats = jnp.broadcast_to(jnp.stack([middle, square])[None], (wgt_size, 2, rows))
+    stats = lax.all_to_all(stats, "wgt", 0, 0, tiled=True)
+    center = jnp.mean(stats[:, 0], axis=0)
+    square = jnp.sum(stats[:, 1] + width * jnp.square(stats[:, 0] - center[None]), axis=0)
+    scale = lax.rsqrt(square / (width * wgt_size) + EPS)
+    stats = jnp.broadcast_to(jnp.stack([center, scale])[None], (req_size, 2, rows))
+    stats = lax.all_to_all(stats, "req", 0, 0, tiled=True)
+    stats = stats.reshape(chips, 2, 2, req_count, fresh_len).transpose(2, 1, 0, 3, 4)
+    stats = jnp.where(core == 0, stats, stats[:, ::-1])
+    stats = jnp.broadcast_to(
+        stats.reshape(2, everyone, fresh_len)[..., None], (2, everyone, fresh_len, LANES)
+    )
+    center, scale = stats[0], stats[1]
+
+    ids = jnp.arange(everyone, dtype=jnp.int32)
+    same_group = group_of[:, None] == group_of[None, :]
+    earlier = ids[None, :] < ids[:, None]
+    rank = jnp.sum((same_group & earlier).astype(jnp.int32), axis=1)
+    part_of, within = rank // half, rank % half
+    wanted = (part_of * req_size + group_of) * half + within
+    origin = ids // req_count
+    row = (((origin & 1) ^ core) * chips + (origin >> 1)) * req_count + ids % req_count
+    sources = jnp.sum(jnp.where(wanted[None, :] == ids[:, None], row[None, :], 0), axis=1)
 
     lane = np.arange(heads * HEAD) % HEAD
     half_rot = ROT // 2
@@ -439,10 +379,8 @@
         value.reshape(req_count, fresh_len, heads * HEAD)
         for value in (cosine, sine_up, sine_down)
     ]
-    layer = lax.axis_index("wgt")
-    per = chips // wgt_size
     gain, shift = (
-        lax.dynamic_slice_in_dim(value, layer * width, width).astype(jnp.float32).reshape(1, width)
+        lax.dynamic_slice_in_dim(value, chip * block, block).astype(jnp.float32).reshape(1, block)
         for value in (ln_gain, ln_bias)
     )
     bias = qkv_bias.astype(jnp.float32).reshape(1, local_cols)
@@ -451,78 +389,33 @@
     span = page_table.shape[1]
     pages = span + (half - 1) * (span // 2)
 
-    measured = [stats] + [
-        lax.ppermute(stats, "wgt", [(at, at ^ distance) for at in range(wgt_size)])
-        for distance in range(1, wgt_size)
-    ]
-    normed = pl.pallas_call(
-        norm_kernel,
-        out_shape=[jax.ShapeDtypeStruct((per, chunk_rows, block), jnp.bfloat16)] * 2,
-        in_specs=[SMEM] + [VMEM] * (3 + wgt_size),
-        out_specs=[VMEM] * 2,
-        compiler_params=pltpu.CompilerParams(vmem_limit_bytes=VMEM_LIMIT),
-        name="norm",
-    )(picks, arrivals, gain, shift, *measured)
-
-    def route(value, turn):
-        pairs = []
-        for device in range(req_size):
-            for at in range(wgt_size):
-                to = device // 2
-                origin = turn ^ (at * per + to % per)
-                pairs.append(
-                    ((2 * origin + device % 2) * wgt_size + to // per, device * wgt_size + at)
-                )
-        return lax.ppermute(value, ("req", "wgt"), pairs)
-
-    pieces = []
-    for part in range(2):
-        received = []
-        for turn in range(chips):
-            sent = normed[part]
-            sent = sent[0] if per == 1 else lax.dynamic_index_in_dim(
-                sent, (chip ^ turn) % per, 0, False
-            )
-            if part:
-                sent = after(sent, pieces[0][turn])
-            received.append(route(sent, turn))
-        pieces.append(received)
-
-    rows_held = after(w_qkv, stats)
-    own_rows = lax.dynamic_slice_in_dim(rows_held, core * half_cols, half_cols, 1)
-    other_rows = swap(
-        lax.dynamic_slice_in_dim(rows_held, (1 - core) * half_cols, half_cols, 1), 1
-    )
+    own_rows = lax.dynamic_slice_in_dim(w_qkv, core * half_cols, half_cols, 1)
+    other_rows = swap(lax.dynamic_slice_in_dim(w_qkv, (1 - core) * half_cols, half_cols, 1), 1)
+
+    received += [swap(piece, 1) for piece in received]
+    received = [piece.reshape(req_count, fresh_len, block) for piece in received]
 
     projected = []
     for part in range(2):
-        tokens = pieces[part] + [swap(piece, 1) for piece in pieces[part]]
-
-        partial = pl.pallas_call(
-            functools.partial(project_kernel, fresh_len, half, part),
-            out_shape=jax.ShapeDtypeStruct((req_size, chunk_rows, half_cols), jnp.bfloat16),
-            in_specs=[SMEM] * 2 + [HBM] * (req_size + 2),
-            out_specs=HBM,
-            scratch_shapes=[
-                pltpu.VMEM((req_size * half, fresh_len, block), jnp.bfloat16),
-                pltpu.VMEM((block, half_cols), jnp.bfloat16),
-                pltpu.VMEM((min(req_size, 4) * chunk_rows, block), jnp.bfloat16),
-                pltpu.VMEM((req_size, chunk_rows, half_cols), jnp.bfloat16),
-                pltpu.SemaphoreType.DMA((req_size,)),
-                pltpu.SemaphoreType.DMA((2,)),
-                pltpu.SemaphoreType.DMA((req_size // min(req_size, 4),)),
-            ],
-            compiler_params=pltpu.CompilerParams(vmem_limit_bytes=VMEM_LIMIT),
-            name="project",
-        )(
-            place,
-            sources,
-            *[token.reshape(half, fresh_len, block) for token in tokens],
-            own_rows,
-            other_rows,
-        )
-
-        projected.append(partial)
+        projected.append(
+            pl.pallas_call(
+                functools.partial(project_kernel, part),
+                out_shape=jax.ShapeDtypeStruct((req_size, chunk_rows, half_cols), jnp.bfloat16),
+                in_specs=[SMEM] * 2 + [HBM] * req_size + [VMEM] * 4 + [HBM] * 2,
+                out_specs=HBM,
+                scratch_shapes=[
+                    pltpu.VMEM((everyone, fresh_len, block), jnp.bfloat16),
+                    pltpu.VMEM((block, half_cols), jnp.bfloat16),
+                    pltpu.VMEM((min(req_size, 4) * chunk_rows, block), jnp.bfloat16),
+                    pltpu.VMEM((req_size, chunk_rows, half_cols), jnp.bfloat16),
+                    pltpu.SemaphoreType.DMA((req_size,)),
+                    pltpu.SemaphoreType.DMA((2,)),
+                    pltpu.SemaphoreType.DMA((req_size // min(req_size, 4),)),
+                ],
+                compiler_params=pltpu.CompilerParams(vmem_limit_bytes=VMEM_LIMIT),
+                name="project",
+            )(place, sources, *received, center, scale, gain, shift, own_rows, other_rows)
+        )
 
     results = []
     for part in range(2):
@@ -531,9 +424,9 @@
             parts = after(parts, projected[1])
 
         operands = [
-            slots, lengths, page_table, parts, bias, *tables, key_pool, value_pool
+            lengths, page_table, parts, bias, *tables, key_pool, value_pool
         ]
-        specs = [SMEM] * 3 + [VMEM] * 5 + [HBM] * 2
+        specs = [SMEM] * 2 + [VMEM] * 5 + [HBM] * 2
         count = half if part == 0 else req_count
         out = jax.ShapeDtypeStruct((count, fresh_len, heads * HEAD), jnp.bfloat16)
         results = pl.pallas_call(
@@ -551,7 +444,7 @@
             compiler_params=pltpu.CompilerParams(vmem_limit_bytes=VMEM_LIMIT),
             name="attend",
         )(*operands, *results)
-    return results
+    return tuple(results)
 
 
 def solution(mesh):

time: 160 us -> 159 us (level); the launches traced: 157 us -> 159 us
  starting transfers between devices: 42.5 us -> 30.1 us
  waiting for transfers between devices: 58.6 us -> 69.6 us
  local copies, waits for them, and re-layouts: 9.89 us -> 13.8 us
  Pallas kernels: 39.3 us -> 35.9 us
  other arithmetic: 5.62 us -> 8.52 us
    all_to_all x0 -> x2, waiting for transfers between devices: none -> 44.1 us  [the longest x1 41.2 us: per_device(): stats = lax.all_to_all(stats, 'wgt', 0, 0, tiled=True)]
    ppermute x8 -> x4, waiting for transfers between devices: 42.3 us -> 0.01 us  [route(): return lax.ppermute(value, ('req', 'wgt'), pairs)]
    all_to_all x2, waiting for transfers between devices: 7.12 us -> 25.5 us  [per_device(): parts = lax.all_to_all(projected[part], 'req', 0, 0, tiled=True)]
    all_to_all x2, starting transfers between devices: 19.8 us -> 7.19 us  [per_device(): parts = lax.all_to_all(projected[part], 'req', 0, 0, tiled=True)]
    all_to_all x0 -> x2, starting transfers between devices: none -> 10.4 us  [the longest x1 6.56 us: per_device(): stats = lax.all_to_all(stats, 'req', 0, 0, tiled=True)]
    ppermute x3 -> x0, waiting for transfers between devices: 6.49 us -> none  [per_device(): lax.ppermute(stats, 'wgt', [(at, at ^ distance) for at in range(wgt_size)])]
    ppermute x3 -> x0, starting transfers between devices: 5.17 us -> none  [per_device(): lax.ppermute(stats, 'wgt', [(at, at ^ distance) for at in range(wgt_size)])]
    ppermute x8 -> x4, starting transfers between devices: 16.4 us -> 11.4 us  [route(): return lax.ppermute(value, ('req', 'wgt'), pairs)]
  transfers between devices with their start and end apart: 22 -> 13, of which waited for: 11 -> 4; matrix products, arithmetic and copies ran while one was open for 5% -> 11% of each run, Pallas kernels for 14% -> 10%
where the time goes in v1:
time: 159 us
  waiting for transfers between devices  69.6 us (44%)
  Pallas kernels  35.9 us (23%)
  starting transfers between devices  30.1 us (19%)
  local copies, waits for them, and re-layouts  13.8 us (9%)
  other arithmetic  8.52 us (5%)
    all_to_all x1, waiting for transfers between devices, per_device(): stats = lax.all_to_all(stats, 'wgt', 0, 0, tiled=True)  41.2 us
    all_to_all x2, waiting for transfers between devices, per_device(): parts = lax.all_to_all(projected[part], 'req', 0, 0, tiled=True)  25.5 us
    pallas_call x2, Pallas kernels, per_device(): pl.pallas_call(functools.partial(project_kernel, part), out_shape=jax.Sha...  18.4 us
    pallas_call x2, Pallas kernels, per_device(): pl.pallas_call(functools.partial(attend_kernel, (req_size, half, fresh_le...  17.5 us
    ppermute x4, starting transfers between devices, route(): return lax.ppermute(value, ('req', 'wgt'), pairs)  11.4 us
    all_to_all x2, starting transfers between devices, per_device(): parts = lax.all_to_all(projected[part], 'req', 0, 0, tiled=True)  7.19 us
    all_to_all x1, starting transfers between devices, per_device(): stats = lax.all_to_all(stats, 'req', 0, 0, tiled=True)  6.56 us
    dynamic_slice x1, local copies, waits for them, and re-layouts, per_device(): lax.dynamic_slice_in_dim(w_qkv, (1 - core) * half_cols, half_cols, 1)  4.09 us
  transfers between devices with their start and end apart: 13, of which 4 were waited for; matrix products, arithmetic and copies ran while one was open for 11% of the time, Pallas kernels for 10%

profile of v1, /device:TPU:0, one launch (start us, length us, event | category | flops | bytes accessed | tf_op | source)
XLA Modules:
  0.0 158.9 jit_solution(6668904062325653579)
XLA Ops:
  0.6 5.1 %collective-permute-start.3 = (bf16[192,1536]{1,0:T(8,128)(2,1)}, bf16[192,1536]{1,0:T(8,128)(2,1)S(1)}, u32[]{:S(2)}, u32[]{:S(2)}) collective-permute-start(bf16[192,1536]{1,0:T(8,128)(2,1)} %bitcast.38), channel_id=1, source_target_pairs={{24,0},{16,1},{8,2},{0,3},{28,4},{20,5},{12,6},{4,7},{25,8},{17,9}... | collective-permute-start | bytes 1769480 | tf_op jit(solution)/shard_map/ppermute | solution.py:334
  5.7 1.7 %collective-permute-start = (bf16[192,1536]{1,0:T(8,128)(2,1)}, bf16[192,1536]{1,0:T(8,128)(2,1)S(1)}, u32[]{:S(2)}, u32[]{:S(2)}) collective-permute-start(bf16[192,1536]{1,0:T(8,128)(2,1)} %bitcast.39), channel_id=1, source_target_pairs={{0,0},{8,1},{16,2},{24,3},{4,4},{12,5},{20,6},{28,7},{1,8},{9,9},{... | collective-permute-start | bytes 1769480 | tf_op jit(solution)/shard_map/ppermute | solution.py:334
  7.4 2.2 %collective-permute-start.1 = (bf16[192,1536]{1,0:T(8,128)(2,1)}, bf16[192,1536]{1,0:T(8,128)(2,1)S(1)}, u32[]{:S(2)}, u32[]{:S(2)}) collective-permute-start(bf16[192,1536]{1,0:T(8,128)(2,1)} %bitcast.40), channel_id=1, source_target_pairs={{8,0},{0,1},{24,2},{16,3},{12,4},{4,5},{28,6},{20,7},{9,8},{1,9},{... | collective-permute-start | bytes 1769480 | tf_op jit(solution)/shard_map/ppermute | solution.py:334
  9.6 2.4 %collective-permute-start.2 = (bf16[192,1536]{1,0:T(8,128)(2,1)}, bf16[192,1536]{1,0:T(8,128)(2,1)}, u32[]{:S(2)}, u32[]{:S(2)}) collective-permute-start(bf16[192,1536]{1,0:T(8,128)(2,1)} %bitcast.41), channel_id=1, source_target_pairs={{16,0},{24,1},{0,2},{8,3},{20,4},{28,5},{4,6},{12,7},{17,8},{25,9}... | collective-permute-start | bytes 1769480 | tf_op jit(solution)/shard_map/ppermute | solution.py:334
  12.0 4.1 %constant_dynamic-slice_fusion = (bf16[768,1152]{1,0:T(8,128)(2,1)}, bf16[768,1152]{1,0:T(8,128)(2,1)}) fusion(bf16[768,2304]{1,0:T(8,128)(2,1)} %param.20, s32[]{:T(128)S(6)} %select_n.80, s32[]{:T(128)S(6)} %select_n.79), kind=kLoop, calls=%fused_computation.43 | loop fusion | bytes 7077896 | tf_op jit(solution)/shard_map/dynamic_slice | solution.py:393
  16.1 0.0 collective-permute-start.8
  16.1 0.0 copy-done.6
  16.1 0.2 convert_reduce_fusion
  16.3 0.3 fusion.1
  16.6 0.1 div.50
  16.7 0.1 stack.24
  16.8 0.6 broadcast_in_dim.78
  17.4 3.9 %all-to-all-start = ((f32[4,2,192]{2,1,0:T(2,128)}), f32[4,2,192]{2,1,0:T(2,128)}, u32[]{:S(2)}, u32[]{:S(2)}) async-start(f32[4,2,192]{2,1,0:T(2,128)} %broadcast_in_dim.78), calls=%async_computation | async-start | bytes 16384 | tf_op jit(solution)/shard_map/all_to_all | solution.py:342
  21.2 0.0 copy-done.10
  21.3 0.2 convert_reduce_fusion.1
  21.5 0.6 select_reduce_fusion.source
  22.1 0.8 dynamic-slice_convert_fusion
  22.9 41.2 %all-to-all-done = f32[4,2,192]{2,1,0:T(2,128)} async-done(((f32[4,2,192]{2,1,0:T(2,128)}), f32[4,2,192]{2,1,0:T(2,128)}, u32[]{:S(2)}, u32[]{:S(2)}) %all-to-all-start) | async-done | bytes 6176 | tf_op jit(solution)/shard_map/all_to_all | solution.py:342
  64.1 0.8 slice_reduce_fusion
  64.9 0.0 collective-permute-done.3
  64.9 0.0 copy-start.3
  64.9 0.1 collective-permute-start.7
  65.0 0.0 collective-permute-done
  65.0 0.0 copy-start.4
  65.0 0.5 collective-permute-start.4
  65.5 0.0 collective-permute-done.1
  65.5 0.1 collective-permute-start.5
  65.6 0.0 collective-permute-done.2
  65.6 0.4 collective-permute-start.6
  66.1 0.6 broadcast_in_dim.79
  66.7 6.6 %all-to-all-start.1 = ((f32[8,2,192]{2,1,0:T(2,128)}), f32[8,2,192]{2,1,0:T(2,128)}, u32[]{:S(2)}, u32[]{:S(2)}) async-start(f32[8,2,192]{2,1,0:T(2,128)} %broadcast_in_dim.79), calls=%async_computation.1 | async-start | bytes 32768 | tf_op jit(solution)/shard_map/all_to_all | solution.py:347
  73.2 0.6 pad_add_fusion.place
  73.8 0.6 reshape.226.refs_10_
  74.4 0.6 reshape.228.refs_11_
  75.0 2.9 %all-to-all-done.1 = f32[8,2,192]{2,1,0:T(2,128)} async-done(((f32[8,2,192]{2,1,0:T(2,128)}), f32[8,2,192]{2,1,0:T(2,128)}, u32[]{:S(2)}, u32[]{:S(2)}) %all-to-all-start.1) | async-done | bytes 12320 | tf_op jit(solution)/shard_map/all_to_all | solution.py:347
  77.9 0.7 copy.30
  78.7 0.7 reshape.218
  79.4 0.8 reverse_select_fusion
  80.2 0.0 collective-permute-done.7
  80.3 0.0 collective-permute-done.4
  80.3 0.0 collective-permute-done.5
  80.3 0.0 collective-permute-done.6
  80.3 0.0 collective-permute-done.8.refs_13_
  80.3 0.0 copy-start.1
  80.3 1.4 broadcast_in_dim.81.refs_8_
  81.7 1.2 broadcast_in_dim.83.refs_9_
  83.0 9.2 %project.3 = bf16[8,96,1152]{2,1,0:T(8,128)(2,1)} custom-call(s32[2]{0:T(128)} %pad_add_fusion.place, s32[32]{0:T(128)} %select_reduce_fusion.source, bf16[4,48,1536]{2,1,0:T(8,128)(2,1)} %bitcast.34, bf16[4,48,1536]{2,1,0:T(8,128)(2,1)} %bitcast.36, bf16[4,48,1536]{2,1,0:T(8,128)(2,1)} %bitcast.5.refs_2_, bf16[4,48,1536]{2,1,0:T(8,128)(2,1)} %bitcast.32, ...), custom_call_target="tpu_custom_call" | custom-call | tf_op jit(solution)/shard_map/project/pallas_call | solution.py:401
  92.2 3.6 %all-to-all-start.3 = ((bf16[8,96,1152]{2,1,0:T(8,128)(2,1)}), bf16[8,96,1152]{2,1,0:T(8,128)(2,1)S(1)}, u32[]{:S(2)}, u32[]{:S(2)}) async-start(bf16[8,96,1152]{2,1,0:T(8,128)(2,1)} %project.3), calls=%async_computation.3 | async-start | bytes 3538944 | tf_op jit(solution)/shard_map/all_to_all | solution.py:422
  95.8 9.2 %project.2 = bf16[8,96,1152]{2,1,0:T(8,128)(2,1)} custom-call(s32[2]{0:T(128)} %pad_add_fusion.place, s32[32]{0:T(128)} %select_reduce_fusion.source, bf16[4,48,1536]{2,1,0:T(8,128)(2,1)} %bitcast.35, bf16[4,48,1536]{2,1,0:T(8,128)(2,1)} %bitcast.37, bf16[4,48,1536]{2,1,0:T(8,128)(2,1)} %bitcast.5.refs_2_, bf16[4,48,1536]{2,1,0:T(8,128)(2,1)} %bitcast.33, ...), custom_call_target="tpu_custom_call" | custom-call | tf_op jit(solution)/shard_map/project/pallas_call | solution.py:401
  105.0 0.0 copy-start.7
  105.0 0.0 copy-start.8
  105.0 0.0 copy-start.9
  105.0 13.8 %all-to-all-done.3.refs_0_ = bf16[8,96,1152]{2,1,0:T(8,128)(2,1)S(1)} async-done(((bf16[8,96,1152]{2,1,0:T(8,128)(2,1)}), bf16[8,96,1152]{2,1,0:T(8,128)(2,1)S(1)}, u32[]{:S(2)}, u32[]{:S(2)}) %all-to-all-start.3) | async-done | bytes 1769504 | tf_op jit(solution)/shard_map/all_to_all | solution.py:422
  118.8 1.2 copy-done.2
  120.0 3.6 %all-to-all-start.2 = ((bf16[8,96,1152]{2,1,0:T(8,128)(2,1)}), bf16[8,96,1152]{2,1,0:T(8,128)(2,1)S(1)}, u32[]{:S(2)}, u32[]{:S(2)}) async-start(bf16[8,96,1152]{2,1,0:T(8,128)(2,1)} %project.2), calls=%async_computation.2 | async-start | bytes 3538944 | tf_op jit(solution)/shard_map/all_to_all | solution.py:422
  123.6 0.0 copy-done.7
  123.6 0.6 reshape.230.refs_1_
  124.2 0.0 copy-done.8
  124.2 0.1 add_convert_fusion
  124.3 4.1 %fusion.2 = (f32[4,48,768]{2,1,0:T(8,128)}, f32[4,48,768]{2,1,0:T(8,128)}, f32[4,48,768]{2,1,0:T(8,128)}) fusion(f32[768]{0:T(1024)S(1)} %copy-done.9, f32[4,48]{1,0:T(4,128)S(1)} %add_convert_fusion, pred[768]{0:T(1024)(128)(4,1)} %constant.124, pred[768]{0:T(1024)(128)(4,1)} %constant.116.clone, pred[768]{0:T(1024)(128)(4,1)} %constant.115.clone), kind=kLoop, calls=%fused_computation.6 | loop fusion | flops 737280 | bytes 1775616 | tf_op jit(solution)/shard_map/jit(_where)/select_n | solution.py:376
  128.4 6.7 %attend.2 = (bf16[2,48,768]{2,1,0:T(8,128)(2,1)}, bf16[2,48,768]{2,1,0:T(8,128)(2,1)}, bf16[2,48,768]{2,1,0:T(8,128)(2,1)}) custom-call(s32[4]{0:T(128)} %all_lengths.3, s32[4,16]{1,0:T(4,128)} %table.3, bf16[8,96,1152]{2,1,0:T(8,128)(2,1)} %copy-done.2, f32[1,2304]{1,0:T(1,128)} %reshape.230.refs_1_, f32[4,48,768]{2,1,0:T(8,128)} %get-tuple-element.20.refs_2_, ...), custom_call_target="tpu_custom_call" | custom-call | tf_op jit(solution)/shard_map/attend/pallas_call | solution.py:432
  135.1 11.6 %all-to-all-done.2.refs_0_ = bf16[8,96,1152]{2,1,0:T(8,128)(2,1)S(1)} async-done(((bf16[8,96,1152]{2,1,0:T(8,128)(2,1)}), bf16[8,96,1152]{2,1,0:T(8,128)(2,1)S(1)}, u32[]{:S(2)}, u32[]{:S(2)}) %all-to-all-start.2) | async-done | bytes 1769504 | tf_op jit(solution)/shard_map/all_to_all | solution.py:422
  146.7 1.2 copy-done
  147.9 10.8 %attend.3 = (bf16[4,48,768]{2,1,0:T(8,128)(2,1)}, bf16[4,48,768]{2,1,0:T(8,128)(2,1)}, bf16[4,48,768]{2,1,0:T(8,128)(2,1)}) custom-call(s32[4]{0:T(128)} %all_lengths.3, s32[4,16]{1,0:T(4,128)} %table.3, bf16[8,96,1152]{2,1,0:T(8,128)(2,1)} %copy-done, f32[1,2304]{1,0:T(1,128)} %reshape.230.refs_1_, f32[4,48,768]{2,1,0:T(8,128)} %get-tuple-element.20.refs_2_, ...), custom_call_target="tpu_custom_call" | custom-call | tf_op jit(solution)/shard_map/attend/pallas_call | solution.py:432
  (20 shorter events, 0.1 us)
Async XLA Ops:
  0.6 64.3 %collective-permute-start.3 = (bf16[192,1536]{1,0:T(8,128)(2,1)}, bf16[192,1536]{1,0:T(8,128)(2,1)S(1)}, u32[]{:S(2)}, u32[]{:S(2)}) collective-permute-start(bf16[192,1536]{1,0:T(8,128)(2,1)} %bitcast.38), channel_id=1, source_target_pairs={{24,0},{16,1},{8,2},{0,3},{28,4},{20,5},{12,6},{4,7},{25,8},{17,9}... | collective-permute-start | bytes 1769480 | tf_op jit(solution)/shard_map/ppermute | solution.py:334
  5.7 59.3 %collective-permute-start = (bf16[192,1536]{1,0:T(8,128)(2,1)}, bf16[192,1536]{1,0:T(8,128)(2,1)S(1)}, u32[]{:S(2)}, u32[]{:S(2)}) collective-permute-start(bf16[192,1536]{1,0:T(8,128)(2,1)} %bitcast.39), channel_id=1, source_target_pairs={{0,0},{8,1},{16,2},{24,3},{4,4},{12,5},{20,6},{28,7},{1,8},{9,9},{... | collective-permute-start | bytes 1769480 | tf_op jit(solution)/shard_map/ppermute | solution.py:334
  7.4 58.1 %collective-permute-start.1 = (bf16[192,1536]{1,0:T(8,128)(2,1)}, bf16[192,1536]{1,0:T(8,128)(2,1)S(1)}, u32[]{:S(2)}, u32[]{:S(2)}) collective-permute-start(bf16[192,1536]{1,0:T(8,128)(2,1)} %bitcast.40), channel_id=1, source_target_pairs={{8,0},{0,1},{24,2},{16,3},{12,4},{4,5},{28,6},{20,7},{9,8},{1,9},{... | collective-permute-start | bytes 1769480 | tf_op jit(solution)/shard_map/ppermute | solution.py:334
  9.6 56.0 %collective-permute-start.2 = (bf16[192,1536]{1,0:T(8,128)(2,1)}, bf16[192,1536]{1,0:T(8,128)(2,1)}, u32[]{:S(2)}, u32[]{:S(2)}) collective-permute-start(bf16[192,1536]{1,0:T(8,128)(2,1)} %bitcast.41), channel_id=1, source_target_pairs={{16,0},{24,1},{0,2},{8,3},{20,4},{28,5},{4,6},{12,7},{17,8},{25,9}... | collective-permute-start | bytes 1769480 | tf_op jit(solution)/shard_map/ppermute | solution.py:334
  12.0 4.1 %copy-start.6 = (bf16[4,48,1536]{2,1,0:T(8,128)(2,1)S(1)}, bf16[4,48,1536]{2,1,0:T(8,128)(2,1)}, u32[]{:S(2)}) copy-start(bf16[4,48,1536]{2,1,0:T(8,128)(2,1)} %param.14) | copy-start | bytes 1769476
  12.0 9.2 %copy-start.10 = (s32[32]{0:T(128)S(1)}, s32[32]{0:T(128)}, u32[]{:S(2)}) copy-start(s32[32]{0:T(128)} %param.15) | copy-start | bytes 388
  16.1 64.2 %collective-permute-start.8 = (bf16[768,1152]{1,0:T(8,128)(2,1)}, bf16[768,1152]{1,0:T(8,128)(2,1)S(1)}, u32[]{:S(2)}, u32[]{:S(2)}) collective-permute-start(bf16[768,1152]{1,0:T(8,128)(2,1)} %get-tuple-element.11), channel_id=1, source_target_pairs={{0,4},{4,0},{8,12},{12,8},{16,20},{20,16},{24,28},{28,24},{1,5},{5... | collective-permute-start | bytes 5308424 | tf_op jit(solution)/shard_map/ppermute | solution.py:310
  17.4 46.7 %all-to-all-start = ((f32[4,2,192]{2,1,0:T(2,128)}), f32[4,2,192]{2,1,0:T(2,128)}, u32[]{:S(2)}, u32[]{:S(2)}) async-start(f32[4,2,192]{2,1,0:T(2,128)} %broadcast_in_dim.78), calls=%async_computation | async-start | bytes 16384 | tf_op jit(solution)/shard_map/all_to_all | solution.py:342
  64.9 18.0 %copy-start.3 = (bf16[192,1536]{1,0:T(8,128)(2,1)}, bf16[192,1536]{1,0:T(8,128)(2,1)S(1)}, u32[]{:S(2)}) copy-start(bf16[192,1536]{1,0:T(8,128)(2,1)S(1)} %collective-permute-done.3) | copy-start | bytes 1769476
  64.9 15.3 %collective-permute-start.7 = (bf16[192,1536]{1,0:T(8,128)(2,1)S(1)}, bf16[192,1536]{1,0:T(8,128)(2,1)}, u32[]{:S(2)}, u32[]{:S(2)}) collective-permute-start(bf16[192,1536]{1,0:T(8,128)(2,1)S(1)} %collective-permute-done.3), channel_id=1, source_target_pairs={{0,4},{4,0},{8,12},{12,8},{16,20},{20,16},{24,28},{28,24},{1,5},{5... | collective-permute-start | bytes 1769480 | tf_op jit(solution)/shard_map/ppermute | solution.py:310
  65.0 17.9 %copy-start.4 = (bf16[192,1536]{1,0:T(8,128)(2,1)}, bf16[192,1536]{1,0:T(8,128)(2,1)S(1)}, u32[]{:S(2)}) copy-start(bf16[192,1536]{1,0:T(8,128)(2,1)S(1)} %collective-permute-done) | copy-start | bytes 1769476
  65.0 15.2 %collective-permute-start.4 = (bf16[192,1536]{1,0:T(8,128)(2,1)S(1)}, bf16[192,1536]{1,0:T(8,128)(2,1)}, u32[]{:S(2)}, u32[]{:S(2)}) collective-permute-start(bf16[192,1536]{1,0:T(8,128)(2,1)S(1)} %collective-permute-done), channel_id=1, source_target_pairs={{0,4},{4,0},{8,12},{12,8},{16,20},{20,16},{24,28},{28,24},{1,5},{5... | collective-permute-start | bytes 1769480 | tf_op jit(solution)/shard_map/ppermute | solution.py:310
  65.5 17.4 %copy-start.5 = (bf16[192,1536]{1,0:T(8,128)(2,1)}, bf16[192,1536]{1,0:T(8,128)(2,1)S(1)}, u32[]{:S(2)}) copy-start(bf16[192,1536]{1,0:T(8,128)(2,1)S(1)} %collective-permute-done.1) | copy-start | bytes 1769476
  65.5 14.7 %collective-permute-start.5 = (bf16[192,1536]{1,0:T(8,128)(2,1)S(1)}, bf16[192,1536]{1,0:T(8,128)(2,1)}, u32[]{:S(2)}, u32[]{:S(2)}) collective-permute-start(bf16[192,1536]{1,0:T(8,128)(2,1)S(1)} %collective-permute-done.1), channel_id=1, source_target_pairs={{0,4},{4,0},{8,12},{12,8},{16,20},{20,16},{24,28},{28,24},{1,5},{5... | collective-permute-start | bytes 1769480 | tf_op jit(solution)/shard_map/ppermute | solution.py:310
  65.6 14.6 %collective-permute-start.6 = (bf16[192,1536]{1,0:T(8,128)(2,1)}, bf16[192,1536]{1,0:T(8,128)(2,1)}, u32[]{:S(2)}, u32[]{:S(2)}) collective-permute-start(bf16[192,1536]{1,0:T(8,128)(2,1)} %collective-permute-done.2), channel_id=1, source_target_pairs={{0,4},{4,0},{8,12},{12,8},{16,20},{20,16},{24,28},{28,24},{1,5},{5... | collective-permute-start | bytes 1769480 | tf_op jit(solution)/shard_map/ppermute | solution.py:310
  66.7 11.3 %all-to-all-start.1 = ((f32[8,2,192]{2,1,0:T(2,128)}), f32[8,2,192]{2,1,0:T(2,128)}, u32[]{:S(2)}, u32[]{:S(2)}) async-start(f32[8,2,192]{2,1,0:T(2,128)} %broadcast_in_dim.79), calls=%async_computation.1 | async-start | bytes 32768 | tf_op jit(solution)/shard_map/all_to_all | solution.py:347
  80.3 2.7 %copy-start.1 = (bf16[768,1152]{1,0:T(8,128)(2,1)}, bf16[768,1152]{1,0:T(8,128)(2,1)S(1)}, u32[]{:S(2)}) copy-start(bf16[768,1152]{1,0:T(8,128)(2,1)S(1)} %collective-permute-done.8.refs_13_) | copy-start | bytes 5308420
  92.2 26.7 %all-to-all-start.3 = ((bf16[8,96,1152]{2,1,0:T(8,128)(2,1)}), bf16[8,96,1152]{2,1,0:T(8,128)(2,1)S(1)}, u32[]{:S(2)}, u32[]{:S(2)}) async-start(bf16[8,96,1152]{2,1,0:T(8,128)(2,1)} %project.3), calls=%async_computation.3 | async-start | bytes 3538944 | tf_op jit(solution)/shard_map/all_to_all | solution.py:422
  105.0 18.7 %copy-start.7 = (bf16[2304]{0:T(1024)(128)(2,1)S(1)}, bf16[2304]{0:T(1024)(128)(2,1)}, u32[]{:S(2)}) copy-start(bf16[2304]{0:T(1024)(128)(2,1)} %param.21) | copy-start | bytes 13828
  105.0 19.3 %copy-start.8 = (s32[4]{0:T(128)S(1)}, s32[4]{0:T(128)}, u32[]{:S(2)}) copy-start(s32[4]{0:T(128)} %all_lengths.3) | copy-start | bytes 52
  105.0 19.3 %copy-start.9 = (f32[768]{0:T(1024)S(1)}, f32[768]{0:T(1024)}, u32[]{:S(2)}) copy-start(f32[768]{0:T(1024)} %constant.123) | copy-start | bytes 9220
  118.8 1.2 copy-start.2
  120.0 26.7 %all-to-all-start.2 = ((bf16[8,96,1152]{2,1,0:T(8,128)(2,1)}), bf16[8,96,1152]{2,1,0:T(8,128)(2,1)S(1)}, u32[]{:S(2)}, u32[]{:S(2)}) async-start(bf16[8,96,1152]{2,1,0:T(8,128)(2,1)} %project.2), calls=%async_computation.2 | async-start | bytes 3538944 | tf_op jit(solution)/shard_map/all_to_all | solution.py:422
  146.7 1.2 copy-start

commit v2 on v1

--- a/solution.py
+++ b/solution.py
@@ -23,10 +23,10 @@
 
 
 def project_kernel(part, place, source, *refs):
-    groups = len(refs) - 14
+    groups = len(refs) - 10
     tokens = refs[:groups]
-    center, scale, gain, bias, own_rows, other_rows = refs[groups : groups + 6]
-    out, held, weights, picked, ready, sems, weight_sems, out_sems = refs[groups + 6 :]
+    own_rows, other_rows = refs[groups : groups + 2]
+    out, held, weights, picked, ready, sems, weight_sems, out_sems = refs[groups + 2 :]
     core, begin = place[0], place[1]
     depth = own_rows.shape[0]
     chips = groups // 2
@@ -63,11 +63,9 @@
     sent = []
     for first in range(0, groups, together):
         for item in range(together * held_count):
-            row = source[(part * groups + first) * held_count + item]
-            value = held[row].astype(jnp.float32)
-            value = (value - center[row][:, 0:1]) * scale[row][:, 0:1]
-            value = value * gain[...] + bias[...]
-            picked[item * fresh_len : (item + 1) * fresh_len, :] = value.astype(jnp.bfloat16)
+            picked[item * fresh_len : (item + 1) * fresh_len, :] = held[
+                source[(part * groups + first) * held_count + item]
+            ]
         result = jnp.dot(picked[...], weights[...], preferred_element_type=jnp.float32).astype(
             jnp.bfloat16
         )
@@ -317,7 +315,24 @@
     half = req_count // 2
     layer = lax.axis_index("wgt")
     per = chips // wgt_size
-    tokens = arrivals.reshape(rows, per, block) if per > 1 else arrivals.reshape(rows, width)
+
+    widened = arrivals.reshape(rows, width).astype(jnp.float32)
+    middle = jnp.mean(widened, axis=-1)
+    square = jnp.sum(jnp.square(widened - middle[:, None]), axis=-1)
+    local = jnp.stack([middle, square])
+    stats = jnp.broadcast_to(local[None], (wgt_size, 2, rows))
+    stats = lax.all_to_all(stats, "wgt", 0, 0, tiled=True)
+    center = jnp.mean(stats[:, 0], axis=0)
+    square = jnp.sum(stats[:, 1] + width * jnp.square(stats[:, 0] - center[None]), axis=0)
+    scale = lax.rsqrt(square / (width * wgt_size) + EPS)
+    gain, shift = (
+        lax.dynamic_slice_in_dim(value, layer * width, width).astype(jnp.float32)
+        for value in (ln_gain, ln_bias)
+    )
+    tokens = (widened - center[:, None]) * scale[:, None] * gain + shift
+    tokens = tokens.astype(jnp.bfloat16)
+    if per > 1:
+        tokens = tokens.reshape(rows, per, block)
 
     def route(turn):
         pairs = []
@@ -335,23 +350,6 @@
 
     received = [route(turn) for turn in range(chips)]
 
-    widened = arrivals.reshape(rows, width).astype(jnp.float32)
-    middle = jnp.mean(widened, axis=-1)
-    square = jnp.sum(jnp.square(widened - middle[:, None]), axis=-1)
-    stats = jnp.broadcast_to(jnp.stack([middle, square])[None], (wgt_size, 2, rows))
-    stats = lax.all_to_all(stats, "wgt", 0, 0, tiled=True)
-    center = jnp.mean(stats[:, 0], axis=0)
-    square = jnp.sum(stats[:, 1] + width * jnp.square(stats[:, 0] - center[None]), axis=0)
-    scale = lax.rsqrt(square / (width * wgt_size) + EPS)
-    stats = jnp.broadcast_to(jnp.stack([center, scale])[None], (req_size, 2, rows))
-    stats = lax.all_to_all(stats, "req", 0, 0, tiled=True)
-    stats = stats.reshape(chips, 2, 2, req_count, fresh_len).transpose(2, 1, 0, 3, 4)
-    stats = jnp.where(core == 0, stats, stats[:, ::-1])
-    stats = jnp.broadcast_to(
-        stats.reshape(2, everyone, fresh_len)[..., None], (2, everyone, fresh_len, LANES)
-    )
-    center, scale = stats[0], stats[1]
-
     ids = jnp.arange(everyone, dtype=jnp.int32)
     same_group = group_of[:, None] == group_of[None, :]
     earlier = ids[None, :] < ids[:, None]
@@ -379,18 +377,15 @@
         value.reshape(req_count, fresh_len, heads * HEAD)
         for value in (cosine, sine_up, sine_down)
     ]
-    gain, shift = (
-        lax.dynamic_slice_in_dim(value, chip * block, block).astype(jnp.float32).reshape(1, block)
-        for value in (ln_gain, ln_bias)
-    )
     bias = qkv_bias.astype(jnp.float32).reshape(1, local_cols)
     place = jnp.stack([core, layer * per + chip % per]).astype(jnp.int32)
     chunk_rows = half * fresh_len
     span = page_table.shape[1]
     pages = span + (half - 1) * (span // 2)
 
-    own_rows = lax.dynamic_slice_in_dim(w_qkv, core * half_cols, half_cols, 1)
-    other_rows = swap(lax.dynamic_slice_in_dim(w_qkv, (1 - core) * half_cols, half_cols, 1), 1)
+    held = after(w_qkv, local)
+    own_rows = lax.dynamic_slice_in_dim(held, core * half_cols, half_cols, 1)
+    other_rows = swap(lax.dynamic_slice_in_dim(held, (1 - core) * half_cols, half_cols, 1), 1)
 
     received += [swap(piece, 1) for piece in received]
     received = [piece.reshape(req_count, fresh_len, block) for piece in received]
@@ -401,7 +396,7 @@
             pl.pallas_call(
                 functools.partial(project_kernel, part),
                 out_shape=jax.ShapeDtypeStruct((req_size, chunk_rows, half_cols), jnp.bfloat16),
-                in_specs=[SMEM] * 2 + [HBM] * req_size + [VMEM] * 4 + [HBM] * 2,
+                in_specs=[SMEM] * 2 + [HBM] * (req_size + 2),
                 out_specs=HBM,
                 scratch_shapes=[
                     pltpu.VMEM((everyone, fresh_len, block), jnp.bfloat16),
@@ -414,7 +409,7 @@
                 ],
                 compiler_params=pltpu.CompilerParams(vmem_limit_bytes=VMEM_LIMIT),
                 name="project",
-            )(place, sources, *received, center, scale, gain, shift, own_rows, other_rows)
+            )(place, sources, *received, own_rows, other_rows)
         )
 
     results = []

time: 159 us -> 154 us (0.969)
  waiting for transfers between devices: 69.6 us -> 56.4 us
  starting transfers between devices: 30.1 us -> 42.4 us
  local copies, waits for them, and re-layouts: 13.8 us -> 10.1 us
  Pallas kernels: 35.9 us -> 33.8 us
    all_to_all x1, waiting for transfers between devices: 41.2 us -> 0.69 us  [per_device(): stats = lax.all_to_all(stats, 'wgt', 0, 0, tiled=True)]
    ppermute x4, waiting for transfers between devices: 0.01 us -> 31.7 us  [route(): return lax.ppermute(value, ('req', 'wgt'), pairs)]
    all_to_all x2, starting transfers between devices: 7.19 us -> 26.9 us  [per_device(): parts = lax.all_to_all(projected[part], 'req', 0, 0, tiled=True)]
    all_to_all x1 -> x0, starting transfers between devices: 6.56 us -> none  [per_device(): stats = lax.all_to_all(stats, 'req', 0, 0, tiled=True)]
    broadcast_in_dim x4 -> x1, local copies, waits for them, and re-layouts: 3.85 us -> 0.6 us  [per_device(): stats = jnp.broadcast_to(local[None], (wgt_size, 2, rows))]
    all_to_all x1 -> x0, waiting for transfers between devices: 2.91 us -> none  [per_device(): stats = lax.all_to_all(stats, 'req', 0, 0, tiled=True)]
    ppermute x4, starting transfers between devices: 11.4 us -> 8.69 us  [route(): return lax.ppermute(value, ('req', 'wgt'), pairs)]
    all_to_all x1, starting transfers between devices: 3.85 us -> 6.32 us  [per_device(): stats = lax.all_to_all(stats, 'wgt', 0, 0, tiled=True)]
  transfers between devices with their start and end apart: 13 -> 12, of which waited for: 4 -> 7; matrix products, arithmetic and copies ran while one was open for 11% -> 8% of each run, Pallas kernels for 10% -> 12%
where the time goes in v2:
time: 154 us; the launch traced here: 153 us
  waiting for transfers between devices  56.4 us (37%)
  starting transfers between devices  42.4 us (28%)
  Pallas kernels  33.8 us (22%)
  local copies, waits for them, and re-layouts  10.1 us (7%)
  other arithmetic  9.52 us (6%)
    ppermute x4, waiting for transfers between devices, route(): return lax.ppermute(value, ('req', 'wgt'), pairs)  31.7 us
    all_to_all x2, starting transfers between devices, per_device(): parts = lax.all_to_all(projected[part], 'req', 0, 0, tiled=True)  26.9 us
    all_to_all x2, waiting for transfers between devices, per_device(): parts = lax.all_to_all(projected[part], 'req', 0, 0, tiled=True)  23.5 us
    pallas_call x2, Pallas kernels, per_device(): pl.pallas_call(functools.partial(attend_kernel, (req_size, half, fresh_le...  17 us
    pallas_call x2, Pallas kernels, per_device(): pl.pallas_call(functools.partial(project_kernel, part), out_shape=jax.Sha...  16.8 us
    ppermute x4, starting transfers between devices, route(): return lax.ppermute(value, ('req', 'wgt'), pairs)  8.69 us
    all_to_all x1, starting transfers between devices, per_device(): stats = lax.all_to_all(stats, 'wgt', 0, 0, tiled=True)  6.32 us
    unnamed x32, local copies, waits for them, and re-layouts  4.62 us
  transfers between devices with their start and end apart: 12, of which 7 were waited for; matrix products, arithmetic and copies ran while one was open for 8% of the time, Pallas kernels for 12%

profile of v2, /device:TPU:0, one launch (start us, length us, event | category | flops | bytes accessed | tf_op | source)
XLA Modules:
  0.0 153.0 jit_solution(3570799469494381446)
XLA Ops:
  0.6 1.2 convert_reduce_fusion
  1.9 1.4 multiply_reduce_fusion
  3.2 0.1 div.48
  3.3 0.1 stack.19
  3.4 0.6 broadcast_in_dim.65
  4.0 6.3 %all-to-all-start = ((f32[4,2,192]{2,1,0:T(2,128)}), f32[4,2,192]{2,1,0:T(2,128)S(1)}, u32[]{:S(2)}, u32[]{:S(2)}) async-start(f32[4,2,192]{2,1,0:T(2,128)} %broadcast_in_dim.65), calls=%async_computation | async-start | bytes 16384 | tf_op jit(solution)/shard_map/all_to_all | solution.py:324
  10.3 0.0 copy-start.3
  10.3 4.1 %constant_dynamic-slice_fusion = (bf16[768,1152]{1,0:T(8,128)(2,1)}, bf16[768,1152]{1,0:T(8,128)(2,1)}) fusion(bf16[768,2304]{1,0:T(8,128)(2,1)} %param.20, s32[]{:T(128)S(6)} %select_n.70, s32[]{:T(128)S(6)} %select_n.69), kind=kLoop, calls=%fused_computation.44 | loop fusion | bytes 7077896 | tf_op jit(solution)/shard_map/dynamic_slice | solution.py:388
  14.4 0.0 copy-start.15
  14.4 0.0 collective-permute-start.8
  14.4 0.8 dynamic-slice_convert_fusion
  15.2 0.7 all-to-all-done
  16.0 0.0 copy-done.3
  16.0 0.4 fusion.3
  16.4 2.3 %collective-permute-start.2 = (bf16[192,1536]{1,0:T(8,128)(2,1)S(1)}, bf16[192,1536]{1,0:T(8,128)(2,1)S(1)}, u32[]{:S(2)}, u32[]{:S(2)}) collective-permute-start(bf16[192,1536]{1,0:T(8,128)(2,1)S(1)} %fusion.3), channel_id=1, source_target_pairs={{16,0},{24,1},{0,2},{8,3},{20,4},{28,5},{4,6},{12,7},{17,8},{25,9}... | collective-permute-start | bytes 1769480 | tf_op jit(solution)/shard_map/ppermute | solution.py:349
  18.7 3.3 %collective-permute-start.3 = (bf16[192,1536]{1,0:T(8,128)(2,1)S(1)}, bf16[192,1536]{1,0:T(8,128)(2,1)S(1)}, u32[]{:S(2)}, u32[]{:S(2)}) collective-permute-start(bf16[192,1536]{1,0:T(8,128)(2,1)S(1)} %fusion.3), channel_id=1, source_target_pairs={{24,0},{16,1},{8,2},{0,3},{28,4},{20,5},{12,6},{4,7},{25,8},{17,9}... | collective-permute-start | bytes 1769480 | tf_op jit(solution)/shard_map/ppermute | solution.py:349
  22.1 0.7 collective-permute-start
  22.8 2.4 %collective-permute-start.1 = (bf16[192,1536]{1,0:T(8,128)(2,1)S(1)}, bf16[192,1536]{1,0:T(8,128)(2,1)S(1)}, u32[]{:S(2)}, u32[]{:S(2)}) collective-permute-start(bf16[192,1536]{1,0:T(8,128)(2,1)S(1)} %fusion.3), channel_id=1, source_target_pairs={{8,0},{0,1},{24,2},{16,3},{12,4},{4,5},{28,6},{20,7},{9,8},{1,9},{... | collective-permute-start | bytes 1769480 | tf_op jit(solution)/shard_map/ppermute | solution.py:349
  25.1 19.0 %collective-permute-done.2 = bf16[192,1536]{1,0:T(8,128)(2,1)S(1)} collective-permute-done((bf16[192,1536]{1,0:T(8,128)(2,1)S(1)}, bf16[192,1536]{1,0:T(8,128)(2,1)S(1)}, u32[]{:S(2)}, u32[]{:S(2)}) %collective-permute-start.2) | collective-permute-done | bytes 589856 | tf_op jit(solution)/shard_map/ppermute | solution.py:349
  44.2 0.0 collective-permute-start.6
  44.2 0.9 collective-permute-done.3
  45.1 0.0 collective-permute-start.7
  45.1 0.0 collective-permute-done
  45.1 0.5 collective-permute-start.4
  45.6 11.7 %collective-permute-done.1 = bf16[192,1536]{1,0:T(8,128)(2,1)S(1)} collective-permute-done((bf16[192,1536]{1,0:T(8,128)(2,1)S(1)}, bf16[192,1536]{1,0:T(8,128)(2,1)S(1)}, u32[]{:S(2)}, u32[]{:S(2)}) %collective-permute-start.1) | collective-permute-done | bytes 589856 | tf_op jit(solution)/shard_map/ppermute | solution.py:349
  57.3 0.0 collective-permute-start.5
  57.3 0.7 pad_add_fusion.place
  58.0 0.0 copy-done.15
  58.0 0.2 convert_reduce_fusion.1
  58.2 0.6 select_reduce_fusion.source
  58.8 0.0 collective-permute-done.6
  58.9 0.0 collective-permute-done.7
  58.9 0.0 collective-permute-done.4
  58.9 0.0 copy-start.10
  58.9 0.5 collective-permute-done.5
  59.3 0.0 collective-permute-done.8.refs_9_
  59.4 0.9 copy-done.11
  60.3 0.0 copy-done.4
  60.3 0.0 copy-done.5
  60.3 0.0 copy-done.6
  60.3 0.0 copy-done.7
  60.3 0.0 copy-done.8
  60.3 0.0 copy-done.9
  60.3 0.0 copy-done.10
  60.3 1.2 copy-done.2
  61.5 8.4 %project.3 = bf16[8,96,1152]{2,1,0:T(8,128)(2,1)} custom-call(s32[2]{0:T(128)} %pad_add_fusion.place, s32[32]{0:T(128)} %select_reduce_fusion.source, bf16[4,48,1536]{2,1,0:T(8,128)(2,1)} %bitcast.38, bf16[4,48,1536]{2,1,0:T(8,128)(2,1)} %bitcast.40, bf16[4,48,1536]{2,1,0:T(8,128)(2,1)} %bitcast.34, bf16[4,48,1536]{2,1,0:T(8,128)(2,1)} %bitcast.36, ...), custom_call_target="tpu_custom_call" | custom-call | tf_op jit(solution)/shard_map/project/pallas_call | solution.py:396
  69.9 23.3 %all-to-all-start.2 = ((bf16[8,96,1152]{2,1,0:T(8,128)(2,1)}), bf16[8,96,1152]{2,1,0:T(8,128)(2,1)S(1)}, u32[]{:S(2)}, u32[]{:S(2)}) async-start(bf16[8,96,1152]{2,1,0:T(8,128)(2,1)} %project.3), calls=%async_computation.2 | async-start | bytes 3538944 | tf_op jit(solution)/shard_map/all_to_all | solution.py:417
  93.2 8.4 %project.2 = bf16[8,96,1152]{2,1,0:T(8,128)(2,1)} custom-call(s32[2]{0:T(128)} %pad_add_fusion.place, s32[32]{0:T(128)} %select_reduce_fusion.source, bf16[4,48,1536]{2,1,0:T(8,128)(2,1)} %bitcast.39, bf16[4,48,1536]{2,1,0:T(8,128)(2,1)} %bitcast.41, bf16[4,48,1536]{2,1,0:T(8,128)(2,1)} %bitcast.35, bf16[4,48,1536]{2,1,0:T(8,128)(2,1)} %bitcast.37, ...), custom_call_target="tpu_custom_call" | custom-call | tf_op jit(solution)/shard_map/project/pallas_call | solution.py:396
  101.6 0.0 copy-start.12
  101.7 0.0 copy-start.13
  101.7 0.0 copy-start.14
  101.7 14.7 %all-to-all-done.2.refs_0_ = bf16[8,96,1152]{2,1,0:T(8,128)(2,1)S(1)} async-done(((bf16[8,96,1152]{2,1,0:T(8,128)(2,1)}), bf16[8,96,1152]{2,1,0:T(8,128)(2,1)S(1)}, u32[]{:S(2)}, u32[]{:S(2)}) %all-to-all-start.2) | async-done | bytes 1769504 | tf_op jit(solution)/shard_map/all_to_all | solution.py:417
  116.4 1.2 copy-done.1
  117.6 3.6 %all-to-all-start.1 = ((bf16[8,96,1152]{2,1,0:T(8,128)(2,1)}), bf16[8,96,1152]{2,1,0:T(8,128)(2,1)S(1)}, u32[]{:S(2)}, u32[]{:S(2)}) async-start(bf16[8,96,1152]{2,1,0:T(8,128)(2,1)} %project.2), calls=%async_computation.1 | async-start | bytes 3538944 | tf_op jit(solution)/shard_map/all_to_all | solution.py:417
  121.2 0.0 copy-done.12
  121.2 0.6 reshape.185.refs_1_
  121.8 0.0 copy-done.13
  121.8 0.1 add_convert_fusion
  121.9 0.0 copy-done.14
  121.9 4.1 %fusion.4 = (f32[4,48,768]{2,1,0:T(8,128)}, f32[4,48,768]{2,1,0:T(8,128)}, f32[4,48,768]{2,1,0:T(8,128)}) fusion(f32[768]{0:T(1024)S(1)} %copy-done.14, f32[4,48]{1,0:T(4,128)S(1)} %add_convert_fusion, pred[768]{0:T(1024)(128)(4,1)} %constant.124, pred[768]{0:T(1024)(128)(4,1)} %constant.116.clone, pred[768]{0:T(1024)(128)(4,1)} %constant.115.clone), kind=kLoop, calls=%fused_computation.8 | loop fusion | flops 737280 | bytes 1775616 | tf_op jit(solution)/shard_map/jit(_where)/select_n | solution.py:374
  125.9 9.5 %attend.2 = (bf16[2,48,768]{2,1,0:T(8,128)(2,1)}, bf16[2,48,768]{2,1,0:T(8,128)(2,1)}, bf16[2,48,768]{2,1,0:T(8,128)(2,1)}) custom-call(s32[4]{0:T(128)} %all_lengths.3, s32[4,16]{1,0:T(4,128)} %table.3, bf16[8,96,1152]{2,1,0:T(8,128)(2,1)} %copy-done.1, f32[1,2304]{1,0:T(1,128)} %reshape.185.refs_1_, f32[4,48,768]{2,1,0:T(8,128)} %get-tuple-element.20.refs_2_, ...), custom_call_target="tpu_custom_call" | custom-call | tf_op jit(solution)/shard_map/attend/pallas_call | solution.py:427
  135.4 8.8 %all-to-all-done.1.refs_0_ = bf16[8,96,1152]{2,1,0:T(8,128)(2,1)S(1)} async-done(((bf16[8,96,1152]{2,1,0:T(8,128)(2,1)}), bf16[8,96,1152]{2,1,0:T(8,128)(2,1)S(1)}, u32[]{:S(2)}, u32[]{:S(2)}) %all-to-all-start.1) | async-done | bytes 1769504 | tf_op jit(solution)/shard_map/all_to_all | solution.py:417
  144.2 1.3 copy-done
  145.5 7.6 %attend.3 = (bf16[4,48,768]{2,1,0:T(8,128)(2,1)}, bf16[4,48,768]{2,1,0:T(8,128)(2,1)}, bf16[4,48,768]{2,1,0:T(8,128)(2,1)}) custom-call(s32[4]{0:T(128)} %all_lengths.3, s32[4,16]{1,0:T(4,128)} %table.3, bf16[8,96,1152]{2,1,0:T(8,128)(2,1)} %copy-done, f32[1,2304]{1,0:T(1,128)} %reshape.185.refs_1_, f32[4,48,768]{2,1,0:T(8,128)} %get-tuple-element.20.refs_2_, ...), custom_call_target="tpu_custom_call" | custom-call | tf_op jit(solution)/shard_map/attend/pallas_call | solution.py:427
  (17 shorter events, 0.1 us)
Async XLA Ops:
  4.0 11.9 %all-to-all-start = ((f32[4,2,192]{2,1,0:T(2,128)}), f32[4,2,192]{2,1,0:T(2,128)S(1)}, u32[]{:S(2)}, u32[]{:S(2)}) async-start(f32[4,2,192]{2,1,0:T(2,128)} %broadcast_in_dim.65), calls=%async_computation | async-start | bytes 16384 | tf_op jit(solution)/shard_map/all_to_all | solution.py:324
  10.3 5.7 %copy-start.3 = (bf16[4,48,1536]{2,1,0:T(8,128)(2,1)S(1)}, bf16[4,48,1536]{2,1,0:T(8,128)(2,1)}, u32[]{:S(2)}) copy-start(bf16[4,48,1536]{2,1,0:T(8,128)(2,1)} %param.14) | copy-start | bytes 1769476
  14.4 43.6 %copy-start.15 = (s32[32]{0:T(128)S(1)}, s32[32]{0:T(128)}, u32[]{:S(2)}) copy-start(s32[32]{0:T(128)} %param.15) | copy-start | bytes 388
  14.4 44.9 %collective-permute-start.8 = (bf16[768,1152]{1,0:T(8,128)(2,1)}, bf16[768,1152]{1,0:T(8,128)(2,1)S(1)}, u32[]{:S(2)}, u32[]{:S(2)}) collective-permute-start(bf16[768,1152]{1,0:T(8,128)(2,1)} %get-tuple-element.13), channel_id=1, source_target_pairs={{0,4},{4,0},{8,12},{12,8},{16,20},{20,16},{24,28},{28,24},{1,5},{5... | collective-permute-start | bytes 5308424 | tf_op jit(solution)/shard_map/ppermute | solution.py:308
  16.4 27.7 %collective-permute-start.2 = (bf16[192,1536]{1,0:T(8,128)(2,1)S(1)}, bf16[192,1536]{1,0:T(8,128)(2,1)S(1)}, u32[]{:S(2)}, u32[]{:S(2)}) collective-permute-start(bf16[192,1536]{1,0:T(8,128)(2,1)S(1)} %fusion.3), channel_id=1, source_target_pairs={{16,0},{24,1},{0,2},{8,3},{20,4},{28,5},{4,6},{12,7},{17,8},{25,9}... | collective-permute-start | bytes 1769480 | tf_op jit(solution)/shard_map/ppermute | solution.py:349
  18.7 26.4 %collective-permute-start.3 = (bf16[192,1536]{1,0:T(8,128)(2,1)S(1)}, bf16[192,1536]{1,0:T(8,128)(2,1)S(1)}, u32[]{:S(2)}, u32[]{:S(2)}) collective-permute-start(bf16[192,1536]{1,0:T(8,128)(2,1)S(1)} %fusion.3), channel_id=1, source_target_pairs={{24,0},{16,1},{8,2},{0,3},{28,4},{20,5},{12,6},{4,7},{25,8},{17,9}... | collective-permute-start | bytes 1769480 | tf_op jit(solution)/shard_map/ppermute | solution.py:349
  22.1 23.0 %collective-permute-start = (bf16[192,1536]{1,0:T(8,128)(2,1)S(1)}, bf16[192,1536]{1,0:T(8,128)(2,1)S(1)}, u32[]{:S(2)}, u32[]{:S(2)}) collective-permute-start(bf16[192,1536]{1,0:T(8,128)(2,1)S(1)} %fusion.3), channel_id=1, source_target_pairs={{0,0},{8,1},{16,2},{24,3},{4,4},{12,5},{20,6},{28,7},{1,8},{9,9},{... | collective-permute-start | bytes 1769480 | tf_op jit(solution)/shard_map/ppermute | solution.py:349
  22.8 34.6 %collective-permute-start.1 = (bf16[192,1536]{1,0:T(8,128)(2,1)S(1)}, bf16[192,1536]{1,0:T(8,128)(2,1)S(1)}, u32[]{:S(2)}, u32[]{:S(2)}) collective-permute-start(bf16[192,1536]{1,0:T(8,128)(2,1)S(1)} %fusion.3), channel_id=1, source_target_pairs={{8,0},{0,1},{24,2},{16,3},{12,4},{4,5},{28,6},{20,7},{9,8},{1,9},{... | collective-permute-start | bytes 1769480 | tf_op jit(solution)/shard_map/ppermute | solution.py:349
  44.2 16.1 %copy-start.4 = (bf16[192,1536]{1,0:T(8,128)(2,1)}, bf16[192,1536]{1,0:T(8,128)(2,1)S(1)}, u32[]{:S(2)}) copy-start(bf16[192,1536]{1,0:T(8,128)(2,1)S(1)} %collective-permute-done.2) | copy-start | bytes 1769476
  44.2 14.7 %collective-permute-start.6 = (bf16[192,1536]{1,0:T(8,128)(2,1)S(1)}, bf16[192,1536]{1,0:T(8,128)(2,1)S(1)}, u32[]{:S(2)}, u32[]{:S(2)}) collective-permute-start(bf16[192,1536]{1,0:T(8,128)(2,1)S(1)} %collective-permute-done.2), channel_id=1, source_target_pairs={{0,4},{4,0},{8,12},{12,8},{16,20},{20,16},{24,28},{28,24},{1,5},{5... | collective-permute-start | bytes 1769480 | tf_op jit(solution)/shard_map/ppermute | solution.py:308
  45.1 15.2 %copy-start.5 = (bf16[192,1536]{1,0:T(8,128)(2,1)}, bf16[192,1536]{1,0:T(8,128)(2,1)S(1)}, u32[]{:S(2)}) copy-start(bf16[192,1536]{1,0:T(8,128)(2,1)S(1)} %collective-permute-done.3) | copy-start | bytes 1769476
  45.1 13.8 %collective-permute-start.7 = (bf16[192,1536]{1,0:T(8,128)(2,1)S(1)}, bf16[192,1536]{1,0:T(8,128)(2,1)S(1)}, u32[]{:S(2)}, u32[]{:S(2)}) collective-permute-start(bf16[192,1536]{1,0:T(8,128)(2,1)S(1)} %collective-permute-done.3), channel_id=1, source_target_pairs={{0,4},{4,0},{8,12},{12,8},{16,20},{20,16},{24,28},{28,24},{1,5},{5... | collective-permute-start | bytes 1769480 | tf_op jit(solution)/shard_map/ppermute | solution.py:308
  45.1 15.2 %copy-start.6 = (bf16[192,1536]{1,0:T(8,128)(2,1)}, bf16[192,1536]{1,0:T(8,128)(2,1)S(1)}, u32[]{:S(2)}) copy-start(bf16[192,1536]{1,0:T(8,128)(2,1)S(1)} %collective-permute-done) | copy-start | bytes 1769476
  45.1 13.8 %collective-permute-start.4 = (bf16[192,1536]{1,0:T(8,128)(2,1)S(1)}, bf16[192,1536]{1,0:T(8,128)(2,1)S(1)}, u32[]{:S(2)}, u32[]{:S(2)}) collective-permute-start(bf16[192,1536]{1,0:T(8,128)(2,1)S(1)} %collective-permute-done), channel_id=1, source_target_pairs={{0,4},{4,0},{8,12},{12,8},{16,20},{20,16},{24,28},{28,24},{1,5},{5... | collective-permute-start | bytes 1769480 | tf_op jit(solution)/shard_map/ppermute | solution.py:308
  57.3 2.9 %copy-start.7 = (bf16[192,1536]{1,0:T(8,128)(2,1)}, bf16[192,1536]{1,0:T(8,128)(2,1)S(1)}, u32[]{:S(2)}) copy-start(bf16[192,1536]{1,0:T(8,128)(2,1)S(1)} %collective-permute-done.1) | copy-start | bytes 1769476
  57.3 2.0 %collective-permute-start.5 = (bf16[192,1536]{1,0:T(8,128)(2,1)S(1)}, bf16[192,1536]{1,0:T(8,128)(2,1)S(1)}, u32[]{:S(2)}, u32[]{:S(2)}) collective-permute-start(bf16[192,1536]{1,0:T(8,128)(2,1)S(1)} %collective-permute-done.1), channel_id=1, source_target_pairs={{0,4},{4,0},{8,12},{12,8},{16,20},{20,16},{24,28},{28,24},{1,5},{5... | collective-permute-start | bytes 1769480 | tf_op jit(solution)/shard_map/ppermute | solution.py:308
  58.8 1.4 copy-start.8
  58.9 1.4 copy-start.9
  58.9 1.4 copy-start.10
  59.3 0.9 copy-start.11
  60.3 1.2 copy-start.2
  69.9 46.5 %all-to-all-start.2 = ((bf16[8,96,1152]{2,1,0:T(8,128)(2,1)}), bf16[8,96,1152]{2,1,0:T(8,128)(2,1)S(1)}, u32[]{:S(2)}, u32[]{:S(2)}) async-start(bf16[8,96,1152]{2,1,0:T(8,128)(2,1)} %project.3), calls=%async_computation.2 | async-start | bytes 3538944 | tf_op jit(solution)/shard_map/all_to_all | solution.py:417
  101.6 19.5 %copy-start.12 = (bf16[2304]{0:T(1024)(128)(2,1)S(1)}, bf16[2304]{0:T(1024)(128)(2,1)}, u32[]{:S(2)}) copy-start(bf16[2304]{0:T(1024)(128)(2,1)} %param.21) | copy-start | bytes 13828
  101.7 20.1 %copy-start.13 = (s32[4]{0:T(128)S(1)}, s32[4]{0:T(128)}, u32[]{:S(2)}) copy-start(s32[4]{0:T(128)} %all_lengths.3) | copy-start | bytes 52
  101.7 20.2 %copy-start.14 = (f32[768]{0:T(1024)S(1)}, f32[768]{0:T(1024)}, u32[]{:S(2)}) copy-start(f32[768]{0:T(1024)} %constant.123) | copy-start | bytes 9220
  116.3 1.2 copy-start.1
  117.6 26.7 %all-to-all-start.1 = ((bf16[8,96,1152]{2,1,0:T(8,128)(2,1)}), bf16[8,96,1152]{2,1,0:T(8,128)(2,1)S(1)}, u32[]{:S(2)}, u32[]{:S(2)}) async-start(bf16[8,96,1152]{2,1,0:T(8,128)(2,1)} %project.2), calls=%async_computation.1 | async-start | bytes 3538944 | tf_op jit(solution)/shard_map/all_to_all | solution.py:417
  144.2 1.3 copy-start

commit v3 on v2

--- a/solution.py
+++ b/solution.py
@@ -22,16 +22,17 @@
 HBM = pl.BlockSpec(memory_space=pltpu.HBM)
 
 
-def project_kernel(part, place, source, *refs):
-    groups = len(refs) - 10
+def project_kernel(part, plan, place, source, *refs):
+    groups = sum(len(members) for members, _ in plan)
     tokens = refs[:groups]
     own_rows, other_rows = refs[groups : groups + 2]
-    out, held, weights, picked, ready, sems, weight_sems, out_sems = refs[groups + 2 :]
+    outs = refs[groups + 2 : -5]
+    held, weights, picked, sems, weight_sems = refs[-5:]
     core, begin = place[0], place[1]
     depth = own_rows.shape[0]
     chips = groups // 2
     req_count, fresh_len = tokens[0].shape[:2]
-    rows = out.shape[1]
+    rows = outs[0].shape[1]
     held_count = rows // fresh_len
     copies = [
         pltpu.make_async_copy(
@@ -60,32 +61,32 @@
     for copy in copies:
         copy.wait()
     together = min(groups, 4)
-    sent = []
+    targets = [
+        (output, index, target)
+        for output, (members, _) in enumerate(plan)
+        for index, target in enumerate(members)
+    ]
     for first in range(0, groups, together):
-        for item in range(together * held_count):
-            picked[item * fresh_len : (item + 1) * fresh_len, :] = held[
-                source[(part * groups + first) * held_count + item]
-            ]
-        result = jnp.dot(picked[...], weights[...], preferred_element_type=jnp.float32).astype(
-            jnp.bfloat16
-        )
-        for index in range(together):
-            ready[first + index] = result[index * rows : (index + 1) * rows]
-        targets = pl.ds(first, together)
-        sent.append(
-            pltpu.make_async_copy(
-                ready.at[targets], out.at[targets], out_sems.at[first // together]
+        these = targets[first : first + together]
+        for count, (_, _, target) in enumerate(these):
+            for item in range(held_count):
+                at = (count * held_count + item) * fresh_len
+                picked[at : at + fresh_len, :] = held[
+                    source[(part * groups + target) * held_count + item]
+                ]
+        result = jnp.dot(picked[...], weights[...], preferred_element_type=jnp.float32)
+        for count, (output, index, _) in enumerate(these):
+            outs[output][index] = result[count * rows : (count + 1) * rows].astype(
+                outs[output].dtype
             )
-        )
-        sent[-1].start()
-    for copy in sent:
-        copy.wait()
-
-
-def attend_kernel(shape, all_lengths, table, *refs):
-    groups, held_count, fresh_len, page, heads, part = shape
-    parts, bias, cosine, sine_up, sine_down, key_pool, value_pool = refs[:7]
-    before = refs[7:-6]
+
+
+def attend_kernel(shape, place, all_lengths, table, *refs):
+    terms, held_count, fresh_len, page, heads, part = shape
+    near, far = refs[: terms[0]], refs[terms[0] : sum(terms)]
+    refs = refs[sum(terms) :]
+    bias, cosine, sine_up, sine_down, key_pool, value_pool = refs[:6]
+    before = refs[6:-6]
     outs = refs[-6:-3]
     keys, values, sems = refs[-3:]
     chunk = CHUNK_PAGES * page
@@ -123,10 +124,9 @@
         ]
         return held.reshape(chunk, WINDOW)
 
-    halves = [
-        sum(parts[index].astype(jnp.float32) for index in range(side, groups, 2))
-        for side in range(2)
-    ]
+    near, far = (sum(ref[0].astype(jnp.float32) for ref in refs) for refs in (near, far))
+    core = place[0]
+    halves = jnp.where(core == 0, near, far), jnp.where(core == 0, far, near)
     halves = [
         half + bias[:, side * half.shape[1] : (side + 1) * half.shape[1]]
         for side, half in enumerate(halves)
@@ -355,7 +355,7 @@
     earlier = ids[None, :] < ids[:, None]
     rank = jnp.sum((same_group & earlier).astype(jnp.int32), axis=1)
     part_of, within = rank // half, rank % half
-    wanted = (part_of * req_size + group_of) * half + within
+    wanted = (part_of * req_size + (group_of ^ me)) * half + within
     origin = ids // req_count
     row = (((origin & 1) ^ core) * chips + (origin >> 1)) * req_count + ids % req_count
     sources = jnp.sum(jnp.where(wanted[None, :] == ids[:, None], row[None, :], 0), axis=1)
@@ -390,22 +390,42 @@
     received += [swap(piece, 1) for piece in received]
     received = [piece.reshape(req_count, fresh_len, block) for piece in received]
 
+    square_plane = chips == 4
+    if square_plane:
+        plan = [([2, 6], jnp.bfloat16), ([5, 7], jnp.bfloat16)]
+        plan += [([distance], jnp.float32) for distance in (0, 4, 1, 3)]
+    else:
+        plan = [([0], jnp.float32)]
+        plan += [([distance], jnp.bfloat16) for distance in range(1, req_size)]
+
+    def collect(blocks):
+        if not square_plane:
+            sums = [blocks[0]]
+            sums += [swap(block, distance) for distance, block in enumerate(blocks[1:], 1)]
+            return sums[::2], sums[1::2]
+        along_x, along_y = swap(blocks[0], 2), swap(blocks[1], 4)
+        own, own_y, other, other_x = blocks[2:]
+        behind_y = swap((own_y + along_x[1:]).astype(jnp.bfloat16), 4)
+        behind_x = swap((other_x + along_y[1:]).astype(jnp.bfloat16), 2)
+        return [own, along_x, behind_y], [swap(other + along_y[:1], 1), swap(behind_x, 1)]
+
     projected = []
     for part in range(2):
         projected.append(
             pl.pallas_call(
-                functools.partial(project_kernel, part),
-                out_shape=jax.ShapeDtypeStruct((req_size, chunk_rows, half_cols), jnp.bfloat16),
+                functools.partial(project_kernel, part, plan),
+                out_shape=[
+                    jax.ShapeDtypeStruct((len(members), chunk_rows, half_cols), kind)
+                    for members, kind in plan
+                ],
                 in_specs=[SMEM] * 2 + [HBM] * (req_size + 2),
-                out_specs=HBM,
+                out_specs=[VMEM] * len(plan),
                 scratch_shapes=[
                     pltpu.VMEM((everyone, fresh_len, block), jnp.bfloat16),
                     pltpu.VMEM((block, half_cols), jnp.bfloat16),
                     pltpu.VMEM((min(req_size, 4) * chunk_rows, block), jnp.bfloat16),
-                    pltpu.VMEM((req_size, chunk_rows, half_cols), jnp.bfloat16),
                     pltpu.SemaphoreType.DMA((req_size,)),
                     pltpu.SemaphoreType.DMA((2,)),
-                    pltpu.SemaphoreType.DMA((req_size // min(req_size, 4),)),
                 ],
                 compiler_params=pltpu.CompilerParams(vmem_limit_bytes=VMEM_LIMIT),
                 name="project",
@@ -414,19 +434,17 @@
 
     results = []
     for part in range(2):
-        parts = lax.all_to_all(projected[part], "req", 0, 0, tiled=True)
-        if part == 0:
-            parts = after(parts, projected[1])
-
+        near, far = collect(projected[part])
         operands = [
-            lengths, page_table, parts, bias, *tables, key_pool, value_pool
+            place, lengths, page_table, *near, *far, bias, *tables, key_pool, value_pool
         ]
-        specs = [SMEM] * 2 + [VMEM] * 5 + [HBM] * 2
+        terms = len(near), len(far)
+        specs = [SMEM] * 3 + [VMEM] * (sum(terms) + 4) + [HBM] * 2
         count = half if part == 0 else req_count
         out = jax.ShapeDtypeStruct((count, fresh_len, heads * HEAD), jnp.bfloat16)
         results = pl.pallas_call(
             functools.partial(
-                attend_kernel, (req_size, half, fresh_len, page, heads, part)
+                attend_kernel, (terms, half, fresh_len, page, heads, part)
             ),
             out_shape=[out] * 3,
             in_specs=specs + [VMEM] * len(results),

time: 154 us -> 149 us (0.968)
  waiting for transfers between devices: 56.4 us -> 48.7 us
  Pallas kernels: 33.8 us -> 35.4 us
    ppermute x5 -> x17, starting transfers between devices: 0.52 us -> 28.9 us  [swap(): lax.ppermute(value, 'req', [(device, device ^ distance) for device in ran...]
    all_to_all x2 -> x0, starting transfers between devices: 26.9 us -> none  [per_device(): parts = lax.all_to_all(projected[part], 'req', 0, 0, tiled=True)]
    all_to_all x2 -> x0, waiting for transfers between devices: 23.5 us -> none  [per_device(): parts = lax.all_to_all(projected[part], 'req', 0, 0, tiled=True)]
    ppermute x5 -> x17, waiting for transfers between devices: 0.48 us -> 16.3 us  [swap(): lax.ppermute(value, 'req', [(device, device ^ distance) for device in ran...]
    pallas_call x4, Pallas kernels: 33.8 us -> 35.4 us  [the longest x2 18.1 us: per_device(): pl.pallas_call(functools.partial(attend_kernel, (terms, half, fresh_len,...]
    unnamed x32 -> x62, local copies, waits for them, and re-layouts: 4.62 us -> 3.89 us
  transfers between devices with their start and end apart: 12 -> 22, of which waited for: 7 -> 9; matrix products, arithmetic and copies ran while one was open for 8% -> 8% of each run, Pallas kernels for 12% -> 13%
where the time goes in v3:
time: 149 us; the launch traced here: 148 us
  waiting for transfers between devices  48.7 us (33%)
  starting transfers between devices  43.9 us (29%)
  Pallas kernels  35.4 us (24%)
  local copies, waits for them, and re-layouts  9.36 us (6%)
  other arithmetic  9.15 us (6%)
    ppermute x4, waiting for transfers between devices, route(): return lax.ppermute(value, ('req', 'wgt'), pairs)  31.7 us
    ppermute x17, starting transfers between devices, swap(): lax.ppermute(value, 'req', [(device, device ^ distance) for device in ran...  28.9 us
    pallas_call x2, Pallas kernels, per_device(): pl.pallas_call(functools.partial(attend_kernel, (terms, half, fresh_len,...  18.1 us
    pallas_call x2, Pallas kernels, per_device(): pl.pallas_call(functools.partial(project_kernel, part, plan), out_shape=[...  17.3 us
    ppermute x17, waiting for transfers between devices, swap(): lax.ppermute(value, 'req', [(device, device ^ distance) for device in ran...  16.3 us
    ppermute x4, starting transfers between devices, route(): return lax.ppermute(value, ('req', 'wgt'), pairs)  8.68 us
    all_to_all x1, starting transfers between devices, per_device(): stats = lax.all_to_all(stats, 'wgt', 0, 0, tiled=True)  6.32 us
    dynamic_slice x1, local copies, waits for them, and re-layouts, per_device(): lax.dynamic_slice_in_dim(held, (1 - core) * half_cols, half_cols, 1)  4.1 us
  transfers between devices with their start and end apart: 22, of which 9 were waited for; matrix products, arithmetic and copies ran while one was open for 8% of the time, Pallas kernels for 13%

profile of v3, /device:TPU:0, one launch (start us, length us, event | category | flops | bytes accessed | tf_op | source)
XLA Modules:
  0.0 147.5 jit_solution(6109414476255013794)
XLA Ops:
  0.6 1.2 convert_reduce_fusion
  1.9 1.4 multiply_reduce_fusion
  3.2 0.1 div.48
  3.3 0.1 stack.19
  3.4 0.6 broadcast_in_dim.65
  4.0 6.3 %all-to-all-start = ((f32[4,2,192]{2,1,0:T(2,128)}), f32[4,2,192]{2,1,0:T(2,128)S(1)}, u32[]{:S(2)}, u32[]{:S(2)}) async-start(f32[4,2,192]{2,1,0:T(2,128)} %broadcast_in_dim.65), calls=%async_computation | async-start | bytes 16384 | tf_op jit(solution)/shard_map/all_to_all | solution.py:324
  10.3 4.1 %constant_dynamic-slice_fusion = (bf16[768,1152]{1,0:T(8,128)(2,1)}, bf16[768,1152]{1,0:T(8,128)(2,1)}) fusion(bf16[768,2304]{1,0:T(8,128)(2,1)} %param.20, s32[]{:T(128)S(6)} %select_n.70, s32[]{:T(128)S(6)} %select_n.69), kind=kLoop, calls=%fused_computation.50 | loop fusion | bytes 7077896 | tf_op jit(solution)/shard_map/dynamic_slice | solution.py:388
  14.4 0.0 collective-permute-start.8
  14.4 0.8 dynamic-slice_convert_fusion
  15.2 0.7 all-to-all-done
  16.0 0.4 fusion.3
  16.4 2.3 %collective-permute-start.2 = (bf16[192,1536]{1,0:T(8,128)(2,1)S(1)}, bf16[192,1536]{1,0:T(8,128)(2,1)S(1)}, u32[]{:S(2)}, u32[]{:S(2)}) collective-permute-start(bf16[192,1536]{1,0:T(8,128)(2,1)S(1)} %fusion.3), channel_id=1, source_target_pairs={{16,0},{24,1},{0,2},{8,3},{20,4},{28,5},{4,6},{12,7},{17,8},{25,9}... | collective-permute-start | bytes 1769480 | tf_op jit(solution)/shard_map/ppermute | solution.py:349
  18.7 3.3 %collective-permute-start.3 = (bf16[192,1536]{1,0:T(8,128)(2,1)S(1)}, bf16[192,1536]{1,0:T(8,128)(2,1)S(1)}, u32[]{:S(2)}, u32[]{:S(2)}) collective-permute-start(bf16[192,1536]{1,0:T(8,128)(2,1)S(1)} %fusion.3), channel_id=1, source_target_pairs={{24,0},{16,1},{8,2},{0,3},{28,4},{20,5},{12,6},{4,7},{25,8},{17,9}... | collective-permute-start | bytes 1769480 | tf_op jit(solution)/shard_map/ppermute | solution.py:349
  22.1 0.7 collective-permute-start
  22.8 2.4 %collective-permute-start.1 = (bf16[192,1536]{1,0:T(8,128)(2,1)S(1)}, bf16[192,1536]{1,0:T(8,128)(2,1)S(1)}, u32[]{:S(2)}, u32[]{:S(2)}) collective-permute-start(bf16[192,1536]{1,0:T(8,128)(2,1)S(1)} %fusion.3), channel_id=1, source_target_pairs={{8,0},{0,1},{24,2},{16,3},{12,4},{4,5},{28,6},{20,7},{9,8},{1,9},{... | collective-permute-start | bytes 1769480 | tf_op jit(solution)/shard_map/ppermute | solution.py:349
  25.1 19.0 %collective-permute-done.2 = bf16[192,1536]{1,0:T(8,128)(2,1)S(1)} collective-permute-done((bf16[192,1536]{1,0:T(8,128)(2,1)S(1)}, bf16[192,1536]{1,0:T(8,128)(2,1)S(1)}, u32[]{:S(2)}, u32[]{:S(2)}) %collective-permute-start.2) | collective-permute-done | bytes 589856 | tf_op jit(solution)/shard_map/ppermute | solution.py:349
  44.2 0.0 collective-permute-start.6
  44.2 0.9 collective-permute-done.3
  45.1 0.5 collective-permute-start.4
  45.6 11.7 %collective-permute-done.1 = bf16[192,1536]{1,0:T(8,128)(2,1)S(1)} collective-permute-done((bf16[192,1536]{1,0:T(8,128)(2,1)S(1)}, bf16[192,1536]{1,0:T(8,128)(2,1)S(1)}, u32[]{:S(2)}, u32[]{:S(2)}) %collective-permute-start.1) | collective-permute-done | bytes 589856 | tf_op jit(solution)/shard_map/ppermute | solution.py:349
  57.3 0.7 pad_add_fusion.place
  58.0 0.2 convert_reduce_fusion.1
  58.2 0.6 select_reduce_fusion.source
  58.9 0.0 collective-permute-done.6
  58.9 0.0 collective-permute-done.4
  58.9 0.5 collective-permute-done.5
  59.4 0.9 copy-done.9
  60.3 1.2 copy-done
  61.5 8.7 %project.3 = (bf16[2,96,1152]{2,1,0:T(8,128)(2,1)}, bf16[2,96,1152]{2,1,0:T(8,128)(2,1)}, f32[1,96,1152]{2,1,0:T(8,128)}, f32[1,96,1152]{2,1,0:T(8,128)}, f32[1,...) custom-call(s32[2]{0:T(128)} %pad_add_fusion.place, s32[32]{0:T(128)} %select_reduce_fusion.source, ...), custom_call_target="tpu_custom_call" | custom-call | tf_op jit(solution)/shard_map/project/pallas_call | solution.py:415
  70.2 22.1 %collective-permute-start.17 = (bf16[2,96,1152]{2,1,0:T(8,128)(2,1)}, bf16[2,96,1152]{2,1,0:T(8,128)(2,1)S(1)}, u32[]{:S(2)}, u32[]{:S(2)}) collective-permute-start(bf16[2,96,1152]{2,1,0:T(8,128)(2,1)} %get-tuple-element.30), channel_id=1, source_target_pairs={{0,16},{4,20},{8,24},{12,28},{16,0},{20,4},{24,8},{28,12},{1,17},{... | collective-permute-start | bytes 1327112 | tf_op jit(solution)/shard_map/ppermute | solution.py:308
  92.3 0.6 reshape.185.refs_5_
  92.9 0.1 add_convert_fusion.4
  93.0 0.0 collective-permute-start.15
  93.0 8.7 %project.2 = (bf16[2,96,1152]{2,1,0:T(8,128)(2,1)}, bf16[2,96,1152]{2,1,0:T(8,128)(2,1)}, f32[1,96,1152]{2,1,0:T(8,128)}, f32[1,96,1152]{2,1,0:T(8,128)}, f32[1,...) custom-call(s32[2]{0:T(128)} %pad_add_fusion.place, s32[32]{0:T(128)} %select_reduce_fusion.source, ...), custom_call_target="tpu_custom_call" | custom-call | tf_op jit(solution)/shard_map/project/pallas_call | solution.py:415
  101.7 0.1 collective-permute-start.11
  101.8 1.9 %collective-permute-start.9 = (bf16[2,96,1152]{2,1,0:T(8,128)(2,1)}, bf16[2,96,1152]{2,1,0:T(8,128)(2,1)S(1)}, u32[]{:S(2)}, u32[]{:S(2)}) collective-permute-start(bf16[2,96,1152]{2,1,0:T(8,128)(2,1)} %get-tuple-element.21), channel_id=1, source_target_pairs={{0,8},{4,12},{8,0},{12,4},{16,24},{20,28},{24,16},{28,20},{1,9},{5... | collective-permute-start | bytes 1327112 | tf_op jit(solution)/shard_map/ppermute | solution.py:308
  103.7 0.1 add_convert_fusion
  103.8 0.2 collective-permute-start.19
  104.0 1.7 %collective-permute-done.15.refs_1_ = bf16[2,96,1152]{2,1,0:T(8,128)(2,1)S(1)} collective-permute-done((bf16[2,96,1152]{2,1,0:T(8,128)(2,1)}, bf16[2,96,1152]{2,1,0:T(8,128)(2,1)S(1)}, u32[]{:S(2)}, u32[]{:S(2)}) %collective-permute-start.15) | collective-permute-done | bytes 442400 | tf_op jit(solution)/shard_map/ppermute | solution.py:308
  105.8 0.1 add_convert_fusion.1
  105.9 0.3 collective-permute-start.16
  106.1 8.8 %collective-permute-done.11 = bf16[2,96,1152]{2,1,0:T(8,128)(2,1)S(1)} collective-permute-done((bf16[2,96,1152]{2,1,0:T(8,128)(2,1)}, bf16[2,96,1152]{2,1,0:T(8,128)(2,1)S(1)}, u32[]{:S(2)}, u32[]{:S(2)}) %collective-permute-start.11) | collective-permute-done | bytes 442400 | tf_op jit(solution)/shard_map/ppermute | solution.py:308
  115.0 0.0 copy-start.28
  115.0 0.0 copy-start.29
  115.0 0.1 add_convert_fusion.2
  115.1 2.0 %collective-permute-start.13 = (bf16[1,96,1152]{2,1,0:T(8,128)(2,1)S(1)}, bf16[1,96,1152]{2,1,0:T(8,128)(2,1)S(1)}, u32[]{:S(2)}, u32[]{:S(2)}) collective-permute-start(bf16[1,96,1152]{2,1,0:T(8,128)(2,1)S(1)} %get-tuple-element.39), channel_id=1, source_target_pairs={{0,8},{4,12},{8,0},{12,4},{16,24},{20,28},{24,16},{28,20},{1,9},{5... | collective-permute-start | bytes 663560 | tf_op jit(solution)/shard_map/ppermute | solution.py:308
  117.1 0.0 collective-permute-done.9.refs_1_
  117.1 0.0 collective-permute-start.12
  117.2 2.8 %collective-permute-done.19 = bf16[1,96,1152]{2,1,0:T(8,128)(2,1)S(1)} collective-permute-done((bf16[1,96,1152]{2,1,0:T(8,128)(2,1)S(1)}, bf16[1,96,1152]{2,1,0:T(8,128)(2,1)S(1)}, u32[]{:S(2)}, u32[]{:S(2)}) %collective-permute-start.19) | collective-permute-done | bytes 221216 | tf_op jit(solution)/shard_map/ppermute | solution.py:308
  120.0 1.8 %collective-permute-start.10 = (bf16[1,96,1152]{2,1,0:T(8,128)(2,1)S(1)}, bf16[1,96,1152]{2,1,0:T(8,128)(2,1)S(1)}, u32[]{:S(2)}, u32[]{:S(2)}) collective-permute-start(bf16[1,96,1152]{2,1,0:T(8,128)(2,1)S(1)} %add_convert_fusion.3), channel_id=1, source_target_pairs={{0,16},{4,20},{8,24},{12,28},{16,0},{20,4},{24,8},{28,12},{1,17},{... | collective-permute-start | bytes 663560 | tf_op jit(solution)/shard_map/ppermute | solution.py:308
  121.8 0.0 collective-permute-done.16.refs_2_
  121.8 0.0 collective-permute-start.20
  121.8 2.4 %collective-permute-done.13 = bf16[1,96,1152]{2,1,0:T(8,128)(2,1)S(1)} collective-permute-done((bf16[1,96,1152]{2,1,0:T(8,128)(2,1)S(1)}, bf16[1,96,1152]{2,1,0:T(8,128)(2,1)S(1)}, u32[]{:S(2)}, u32[]{:S(2)}) %collective-permute-start.13) | collective-permute-done | bytes 221216 | tf_op jit(solution)/shard_map/ppermute | solution.py:308
  124.2 0.0 collective-permute-start.14
  124.2 3.4 %fusion.4 = (f32[4,48,768]{2,1,0:T(8,128)}, f32[4,48,768]{2,1,0:T(8,128)}, f32[4,48,768]{2,1,0:T(8,128)}) fusion(f32[768]{0:T(1024)S(1)} %copy-done.26, f32[4,48]{1,0:T(4,128)S(1)} %add_convert_fusion.4, pred[768]{0:T(1024)(128)(4,1)S(1)} %copy-done.29, pred[768]{0:T(1024)(128)(4,1)S(1)} %copy-done.28, pred[768]{0:T(1024)(128)(4,1)S(1)} %copy-done.27), kind=kLoop, calls=%fused_computation.8 | loop fusion | flops 737280 | bytes 1775616 | tf_op jit(solution)/shard_map/jit(_where)/select_n | solution.py:374
  127.7 0.0 collective-permute-done.20.refs_4_
  127.7 0.0 collective-permute-done.18.refs_3_
  127.7 0.6 copy-done.23
  128.3 0.2 copy-done.12
  128.5 10.5 %attend.2 = (bf16[2,48,768]{2,1,0:T(8,128)(2,1)}, bf16[2,48,768]{2,1,0:T(8,128)(2,1)}, bf16[2,48,768]{2,1,0:T(8,128)(2,1)}) custom-call(s32[2]{0:T(128)} %pad_add_fusion.place, s32[4]{0:T(128)} %all_lengths.3, s32[4,16]{1,0:T(4,128)} %table.3, f32[1,96,1152]{2,1,0:T(8,128)} %get-tuple-element.26.refs_0_, bf16[2,96,1152]{2,1,0:T(8,128)(2,1)} %copy-done.10, ...), custom_call_target="tpu_custom_call" | custom-call | tf_op jit(solution)/shard_map/attend/pallas_call | solution.py:445
  139.1 0.6 copy-done.21
  139.8 0.1 copy-done.22
  139.8 0.2 copy-done.19
  140.0 7.6 %attend.3 = (bf16[4,48,768]{2,1,0:T(8,128)(2,1)}, bf16[4,48,768]{2,1,0:T(8,128)(2,1)}, bf16[4,48,768]{2,1,0:T(8,128)(2,1)}) custom-call(s32[2]{0:T(128)} %pad_add_fusion.place, s32[4]{0:T(128)} %all_lengths.3, s32[4,16]{1,0:T(4,128)} %table.3, f32[1,96,1152]{2,1,0:T(8,128)} %get-tuple-element.20.refs_0_, bf16[2,96,1152]{2,1,0:T(8,128)(2,1)} %copy-done.11, ...), custom_call_target="tpu_custom_call" | custom-call | tf_op jit(solution)/shard_map/attend/pallas_call | solution.py:445
  (71 shorter events, 0.3 us)
Async XLA Ops:
  4.0 11.9 %all-to-all-start = ((f32[4,2,192]{2,1,0:T(2,128)}), f32[4,2,192]{2,1,0:T(2,128)S(1)}, u32[]{:S(2)}, u32[]{:S(2)}) async-start(f32[4,2,192]{2,1,0:T(2,128)} %broadcast_in_dim.65), calls=%async_computation | async-start | bytes 16384 | tf_op jit(solution)/shard_map/all_to_all | solution.py:324
  10.3 5.7 %copy-start.1 = (bf16[4,48,1536]{2,1,0:T(8,128)(2,1)S(1)}, bf16[4,48,1536]{2,1,0:T(8,128)(2,1)}, u32[]{:S(2)}) copy-start(bf16[4,48,1536]{2,1,0:T(8,128)(2,1)} %param.14) | copy-start | bytes 1769476
  14.4 43.6 %copy-start.30 = (s32[32]{0:T(128)S(1)}, s32[32]{0:T(128)}, u32[]{:S(2)}) copy-start(s32[32]{0:T(128)} %param.15) | copy-start | bytes 388
  14.4 44.9 %collective-permute-start.8 = (bf16[768,1152]{1,0:T(8,128)(2,1)}, bf16[768,1152]{1,0:T(8,128)(2,1)S(1)}, u32[]{:S(2)}, u32[]{:S(2)}) collective-permute-start(bf16[768,1152]{1,0:T(8,128)(2,1)} %get-tuple-element.35), channel_id=1, source_target_pairs={{0,4},{4,0},{8,12},{12,8},{16,20},{20,16},{24,28},{28,24},{1,5},{5... | collective-permute-start | bytes 5308424 | tf_op jit(solution)/shard_map/ppermute | solution.py:308
  16.4 27.7 %collective-permute-start.2 = (bf16[192,1536]{1,0:T(8,128)(2,1)S(1)}, bf16[192,1536]{1,0:T(8,128)(2,1)S(1)}, u32[]{:S(2)}, u32[]{:S(2)}) collective-permute-start(bf16[192,1536]{1,0:T(8,128)(2,1)S(1)} %fusion.3), channel_id=1, source_target_pairs={{16,0},{24,1},{0,2},{8,3},{20,4},{28,5},{4,6},{12,7},{17,8},{25,9}... | collective-permute-start | bytes 1769480 | tf_op jit(solution)/shard_map/ppermute | solution.py:349
  18.7 26.4 %collective-permute-start.3 = (bf16[192,1536]{1,0:T(8,128)(2,1)S(1)}, bf16[192,1536]{1,0:T(8,128)(2,1)S(1)}, u32[]{:S(2)}, u32[]{:S(2)}) collective-permute-start(bf16[192,1536]{1,0:T(8,128)(2,1)S(1)} %fusion.3), channel_id=1, source_target_pairs={{24,0},{16,1},{8,2},{0,3},{28,4},{20,5},{12,6},{4,7},{25,8},{17,9}... | collective-permute-start | bytes 1769480 | tf_op jit(solution)/shard_map/ppermute | solution.py:349
  22.1 23.0 %collective-permute-start = (bf16[192,1536]{1,0:T(8,128)(2,1)S(1)}, bf16[192,1536]{1,0:T(8,128)(2,1)S(1)}, u32[]{:S(2)}, u32[]{:S(2)}) collective-permute-start(bf16[192,1536]{1,0:T(8,128)(2,1)S(1)} %fusion.3), channel_id=1, source_target_pairs={{0,0},{8,1},{16,2},{24,3},{4,4},{12,5},{20,6},{28,7},{1,8},{9,9},{... | collective-permute-start | bytes 1769480 | tf_op jit(solution)/shard_map/ppermute | solution.py:349
  22.8 34.6 %collective-permute-start.1 = (bf16[192,1536]{1,0:T(8,128)(2,1)S(1)}, bf16[192,1536]{1,0:T(8,128)(2,1)S(1)}, u32[]{:S(2)}, u32[]{:S(2)}) collective-permute-start(bf16[192,1536]{1,0:T(8,128)(2,1)S(1)} %fusion.3), channel_id=1, source_target_pairs={{8,0},{0,1},{24,2},{16,3},{12,4},{4,5},{28,6},{20,7},{9,8},{1,9},{... | collective-permute-start | bytes 1769480 | tf_op jit(solution)/shard_map/ppermute | solution.py:349
  44.2 16.1 %copy-start.2 = (bf16[192,1536]{1,0:T(8,128)(2,1)}, bf16[192,1536]{1,0:T(8,128)(2,1)S(1)}, u32[]{:S(2)}) copy-start(bf16[192,1536]{1,0:T(8,128)(2,1)S(1)} %collective-permute-done.2) | copy-start | bytes 1769476
  44.2 14.7 %collective-permute-start.6 = (bf16[192,1536]{1,0:T(8,128)(2,1)S(1)}, bf16[192,1536]{1,0:T(8,128)(2,1)S(1)}, u32[]{:S(2)}, u32[]{:S(2)}) collective-permute-start(bf16[192,1536]{1,0:T(8,128)(2,1)S(1)} %collective-permute-done.2), channel_id=1, source_target_pairs={{0,4},{4,0},{8,12},{12,8},{16,20},{20,16},{24,28},{28,24},{1,5},{5... | collective-permute-start | bytes 1769480 | tf_op jit(solution)/shard_map/ppermute | solution.py:308
  45.1 15.2 %copy-start.3 = (bf16[192,1536]{1,0:T(8,128)(2,1)}, bf16[192,1536]{1,0:T(8,128)(2,1)S(1)}, u32[]{:S(2)}) copy-start(bf16[192,1536]{1,0:T(8,128)(2,1)S(1)} %collective-permute-done.3) | copy-start | bytes 1769476
  45.1 13.8 %collective-permute-start.7 = (bf16[192,1536]{1,0:T(8,128)(2,1)S(1)}, bf16[192,1536]{1,0:T(8,128)(2,1)S(1)}, u32[]{:S(2)}, u32[]{:S(2)}) collective-permute-start(bf16[192,1536]{1,0:T(8,128)(2,1)S(1)} %collective-permute-done.3), channel_id=1, source_target_pairs={{0,4},{4,0},{8,12},{12,8},{16,20},{20,16},{24,28},{28,24},{1,5},{5... | collective-permute-start | bytes 1769480 | tf_op jit(solution)/shard_map/ppermute | solution.py:308
  45.1 15.2 %copy-start.4 = (bf16[192,1536]{1,0:T(8,128)(2,1)}, bf16[192,1536]{1,0:T(8,128)(2,1)S(1)}, u32[]{:S(2)}) copy-start(bf16[192,1536]{1,0:T(8,128)(2,1)S(1)} %collective-permute-done) | copy-start | bytes 1769476
  45.1 13.8 %collective-permute-start.4 = (bf16[192,1536]{1,0:T(8,128)(2,1)S(1)}, bf16[192,1536]{1,0:T(8,128)(2,1)S(1)}, u32[]{:S(2)}, u32[]{:S(2)}) collective-permute-start(bf16[192,1536]{1,0:T(8,128)(2,1)S(1)} %collective-permute-done), channel_id=1, source_target_pairs={{0,4},{4,0},{8,12},{12,8},{16,20},{20,16},{24,28},{28,24},{1,5},{5... | collective-permute-start | bytes 1769480 | tf_op jit(solution)/shard_map/ppermute | solution.py:308
  57.3 3.0 %copy-start.5 = (bf16[192,1536]{1,0:T(8,128)(2,1)}, bf16[192,1536]{1,0:T(8,128)(2,1)S(1)}, u32[]{:S(2)}) copy-start(bf16[192,1536]{1,0:T(8,128)(2,1)S(1)} %collective-permute-done.1) | copy-start | bytes 1769476
  57.3 2.0 %collective-permute-start.5 = (bf16[192,1536]{1,0:T(8,128)(2,1)S(1)}, bf16[192,1536]{1,0:T(8,128)(2,1)S(1)}, u32[]{:S(2)}, u32[]{:S(2)}) collective-permute-start(bf16[192,1536]{1,0:T(8,128)(2,1)S(1)} %collective-permute-done.1), channel_id=1, source_target_pairs={{0,4},{4,0},{8,12},{12,8},{16,20},{20,16},{24,28},{28,24},{1,5},{5... | collective-permute-start | bytes 1769480 | tf_op jit(solution)/shard_map/ppermute | solution.py:308
  58.9 1.5 copy-start.6
  58.9 1.5 copy-start.7
  58.9 1.4 copy-start.8
  59.3 0.9 copy-start.9
  60.3 1.2 copy-start
  61.5 30.8 %copy-start.24 = (bf16[2304]{0:T(1024)(128)(2,1)S(1)}, bf16[2304]{0:T(1024)(128)(2,1)}, u32[]{:S(2)}) copy-start(bf16[2304]{0:T(1024)(128)(2,1)} %param.21) | copy-start | bytes 13828
  61.5 31.4 %copy-start.25 = (s32[4]{0:T(128)S(1)}, s32[4]{0:T(128)}, u32[]{:S(2)}) copy-start(s32[4]{0:T(128)} %all_lengths.3) | copy-start | bytes 52
  70.2 33.5 %collective-permute-start.17 = (bf16[2,96,1152]{2,1,0:T(8,128)(2,1)}, bf16[2,96,1152]{2,1,0:T(8,128)(2,1)S(1)}, u32[]{:S(2)}, u32[]{:S(2)}) collective-permute-start(bf16[2,96,1152]{2,1,0:T(8,128)(2,1)} %get-tuple-element.30), channel_id=1, source_target_pairs={{0,16},{4,20},{8,24},{12,28},{16,0},{20,4},{24,8},{28,12},{1,17},{... | collective-permute-start | bytes 1327112 | tf_op jit(solution)/shard_map/ppermute | solution.py:308
  93.0 10.7 %copy-start.17 = (f32[1,96,1152]{2,1,0:T(8,128)S(1)}, f32[1,96,1152]{2,1,0:T(8,128)}, u32[]{:S(2)}) copy-start(f32[1,96,1152]{2,1,0:T(8,128)} %get-tuple-element.29) | copy-start | bytes 1327108
  93.0 10.7 %copy-start.18 = (f32[1,96,1152]{2,1,0:T(8,128)S(1)}, f32[1,96,1152]{2,1,0:T(8,128)}, u32[]{:S(2)}) copy-start(f32[1,96,1152]{2,1,0:T(8,128)} %get-tuple-element.31) | copy-start | bytes 1327108
  93.0 12.8 %collective-permute-start.15 = (bf16[2,96,1152]{2,1,0:T(8,128)(2,1)}, bf16[2,96,1152]{2,1,0:T(8,128)(2,1)S(1)}, u32[]{:S(2)}, u32[]{:S(2)}) collective-permute-start(bf16[2,96,1152]{2,1,0:T(8,128)(2,1)} %get-tuple-element.27), channel_id=1, source_target_pairs={{0,8},{4,12},{8,0},{12,4},{16,24},{20,28},{24,16},{28,20},{1,9},{5... | collective-permute-start | bytes 1327112 | tf_op jit(solution)/shard_map/ppermute | solution.py:308
  101.7 4.1 %copy-start.14 = (f32[1,96,1152]{2,1,0:T(8,128)S(1)}, f32[1,96,1152]{2,1,0:T(8,128)}, u32[]{:S(2)}) copy-start(f32[1,96,1152]{2,1,0:T(8,128)} %get-tuple-element.28) | copy-start | bytes 1327108
  101.7 13.3 %collective-permute-start.11 = (bf16[2,96,1152]{2,1,0:T(8,128)(2,1)}, bf16[2,96,1152]{2,1,0:T(8,128)(2,1)S(1)}, u32[]{:S(2)}, u32[]{:S(2)}) collective-permute-start(bf16[2,96,1152]{2,1,0:T(8,128)(2,1)} %get-tuple-element.24), channel_id=1, source_target_pairs={{0,16},{4,20},{8,24},{12,28},{16,0},{20,4},{24,8},{28,12},{1,17},{... | collective-permute-start | bytes 1327112 | tf_op jit(solution)/shard_map/ppermute | solution.py:308
  101.8 15.3 %collective-permute-start.9 = (bf16[2,96,1152]{2,1,0:T(8,128)(2,1)}, bf16[2,96,1152]{2,1,0:T(8,128)(2,1)S(1)}, u32[]{:S(2)}, u32[]{:S(2)}) collective-permute-start(bf16[2,96,1152]{2,1,0:T(8,128)(2,1)} %get-tuple-element.21), channel_id=1, source_target_pairs={{0,8},{4,12},{8,0},{12,4},{16,24},{20,28},{24,16},{28,20},{1,9},{5... | collective-permute-start | bytes 1327112 | tf_op jit(solution)/shard_map/ppermute | solution.py:308
  103.7 11.3 %copy-start.15 = (f32[1,96,1152]{2,1,0:T(8,128)S(1)}, f32[1,96,1152]{2,1,0:T(8,128)}, u32[]{:S(2)}) copy-start(f32[1,96,1152]{2,1,0:T(8,128)} %get-tuple-element.23) | copy-start | bytes 1327108
  103.7 11.3 %copy-start.16 = (f32[1,96,1152]{2,1,0:T(8,128)S(1)}, f32[1,96,1152]{2,1,0:T(8,128)}, u32[]{:S(2)}) copy-start(f32[1,96,1152]{2,1,0:T(8,128)} %get-tuple-element.25) | copy-start | bytes 1327108
  103.8 16.2 %collective-permute-start.19 = (bf16[1,96,1152]{2,1,0:T(8,128)(2,1)S(1)}, bf16[1,96,1152]{2,1,0:T(8,128)(2,1)S(1)}, u32[]{:S(2)}, u32[]{:S(2)}) collective-permute-start(bf16[1,96,1152]{2,1,0:T(8,128)(2,1)S(1)} %get-tuple-element.37), channel_id=1, source_target_pairs={{0,8},{4,12},{8,0},{12,4},{16,24},{20,28},{24,16},{28,20},{1,9},{5... | collective-permute-start | bytes 663560 | tf_op jit(solution)/shard_map/ppermute | solution.py:308
  104.0 23.6 %collective-permute-start.18 = (f32[1,96,1152]{2,1,0:T(8,128)S(1)}, f32[1,96,1152]{2,1,0:T(8,128)S(1)}, u32[]{:S(2)}, u32[]{:S(2)}) collective-permute-start(f32[1,96,1152]{2,1,0:T(8,128)S(1)} %get-tuple-element.38), channel_id=1, source_target_pairs={{0,4},{4,0},{8,12},{12,8},{16,20},{20,16},{24,28},{28,24},{1,5},{5... | collective-permute-start | bytes 1327112 | tf_op jit(solution)/shard_map/ppermute | solution.py:308
  105.8 9.3 %copy-start.10 = (bf16[2,96,1152]{2,1,0:T(8,128)(2,1)}, bf16[2,96,1152]{2,1,0:T(8,128)(2,1)S(1)}, u32[]{:S(2)}) copy-start(bf16[2,96,1152]{2,1,0:T(8,128)(2,1)S(1)} %collective-permute-done.15.refs_1_) | copy-start | bytes 1327108
  105.9 11.3 %copy-start.13 = (f32[1,96,1152]{2,1,0:T(8,128)S(1)}, f32[1,96,1152]{2,1,0:T(8,128)}, u32[]{:S(2)}) copy-start(f32[1,96,1152]{2,1,0:T(8,128)} %get-tuple-element.22) | copy-start | bytes 1327108
  105.9 15.9 %collective-permute-start.16 = (bf16[1,96,1152]{2,1,0:T(8,128)(2,1)S(1)}, bf16[1,96,1152]{2,1,0:T(8,128)(2,1)S(1)}, u32[]{:S(2)}, u32[]{:S(2)}) collective-permute-start(bf16[1,96,1152]{2,1,0:T(8,128)(2,1)S(1)} %add_convert_fusion.1), channel_id=1, source_target_pairs={{0,16},{4,20},{8,24},{12,28},{16,0},{20,4},{24,8},{28,12},{1,17},{... | collective-permute-start | bytes 663560 | tf_op jit(solution)/shard_map/ppermute | solution.py:308
  115.0 9.2 %copy-start.26 = (f32[768]{0:T(1024)S(1)}, f32[768]{0:T(1024)}, u32[]{:S(2)}) copy-start(f32[768]{0:T(1024)} %constant.123) | copy-start | bytes 9220
  115.0 9.2 %copy-start.27 = (pred[768]{0:T(1024)(128)(4,1)S(1)}, pred[768]{0:T(1024)(128)(4,1)}, u32[]{:S(2)}) copy-start(pred[768]{0:T(1024)(128)(4,1)} %constant.115.clone) | copy-start | bytes 2308
  115.0 9.2 %copy-start.28 = (pred[768]{0:T(1024)(128)(4,1)S(1)}, pred[768]{0:T(1024)(128)(4,1)}, u32[]{:S(2)}) copy-start(pred[768]{0:T(1024)(128)(4,1)} %constant.116.clone) | copy-start | bytes 2308
  115.0 9.2 %copy-start.29 = (pred[768]{0:T(1024)(128)(4,1)S(1)}, pred[768]{0:T(1024)(128)(4,1)}, u32[]{:S(2)}) copy-start(pred[768]{0:T(1024)(128)(4,1)} %constant.124) | copy-start | bytes 2308
  115.1 9.1 %collective-permute-start.13 = (bf16[1,96,1152]{2,1,0:T(8,128)(2,1)S(1)}, bf16[1,96,1152]{2,1,0:T(8,128)(2,1)S(1)}, u32[]{:S(2)}, u32[]{:S(2)}) collective-permute-start(bf16[1,96,1152]{2,1,0:T(8,128)(2,1)S(1)} %get-tuple-element.39), channel_id=1, source_target_pairs={{0,8},{4,12},{8,0},{12,4},{16,24},{20,28},{24,16},{28,20},{1,9},{5... | collective-permute-start | bytes 663560 | tf_op jit(solution)/shard_map/ppermute | solution.py:308
  117.1 10.6 %copy-start.11 = (bf16[2,96,1152]{2,1,0:T(8,128)(2,1)}, bf16[2,96,1152]{2,1,0:T(8,128)(2,1)S(1)}, u32[]{:S(2)}) copy-start(bf16[2,96,1152]{2,1,0:T(8,128)(2,1)S(1)} %collective-permute-done.9.refs_1_) | copy-start | bytes 1327108
  117.1 22.0 %collective-permute-start.12 = (f32[1,96,1152]{2,1,0:T(8,128)S(1)}, f32[1,96,1152]{2,1,0:T(8,128)S(1)}, u32[]{:S(2)}, u32[]{:S(2)}) collective-permute-start(f32[1,96,1152]{2,1,0:T(8,128)S(1)} %get-tuple-element.40), channel_id=1, source_target_pairs={{0,4},{4,0},{8,12},{12,8},{16,20},{20,16},{24,28},{28,24},{1,5},{5... | collective-permute-start | bytes 1327112 | tf_op jit(solution)/shard_map/ppermute | solution.py:308
  120.0 19.0 %collective-permute-start.10 = (bf16[1,96,1152]{2,1,0:T(8,128)(2,1)S(1)}, bf16[1,96,1152]{2,1,0:T(8,128)(2,1)S(1)}, u32[]{:S(2)}, u32[]{:S(2)}) collective-permute-start(bf16[1,96,1152]{2,1,0:T(8,128)(2,1)S(1)} %add_convert_fusion.3), channel_id=1, source_target_pairs={{0,16},{4,20},{8,24},{12,28},{16,0},{20,4},{24,8},{28,12},{1,17},{... | collective-permute-start | bytes 663560 | tf_op jit(solution)/shard_map/ppermute | solution.py:308
  121.8 5.9 %copy-start.20 = (bf16[1,96,1152]{2,1,0:T(8,128)(2,1)}, bf16[1,96,1152]{2,1,0:T(8,128)(2,1)S(1)}, u32[]{:S(2)}) copy-start(bf16[1,96,1152]{2,1,0:T(8,128)(2,1)S(1)} %collective-permute-done.16.refs_2_) | copy-start | bytes 663556
  121.8 5.9 %collective-permute-start.20 = (bf16[1,96,1152]{2,1,0:T(8,128)(2,1)S(1)}, bf16[1,96,1152]{2,1,0:T(8,128)(2,1)S(1)}, u32[]{:S(2)}, u32[]{:S(2)}) collective-permute-start(bf16[1,96,1152]{2,1,0:T(8,128)(2,1)S(1)} %collective-permute-done.19), channel_id=1, source_target_pairs={{0,4},{4,0},{8,12},{12,8},{16,20},{20,16},{24,28},{28,24},{1,5},{5... | collective-permute-start | bytes 663560 | tf_op jit(solution)/shard_map/ppermute | solution.py:308
  124.2 14.9 %collective-permute-start.14 = (bf16[1,96,1152]{2,1,0:T(8,128)(2,1)S(1)}, bf16[1,96,1152]{2,1,0:T(8,128)(2,1)S(1)}, u32[]{:S(2)}, u32[]{:S(2)}) collective-permute-start(bf16[1,96,1152]{2,1,0:T(8,128)(2,1)S(1)} %collective-permute-done.13), channel_id=1, source_target_pairs={{0,4},{4,0},{8,12},{12,8},{16,20},{20,16},{24,28},{28,24},{1,5},{5... | collective-permute-start | bytes 663560 | tf_op jit(solution)/shard_map/ppermute | solution.py:308
  127.7 0.7 copy-start.23
  127.7 0.8 copy-start.12
  139.1 0.7 copy-start.21
  139.1 0.7 copy-start.22
  139.1 0.9 copy-start.19

commit v4 on v3

--- a/solution.py
+++ b/solution.py
@@ -22,85 +22,105 @@
 HBM = pl.BlockSpec(memory_space=pltpu.HBM)
 
 
-def project_kernel(part, plan, place, source, *refs):
+def project_kernel(part, plan, place, position, *refs):
     groups = sum(len(members) for members, _ in plan)
     tokens = refs[:groups]
     own_rows, other_rows = refs[groups : groups + 2]
-    outs = refs[groups + 2 : -5]
-    held, weights, picked, sems, weight_sems = refs[-5:]
+    outs = refs[groups + 2 : -4]
+    weights, picked, sems, weight_sems = refs[-4:]
     core, begin = place[0], place[1]
     depth = own_rows.shape[0]
     chips = groups // 2
-    req_count, fresh_len = tokens[0].shape[:2]
+    req_count, fresh_len, width = tokens[0].shape
+    half_cols = weights.shape[1]
     rows = outs[0].shape[1]
     held_count = rows // fresh_len
+
+    def columns(ref):
+        if ref.shape[1] == half_cols:
+            return ref
+        return ref.at[:, pl.ds(pl.multiple_of(core * half_cols, LANES), half_cols)]
+
     copies = [
         pltpu.make_async_copy(
-            token,
-            held.at[
-                pl.ds((index // chips * chips + (index % chips ^ begin)) * req_count, req_count)
-            ],
-            sems.at[index],
-        )
-        for index, token in enumerate(tokens)
-    ]
-    copies += [
-        pltpu.make_async_copy(
-            own_rows,
+            columns(own_rows),
             weights.at[pl.ds(pl.multiple_of(core * depth, 16), depth)],
             weight_sems.at[0],
         ),
         pltpu.make_async_copy(
-            other_rows,
+            columns(other_rows),
             weights.at[pl.ds(pl.multiple_of((1 - core) * depth, 16), depth)],
             weight_sems.at[1],
         ),
     ]
+    fetches = []
+    for index, token in enumerate(tokens):
+        row = (index // chips * chips + (index % chips ^ begin)) * req_count
+        for item in range(req_count):
+            to = position[row + item] - part * groups * held_count
+            mine = (to >= 0) & (to < groups * held_count)
+            to = jnp.where(mine, to, 0)
+            fetches.append(
+                (
+                    mine,
+                    pltpu.make_async_copy(
+                        token.at[item], picked.at[to], sems.at[index * req_count + item]
+                    ),
+                )
+            )
+    for mine, fetch in fetches:
+
+        @pl.when(mine)
+        def _():
+            fetch.start()
+
     for copy in copies:
         copy.start()
+    for mine, fetch in fetches:
+
+        @pl.when(mine)
+        def _():
+            fetch.wait()
+
     for copy in copies:
         copy.wait()
     together = min(groups, 4)
     targets = [
-        (output, index, target)
-        for output, (members, _) in enumerate(plan)
-        for index, target in enumerate(members)
+        (output, index) for output, (members, _) in enumerate(plan) for index in range(len(members))
     ]
     for first in range(0, groups, together):
         these = targets[first : first + together]
-        for count, (_, _, target) in enumerate(these):
-            for item in range(held_count):
-                at = (count * held_count + item) * fresh_len
-                picked[at : at + fresh_len, :] = held[
-                    source[(part * groups + target) * held_count + item]
-                ]
-        result = jnp.dot(picked[...], weights[...], preferred_element_type=jnp.float32)
-        for count, (output, index, _) in enumerate(these):
+        value = picked[first * held_count : (first + together) * held_count]
+        result = jnp.dot(
+            value.reshape(together * rows, width),
+            weights[...],
+            preferred_element_type=jnp.float32,
+        )
+        for count, (output, index) in enumerate(these):
             outs[output][index] = result[count * rows : (count + 1) * rows].astype(
                 outs[output].dtype
             )
 
 
 def attend_kernel(shape, place, all_lengths, table, *refs):
-    terms, held_count, fresh_len, page, heads, part = shape
-    near, far = refs[: terms[0]], refs[terms[0] : sum(terms)]
-    refs = refs[sum(terms) :]
-    bias, cosine, sine_up, sine_down, key_pool, value_pool = refs[:6]
-    before = refs[6:-6]
-    outs = refs[-6:-3]
+    terms, held_count, fresh_len, page, heads = shape
+    sums = []
+    for count in terms:
+        sums.append(sum(ref[0].astype(jnp.float32) for ref in refs[:count]))
+        refs = refs[count:]
+    bias, cosine, sine_up, sine_down, key_pool, value_pool, *outs = refs[:-3]
     keys, values, sems = refs[-3:]
     chunk = CHUNK_PAGES * page
     pairs = heads // 2
 
-    slot = [part * held_count + index for index in range(held_count)]
-    lengths = [all_lengths[slot[index]] for index in range(held_count)]
+    lengths = [all_lengths[index] for index in range(held_count)]
     counts = [pl.cdiv(lengths[index], chunk) for index in range(held_count)]
     bases = [jnp.int32(0)]
     for count in counts[:-1]:
         bases.append(bases[-1] + count * CHUNK_PAGES)
 
     def copies(index, entry):
-        number = table[slot[index], entry]
+        number = table[index, entry]
         to = bases[index] + entry
         return (
             pltpu.make_async_copy(key_pool.at[number], keys.at[to], sems.at[index]),
@@ -124,7 +144,8 @@
         ]
         return held.reshape(chunk, WINDOW)
 
-    near, far = (sum(ref[0].astype(jnp.float32) for ref in refs) for refs in (near, far))
+    near = jnp.concatenate(sums[::2], axis=0)
+    far = jnp.concatenate(sums[1::2], axis=0)
     core = place[0]
     halves = jnp.where(core == 0, near, far), jnp.where(core == 0, far, near)
     halves = [
@@ -143,7 +164,7 @@
     width = heads * HEAD
 
     def rows_of(ref):
-        return jnp.concatenate([ref[slot[index]] for index in range(held_count)], axis=0)
+        return ref[...].reshape(held_count * fresh_len, width)
 
     cosine, sine_up, sine_down = rows_of(cosine), rows_of(sine_up), rows_of(sine_down)
 
@@ -159,16 +180,10 @@
     turned = turn(kind(1)).astype(jnp.bfloat16)
     plain = kind(2).astype(jnp.bfloat16)
 
-    def put(which, index, value):
-        outs[which][slot[index] if before else index] = value
-
-    for which, held in enumerate(before):
-        for index in range(held_count):
-            outs[which][index] = held[index]
     for index in range(held_count):
         rows = slice(index * fresh_len, (index + 1) * fresh_len)
-        put(1, index, turned[rows])
-        put(2, index, plain[rows])
+        outs[1][index] = turned[rows]
+        outs[2][index] = plain[rows]
 
     factor = 1.0 / math.sqrt(HEAD) / math.log(2.0)
     starts = [(2 * HEAD * pair) // LANES * LANES for pair in range(pairs)]
@@ -273,7 +288,7 @@
                     place_at = starts[pair] // LANES + side
                     tile = part[:, side * LANES : (side + 1) * LANES]
                     tiles[place_at] = tile if tiles[place_at] is None else tiles[place_at] + tile
-        put(0, index, jnp.concatenate(tiles, axis=1).astype(jnp.bfloat16))
+        outs[0][index] = jnp.concatenate(tiles, axis=1).astype(jnp.bfloat16)
 
 
 def per_device(
@@ -350,15 +365,26 @@
 
     received = [route(turn) for turn in range(chips)]
 
+    square_plane = chips == 4
+    if square_plane:
+        plan = [([2, 6], jnp.bfloat16), ([5, 7], jnp.bfloat16)]
+        plan += [([distance], jnp.float32) for distance in (0, 4, 1, 3)]
+    else:
+        plan = [([0], jnp.float32)]
+        plan += [([distance], jnp.bfloat16) for distance in range(1, req_size)]
+
     ids = jnp.arange(everyone, dtype=jnp.int32)
     same_group = group_of[:, None] == group_of[None, :]
     earlier = ids[None, :] < ids[:, None]
     rank = jnp.sum((same_group & earlier).astype(jnp.int32), axis=1)
     part_of, within = rank // half, rank % half
-    wanted = (part_of * req_size + (group_of ^ me)) * half + within
+    place_of = np.zeros(req_size, np.int32)
+    place_of[[target for members, _ in plan for target in members]] = np.arange(req_size)
+    place_of = jnp.asarray(place_of)[group_of ^ me]
+    spot = (part_of * req_size + place_of) * half + within
     origin = ids // req_count
     row = (((origin & 1) ^ core) * chips + (origin >> 1)) * req_count + ids % req_count
-    sources = jnp.sum(jnp.where(wanted[None, :] == ids[:, None], row[None, :], 0), axis=1)
+    position = jnp.sum(jnp.where(row[None, :] == ids[:, None], spot[None, :], 0), axis=1)
 
     lane = np.arange(heads * HEAD) % HEAD
     half_rot = ROT // 2
@@ -381,22 +407,18 @@
     place = jnp.stack([core, layer * per + chip % per]).astype(jnp.int32)
     chunk_rows = half * fresh_len
     span = page_table.shape[1]
-    pages = span + (half - 1) * (span // 2)
-
-    held = after(w_qkv, local)
-    own_rows = lax.dynamic_slice_in_dim(held, core * half_cols, half_cols, 1)
-    other_rows = swap(lax.dynamic_slice_in_dim(held, (1 - core) * half_cols, half_cols, 1), 1)
+    pages = span + (req_count - 1) * (span // 2)
+
+    if half_cols % LANES == 0:
+        own_rows, other_rows = w_qkv, swap(after(w_qkv, scale), 1)
+    else:
+        own_rows = lax.dynamic_slice_in_dim(w_qkv, core * half_cols, half_cols, 1)
+        other_rows = lax.dynamic_slice_in_dim(w_qkv, (1 - core) * half_cols, half_cols, 1)
+        other_rows = swap(other_rows, 1)
 
     received += [swap(piece, 1) for piece in received]
     received = [piece.reshape(req_count, fresh_len, block) for piece in received]
-
-    square_plane = chips == 4
-    if square_plane:
-        plan = [([2, 6], jnp.bfloat16), ([5, 7], jnp.bfloat16)]
-        plan += [([distance], jnp.float32) for distance in (0, 4, 1, 3)]
-    else:
-        plan = [([0], jnp.float32)]
-        plan += [([distance], jnp.bfloat16) for distance in range(1, req_size)]
+    received[0] = after(received[0], tables)
 
     def collect(blocks):
         if not square_plane:
@@ -421,43 +443,37 @@
                 in_specs=[SMEM] * 2 + [HBM] * (req_size + 2),
                 out_specs=[VMEM] * len(plan),
                 scratch_shapes=[
-                    pltpu.VMEM((everyone, fresh_len, block), jnp.bfloat16),
                     pltpu.VMEM((block, half_cols), jnp.bfloat16),
-                    pltpu.VMEM((min(req_size, 4) * chunk_rows, block), jnp.bfloat16),
-                    pltpu.SemaphoreType.DMA((req_size,)),
+                    pltpu.VMEM((req_size * half, fresh_len, block), jnp.bfloat16),
+                    pltpu.SemaphoreType.DMA((everyone,)),
                     pltpu.SemaphoreType.DMA((2,)),
                 ],
                 compiler_params=pltpu.CompilerParams(vmem_limit_bytes=VMEM_LIMIT),
                 name="project",
-            )(place, sources, *received, own_rows, other_rows)
-        )
-
-    results = []
-    for part in range(2):
-        near, far = collect(projected[part])
-        operands = [
-            place, lengths, page_table, *near, *far, bias, *tables, key_pool, value_pool
-        ]
-        terms = len(near), len(far)
-        specs = [SMEM] * 3 + [VMEM] * (sum(terms) + 4) + [HBM] * 2
-        count = half if part == 0 else req_count
-        out = jax.ShapeDtypeStruct((count, fresh_len, heads * HEAD), jnp.bfloat16)
-        results = pl.pallas_call(
-            functools.partial(
-                attend_kernel, (terms, half, fresh_len, page, heads, part)
-            ),
+            )(place, position, *received, own_rows, other_rows)
+        )
+
+    terms, sums = [], []
+    for blocks in projected:
+        for side in collect(blocks):
+            terms.append(len(side))
+            sums += side
+    out = jax.ShapeDtypeStruct((req_count, fresh_len, heads * HEAD), jnp.bfloat16)
+    return tuple(
+        pl.pallas_call(
+            functools.partial(attend_kernel, (terms, req_count, fresh_len, page, heads)),
             out_shape=[out] * 3,
-            in_specs=specs + [VMEM] * len(results),
+            in_specs=[SMEM] * 3 + [VMEM] * (len(sums) + 4) + [HBM] * 2,
             out_specs=[VMEM] * 3,
             scratch_shapes=[
                 pltpu.VMEM((pages, page, heads * HEAD), jnp.bfloat16),
                 pltpu.VMEM((pages, page, heads * HEAD), jnp.bfloat16),
-                pltpu.SemaphoreType.DMA((half,)),
+                pltpu.SemaphoreType.DMA((req_count,)),
             ],
             compiler_params=pltpu.CompilerParams(vmem_limit_bytes=VMEM_LIMIT),
             name="attend",
-        )(*operands, *results)
-    return tuple(results)
+        )(place, lengths, page_table, *sums, bias, *tables, key_pool, value_pool)
+    )
 
 
 def solution(mesh):

time: 149 us -> 149 us (level)
  the two profiles are of different devices: /device:TPU:0 before, /device:TPU:1 now
where the time goes in v4:
time: 149 us; the launch traced here: 148 us
  starting transfers between devices  48.8 us (33%)
  waiting for transfers between devices  44.2 us (30%)
  Pallas kernels  33.1 us (22%)
  other arithmetic  15 us (10%)
  local copies, waits for them, and re-layouts  5.95 us (4%)
    ppermute x17, starting transfers between devices, swap(): lax.ppermute(value, 'req', [(device, device ^ distance) for device in ran...  33.7 us
    ppermute x4, waiting for transfers between devices, route(): return lax.ppermute(value, ('req', 'wgt'), pairs)  29.8 us
    pallas_call x1, Pallas kernels, per_device(): pl.pallas_call(functools.partial(attend_kernel, (terms, req_count, fresh_...  16.6 us
    pallas_call x2, Pallas kernels, per_device(): pl.pallas_call(functools.partial(project_kernel, part, plan), out_shape=[...  16.6 us
    ppermute x17, waiting for transfers between devices, swap(): lax.ppermute(value, 'req', [(device, device ^ distance) for device in ran...  11.2 us
    ppermute x4, starting transfers between devices, route(): return lax.ppermute(value, ('req', 'wgt'), pairs)  9.02 us
    all_to_all x1, starting transfers between devices, per_device(): stats = lax.all_to_all(stats, 'wgt', 0, 0, tiled=True)  6.04 us
    select_n x1, other arithmetic, per_device(): jnp.where(turns & jnp.asarray(lane >= half_rot)[None, :], sine, 0.0)  4.09 us
  transfers between devices with their start and end apart: 22, of which 8 were waited for; matrix products, arithmetic and copies ran while one was open for 12% of the time, Pallas kernels for 6%

profile of v4, /device:TPU:1, one launch (start us, length us, event | category | flops | bytes accessed | tf_op | source)
XLA Modules:
  0.0 147.9 jit_solution(18375969857777936473)
XLA Ops:
  0.6 0.0 copy-start
  0.6 0.1 collective-permute-start.8
  0.8 1.2 convert_reduce_fusion
  2.0 0.6 div.51
  2.6 1.4 multiply_reduce_fusion
  4.0 0.1 stack.19
  4.1 0.7 pad_maximum_fusion
  4.8 0.6 broadcast_in_dim.69
  5.4 6.0 %all-to-all-start = ((f32[4,2,192]{2,1,0:T(2,128)}), f32[4,2,192]{2,1,0:T(2,128)}, u32[]{:S(2)}, u32[]{:S(2)}) async-start(f32[4,2,192]{2,1,0:T(2,128)} %broadcast_in_dim.69), calls=%async_computation | async-start | bytes 16384 | tf_op jit(solution)/shard_map/all_to_all | solution.py:339
  11.4 1.4 dynamic-slice_convert_fusion
  12.8 3.2 %all-to-all-done = f32[4,2,192]{2,1,0:T(2,128)} async-done(((f32[4,2,192]{2,1,0:T(2,128)}), f32[4,2,192]{2,1,0:T(2,128)}, u32[]{:S(2)}, u32[]{:S(2)}) %all-to-all-start) | async-done | bytes 6176 | tf_op jit(solution)/shard_map/all_to_all | solution.py:339
  16.0 0.8 slice_reduce_fusion
  16.8 2.3 %fusion.3 = bf16[192,1536]{1,0:T(8,128)(2,1)} fusion(bf16[4,48,1536]{2,1,0:T(8,128)(2,1)} %param.15, f32[1536]{0:T(1024)S(1)} %get-tuple-element.41, f32[1536]{0:T(1024)} %get-tuple-element.42, f32[192]{0:T(256)S(1)} %add_rsqrt_fusion, f32[192]{0:T(256)S(1)} %broadcast_multiply_fusion.1), kind=kLoop, calls=%fused_computation.5 | loop fusion | flops 1769472 | bytes 1193472 | tf_op jit(solution)/shard_map/convert_element_type | solution.py:348
  19.1 6.0 %collective-permute-start = (bf16[192,1536]{1,0:T(8,128)(2,1)}, bf16[192,1536]{1,0:T(8,128)(2,1)}, u32[]{:S(2)}, u32[]{:S(2)}) collective-permute-start(bf16[192,1536]{1,0:T(8,128)(2,1)} %fusion.3), channel_id=1, source_target_pairs={{0,0},{8,1},{16,2},{24,3},{4,4},{12,5},{20,6},{28,7},{1,8},{9,9},{... | collective-permute-start | bytes 1769480 | tf_op jit(solution)/shard_map/ppermute | solution.py:364
  25.1 0.0 collective-permute-start.2
  25.1 1.2 collective-permute-start.3
  26.3 1.8 %collective-permute-start.1 = (bf16[192,1536]{1,0:T(8,128)(2,1)}, bf16[192,1536]{1,0:T(8,128)(2,1)}, u32[]{:S(2)}, u32[]{:S(2)}) collective-permute-start(bf16[192,1536]{1,0:T(8,128)(2,1)} %fusion.3), channel_id=1, source_target_pairs={{8,0},{0,1},{24,2},{16,3},{12,4},{4,5},{28,6},{20,7},{9,8},{1,9},{... | collective-permute-start | bytes 1769480 | tf_op jit(solution)/shard_map/ppermute | solution.py:364
  28.2 0.7 gather_fusion
  28.9 0.9 convert_reduce_fusion.1
  29.8 0.6 select_reduce_fusion.position
  30.4 21.9 %collective-permute-done.2 = bf16[192,1536]{1,0:T(8,128)(2,1)} collective-permute-done((bf16[192,1536]{1,0:T(8,128)(2,1)}, bf16[192,1536]{1,0:T(8,128)(2,1)}, u32[]{:S(2)}, u32[]{:S(2)}) %collective-permute-start.2) | collective-permute-done | bytes 589856 | tf_op jit(solution)/shard_map/ppermute | solution.py:364
  52.3 1.5 collective-permute-start.6
  53.8 0.0 collective-permute-start.7
  53.8 0.5 collective-permute-start.4
  54.3 7.9 %collective-permute-done.1 = bf16[192,1536]{1,0:T(8,128)(2,1)} collective-permute-done((bf16[192,1536]{1,0:T(8,128)(2,1)}, bf16[192,1536]{1,0:T(8,128)(2,1)}, u32[]{:S(2)}, u32[]{:S(2)}) %collective-permute-start.1) | collective-permute-done | bytes 589856 | tf_op jit(solution)/shard_map/ppermute | solution.py:364
  62.2 2.0 %collective-permute-start.5 = (bf16[192,1536]{1,0:T(8,128)(2,1)}, bf16[192,1536]{1,0:T(8,128)(2,1)S(1)}, u32[]{:S(2)}, u32[]{:S(2)}) collective-permute-start(bf16[192,1536]{1,0:T(8,128)(2,1)} %collective-permute-done.1), channel_id=1, source_target_pairs={{0,4},{4,0},{8,12},{12,8},{16,20},{20,16},{24,28},{28,24},{1,5},{5... | collective-permute-start | bytes 1769480 | tf_op jit(solution)/shard_map/ppermute | solution.py:323
  64.3 0.6 pad_add_fusion.place
  64.9 0.7 add_convert_fusion.4
  65.6 4.1 %fusion.4 = (f32[4,48,768]{2,1,0:T(8,128)}, f32[4,48,768]{2,1,0:T(8,128)}, f32[4,48,768]{2,1,0:T(8,128)}) fusion(f32[768]{0:T(1024)S(1)} %copy-done.21, f32[4,48]{1,0:T(4,128)S(1)} %add_convert_fusion.4, pred[768]{0:T(1024)(128)(4,1)} %constant.124, pred[768]{0:T(1024)(128)(4,1)} %constant.116.clone, pred[768]{0:T(1024)(128)(4,1)} %constant.115.clone), kind=kLoop, calls=%fused_computation.9 | loop fusion | flops 737280 | bytes 1775616 | tf_op jit(solution)/shard_map/jit(_where)/select_n | solution.py:400
  69.8 0.7 copy-done.2
  70.5 0.2 copy-done.3
  70.7 0.3 copy-done.4
  71.0 0.2 copy-done.5
  71.2 1.0 copy-done.1
  72.2 8.2 %project.3 = (bf16[2,96,1152]{2,1,0:T(8,128)(2,1)}, bf16[2,96,1152]{2,1,0:T(8,128)(2,1)}, f32[1,96,1152]{2,1,0:T(8,128)}, f32[1,96,1152]{2,1,0:T(8,128)}, f32[1,...) custom-call(s32[2]{0:T(128)} %pad_add_fusion.place, s32[32]{0:T(128)} %select_reduce_fusion.position, ...), custom_call_target="tpu_custom_call" | custom-call | tf_op jit(solution)/shard_map/project/pallas_call | solution.py:437
  80.4 17.2 %collective-permute-start.17 = (bf16[2,96,1152]{2,1,0:T(8,128)(2,1)}, bf16[2,96,1152]{2,1,0:T(8,128)(2,1)S(1)}, u32[]{:S(2)}, u32[]{:S(2)}) collective-permute-start(bf16[2,96,1152]{2,1,0:T(8,128)(2,1)} %get-tuple-element.27), channel_id=1, source_target_pairs={{0,16},{4,20},{8,24},{12,28},{16,0},{20,4},{24,8},{28,12},{1,17},{... | collective-permute-start | bytes 1327112 | tf_op jit(solution)/shard_map/ppermute | solution.py:323
  97.7 8.4 %project.2 = (bf16[2,96,1152]{2,1,0:T(8,128)(2,1)}, bf16[2,96,1152]{2,1,0:T(8,128)(2,1)}, f32[1,96,1152]{2,1,0:T(8,128)}, f32[1,96,1152]{2,1,0:T(8,128)}, f32[1,...) custom-call(s32[2]{0:T(128)} %pad_add_fusion.place, s32[32]{0:T(128)} %select_reduce_fusion.position, ...), custom_call_target="tpu_custom_call" | custom-call | tf_op jit(solution)/shard_map/project/pallas_call | solution.py:437
  106.0 0.2 collective-permute-start.11
  106.2 1.3 collective-permute-start.9
  107.5 0.8 collective-permute-done.17
  108.3 0.1 add_convert_fusion
  108.4 0.1 collective-permute-start.19
  108.5 0.7 collective-permute-start.18
  109.2 0.0 collective-permute-done.15.refs_6_
  109.3 0.1 add_convert_fusion.1
  109.3 1.9 %collective-permute-start.16 = (bf16[1,96,1152]{2,1,0:T(8,128)(2,1)S(1)}, bf16[1,96,1152]{2,1,0:T(8,128)(2,1)S(1)}, u32[]{:S(2)}, u32[]{:S(2)}) collective-permute-start(bf16[1,96,1152]{2,1,0:T(8,128)(2,1)S(1)} %add_convert_fusion.1), channel_id=1, source_target_pairs={{0,16},{4,20},{8,24},{12,28},{16,0},{20,4},{24,8},{28,12},{1,17},{... | collective-permute-start | bytes 663560 | tf_op jit(solution)/shard_map/ppermute | solution.py:323
  111.3 6.4 %collective-permute-done.11 = bf16[2,96,1152]{2,1,0:T(8,128)(2,1)S(1)} collective-permute-done((bf16[2,96,1152]{2,1,0:T(8,128)(2,1)}, bf16[2,96,1152]{2,1,0:T(8,128)(2,1)S(1)}, u32[]{:S(2)}, u32[]{:S(2)}) %collective-permute-start.11) | collective-permute-done | bytes 442400 | tf_op jit(solution)/shard_map/ppermute | solution.py:323
  117.7 0.1 add_convert_fusion.2
  117.8 1.1 collective-permute-start.13
  118.9 2.9 %collective-permute-start.12 = (f32[1,96,1152]{2,1,0:T(8,128)S(1)}, f32[1,96,1152]{2,1,0:T(8,128)S(1)}, u32[]{:S(2)}, u32[]{:S(2)}) collective-permute-start(f32[1,96,1152]{2,1,0:T(8,128)S(1)} %get-tuple-element.32), channel_id=1, source_target_pairs={{0,4},{4,0},{8,12},{12,8},{16,20},{20,16},{24,28},{28,24},{1,5},{5... | collective-permute-start | bytes 1327112 | tf_op jit(solution)/shard_map/ppermute | solution.py:323
  121.8 0.1 add_convert_fusion.3
  121.8 1.7 %collective-permute-done.19 = bf16[1,96,1152]{2,1,0:T(8,128)(2,1)S(1)} collective-permute-done((bf16[1,96,1152]{2,1,0:T(8,128)(2,1)S(1)}, bf16[1,96,1152]{2,1,0:T(8,128)(2,1)S(1)}, u32[]{:S(2)}, u32[]{:S(2)}) %collective-permute-start.19) | collective-permute-done | bytes 221216 | tf_op jit(solution)/shard_map/ppermute | solution.py:323
  123.5 0.1 collective-permute-start.10
  123.6 2.9 %collective-permute-start.20 = (bf16[1,96,1152]{2,1,0:T(8,128)(2,1)S(1)}, bf16[1,96,1152]{2,1,0:T(8,128)(2,1)S(1)}, u32[]{:S(2)}, u32[]{:S(2)}) collective-permute-start(bf16[1,96,1152]{2,1,0:T(8,128)(2,1)S(1)} %collective-permute-done.19), channel_id=1, source_target_pairs={{0,4},{4,0},{8,12},{12,8},{16,20},{20,16},{24,28},{28,24},{1,5},{5... | collective-permute-start | bytes 663560 | tf_op jit(solution)/shard_map/ppermute | solution.py:323
  126.5 1.7 %collective-permute-done.13 = bf16[1,96,1152]{2,1,0:T(8,128)(2,1)S(1)} collective-permute-done((bf16[1,96,1152]{2,1,0:T(8,128)(2,1)S(1)}, bf16[1,96,1152]{2,1,0:T(8,128)(2,1)S(1)}, u32[]{:S(2)}, u32[]{:S(2)}) %collective-permute-start.13) | collective-permute-done | bytes 221216 | tf_op jit(solution)/shard_map/ppermute | solution.py:323
  128.2 1.2 collective-permute-start.14
  129.4 0.6 reshape.218.refs_10_
  130.1 0.5 collective-permute-done.14.refs_4_
  130.5 0.2 copy-done.17
  130.7 0.1 copy-done.18
  130.8 0.1 copy-done.14
  131.0 0.2 copy-done.19
  131.2 0.2 copy-done.15
  131.3 16.6 %attend.1 = (bf16[4,48,768]{2,1,0:T(8,128)(2,1)}, bf16[4,48,768]{2,1,0:T(8,128)(2,1)}, bf16[4,48,768]{2,1,0:T(8,128)(2,1)}) custom-call(s32[2]{0:T(128)} %pad_add_fusion.place, s32[4]{0:T(128)} %all_lengths.1, s32[4,16]{1,0:T(4,128)} %table.1, f32[1,96,1152]{2,1,0:T(8,128)} %get-tuple-element.17.refs_0_, bf16[2,96,1152]{2,1,0:T(8,128)(2,1)} %copy-done.7, ...), custom_call_target="tpu_custom_call" | custom-call | tf_op jit(solution)/shard_map/attend/pallas_call | solution.py:463
  (56 shorter events, 0.2 us)
Async XLA Ops:
  0.6 27.5 %copy-start = (s32[8]{0:T(128)S(1)}, s32[8]{0:T(128)}, u32[]{:S(2)}) copy-start(s32[8]{0:T(128)} %constant.113.clone) | copy-start | bytes 100
  0.6 69.1 %collective-permute-start.8 = (bf16[768,2304]{1,0:T(8,128)(2,1)}, bf16[768,2304]{1,0:T(8,128)(2,1)S(1)}, u32[]{:S(2)}, u32[]{:S(2)}) collective-permute-start(bf16[768,2304]{1,0:T(8,128)(2,1)} %refs_8_.3), channel_id=1, source_target_pairs={{0,4},{4,0},{8,12},{12,8},{16,20},{20,16},{24,28},{28,24},{1,5},{5... | collective-permute-start | bytes 10616840 | tf_op jit(solution)/shard_map/ppermute | solution.py:323
  2.6 63.0 %copy-start.21 = (f32[768]{0:T(1024)S(1)}, f32[768]{0:T(1024)}, u32[]{:S(2)}) copy-start(f32[768]{0:T(1024)} %constant.123) | copy-start | bytes 9220
  5.4 10.6 %all-to-all-start = ((f32[4,2,192]{2,1,0:T(2,128)}), f32[4,2,192]{2,1,0:T(2,128)}, u32[]{:S(2)}, u32[]{:S(2)}) async-start(f32[4,2,192]{2,1,0:T(2,128)} %broadcast_in_dim.69), calls=%async_computation | async-start | bytes 16384 | tf_op jit(solution)/shard_map/all_to_all | solution.py:339
  16.0 12.2 %copy-start.22 = (s32[32]{0:T(128)S(1)}, s32[32]{0:T(128)}, u32[]{:S(2)}) copy-start(s32[32]{0:T(128)} %param.16) | copy-start | bytes 388
  19.1 34.7 %collective-permute-start = (bf16[192,1536]{1,0:T(8,128)(2,1)}, bf16[192,1536]{1,0:T(8,128)(2,1)}, u32[]{:S(2)}, u32[]{:S(2)}) collective-permute-start(bf16[192,1536]{1,0:T(8,128)(2,1)} %fusion.3), channel_id=1, source_target_pairs={{0,0},{8,1},{16,2},{24,3},{4,4},{12,5},{20,6},{28,7},{1,8},{9,9},{... | collective-permute-start | bytes 1769480 | tf_op jit(solution)/shard_map/ppermute | solution.py:364
  25.1 27.2 %collective-permute-start.2 = (bf16[192,1536]{1,0:T(8,128)(2,1)}, bf16[192,1536]{1,0:T(8,128)(2,1)}, u32[]{:S(2)}, u32[]{:S(2)}) collective-permute-start(bf16[192,1536]{1,0:T(8,128)(2,1)} %fusion.3), channel_id=1, source_target_pairs={{16,0},{24,1},{0,2},{8,3},{20,4},{28,5},{4,6},{12,7},{17,8},{25,9}... | collective-permute-start | bytes 1769480 | tf_op jit(solution)/shard_map/ppermute | solution.py:364
  25.1 28.7 %collective-permute-start.3 = (bf16[192,1536]{1,0:T(8,128)(2,1)}, bf16[192,1536]{1,0:T(8,128)(2,1)}, u32[]{:S(2)}, u32[]{:S(2)}) collective-permute-start(bf16[192,1536]{1,0:T(8,128)(2,1)} %fusion.3), channel_id=1, source_target_pairs={{24,0},{16,1},{8,2},{0,3},{28,4},{20,5},{12,6},{4,7},{25,8},{17,9}... | collective-permute-start | bytes 1769480 | tf_op jit(solution)/shard_map/ppermute | solution.py:364
  26.3 35.9 %collective-permute-start.1 = (bf16[192,1536]{1,0:T(8,128)(2,1)}, bf16[192,1536]{1,0:T(8,128)(2,1)}, u32[]{:S(2)}, u32[]{:S(2)}) collective-permute-start(bf16[192,1536]{1,0:T(8,128)(2,1)} %fusion.3), channel_id=1, source_target_pairs={{8,0},{0,1},{24,2},{16,3},{12,4},{4,5},{28,6},{20,7},{9,8},{1,9},{... | collective-permute-start | bytes 1769480 | tf_op jit(solution)/shard_map/ppermute | solution.py:364
  52.3 17.4 %collective-permute-start.6 = (bf16[192,1536]{1,0:T(8,128)(2,1)}, bf16[192,1536]{1,0:T(8,128)(2,1)S(1)}, u32[]{:S(2)}, u32[]{:S(2)}) collective-permute-start(bf16[192,1536]{1,0:T(8,128)(2,1)} %collective-permute-done.2), channel_id=1, source_target_pairs={{0,4},{4,0},{8,12},{12,8},{16,20},{20,16},{24,28},{28,24},{1,5},{5... | collective-permute-start | bytes 1769480 | tf_op jit(solution)/shard_map/ppermute | solution.py:323
  53.8 15.9 %collective-permute-start.7 = (bf16[192,1536]{1,0:T(8,128)(2,1)}, bf16[192,1536]{1,0:T(8,128)(2,1)S(1)}, u32[]{:S(2)}, u32[]{:S(2)}) collective-permute-start(bf16[192,1536]{1,0:T(8,128)(2,1)} %collective-permute-done.3), channel_id=1, source_target_pairs={{0,4},{4,0},{8,12},{12,8},{16,20},{20,16},{24,28},{28,24},{1,5},{5... | collective-permute-start | bytes 1769480 | tf_op jit(solution)/shard_map/ppermute | solution.py:323
  53.8 15.9 %collective-permute-start.4 = (bf16[192,1536]{1,0:T(8,128)(2,1)}, bf16[192,1536]{1,0:T(8,128)(2,1)S(1)}, u32[]{:S(2)}, u32[]{:S(2)}) collective-permute-start(bf16[192,1536]{1,0:T(8,128)(2,1)} %collective-permute-done), channel_id=1, source_target_pairs={{0,4},{4,0},{8,12},{12,8},{16,20},{20,16},{24,28},{28,24},{1,5},{5... | collective-permute-start | bytes 1769480 | tf_op jit(solution)/shard_map/ppermute | solution.py:323
  62.2 7.5 %collective-permute-start.5 = (bf16[192,1536]{1,0:T(8,128)(2,1)}, bf16[192,1536]{1,0:T(8,128)(2,1)S(1)}, u32[]{:S(2)}, u32[]{:S(2)}) collective-permute-start(bf16[192,1536]{1,0:T(8,128)(2,1)} %collective-permute-done.1), channel_id=1, source_target_pairs={{0,4},{4,0},{8,12},{12,8},{16,20},{20,16},{24,28},{28,24},{1,5},{5... | collective-permute-start | bytes 1769480 | tf_op jit(solution)/shard_map/ppermute | solution.py:323
  69.7 0.8 copy-start.2
  69.7 1.0 copy-start.3
  69.7 1.2 copy-start.4
  69.8 1.4 copy-start.5
  69.8 2.4 %copy-start.1 = (bf16[768,2304]{1,0:T(8,128)(2,1)}, bf16[768,2304]{1,0:T(8,128)(2,1)S(1)}, u32[]{:S(2)}) copy-start(bf16[768,2304]{1,0:T(8,128)(2,1)S(1)} %collective-permute-done.8.refs_9_) | copy-start | bytes 10616836
  80.4 27.9 %collective-permute-start.17 = (bf16[2,96,1152]{2,1,0:T(8,128)(2,1)}, bf16[2,96,1152]{2,1,0:T(8,128)(2,1)S(1)}, u32[]{:S(2)}, u32[]{:S(2)}) collective-permute-start(bf16[2,96,1152]{2,1,0:T(8,128)(2,1)} %get-tuple-element.27), channel_id=1, source_target_pairs={{0,16},{4,20},{8,24},{12,28},{16,0},{20,4},{24,8},{28,12},{1,17},{... | collective-permute-start | bytes 1327112 | tf_op jit(solution)/shard_map/ppermute | solution.py:323
  97.6 10.7 %copy-start.12 = (f32[1,96,1152]{2,1,0:T(8,128)S(1)}, f32[1,96,1152]{2,1,0:T(8,128)}, u32[]{:S(2)}) copy-start(f32[1,96,1152]{2,1,0:T(8,128)} %get-tuple-element.26) | copy-start | bytes 1327108
  97.7 10.7 %copy-start.13 = (f32[1,96,1152]{2,1,0:T(8,128)S(1)}, f32[1,96,1152]{2,1,0:T(8,128)}, u32[]{:S(2)}) copy-start(f32[1,96,1152]{2,1,0:T(8,128)} %get-tuple-element.28) | copy-start | bytes 1327108
  97.7 11.6 %collective-permute-start.15 = (bf16[2,96,1152]{2,1,0:T(8,128)(2,1)}, bf16[2,96,1152]{2,1,0:T(8,128)(2,1)S(1)}, u32[]{:S(2)}, u32[]{:S(2)}) collective-permute-start(bf16[2,96,1152]{2,1,0:T(8,128)(2,1)} %get-tuple-element.24), channel_id=1, source_target_pairs={{0,8},{4,12},{8,0},{12,4},{16,24},{20,28},{24,16},{28,20},{1,9},{5... | collective-permute-start | bytes 1327112 | tf_op jit(solution)/shard_map/ppermute | solution.py:323
  106.0 3.2 %copy-start.9 = (f32[1,96,1152]{2,1,0:T(8,128)S(1)}, f32[1,96,1152]{2,1,0:T(8,128)}, u32[]{:S(2)}) copy-start(f32[1,96,1152]{2,1,0:T(8,128)} %get-tuple-element.25) | copy-start | bytes 1327108
  106.0 11.7 %collective-permute-start.11 = (bf16[2,96,1152]{2,1,0:T(8,128)(2,1)}, bf16[2,96,1152]{2,1,0:T(8,128)(2,1)S(1)}, u32[]{:S(2)}, u32[]{:S(2)}) collective-permute-start(bf16[2,96,1152]{2,1,0:T(8,128)(2,1)} %get-tuple-element.21), channel_id=1, source_target_pairs={{0,16},{4,20},{8,24},{12,28},{16,0},{20,4},{24,8},{28,12},{1,17},{... | collective-permute-start | bytes 1327112 | tf_op jit(solution)/shard_map/ppermute | solution.py:323
  106.2 12.7 %collective-permute-start.9 = (bf16[2,96,1152]{2,1,0:T(8,128)(2,1)}, bf16[2,96,1152]{2,1,0:T(8,128)(2,1)S(1)}, u32[]{:S(2)}, u32[]{:S(2)}) collective-permute-start(bf16[2,96,1152]{2,1,0:T(8,128)(2,1)} %get-tuple-element.18), channel_id=1, source_target_pairs={{0,8},{4,12},{8,0},{12,4},{16,24},{20,28},{24,16},{28,20},{1,9},{5... | collective-permute-start | bytes 1327112 | tf_op jit(solution)/shard_map/ppermute | solution.py:323
  108.3 9.4 %copy-start.10 = (f32[1,96,1152]{2,1,0:T(8,128)S(1)}, f32[1,96,1152]{2,1,0:T(8,128)}, u32[]{:S(2)}) copy-start(f32[1,96,1152]{2,1,0:T(8,128)} %get-tuple-element.20) | copy-start | bytes 1327108
  108.3 9.4 %copy-start.11 = (f32[1,96,1152]{2,1,0:T(8,128)S(1)}, f32[1,96,1152]{2,1,0:T(8,128)}, u32[]{:S(2)}) copy-start(f32[1,96,1152]{2,1,0:T(8,128)} %get-tuple-element.22) | copy-start | bytes 1327108
  108.4 15.1 %collective-permute-start.19 = (bf16[1,96,1152]{2,1,0:T(8,128)(2,1)S(1)}, bf16[1,96,1152]{2,1,0:T(8,128)(2,1)S(1)}, u32[]{:S(2)}, u32[]{:S(2)}) collective-permute-start(bf16[1,96,1152]{2,1,0:T(8,128)(2,1)S(1)} %get-tuple-element.29), channel_id=1, source_target_pairs={{0,8},{4,12},{8,0},{12,4},{16,24},{20,28},{24,16},{28,20},{1,9},{5... | collective-permute-start | bytes 663560 | tf_op jit(solution)/shard_map/ppermute | solution.py:323
  108.5 21.5 %collective-permute-start.18 = (f32[1,96,1152]{2,1,0:T(8,128)S(1)}, f32[1,96,1152]{2,1,0:T(8,128)S(1)}, u32[]{:S(2)}, u32[]{:S(2)}) collective-permute-start(f32[1,96,1152]{2,1,0:T(8,128)S(1)} %get-tuple-element.30), channel_id=1, source_target_pairs={{0,4},{4,0},{8,12},{12,8},{16,20},{20,16},{24,28},{28,24},{1,5},{5... | collective-permute-start | bytes 1327112 | tf_op jit(solution)/shard_map/ppermute | solution.py:323
  109.3 8.5 %copy-start.6 = (bf16[2,96,1152]{2,1,0:T(8,128)(2,1)}, bf16[2,96,1152]{2,1,0:T(8,128)(2,1)S(1)}, u32[]{:S(2)}) copy-start(bf16[2,96,1152]{2,1,0:T(8,128)(2,1)S(1)} %collective-permute-done.15.refs_6_) | copy-start | bytes 1327108
  109.3 12.4 %copy-start.8 = (f32[1,96,1152]{2,1,0:T(8,128)S(1)}, f32[1,96,1152]{2,1,0:T(8,128)}, u32[]{:S(2)}) copy-start(f32[1,96,1152]{2,1,0:T(8,128)} %get-tuple-element.19) | copy-start | bytes 1327108
  109.3 14.3 %collective-permute-start.16 = (bf16[1,96,1152]{2,1,0:T(8,128)(2,1)S(1)}, bf16[1,96,1152]{2,1,0:T(8,128)(2,1)S(1)}, u32[]{:S(2)}, u32[]{:S(2)}) collective-permute-start(bf16[1,96,1152]{2,1,0:T(8,128)(2,1)S(1)} %add_convert_fusion.1), channel_id=1, source_target_pairs={{0,16},{4,20},{8,24},{12,28},{16,0},{20,4},{24,8},{28,12},{1,17},{... | collective-permute-start | bytes 663560 | tf_op jit(solution)/shard_map/ppermute | solution.py:323
  117.7 11.7 %copy-start.20 = (bf16[2304]{0:T(1024)(128)(2,1)S(1)}, bf16[2304]{0:T(1024)(128)(2,1)}, u32[]{:S(2)}) copy-start(bf16[2304]{0:T(1024)(128)(2,1)} %param.22) | copy-start | bytes 13828
  117.8 10.4 %collective-permute-start.13 = (bf16[1,96,1152]{2,1,0:T(8,128)(2,1)S(1)}, bf16[1,96,1152]{2,1,0:T(8,128)(2,1)S(1)}, u32[]{:S(2)}, u32[]{:S(2)}) collective-permute-start(bf16[1,96,1152]{2,1,0:T(8,128)(2,1)S(1)} %get-tuple-element.31), channel_id=1, source_target_pairs={{0,8},{4,12},{8,0},{12,4},{16,24},{20,28},{24,16},{28,20},{1,9},{5... | collective-permute-start | bytes 663560 | tf_op jit(solution)/shard_map/ppermute | solution.py:323
  118.9 11.6 %copy-start.7 = (bf16[2,96,1152]{2,1,0:T(8,128)(2,1)}, bf16[2,96,1152]{2,1,0:T(8,128)(2,1)S(1)}, u32[]{:S(2)}) copy-start(bf16[2,96,1152]{2,1,0:T(8,128)(2,1)S(1)} %collective-permute-done.9.refs_1_) | copy-start | bytes 1327108
  118.9 11.6 %collective-permute-start.12 = (f32[1,96,1152]{2,1,0:T(8,128)S(1)}, f32[1,96,1152]{2,1,0:T(8,128)S(1)}, u32[]{:S(2)}, u32[]{:S(2)}) collective-permute-start(f32[1,96,1152]{2,1,0:T(8,128)S(1)} %get-tuple-element.32), channel_id=1, source_target_pairs={{0,4},{4,0},{8,12},{12,8},{16,20},{20,16},{24,28},{28,24},{1,5},{5... | collective-permute-start | bytes 1327112 | tf_op jit(solution)/shard_map/ppermute | solution.py:323
  123.5 6.5 %collective-permute-start.10 = (bf16[1,96,1152]{2,1,0:T(8,128)(2,1)S(1)}, bf16[1,96,1152]{2,1,0:T(8,128)(2,1)S(1)}, u32[]{:S(2)}, u32[]{:S(2)}) collective-permute-start(bf16[1,96,1152]{2,1,0:T(8,128)(2,1)S(1)} %add_convert_fusion.3), channel_id=1, source_target_pairs={{0,16},{4,20},{8,24},{12,28},{16,0},{20,4},{24,8},{28,12},{1,17},{... | collective-permute-start | bytes 663560 | tf_op jit(solution)/shard_map/ppermute | solution.py:323
  123.6 6.9 %copy-start.16 = (bf16[1,96,1152]{2,1,0:T(8,128)(2,1)}, bf16[1,96,1152]{2,1,0:T(8,128)(2,1)S(1)}, u32[]{:S(2)}) copy-start(bf16[1,96,1152]{2,1,0:T(8,128)(2,1)S(1)} %collective-permute-done.16.refs_7_) | copy-start | bytes 663556
  123.6 6.4 %collective-permute-start.20 = (bf16[1,96,1152]{2,1,0:T(8,128)(2,1)S(1)}, bf16[1,96,1152]{2,1,0:T(8,128)(2,1)S(1)}, u32[]{:S(2)}, u32[]{:S(2)}) collective-permute-start(bf16[1,96,1152]{2,1,0:T(8,128)(2,1)S(1)} %collective-permute-done.19), channel_id=1, source_target_pairs={{0,4},{4,0},{8,12},{12,8},{16,20},{20,16},{24,28},{28,24},{1,5},{5... | collective-permute-start | bytes 663560 | tf_op jit(solution)/shard_map/ppermute | solution.py:323
  128.2 2.3 %collective-permute-start.14 = (bf16[1,96,1152]{2,1,0:T(8,128)(2,1)S(1)}, bf16[1,96,1152]{2,1,0:T(8,128)(2,1)S(1)}, u32[]{:S(2)}, u32[]{:S(2)}) collective-permute-start(bf16[1,96,1152]{2,1,0:T(8,128)(2,1)S(1)} %collective-permute-done.13), channel_id=1, source_target_pairs={{0,4},{4,0},{8,12},{12,8},{16,20},{20,16},{24,28},{28,24},{1,5},{5... | collective-permute-start | bytes 663560 | tf_op jit(solution)/shard_map/ppermute | solution.py:323
  130.0 0.7 copy-start.17
  130.0 0.8 copy-start.18
  130.0 0.9 copy-start.14
  130.5 0.7 copy-start.19
  130.5 0.8 copy-start.15

commit v5 on v4

--- a/solution.py
+++ b/solution.py
@@ -22,12 +22,37 @@
 HBM = pl.BlockSpec(memory_space=pltpu.HBM)
 
 
+def measure_kernel(arrivals, out):
+    requests, fresh_len, width = arrivals.shape
+    lane = lax.broadcasted_iota(jnp.int32, (fresh_len, LANES), 1)
+    for index in range(requests):
+        value = arrivals[index].astype(jnp.float32)
+        center = jnp.sum(value, axis=-1, keepdims=True) / width
+        square = jnp.sum(jnp.square(value - center), axis=-1, keepdims=True)
+        packed = jnp.where(lane == 0, center, jnp.where(lane == 1, square, 0.0))
+        for layer in range(out.shape[0]):
+            out[layer, index] = packed
+
+
+def norm_kernel(arrivals, stats, gain, bias, out):
+    requests, _, width = arrivals.shape
+    depth = stats.shape[0]
+    for index in range(requests):
+        pairs = [stats[layer, index] for layer in range(depth)]
+        center = sum(pair[:, 0:1] for pair in pairs) / depth
+        square = sum(pair[:, 1:2] + width * jnp.square(pair[:, 0:1] - center) for pair in pairs)
+        scale = lax.rsqrt(square / (depth * width) + EPS)
+        value = (arrivals[index].astype(jnp.float32) - center) * scale
+        out[index] = (value * gain[...] + bias[...]).astype(jnp.bfloat16)
+
+
 def project_kernel(part, plan, place, position, *refs):
     groups = sum(len(members) for members, _ in plan)
     tokens = refs[:groups]
     own_rows, other_rows = refs[groups : groups + 2]
-    outs = refs[groups + 2 : -4]
-    weights, picked, sems, weight_sems = refs[-4:]
+    outs = refs[groups + 2 : groups + 2 + len(plan)]
+    weights, picked, sems, weight_sems, out_sems, *ready = refs[groups + 2 + len(plan) :]
+    stores = []
     core, begin = place[0], place[1]
     depth = own_rows.shape[0]
     chips = groups // 2
@@ -53,43 +78,28 @@
             weight_sems.at[1],
         ),
     ]
-    fetches = []
     for index, token in enumerate(tokens):
         row = (index // chips * chips + (index % chips ^ begin)) * req_count
         for item in range(req_count):
             to = position[row + item] - part * groups * held_count
-            mine = (to >= 0) & (to < groups * held_count)
-            to = jnp.where(mine, to, 0)
-            fetches.append(
-                (
-                    mine,
-                    pltpu.make_async_copy(
-                        token.at[item], picked.at[to], sems.at[index * req_count + item]
-                    ),
-                )
-            )
-    for mine, fetch in fetches:
-
-        @pl.when(mine)
-        def _():
-            fetch.start()
+
+            @pl.when((to >= 0) & (to < groups * held_count))
+            def _(token=token, item=item, to=to):
+                pltpu.make_async_copy(token.at[item], picked.at[to], sems.at[to]).start()
 
     for copy in copies:
         copy.start()
-    for mine, fetch in fetches:
-
-        @pl.when(mine)
-        def _():
-            fetch.wait()
-
-    for copy in copies:
-        copy.wait()
     together = min(groups, 4)
     targets = [
         (output, index) for output, (members, _) in enumerate(plan) for index in range(len(members))
     ]
     for first in range(0, groups, together):
         these = targets[first : first + together]
+        for at in range(first * held_count, (first + together) * held_count):
+            pltpu.make_async_copy(tokens[0].at[0], picked.at[at], sems.at[at]).wait()
+        if first == 0:
+            for copy in copies:
+                copy.wait()
         value = picked[first * held_count : (first + together) * held_count]
         result = jnp.dot(
             value.reshape(together * rows, width),
@@ -97,9 +107,19 @@
             preferred_element_type=jnp.float32,
         )
         for count, (output, index) in enumerate(these):
-            outs[output][index] = result[count * rows : (count + 1) * rows].astype(
-                outs[output].dtype
+            ready[output][index] = result[count * rows : (count + 1) * rows].astype(
+                ready[output].dtype
             )
+            stores.append(
+                pltpu.make_async_copy(
+                    ready[output].at[index],
+                    outs[output].at[index],
+                    out_sems.at[first + count],
+                )
+            )
+            stores[-1].start()
+    for store in stores:
+        store.wait()
 
 
 def attend_kernel(shape, place, all_lengths, table, *refs):
@@ -164,7 +184,8 @@
     width = heads * HEAD
 
     def rows_of(ref):
-        return ref[...].reshape(held_count * fresh_len, width)
+        table = ref[...].reshape(held_count * fresh_len, HEAD)
+        return jnp.concatenate([table] * heads, axis=1)
 
     cosine, sine_up, sine_down = rows_of(cosine), rows_of(sine_up), rows_of(sine_down)
 
@@ -331,23 +352,37 @@
     layer = lax.axis_index("wgt")
     per = chips // wgt_size
 
-    widened = arrivals.reshape(rows, width).astype(jnp.float32)
-    middle = jnp.mean(widened, axis=-1)
-    square = jnp.sum(jnp.square(widened - middle[:, None]), axis=-1)
-    local = jnp.stack([middle, square])
-    stats = jnp.broadcast_to(local[None], (wgt_size, 2, rows))
+    other_rows = lax.dynamic_slice_in_dim(w_qkv, (1 - core) * half_cols, half_cols, 1)
+    if half_cols % LANES == 0:
+        own_rows = w_qkv
+    else:
+        own_rows = lax.dynamic_slice_in_dim(w_qkv, core * half_cols, half_cols, 1)
+    arrivals = after(arrivals, other_rows)
+    other_rows = swap(other_rows, 1)
+
+    params = pltpu.CompilerParams(vmem_limit_bytes=VMEM_LIMIT)
+    stats = pl.pallas_call(
+        measure_kernel,
+        out_shape=jax.ShapeDtypeStruct((wgt_size, req_count, fresh_len, LANES), jnp.float32),
+        in_specs=[VMEM],
+        out_specs=VMEM,
+        compiler_params=params,
+        name="measure",
+    )(arrivals)
     stats = lax.all_to_all(stats, "wgt", 0, 0, tiled=True)
-    center = jnp.mean(stats[:, 0], axis=0)
-    square = jnp.sum(stats[:, 1] + width * jnp.square(stats[:, 0] - center[None]), axis=0)
-    scale = lax.rsqrt(square / (width * wgt_size) + EPS)
     gain, shift = (
-        lax.dynamic_slice_in_dim(value, layer * width, width).astype(jnp.float32)
+        lax.dynamic_slice_in_dim(value, layer * width, width).astype(jnp.float32).reshape(1, width)
         for value in (ln_gain, ln_bias)
     )
-    tokens = (widened - center[:, None]) * scale[:, None] * gain + shift
-    tokens = tokens.astype(jnp.bfloat16)
-    if per > 1:
-        tokens = tokens.reshape(rows, per, block)
+    tokens = pl.pallas_call(
+        norm_kernel,
+        out_shape=jax.ShapeDtypeStruct((req_count, fresh_len, width), jnp.bfloat16),
+        in_specs=[VMEM] * 4,
+        out_specs=VMEM,
+        compiler_params=params,
+        name="norm",
+    )(arrivals, stats, gain, shift)
+    tokens = tokens.reshape(rows, per, block) if per > 1 else tokens.reshape(rows, width)
 
     def route(turn):
         pairs = []
@@ -386,7 +421,7 @@
     row = (((origin & 1) ^ core) * chips + (origin >> 1)) * req_count + ids % req_count
     position = jnp.sum(jnp.where(row[None, :] == ids[:, None], spot[None, :], 0), axis=1)
 
-    lane = np.arange(heads * HEAD) % HEAD
+    lane = np.arange(HEAD)
     half_rot = ROT // 2
     inverse = jnp.power(10000.0, -jnp.asarray(lane % half_rot, jnp.float32) * 2.0 / ROT)
     positions = (
@@ -400,8 +435,7 @@
     sine_down = jnp.where(turns & jnp.asarray(lane >= half_rot)[None, :], sine, 0.0)
 
     tables = [
-        value.reshape(req_count, fresh_len, heads * HEAD)
-        for value in (cosine, sine_up, sine_down)
+        value.reshape(req_count, fresh_len, HEAD) for value in (cosine, sine_up, sine_down)
     ]
     bias = qkv_bias.astype(jnp.float32).reshape(1, local_cols)
     place = jnp.stack([core, layer * per + chip % per]).astype(jnp.int32)
@@ -409,16 +443,8 @@
     span = page_table.shape[1]
     pages = span + (req_count - 1) * (span // 2)
 
-    if half_cols % LANES == 0:
-        own_rows, other_rows = w_qkv, swap(after(w_qkv, scale), 1)
-    else:
-        own_rows = lax.dynamic_slice_in_dim(w_qkv, core * half_cols, half_cols, 1)
-        other_rows = lax.dynamic_slice_in_dim(w_qkv, (1 - core) * half_cols, half_cols, 1)
-        other_rows = swap(other_rows, 1)
-
     received += [swap(piece, 1) for piece in received]
     received = [piece.reshape(req_count, fresh_len, block) for piece in received]
-    received[0] = after(received[0], tables)
 
     def collect(blocks):
         if not square_plane:
@@ -441,12 +467,17 @@
                     for members, kind in plan
                 ],
                 in_specs=[SMEM] * 2 + [HBM] * (req_size + 2),
-                out_specs=[VMEM] * len(plan),
+                out_specs=[HBM] * len(plan),
                 scratch_shapes=[
                     pltpu.VMEM((block, half_cols), jnp.bfloat16),
                     pltpu.VMEM((req_size * half, fresh_len, block), jnp.bfloat16),
-                    pltpu.SemaphoreType.DMA((everyone,)),
+                    pltpu.SemaphoreType.DMA((req_size * half,)),
                     pltpu.SemaphoreType.DMA((2,)),
+                    pltpu.SemaphoreType.DMA((req_size,)),
+                ]
+                + [
+                    pltpu.VMEM((len(members), chunk_rows, half_cols), kind)
+                    for members, kind in plan
                 ],
                 compiler_params=pltpu.CompilerParams(vmem_limit_bytes=VMEM_LIMIT),
                 name="project",

time: 149 us -> 153 us (1.027)
  the two profiles are of different devices: /device:TPU:1 before, /device:TPU:16 now
where the time goes in v5:
time: 153 us
  waiting for transfers between devices  72 us (47%)
  Pallas kernels  38.3 us (25%)
  starting transfers between devices  28.4 us (19%)
  local copies, waits for them, and re-layouts  8.47 us (6%)
  other arithmetic  4.88 us (3%)
    ppermute x4, waiting for transfers between devices, route(): return lax.ppermute(value, ('req', 'wgt'), pairs)  46.3 us
    ppermute x17, waiting for transfers between devices, swap(): lax.ppermute(value, 'req', [(device, device ^ distance) for device in ran...  19.3 us
    pallas_call x2, Pallas kernels, per_device(): pl.pallas_call(functools.partial(project_kernel, part, plan), out_shape=[...  18.1 us
    pallas_call x1, Pallas kernels, per_device(): pl.pallas_call(functools.partial(attend_kernel, (terms, req_count, fresh_...  15.7 us
    ppermute x17, starting transfers between devices, swap(): lax.ppermute(value, 'req', [(device, device ^ distance) for device in ran...  13.5 us
    ppermute x4, starting transfers between devices, route(): return lax.ppermute(value, ('req', 'wgt'), pairs)  9.67 us
    all_to_all x1, waiting for transfers between devices, per_device(): stats = lax.all_to_all(stats, 'wgt', 0, 0, tiled=True)  6.42 us
    all_to_all x1, starting transfers between devices, per_device(): stats = lax.all_to_all(stats, 'wgt', 0, 0, tiled=True)  5.2 us
  transfers between devices with their start and end apart: 22, of which 10 were waited for; matrix products, arithmetic and copies ran while one was open for 5% of the time, Pallas kernels for 7%

profile of v5, /device:TPU:16, one launch (start us, length us, event | category | flops | bytes accessed | tf_op | source)
XLA Modules:
  0.0 153.2 jit_solution(6379707415520309987)
XLA Ops:
  0.6 0.0 copy-start
  0.7 2.9 %constant_dynamic-slice_fusion = bf16[768,1152]{1,0:T(8,128)(2,1)} fusion(bf16[768,2304]{1,0:T(8,128)(2,1)} %refs_8_.3, s32[]{:T(128)S(6)} %select_n.77), kind=kLoop, calls=%fused_computation.36 | loop fusion | bytes 3538948 | tf_op jit(solution)/shard_map/dynamic_slice | solution.py:355
  3.5 2.1 %measure.1 = f32[4,4,48,128]{3,2,1,0:T(8,128)} custom-call(bf16[4,48,1536]{2,1,0:T(8,128)(2,1)} %arrivals.1), custom_call_target="tpu_custom_call" | custom-call | tf_op jit(solution)/shard_map/measure/pallas_call | solution.py:364
  5.7 5.2 %all-to-all-start = ((f32[4,4,48,128]{3,2,1,0:T(8,128)}), f32[4,4,48,128]{3,2,1,0:T(8,128)S(1)}, u32[]{:S(2)}, u32[]{:S(2)}) async-start(f32[4,4,48,128]{3,2,1,0:T(8,128)} %measure.1), calls=%async_computation | async-start | bytes 786432 | tf_op jit(solution)/shard_map/all_to_all | solution.py:372
  10.9 0.8 dynamic-slice_convert_fusion
  11.7 0.6 reshape.192.gain
  12.3 0.6 reshape.194.bias
  12.9 6.4 %all-to-all-done.stats = f32[4,4,48,128]{3,2,1,0:T(8,128)S(1)} async-done(((f32[4,4,48,128]{3,2,1,0:T(8,128)}), f32[4,4,48,128]{3,2,1,0:T(8,128)S(1)}, u32[]{:S(2)}, u32[]{:S(2)}) %all-to-all-start) | async-done | bytes 393248 | tf_op jit(solution)/shard_map/all_to_all | solution.py:372
  19.3 0.7 copy-done.5
  20.0 2.4 %norm.1 = bf16[4,48,1536]{2,1,0:T(8,128)(2,1)} custom-call(bf16[4,48,1536]{2,1,0:T(8,128)(2,1)} %arrivals.1, f32[4,4,48,128]{3,2,1,0:T(8,128)} %copy-done.5, f32[1,1536]{1,0:T(1,128)} %reshape.192.gain, f32[1,1536]{1,0:T(1,128)} %reshape.194.bias), custom_call_target="tpu_custom_call" | custom-call | tf_op jit(solution)/shard_map/norm/pallas_call | solution.py:377
  22.5 3.3 %collective-permute-start.3 = (bf16[192,1536]{1,0:T(8,128)(2,1)}, bf16[192,1536]{1,0:T(8,128)(2,1)S(1)}, u32[]{:S(2)}, u32[]{:S(2)}) collective-permute-start(bf16[192,1536]{1,0:T(8,128)(2,1)} %bitcast.17), channel_id=1, source_target_pairs={{24,0},{16,1},{8,2},{0,3},{28,4},{20,5},{12,6},{4,7},{25,8},{17,9}... | collective-permute-start | bytes 1769480 | tf_op jit(solution)/shard_map/ppermute | solution.py:399
  25.8 2.8 %collective-permute-start = (bf16[192,1536]{1,0:T(8,128)(2,1)}, bf16[192,1536]{1,0:T(8,128)(2,1)S(1)}, u32[]{:S(2)}, u32[]{:S(2)}) collective-permute-start(bf16[192,1536]{1,0:T(8,128)(2,1)} %bitcast.18), channel_id=1, source_target_pairs={{0,0},{8,1},{16,2},{24,3},{4,4},{12,5},{20,6},{28,7},{1,8},{9,9},{... | collective-permute-start | bytes 1769480 | tf_op jit(solution)/shard_map/ppermute | solution.py:399
  28.6 1.2 collective-permute-start.1
  29.8 2.4 %collective-permute-start.2 = (bf16[192,1536]{1,0:T(8,128)(2,1)}, bf16[192,1536]{1,0:T(8,128)(2,1)}, u32[]{:S(2)}, u32[]{:S(2)}) collective-permute-start(bf16[192,1536]{1,0:T(8,128)(2,1)} %bitcast.20), channel_id=1, source_target_pairs={{16,0},{24,1},{0,2},{8,3},{20,4},{28,5},{4,6},{12,7},{17,8},{25,9}... | collective-permute-start | bytes 1769480 | tf_op jit(solution)/shard_map/ppermute | solution.py:399
  32.2 30.7 %collective-permute-done.3 = bf16[192,1536]{1,0:T(8,128)(2,1)S(1)} collective-permute-done((bf16[192,1536]{1,0:T(8,128)(2,1)}, bf16[192,1536]{1,0:T(8,128)(2,1)S(1)}, u32[]{:S(2)}, u32[]{:S(2)}) %collective-permute-start.3) | collective-permute-done | bytes 589856 | tf_op jit(solution)/shard_map/ppermute | solution.py:399
  62.9 0.0 collective-permute-start.7
  62.9 5.0 %collective-permute-done = bf16[192,1536]{1,0:T(8,128)(2,1)S(1)} collective-permute-done((bf16[192,1536]{1,0:T(8,128)(2,1)}, bf16[192,1536]{1,0:T(8,128)(2,1)S(1)}, u32[]{:S(2)}, u32[]{:S(2)}) %collective-permute-start) | collective-permute-done | bytes 589856 | tf_op jit(solution)/shard_map/ppermute | solution.py:399
  67.9 0.0 collective-permute-start.4
  67.9 10.6 %collective-permute-done.1 = bf16[192,1536]{1,0:T(8,128)(2,1)S(1)} collective-permute-done((bf16[192,1536]{1,0:T(8,128)(2,1)}, bf16[192,1536]{1,0:T(8,128)(2,1)S(1)}, u32[]{:S(2)}, u32[]{:S(2)}) %collective-permute-start.1) | collective-permute-done | bytes 589856 | tf_op jit(solution)/shard_map/ppermute | solution.py:399
  78.5 0.5 collective-permute-start.6
  79.0 0.7 gather_fusion
  79.7 0.7 pad_add_fusion.place
  80.3 0.2 convert_reduce_fusion
  80.5 0.6 select_reduce_fusion.position
  81.2 0.0 collective-permute-done.7
  81.2 0.0 collective-permute-done.4
  81.2 0.5 collective-permute-done.6
  81.6 0.0 collective-permute-done.8.refs_9_
  81.7 1.2 copy-done.1
  82.9 9.1 %project.3 = (bf16[2,96,1152]{2,1,0:T(8,128)(2,1)}, bf16[2,96,1152]{2,1,0:T(8,128)(2,1)}, f32[1,96,1152]{2,1,0:T(8,128)}, f32[1,96,1152]{2,1,0:T(8,128)}, f32[1,...) custom-call(s32[2]{0:T(128)} %pad_add_fusion.place, s32[32]{0:T(128)} %select_reduce_fusion.position, ...), custom_call_target="tpu_custom_call" | custom-call | tf_op jit(solution)/shard_map/project/pallas_call | solution.py:463
  92.0 0.1 collective-permute-start.17
  92.1 0.6 reshape.196.refs_10_
  92.7 0.1 add_convert_fusion.4
  92.8 8.4 %collective-permute-start.15 = (bf16[2,96,1152]{2,1,0:T(8,128)(2,1)}, bf16[2,96,1152]{2,1,0:T(8,128)(2,1)S(1)}, u32[]{:S(2)}, u32[]{:S(2)}) collective-permute-start(bf16[2,96,1152]{2,1,0:T(8,128)(2,1)} %get-tuple-element.24), channel_id=1, source_target_pairs={{0,8},{4,12},{8,0},{12,4},{16,24},{20,28},{24,16},{28,20},{1,9},{5... | collective-permute-start | bytes 1327112 | tf_op jit(solution)/shard_map/ppermute | solution.py:344
  101.2 9.0 %project.2 = (bf16[2,96,1152]{2,1,0:T(8,128)(2,1)}, bf16[2,96,1152]{2,1,0:T(8,128)(2,1)}, f32[1,96,1152]{2,1,0:T(8,128)}, f32[1,96,1152]{2,1,0:T(8,128)}, f32[1,...) custom-call(s32[2]{0:T(128)} %pad_add_fusion.place, s32[32]{0:T(128)} %select_reduce_fusion.position, ...), custom_call_target="tpu_custom_call" | custom-call | tf_op jit(solution)/shard_map/project/pallas_call | solution.py:463
  110.2 0.0 copy-start.20
  110.2 0.0 copy-start.21
  110.2 0.0 copy-start.22
  110.2 0.0 copy-start.23
  110.2 2.1 %collective-permute-start.11 = (bf16[2,96,1152]{2,1,0:T(8,128)(2,1)}, bf16[2,96,1152]{2,1,0:T(8,128)(2,1)S(1)}, u32[]{:S(2)}, u32[]{:S(2)}) collective-permute-start(bf16[2,96,1152]{2,1,0:T(8,128)(2,1)} %get-tuple-element.21), channel_id=1, source_target_pairs={{0,16},{4,20},{8,24},{12,28},{16,0},{20,4},{24,8},{28,12},{1,17},{... | collective-permute-start | bytes 1327112 | tf_op jit(solution)/shard_map/ppermute | solution.py:344
  112.3 0.2 collective-permute-start.9
  112.4 0.0 collective-permute-done.17
  112.5 0.1 add_convert_fusion
  112.5 1.9 %collective-permute-start.19 = (bf16[1,96,1152]{2,1,0:T(8,128)(2,1)S(1)}, bf16[1,96,1152]{2,1,0:T(8,128)(2,1)S(1)}, u32[]{:S(2)}, u32[]{:S(2)}) collective-permute-start(bf16[1,96,1152]{2,1,0:T(8,128)(2,1)S(1)} %get-tuple-element.29), channel_id=1, source_target_pairs={{0,8},{4,12},{8,0},{12,4},{16,24},{20,28},{24,16},{28,20},{1,9},{5... | collective-permute-start | bytes 663560 | tf_op jit(solution)/shard_map/ppermute | solution.py:344
  114.5 0.1 collective-permute-start.16
  114.7 8.8 %collective-permute-done.11 = bf16[2,96,1152]{2,1,0:T(8,128)(2,1)S(1)} collective-permute-done((bf16[2,96,1152]{2,1,0:T(8,128)(2,1)}, bf16[2,96,1152]{2,1,0:T(8,128)(2,1)S(1)}, u32[]{:S(2)}, u32[]{:S(2)}) %collective-permute-start.11) | collective-permute-done | bytes 442400 | tf_op jit(solution)/shard_map/ppermute | solution.py:344
  123.5 1.2 add_convert_fusion.2
  124.7 0.2 collective-permute-start.13
  124.9 0.7 collective-permute-done.9.refs_1_
  125.6 0.0 collective-permute-start.12
  125.6 4.7 %collective-permute-done.19 = bf16[1,96,1152]{2,1,0:T(8,128)(2,1)S(1)} collective-permute-done((bf16[1,96,1152]{2,1,0:T(8,128)(2,1)S(1)}, bf16[1,96,1152]{2,1,0:T(8,128)(2,1)S(1)}, u32[]{:S(2)}, u32[]{:S(2)}) %collective-permute-start.19) | collective-permute-done | bytes 221216 | tf_op jit(solution)/shard_map/ppermute | solution.py:344
  130.3 0.0 collective-permute-start.10
  130.4 0.0 collective-permute-start.20
  130.4 3.2 %collective-permute-done.13 = bf16[1,96,1152]{2,1,0:T(8,128)(2,1)S(1)} collective-permute-done((bf16[1,96,1152]{2,1,0:T(8,128)(2,1)S(1)}, bf16[1,96,1152]{2,1,0:T(8,128)(2,1)S(1)}, u32[]{:S(2)}, u32[]{:S(2)}) %collective-permute-start.13) | collective-permute-done | bytes 221216 | tf_op jit(solution)/shard_map/ppermute | solution.py:344
  133.6 0.0 collective-permute-start.14
  133.7 1.1 fusion
  134.8 1.4 collective-permute-done.10.refs_2_
  136.3 0.0 collective-permute-done.12.refs_3_
  136.4 0.6 copy-done.15
  137.0 0.1 copy-done.16
  137.0 0.1 copy-done.8
  137.2 0.1 copy-done.17
  137.2 0.2 copy-done.9
  137.4 15.7 %attend.1 = (bf16[4,48,768]{2,1,0:T(8,128)(2,1)}, bf16[4,48,768]{2,1,0:T(8,128)(2,1)}, bf16[4,48,768]{2,1,0:T(8,128)(2,1)}) custom-call(s32[2]{0:T(128)} %pad_add_fusion.place, s32[4]{0:T(128)} %all_lengths.1, s32[4,16]{1,0:T(4,128)} %table.1, f32[1,96,1152]{2,1,0:T(8,128)} %get-tuple-element.17.refs_0_, bf16[2,96,1152]{2,1,0:T(8,128)(2,1)} %copy-done.7, ...), custom_call_target="tpu_custom_call" | custom-call | tf_op jit(solution)/shard_map/attend/pallas_call | solution.py:494
  (53 shorter events, 0.2 us)
Async XLA Ops:
  0.6 78.3 %copy-start = (s32[8]{0:T(128)S(1)}, s32[8]{0:T(128)}, u32[]{:S(2)}) copy-start(s32[8]{0:T(128)} %constant.104.clone) | copy-start | bytes 100
  0.6 31.5 %copy-start.24 = (s32[32]{0:T(128)S(1)}, s32[32]{0:T(128)}, u32[]{:S(2)}) copy-start(s32[32]{0:T(128)} %param.16) | copy-start | bytes 388
  5.7 13.6 %all-to-all-start = ((f32[4,4,48,128]{3,2,1,0:T(8,128)}), f32[4,4,48,128]{3,2,1,0:T(8,128)S(1)}, u32[]{:S(2)}, u32[]{:S(2)}) async-start(f32[4,4,48,128]{3,2,1,0:T(8,128)} %measure.1), calls=%async_computation | async-start | bytes 786432 | tf_op jit(solution)/shard_map/all_to_all | solution.py:372
  10.9 70.8 %collective-permute-start.8 = (bf16[768,1152]{1,0:T(8,128)(2,1)}, bf16[768,1152]{1,0:T(8,128)(2,1)S(1)}, u32[]{:S(2)}, u32[]{:S(2)}) collective-permute-start(bf16[768,1152]{1,0:T(8,128)(2,1)} %constant_dynamic-slice_fusion), channel_id=1, source_target_pairs={{0,4},{4,0},{8,12},{12,8},{16,20},{20,16},{24,28},{28,24},{1,5},{5... | collective-permute-start | bytes 5308424 | tf_op jit(solution)/shard_map/ppermute | solution.py:344
  19.3 0.7 copy-start.5
  22.5 40.4 %collective-permute-start.3 = (bf16[192,1536]{1,0:T(8,128)(2,1)}, bf16[192,1536]{1,0:T(8,128)(2,1)S(1)}, u32[]{:S(2)}, u32[]{:S(2)}) collective-permute-start(bf16[192,1536]{1,0:T(8,128)(2,1)} %bitcast.17), channel_id=1, source_target_pairs={{24,0},{16,1},{8,2},{0,3},{28,4},{20,5},{12,6},{4,7},{25,8},{17,9}... | collective-permute-start | bytes 1769480 | tf_op jit(solution)/shard_map/ppermute | solution.py:399
  25.8 42.1 %collective-permute-start = (bf16[192,1536]{1,0:T(8,128)(2,1)}, bf16[192,1536]{1,0:T(8,128)(2,1)S(1)}, u32[]{:S(2)}, u32[]{:S(2)}) collective-permute-start(bf16[192,1536]{1,0:T(8,128)(2,1)} %bitcast.18), channel_id=1, source_target_pairs={{0,0},{8,1},{16,2},{24,3},{4,4},{12,5},{20,6},{28,7},{1,8},{9,9},{... | collective-permute-start | bytes 1769480 | tf_op jit(solution)/shard_map/ppermute | solution.py:399
  28.6 49.8 %collective-permute-start.1 = (bf16[192,1536]{1,0:T(8,128)(2,1)}, bf16[192,1536]{1,0:T(8,128)(2,1)S(1)}, u32[]{:S(2)}, u32[]{:S(2)}) collective-permute-start(bf16[192,1536]{1,0:T(8,128)(2,1)} %bitcast.19), channel_id=1, source_target_pairs={{8,0},{0,1},{24,2},{16,3},{12,4},{4,5},{28,6},{20,7},{9,8},{1,9},{... | collective-permute-start | bytes 1769480 | tf_op jit(solution)/shard_map/ppermute | solution.py:399
  29.8 48.7 %collective-permute-start.2 = (bf16[192,1536]{1,0:T(8,128)(2,1)}, bf16[192,1536]{1,0:T(8,128)(2,1)}, u32[]{:S(2)}, u32[]{:S(2)}) collective-permute-start(bf16[192,1536]{1,0:T(8,128)(2,1)} %bitcast.20), channel_id=1, source_target_pairs={{16,0},{24,1},{0,2},{8,3},{20,4},{28,5},{4,6},{12,7},{17,8},{25,9}... | collective-permute-start | bytes 1769480 | tf_op jit(solution)/shard_map/ppermute | solution.py:399
  62.9 18.8 %copy-start.2 = (bf16[192,1536]{1,0:T(8,128)(2,1)}, bf16[192,1536]{1,0:T(8,128)(2,1)S(1)}, u32[]{:S(2)}) copy-start(bf16[192,1536]{1,0:T(8,128)(2,1)S(1)} %collective-permute-done.3) | copy-start | bytes 1769476
  62.9 18.3 %collective-permute-start.7 = (bf16[192,1536]{1,0:T(8,128)(2,1)S(1)}, bf16[192,1536]{1,0:T(8,128)(2,1)}, u32[]{:S(2)}, u32[]{:S(2)}) collective-permute-start(bf16[192,1536]{1,0:T(8,128)(2,1)S(1)} %collective-permute-done.3), channel_id=1, source_target_pairs={{0,4},{4,0},{8,12},{12,8},{16,20},{20,16},{24,28},{28,24},{1,5},{5... | collective-permute-start | bytes 1769480 | tf_op jit(solution)/shard_map/ppermute | solution.py:344
  67.9 13.8 %copy-start.3 = (bf16[192,1536]{1,0:T(8,128)(2,1)}, bf16[192,1536]{1,0:T(8,128)(2,1)S(1)}, u32[]{:S(2)}) copy-start(bf16[192,1536]{1,0:T(8,128)(2,1)S(1)} %collective-permute-done) | copy-start | bytes 1769476
  67.9 13.3 %collective-permute-start.4 = (bf16[192,1536]{1,0:T(8,128)(2,1)S(1)}, bf16[192,1536]{1,0:T(8,128)(2,1)}, u32[]{:S(2)}, u32[]{:S(2)}) collective-permute-start(bf16[192,1536]{1,0:T(8,128)(2,1)S(1)} %collective-permute-done), channel_id=1, source_target_pairs={{0,4},{4,0},{8,12},{12,8},{16,20},{20,16},{24,28},{28,24},{1,5},{5... | collective-permute-start | bytes 1769480 | tf_op jit(solution)/shard_map/ppermute | solution.py:344
  78.5 3.2 %copy-start.4 = (bf16[192,1536]{1,0:T(8,128)(2,1)}, bf16[192,1536]{1,0:T(8,128)(2,1)S(1)}, u32[]{:S(2)}) copy-start(bf16[192,1536]{1,0:T(8,128)(2,1)S(1)} %collective-permute-done.1) | copy-start | bytes 1769476
  78.5 2.7 %collective-permute-start.5 = (bf16[192,1536]{1,0:T(8,128)(2,1)S(1)}, bf16[192,1536]{1,0:T(8,128)(2,1)}, u32[]{:S(2)}, u32[]{:S(2)}) collective-permute-start(bf16[192,1536]{1,0:T(8,128)(2,1)S(1)} %collective-permute-done.1), channel_id=1, source_target_pairs={{0,4},{4,0},{8,12},{12,8},{16,20},{20,16},{24,28},{28,24},{1,5},{5... | collective-permute-start | bytes 1769480 | tf_op jit(solution)/shard_map/ppermute | solution.py:344
  78.5 3.2 %collective-permute-start.6 = (bf16[192,1536]{1,0:T(8,128)(2,1)}, bf16[192,1536]{1,0:T(8,128)(2,1)}, u32[]{:S(2)}, u32[]{:S(2)}) collective-permute-start(bf16[192,1536]{1,0:T(8,128)(2,1)} %collective-permute-done.2), channel_id=1, source_target_pairs={{0,4},{4,0},{8,12},{12,8},{16,20},{20,16},{24,28},{28,24},{1,5},{5... | collective-permute-start | bytes 1769480 | tf_op jit(solution)/shard_map/ppermute | solution.py:344
  81.6 1.2 copy-start.1
  82.9 9.2 %copy-start.18 = (bf16[2304]{0:T(1024)(128)(2,1)S(1)}, bf16[2304]{0:T(1024)(128)(2,1)}, u32[]{:S(2)}) copy-start(bf16[2304]{0:T(1024)(128)(2,1)} %param.22) | copy-start | bytes 13828
  82.9 9.8 %copy-start.19 = (s32[4]{0:T(128)S(1)}, s32[4]{0:T(128)}, u32[]{:S(2)}) copy-start(s32[4]{0:T(128)} %all_lengths.1) | copy-start | bytes 52
  92.0 20.4 %collective-permute-start.17 = (bf16[2,96,1152]{2,1,0:T(8,128)(2,1)}, bf16[2,96,1152]{2,1,0:T(8,128)(2,1)S(1)}, u32[]{:S(2)}, u32[]{:S(2)}) collective-permute-start(bf16[2,96,1152]{2,1,0:T(8,128)(2,1)} %get-tuple-element.27), channel_id=1, source_target_pairs={{0,16},{4,20},{8,24},{12,28},{16,0},{20,4},{24,8},{28,12},{1,17},{... | collective-permute-start | bytes 1327112 | tf_op jit(solution)/shard_map/ppermute | solution.py:344
  92.8 19.6 %copy-start.12 = (f32[1,96,1152]{2,1,0:T(8,128)S(1)}, f32[1,96,1152]{2,1,0:T(8,128)}, u32[]{:S(2)}) copy-start(f32[1,96,1152]{2,1,0:T(8,128)} %get-tuple-element.26) | copy-start | bytes 1327108
  92.8 19.6 %copy-start.13 = (f32[1,96,1152]{2,1,0:T(8,128)S(1)}, f32[1,96,1152]{2,1,0:T(8,128)}, u32[]{:S(2)}) copy-start(f32[1,96,1152]{2,1,0:T(8,128)} %get-tuple-element.28) | copy-start | bytes 1327108
  92.8 21.7 %copy-start.11 = (f32[1,96,1152]{2,1,0:T(8,128)S(1)}, f32[1,96,1152]{2,1,0:T(8,128)}, u32[]{:S(2)}) copy-start(f32[1,96,1152]{2,1,0:T(8,128)} %get-tuple-element.25) | copy-start | bytes 1327108
  92.8 21.7 %collective-permute-start.15 = (bf16[2,96,1152]{2,1,0:T(8,128)(2,1)}, bf16[2,96,1152]{2,1,0:T(8,128)(2,1)S(1)}, u32[]{:S(2)}, u32[]{:S(2)}) collective-permute-start(bf16[2,96,1152]{2,1,0:T(8,128)(2,1)} %get-tuple-element.24), channel_id=1, source_target_pairs={{0,8},{4,12},{8,0},{12,4},{16,24},{20,28},{24,16},{28,20},{1,9},{5... | collective-permute-start | bytes 1327112 | tf_op jit(solution)/shard_map/ppermute | solution.py:344
  110.2 15.4 %copy-start.10 = (f32[1,96,1152]{2,1,0:T(8,128)S(1)}, f32[1,96,1152]{2,1,0:T(8,128)}, u32[]{:S(2)}) copy-start(f32[1,96,1152]{2,1,0:T(8,128)} %get-tuple-element.19) | copy-start | bytes 1327108
  110.2 23.5 %copy-start.20 = (pred[96]{0:T(512)(128)(4,1)S(1)}, pred[96]{0:T(512)(128)(4,1)}, u32[]{:S(2)}) copy-start(pred[96]{0:T(512)(128)(4,1)} %constant.106.clone) | copy-start | bytes 292
  110.2 23.5 %copy-start.21 = (pred[96]{0:T(512)(128)(4,1)S(1)}, pred[96]{0:T(512)(128)(4,1)}, u32[]{:S(2)}) copy-start(pred[96]{0:T(512)(128)(4,1)} %constant.107.clone) | copy-start | bytes 292
  110.2 23.5 %copy-start.22 = (f32[96]{0:T(128)S(1)}, f32[96]{0:T(128)}, u32[]{:S(2)}) copy-start(f32[96]{0:T(128)} %constant.114) | copy-start | bytes 1156
  110.2 23.5 %copy-start.23 = (pred[96]{0:T(512)(128)(4,1)S(1)}, pred[96]{0:T(512)(128)(4,1)}, u32[]{:S(2)}) copy-start(pred[96]{0:T(512)(128)(4,1)} %constant.115) | copy-start | bytes 292
  110.2 13.3 %collective-permute-start.11 = (bf16[2,96,1152]{2,1,0:T(8,128)(2,1)}, bf16[2,96,1152]{2,1,0:T(8,128)(2,1)S(1)}, u32[]{:S(2)}, u32[]{:S(2)}) collective-permute-start(bf16[2,96,1152]{2,1,0:T(8,128)(2,1)} %get-tuple-element.21), channel_id=1, source_target_pairs={{0,16},{4,20},{8,24},{12,28},{16,0},{20,4},{24,8},{28,12},{1,17},{... | collective-permute-start | bytes 1327112 | tf_op jit(solution)/shard_map/ppermute | solution.py:344
  112.3 13.3 %collective-permute-start.9 = (bf16[2,96,1152]{2,1,0:T(8,128)(2,1)}, bf16[2,96,1152]{2,1,0:T(8,128)(2,1)S(1)}, u32[]{:S(2)}, u32[]{:S(2)}) collective-permute-start(bf16[2,96,1152]{2,1,0:T(8,128)(2,1)} %get-tuple-element.18), channel_id=1, source_target_pairs={{0,8},{4,12},{8,0},{12,4},{16,24},{20,28},{24,16},{28,20},{1,9},{5... | collective-permute-start | bytes 1327112 | tf_op jit(solution)/shard_map/ppermute | solution.py:344
  112.5 17.8 %collective-permute-start.19 = (bf16[1,96,1152]{2,1,0:T(8,128)(2,1)S(1)}, bf16[1,96,1152]{2,1,0:T(8,128)(2,1)S(1)}, u32[]{:S(2)}, u32[]{:S(2)}) collective-permute-start(bf16[1,96,1152]{2,1,0:T(8,128)(2,1)S(1)} %get-tuple-element.29), channel_id=1, source_target_pairs={{0,8},{4,12},{8,0},{12,4},{16,24},{20,28},{24,16},{28,20},{1,9},{5... | collective-permute-start | bytes 663560 | tf_op jit(solution)/shard_map/ppermute | solution.py:344
  114.5 21.8 %collective-permute-start.18 = (f32[1,96,1152]{2,1,0:T(8,128)S(1)}, f32[1,96,1152]{2,1,0:T(8,128)S(1)}, u32[]{:S(2)}, u32[]{:S(2)}) collective-permute-start(f32[1,96,1152]{2,1,0:T(8,128)S(1)} %get-tuple-element.30), channel_id=1, source_target_pairs={{0,4},{4,0},{8,12},{12,8},{16,20},{20,16},{24,28},{28,24},{1,5},{5... | collective-permute-start | bytes 1327112 | tf_op jit(solution)/shard_map/ppermute | solution.py:344
  114.5 21.9 %copy-start.6 = (bf16[2,96,1152]{2,1,0:T(8,128)(2,1)}, bf16[2,96,1152]{2,1,0:T(8,128)(2,1)S(1)}, u32[]{:S(2)}) copy-start(bf16[2,96,1152]{2,1,0:T(8,128)(2,1)S(1)} %collective-permute-done.15.refs_6_) | copy-start | bytes 1327108
  114.5 15.8 %collective-permute-start.16 = (bf16[1,96,1152]{2,1,0:T(8,128)(2,1)S(1)}, bf16[1,96,1152]{2,1,0:T(8,128)(2,1)S(1)}, u32[]{:S(2)}, u32[]{:S(2)}) collective-permute-start(bf16[1,96,1152]{2,1,0:T(8,128)(2,1)S(1)} %add_convert_fusion.1), channel_id=1, source_target_pairs={{0,16},{4,20},{8,24},{12,28},{16,0},{20,4},{24,8},{28,12},{1,17},{... | collective-permute-start | bytes 663560 | tf_op jit(solution)/shard_map/ppermute | solution.py:344
  124.7 8.9 %collective-permute-start.13 = (bf16[1,96,1152]{2,1,0:T(8,128)(2,1)S(1)}, bf16[1,96,1152]{2,1,0:T(8,128)(2,1)S(1)}, u32[]{:S(2)}, u32[]{:S(2)}) collective-permute-start(bf16[1,96,1152]{2,1,0:T(8,128)(2,1)S(1)} %get-tuple-element.31), channel_id=1, source_target_pairs={{0,8},{4,12},{8,0},{12,4},{16,24},{20,28},{24,16},{28,20},{1,9},{5... | collective-permute-start | bytes 663560 | tf_op jit(solution)/shard_map/ppermute | solution.py:344
  125.6 10.8 %copy-start.7 = (bf16[2,96,1152]{2,1,0:T(8,128)(2,1)}, bf16[2,96,1152]{2,1,0:T(8,128)(2,1)S(1)}, u32[]{:S(2)}) copy-start(bf16[2,96,1152]{2,1,0:T(8,128)(2,1)S(1)} %collective-permute-done.9.refs_1_) | copy-start | bytes 1327108
  125.6 10.7 %collective-permute-start.12 = (f32[1,96,1152]{2,1,0:T(8,128)S(1)}, f32[1,96,1152]{2,1,0:T(8,128)S(1)}, u32[]{:S(2)}, u32[]{:S(2)}) collective-permute-start(f32[1,96,1152]{2,1,0:T(8,128)S(1)} %get-tuple-element.32), channel_id=1, source_target_pairs={{0,4},{4,0},{8,12},{12,8},{16,20},{20,16},{24,28},{28,24},{1,5},{5... | collective-permute-start | bytes 1327112 | tf_op jit(solution)/shard_map/ppermute | solution.py:344
  130.3 5.9 %collective-permute-start.10 = (bf16[1,96,1152]{2,1,0:T(8,128)(2,1)S(1)}, bf16[1,96,1152]{2,1,0:T(8,128)(2,1)S(1)}, u32[]{:S(2)}, u32[]{:S(2)}) collective-permute-start(bf16[1,96,1152]{2,1,0:T(8,128)(2,1)S(1)} %add_convert_fusion.3), channel_id=1, source_target_pairs={{0,16},{4,20},{8,24},{12,28},{16,0},{20,4},{24,8},{28,12},{1,17},{... | collective-permute-start | bytes 663560 | tf_op jit(solution)/shard_map/ppermute | solution.py:344
  130.4 6.0 %copy-start.14 = (bf16[1,96,1152]{2,1,0:T(8,128)(2,1)}, bf16[1,96,1152]{2,1,0:T(8,128)(2,1)S(1)}, u32[]{:S(2)}) copy-start(bf16[1,96,1152]{2,1,0:T(8,128)(2,1)S(1)} %collective-permute-done.16.refs_7_) | copy-start | bytes 663556
  130.4 5.9 %collective-permute-start.20 = (bf16[1,96,1152]{2,1,0:T(8,128)(2,1)S(1)}, bf16[1,96,1152]{2,1,0:T(8,128)(2,1)S(1)}, u32[]{:S(2)}, u32[]{:S(2)}) collective-permute-start(bf16[1,96,1152]{2,1,0:T(8,128)(2,1)S(1)} %collective-permute-done.19), channel_id=1, source_target_pairs={{0,4},{4,0},{8,12},{12,8},{16,20},{20,16},{24,28},{28,24},{1,5},{5... | collective-permute-start | bytes 663560 | tf_op jit(solution)/shard_map/ppermute | solution.py:344
  133.6 2.6 %collective-permute-start.14 = (bf16[1,96,1152]{2,1,0:T(8,128)(2,1)S(1)}, bf16[1,96,1152]{2,1,0:T(8,128)(2,1)S(1)}, u32[]{:S(2)}, u32[]{:S(2)}) collective-permute-start(bf16[1,96,1152]{2,1,0:T(8,128)(2,1)S(1)} %collective-permute-done.13), channel_id=1, source_target_pairs={{0,4},{4,0},{8,12},{12,8},{16,20},{20,16},{24,28},{28,24},{1,5},{5... | collective-permute-start | bytes 663560 | tf_op jit(solution)/shard_map/ppermute | solution.py:344
  136.3 0.7 copy-start.15
  136.3 0.8 copy-start.16
  136.3 0.9 copy-start.8
  136.3 1.0 copy-start.17
  136.3 1.1 copy-start.9

commit v6 on v4

--- a/solution.py
+++ b/solution.py
@@ -164,7 +164,8 @@
     width = heads * HEAD
 
     def rows_of(ref):
-        return ref[...].reshape(held_count * fresh_len, width)
+        table = ref[...].reshape(held_count * fresh_len, HEAD)
+        return jnp.concatenate([table] * heads, axis=1)
 
     cosine, sine_up, sine_down = rows_of(cosine), rows_of(sine_up), rows_of(sine_down)
 
@@ -386,7 +387,7 @@
     row = (((origin & 1) ^ core) * chips + (origin >> 1)) * req_count + ids % req_count
     position = jnp.sum(jnp.where(row[None, :] == ids[:, None], spot[None, :], 0), axis=1)
 
-    lane = np.arange(heads * HEAD) % HEAD
+    lane = np.arange(HEAD)
     half_rot = ROT // 2
     inverse = jnp.power(10000.0, -jnp.asarray(lane % half_rot, jnp.float32) * 2.0 / ROT)
     positions = (
@@ -400,8 +401,7 @@
     sine_down = jnp.where(turns & jnp.asarray(lane >= half_rot)[None, :], sine, 0.0)
 
     tables = [
-        value.reshape(req_count, fresh_len, heads * HEAD)
-        for value in (cosine, sine_up, sine_down)
+        value.reshape(req_count, fresh_len, HEAD) for value in (cosine, sine_up, sine_down)
     ]
     bias = qkv_bias.astype(jnp.float32).reshape(1, local_cols)
     place = jnp.stack([core, layer * per + chip % per]).astype(jnp.int32)
@@ -409,16 +409,15 @@
     span = page_table.shape[1]
     pages = span + (req_count - 1) * (span // 2)
 
+    held = after(w_qkv, local)
     if half_cols % LANES == 0:
-        own_rows, other_rows = w_qkv, swap(after(w_qkv, scale), 1)
+        own_rows = w_qkv
     else:
-        own_rows = lax.dynamic_slice_in_dim(w_qkv, core * half_cols, half_cols, 1)
-        other_rows = lax.dynamic_slice_in_dim(w_qkv, (1 - core) * half_cols, half_cols, 1)
-        other_rows = swap(other_rows, 1)
+        own_rows = lax.dynamic_slice_in_dim(held, core * half_cols, half_cols, 1)
+    other_rows = swap(lax.dynamic_slice_in_dim(held, (1 - core) * half_cols, half_cols, 1), 1)
 
     received += [swap(piece, 1) for piece in received]
     received = [piece.reshape(req_count, fresh_len, block) for piece in received]
-    received[0] = after(received[0], tables)
 
     def collect(blocks):
         if not square_plane:

time: 149 us -> 140 us (0.940)
  the two profiles are of different devices: /device:TPU:1 before, /device:TPU:0 now
where the time goes in v6:
time: 140 us
  waiting for transfers between devices  51.8 us (37%)
  starting transfers between devices  41.9 us (30%)
  Pallas kernels  31.2 us (22%)
  local copies, waits for them, and re-layouts  7.38 us (5%)
  other arithmetic  6.79 us (5%)
    ppermute x4, waiting for transfers between devices, route(): return lax.ppermute(value, ('req', 'wgt'), pairs)  31.7 us
    ppermute x17, starting transfers between devices, swap(): lax.ppermute(value, 'req', [(device, device ^ distance) for device in ran...  28.1 us
    ppermute x17, waiting for transfers between devices, swap(): lax.ppermute(value, 'req', [(device, device ^ distance) for device in ran...  18.3 us
    pallas_call x2, Pallas kernels, per_device(): pl.pallas_call(functools.partial(project_kernel, part, plan), out_shape=[...  16.7 us
    pallas_call x1, Pallas kernels, per_device(): pl.pallas_call(functools.partial(attend_kernel, (terms, req_count, fresh_...  14.5 us
    ppermute x4, starting transfers between devices, route(): return lax.ppermute(value, ('req', 'wgt'), pairs)  7.5 us
    all_to_all x1, starting transfers between devices, per_device(): stats = lax.all_to_all(stats, 'wgt', 0, 0, tiled=True)  6.32 us
    dynamic_slice x1, local copies, waits for them, and re-layouts, per_device(): lax.dynamic_slice_in_dim(held, (1 - core) * half_cols, half_cols, 1)  2.9 us
  transfers between devices with their start and end apart: 22, of which 10 were waited for; matrix products, arithmetic and copies ran while one was open for 6% of the time, Pallas kernels for 6%

profile of v6, /device:TPU:0, one launch (start us, length us, event | category | flops | bytes accessed | tf_op | source)
XLA Modules:
  0.0 140.1 jit_solution(11193572644204233540)
XLA Ops:
  0.6 1.2 convert_reduce_fusion
  1.9 1.4 multiply_reduce_fusion
  3.2 0.1 div.51
  3.3 0.1 stack.19
  3.4 0.6 broadcast_in_dim.69
  4.0 6.3 %all-to-all-start = ((f32[4,2,192]{2,1,0:T(2,128)}), f32[4,2,192]{2,1,0:T(2,128)S(1)}, u32[]{:S(2)}, u32[]{:S(2)}) async-start(f32[4,2,192]{2,1,0:T(2,128)} %broadcast_in_dim.69), calls=%async_computation | async-start | bytes 16384 | tf_op jit(solution)/shard_map/all_to_all | solution.py:340
  10.3 2.9 %constant_dynamic-slice_fusion = bf16[768,1152]{1,0:T(8,128)(2,1)} fusion(bf16[768,2304]{1,0:T(8,128)(2,1)} %refs_8_.3, s32[]{:T(128)S(6)} %select_n.78), kind=kLoop, calls=%fused_computation.53 | loop fusion | bytes 3538948 | tf_op jit(solution)/shard_map/dynamic_slice | solution.py:417
  13.2 0.0 collective-permute-start.8
  13.2 0.8 dynamic-slice_convert_fusion
  14.1 1.9 %all-to-all-done = f32[4,2,192]{2,1,0:T(2,128)S(1)} async-done(((f32[4,2,192]{2,1,0:T(2,128)}), f32[4,2,192]{2,1,0:T(2,128)S(1)}, u32[]{:S(2)}, u32[]{:S(2)}) %all-to-all-start) | async-done | bytes 6176 | tf_op jit(solution)/shard_map/all_to_all | solution.py:340
  16.0 0.4 fusion.3
  16.4 1.1 collective-permute-start.2
  17.5 3.3 %collective-permute-start.3 = (bf16[192,1536]{1,0:T(8,128)(2,1)S(1)}, bf16[192,1536]{1,0:T(8,128)(2,1)S(1)}, u32[]{:S(2)}, u32[]{:S(2)}) collective-permute-start(bf16[192,1536]{1,0:T(8,128)(2,1)S(1)} %fusion.3), channel_id=1, source_target_pairs={{24,0},{16,1},{8,2},{0,3},{28,4},{20,5},{12,6},{4,7},{25,8},{17,9}... | collective-permute-start | bytes 1769480 | tf_op jit(solution)/shard_map/ppermute | solution.py:365
  20.9 0.7 collective-permute-start
  21.6 2.4 %collective-permute-start.1 = (bf16[192,1536]{1,0:T(8,128)(2,1)S(1)}, bf16[192,1536]{1,0:T(8,128)(2,1)}, u32[]{:S(2)}, u32[]{:S(2)}) collective-permute-start(bf16[192,1536]{1,0:T(8,128)(2,1)S(1)} %fusion.3), channel_id=1, source_target_pairs={{8,0},{0,1},{24,2},{16,3},{12,4},{4,5},{28,6},{20,7},{9,8},{1,9},{... | collective-permute-start | bytes 1769480 | tf_op jit(solution)/shard_map/ppermute | solution.py:365
  23.9 19.0 %collective-permute-done.2 = bf16[192,1536]{1,0:T(8,128)(2,1)S(1)} collective-permute-done((bf16[192,1536]{1,0:T(8,128)(2,1)S(1)}, bf16[192,1536]{1,0:T(8,128)(2,1)S(1)}, u32[]{:S(2)}, u32[]{:S(2)}) %collective-permute-start.2) | collective-permute-done | bytes 589856 | tf_op jit(solution)/shard_map/ppermute | solution.py:365
  43.0 0.0 collective-permute-start.6
  43.0 0.9 collective-permute-done.3
  43.9 0.0 collective-permute-start.7
  43.9 0.0 collective-permute-done
  43.9 0.5 collective-permute-start.4
  44.4 11.7 %collective-permute-done.1 = bf16[192,1536]{1,0:T(8,128)(2,1)} collective-permute-done((bf16[192,1536]{1,0:T(8,128)(2,1)S(1)}, bf16[192,1536]{1,0:T(8,128)(2,1)}, u32[]{:S(2)}, u32[]{:S(2)}) %collective-permute-start.1) | collective-permute-done | bytes 589856 | tf_op jit(solution)/shard_map/ppermute | solution.py:365
  56.1 0.0 collective-permute-start.5
  56.2 0.7 gather_fusion
  56.9 0.6 pad_add_fusion.place
  57.5 0.2 convert_reduce_fusion.1
  57.7 0.6 select_reduce_fusion.position
  58.3 0.0 collective-permute-done.7
  58.3 0.0 collective-permute-done.4
  58.3 0.2 collective-permute-done.5
  58.5 1.2 copy-done.1
  59.7 8.3 %project.3 = (bf16[2,96,1152]{2,1,0:T(8,128)(2,1)}, bf16[2,96,1152]{2,1,0:T(8,128)(2,1)}, f32[1,96,1152]{2,1,0:T(8,128)}, f32[1,96,1152]{2,1,0:T(8,128)}, f32[1,...) custom-call(s32[2]{0:T(128)} %pad_add_fusion.place, s32[32]{0:T(128)} %select_reduce_fusion.position, ...), custom_call_target="tpu_custom_call" | custom-call | tf_op jit(solution)/shard_map/project/pallas_call | solution.py:436
  68.1 22.2 %collective-permute-start.17 = (bf16[2,96,1152]{2,1,0:T(8,128)(2,1)}, bf16[2,96,1152]{2,1,0:T(8,128)(2,1)S(1)}, u32[]{:S(2)}, u32[]{:S(2)}) collective-permute-start(bf16[2,96,1152]{2,1,0:T(8,128)(2,1)} %get-tuple-element.27), channel_id=1, source_target_pairs={{0,16},{4,20},{8,24},{12,28},{16,0},{20,4},{24,8},{28,12},{1,17},{... | collective-permute-start | bytes 1327112 | tf_op jit(solution)/shard_map/ppermute | solution.py:324
  90.3 0.6 reshape.218.refs_10_
  90.9 0.1 add_convert_fusion.4
  91.0 0.0 collective-permute-start.15
  91.0 8.4 %project.2 = (bf16[2,96,1152]{2,1,0:T(8,128)(2,1)}, bf16[2,96,1152]{2,1,0:T(8,128)(2,1)}, f32[1,96,1152]{2,1,0:T(8,128)}, f32[1,96,1152]{2,1,0:T(8,128)}, f32[1,...) custom-call(s32[2]{0:T(128)} %pad_add_fusion.place, s32[32]{0:T(128)} %select_reduce_fusion.position, ...), custom_call_target="tpu_custom_call" | custom-call | tf_op jit(solution)/shard_map/project/pallas_call | solution.py:436
  99.4 0.1 collective-permute-start.11
  99.5 1.9 %collective-permute-start.9 = (bf16[2,96,1152]{2,1,0:T(8,128)(2,1)}, bf16[2,96,1152]{2,1,0:T(8,128)(2,1)S(1)}, u32[]{:S(2)}, u32[]{:S(2)}) collective-permute-start(bf16[2,96,1152]{2,1,0:T(8,128)(2,1)} %get-tuple-element.18), channel_id=1, source_target_pairs={{0,8},{4,12},{8,0},{12,4},{16,24},{20,28},{24,16},{28,20},{1,9},{5... | collective-permute-start | bytes 1327112 | tf_op jit(solution)/shard_map/ppermute | solution.py:324
  101.4 0.0 collective-permute-done.17
  101.4 0.1 add_convert_fusion
  101.5 0.2 collective-permute-start.19
  101.7 0.0 collective-permute-start.18
  101.7 2.5 %collective-permute-done.15.refs_6_ = bf16[2,96,1152]{2,1,0:T(8,128)(2,1)S(1)} collective-permute-done((bf16[2,96,1152]{2,1,0:T(8,128)(2,1)}, bf16[2,96,1152]{2,1,0:T(8,128)(2,1)S(1)}, u32[]{:S(2)}, u32[]{:S(2)}) %collective-permute-start.15) | collective-permute-done | bytes 442400 | tf_op jit(solution)/shard_map/ppermute | solution.py:324
  104.3 0.1 collective-permute-start.16
  104.4 8.3 %collective-permute-done.11 = bf16[2,96,1152]{2,1,0:T(8,128)(2,1)S(1)} collective-permute-done((bf16[2,96,1152]{2,1,0:T(8,128)(2,1)}, bf16[2,96,1152]{2,1,0:T(8,128)(2,1)S(1)}, u32[]{:S(2)}, u32[]{:S(2)}) %collective-permute-start.11) | collective-permute-done | bytes 442400 | tf_op jit(solution)/shard_map/ppermute | solution.py:324
  112.7 0.0 copy-start.24
  112.7 0.0 copy-start.25
  112.7 0.1 add_convert_fusion.2
  112.8 2.0 %collective-permute-start.13 = (bf16[1,96,1152]{2,1,0:T(8,128)(2,1)S(1)}, bf16[1,96,1152]{2,1,0:T(8,128)(2,1)S(1)}, u32[]{:S(2)}, u32[]{:S(2)}) collective-permute-start(bf16[1,96,1152]{2,1,0:T(8,128)(2,1)S(1)} %get-tuple-element.31), channel_id=1, source_target_pairs={{0,8},{4,12},{8,0},{12,4},{16,24},{20,28},{24,16},{28,20},{1,9},{5... | collective-permute-start | bytes 663560 | tf_op jit(solution)/shard_map/ppermute | solution.py:324
  114.9 3.6 %collective-permute-done.19 = bf16[1,96,1152]{2,1,0:T(8,128)(2,1)S(1)} collective-permute-done((bf16[1,96,1152]{2,1,0:T(8,128)(2,1)S(1)}, bf16[1,96,1152]{2,1,0:T(8,128)(2,1)S(1)}, u32[]{:S(2)}, u32[]{:S(2)}) %collective-permute-start.19) | collective-permute-done | bytes 221216 | tf_op jit(solution)/shard_map/ppermute | solution.py:324
  118.5 1.0 collective-permute-start.10
  119.5 0.0 collective-permute-done.16.refs_7_
  119.5 2.8 %collective-permute-done.13 = bf16[1,96,1152]{2,1,0:T(8,128)(2,1)S(1)} collective-permute-done((bf16[1,96,1152]{2,1,0:T(8,128)(2,1)S(1)}, bf16[1,96,1152]{2,1,0:T(8,128)(2,1)S(1)}, u32[]{:S(2)}, u32[]{:S(2)}) %collective-permute-start.13) | collective-permute-done | bytes 221216 | tf_op jit(solution)/shard_map/ppermute | solution.py:324
  122.3 1.2 fusion.4
  123.5 0.9 collective-permute-done.10.refs_2_
  124.4 0.0 collective-permute-done.18.refs_8_
  124.4 0.0 collective-permute-done.12.refs_3_
  124.5 0.6 copy-done.17
  125.1 0.1 copy-done.18
  125.2 0.1 copy-done.8
  125.3 0.1 copy-done.19
  125.4 0.2 copy-done.9
  125.6 14.5 %attend.1 = (bf16[4,48,768]{2,1,0:T(8,128)(2,1)}, bf16[4,48,768]{2,1,0:T(8,128)(2,1)}, bf16[4,48,768]{2,1,0:T(8,128)(2,1)}) custom-call(s32[2]{0:T(128)} %pad_add_fusion.place, s32[4]{0:T(128)} %all_lengths.1, s32[4,16]{1,0:T(4,128)} %table.1, f32[1,96,1152]{2,1,0:T(8,128)} %get-tuple-element.17.refs_0_, bf16[2,96,1152]{2,1,0:T(8,128)(2,1)} %copy-done.7, ...), custom_call_target="tpu_custom_call" | custom-call | tf_op jit(solution)/shard_map/attend/pallas_call | solution.py:462
  (65 shorter events, 0.3 us)
Async XLA Ops:
  4.0 11.9 %all-to-all-start = ((f32[4,2,192]{2,1,0:T(2,128)}), f32[4,2,192]{2,1,0:T(2,128)S(1)}, u32[]{:S(2)}, u32[]{:S(2)}) async-start(f32[4,2,192]{2,1,0:T(2,128)} %broadcast_in_dim.69), calls=%async_computation | async-start | bytes 16384 | tf_op jit(solution)/shard_map/all_to_all | solution.py:340
  10.3 5.7 %copy-start.2 = (bf16[4,48,1536]{2,1,0:T(8,128)(2,1)S(1)}, bf16[4,48,1536]{2,1,0:T(8,128)(2,1)}, u32[]{:S(2)}) copy-start(bf16[4,48,1536]{2,1,0:T(8,128)(2,1)} %param.15) | copy-start | bytes 1769476
  13.2 10.7 %copy-start.26 = (s32[32]{0:T(128)S(1)}, s32[32]{0:T(128)}, u32[]{:S(2)}) copy-start(s32[32]{0:T(128)} %param.16) | copy-start | bytes 388
  13.2 42.9 %copy-start = (s32[8]{0:T(128)S(1)}, s32[8]{0:T(128)}, u32[]{:S(2)}) copy-start(s32[8]{0:T(128)} %constant.117.clone) | copy-start | bytes 100
  13.2 45.2 %collective-permute-start.8 = (bf16[768,1152]{1,0:T(8,128)(2,1)}, bf16[768,1152]{1,0:T(8,128)(2,1)S(1)}, u32[]{:S(2)}, u32[]{:S(2)}) collective-permute-start(bf16[768,1152]{1,0:T(8,128)(2,1)} %constant_dynamic-slice_fusion), channel_id=1, source_target_pairs={{0,4},{4,0},{8,12},{12,8},{16,20},{20,16},{24,28},{28,24},{1,5},{5... | collective-permute-start | bytes 5308424 | tf_op jit(solution)/shard_map/ppermute | solution.py:324
  16.4 26.5 %collective-permute-start.2 = (bf16[192,1536]{1,0:T(8,128)(2,1)S(1)}, bf16[192,1536]{1,0:T(8,128)(2,1)S(1)}, u32[]{:S(2)}, u32[]{:S(2)}) collective-permute-start(bf16[192,1536]{1,0:T(8,128)(2,1)S(1)} %fusion.3), channel_id=1, source_target_pairs={{16,0},{24,1},{0,2},{8,3},{20,4},{28,5},{4,6},{12,7},{17,8},{25,9}... | collective-permute-start | bytes 1769480 | tf_op jit(solution)/shard_map/ppermute | solution.py:365
  17.5 26.4 %collective-permute-start.3 = (bf16[192,1536]{1,0:T(8,128)(2,1)S(1)}, bf16[192,1536]{1,0:T(8,128)(2,1)S(1)}, u32[]{:S(2)}, u32[]{:S(2)}) collective-permute-start(bf16[192,1536]{1,0:T(8,128)(2,1)S(1)} %fusion.3), channel_id=1, source_target_pairs={{24,0},{16,1},{8,2},{0,3},{28,4},{20,5},{12,6},{4,7},{25,8},{17,9}... | collective-permute-start | bytes 1769480 | tf_op jit(solution)/shard_map/ppermute | solution.py:365
  20.9 23.0 %collective-permute-start = (bf16[192,1536]{1,0:T(8,128)(2,1)S(1)}, bf16[192,1536]{1,0:T(8,128)(2,1)S(1)}, u32[]{:S(2)}, u32[]{:S(2)}) collective-permute-start(bf16[192,1536]{1,0:T(8,128)(2,1)S(1)} %fusion.3), channel_id=1, source_target_pairs={{0,0},{8,1},{16,2},{24,3},{4,4},{12,5},{20,6},{28,7},{1,8},{9,9},{... | collective-permute-start | bytes 1769480 | tf_op jit(solution)/shard_map/ppermute | solution.py:365
  21.6 34.6 %collective-permute-start.1 = (bf16[192,1536]{1,0:T(8,128)(2,1)S(1)}, bf16[192,1536]{1,0:T(8,128)(2,1)}, u32[]{:S(2)}, u32[]{:S(2)}) collective-permute-start(bf16[192,1536]{1,0:T(8,128)(2,1)S(1)} %fusion.3), channel_id=1, source_target_pairs={{8,0},{0,1},{24,2},{16,3},{12,4},{4,5},{28,6},{20,7},{9,8},{1,9},{... | collective-permute-start | bytes 1769480 | tf_op jit(solution)/shard_map/ppermute | solution.py:365
  43.0 15.5 %copy-start.3 = (bf16[192,1536]{1,0:T(8,128)(2,1)}, bf16[192,1536]{1,0:T(8,128)(2,1)S(1)}, u32[]{:S(2)}) copy-start(bf16[192,1536]{1,0:T(8,128)(2,1)S(1)} %collective-permute-done.2) | copy-start | bytes 1769476
  43.0 15.3 %collective-permute-start.6 = (bf16[192,1536]{1,0:T(8,128)(2,1)S(1)}, bf16[192,1536]{1,0:T(8,128)(2,1)}, u32[]{:S(2)}, u32[]{:S(2)}) collective-permute-start(bf16[192,1536]{1,0:T(8,128)(2,1)S(1)} %collective-permute-done.2), channel_id=1, source_target_pairs={{0,4},{4,0},{8,12},{12,8},{16,20},{20,16},{24,28},{28,24},{1,5},{5... | collective-permute-start | bytes 1769480 | tf_op jit(solution)/shard_map/ppermute | solution.py:324
  43.9 14.6 %copy-start.4 = (bf16[192,1536]{1,0:T(8,128)(2,1)}, bf16[192,1536]{1,0:T(8,128)(2,1)S(1)}, u32[]{:S(2)}) copy-start(bf16[192,1536]{1,0:T(8,128)(2,1)S(1)} %collective-permute-done.3) | copy-start | bytes 1769476
  43.9 14.4 %collective-permute-start.7 = (bf16[192,1536]{1,0:T(8,128)(2,1)S(1)}, bf16[192,1536]{1,0:T(8,128)(2,1)}, u32[]{:S(2)}, u32[]{:S(2)}) collective-permute-start(bf16[192,1536]{1,0:T(8,128)(2,1)S(1)} %collective-permute-done.3), channel_id=1, source_target_pairs={{0,4},{4,0},{8,12},{12,8},{16,20},{20,16},{24,28},{28,24},{1,5},{5... | collective-permute-start | bytes 1769480 | tf_op jit(solution)/shard_map/ppermute | solution.py:324
  43.9 14.6 %copy-start.5 = (bf16[192,1536]{1,0:T(8,128)(2,1)}, bf16[192,1536]{1,0:T(8,128)(2,1)S(1)}, u32[]{:S(2)}) copy-start(bf16[192,1536]{1,0:T(8,128)(2,1)S(1)} %collective-permute-done) | copy-start | bytes 1769476
  43.9 14.4 %collective-permute-start.4 = (bf16[192,1536]{1,0:T(8,128)(2,1)S(1)}, bf16[192,1536]{1,0:T(8,128)(2,1)}, u32[]{:S(2)}, u32[]{:S(2)}) collective-permute-start(bf16[192,1536]{1,0:T(8,128)(2,1)S(1)} %collective-permute-done), channel_id=1, source_target_pairs={{0,4},{4,0},{8,12},{12,8},{16,20},{20,16},{24,28},{28,24},{1,5},{5... | collective-permute-start | bytes 1769480 | tf_op jit(solution)/shard_map/ppermute | solution.py:324
  56.1 2.3 %collective-permute-start.5 = (bf16[192,1536]{1,0:T(8,128)(2,1)}, bf16[192,1536]{1,0:T(8,128)(2,1)}, u32[]{:S(2)}, u32[]{:S(2)}) collective-permute-start(bf16[192,1536]{1,0:T(8,128)(2,1)} %collective-permute-done.1), channel_id=1, source_target_pairs={{0,4},{4,0},{8,12},{12,8},{16,20},{20,16},{24,28},{28,24},{1,5},{5... | collective-permute-start | bytes 1769480 | tf_op jit(solution)/shard_map/ppermute | solution.py:324
  58.5 1.2 copy-start.1
  59.7 30.6 %copy-start.20 = (bf16[2304]{0:T(1024)(128)(2,1)S(1)}, bf16[2304]{0:T(1024)(128)(2,1)}, u32[]{:S(2)}) copy-start(bf16[2304]{0:T(1024)(128)(2,1)} %param.22) | copy-start | bytes 13828
  59.7 31.2 %copy-start.21 = (s32[4]{0:T(128)S(1)}, s32[4]{0:T(128)}, u32[]{:S(2)}) copy-start(s32[4]{0:T(128)} %all_lengths.1) | copy-start | bytes 52
  68.1 33.3 %collective-permute-start.17 = (bf16[2,96,1152]{2,1,0:T(8,128)(2,1)}, bf16[2,96,1152]{2,1,0:T(8,128)(2,1)S(1)}, u32[]{:S(2)}, u32[]{:S(2)}) collective-permute-start(bf16[2,96,1152]{2,1,0:T(8,128)(2,1)} %get-tuple-element.27), channel_id=1, source_target_pairs={{0,16},{4,20},{8,24},{12,28},{16,0},{20,4},{24,8},{28,12},{1,17},{... | collective-permute-start | bytes 1327112 | tf_op jit(solution)/shard_map/ppermute | solution.py:324
  91.0 10.4 %copy-start.14 = (f32[1,96,1152]{2,1,0:T(8,128)S(1)}, f32[1,96,1152]{2,1,0:T(8,128)}, u32[]{:S(2)}) copy-start(f32[1,96,1152]{2,1,0:T(8,128)} %get-tuple-element.26) | copy-start | bytes 1327108
  91.0 10.4 %copy-start.15 = (f32[1,96,1152]{2,1,0:T(8,128)S(1)}, f32[1,96,1152]{2,1,0:T(8,128)}, u32[]{:S(2)}) copy-start(f32[1,96,1152]{2,1,0:T(8,128)} %get-tuple-element.28) | copy-start | bytes 1327108
  91.0 13.3 %collective-permute-start.15 = (bf16[2,96,1152]{2,1,0:T(8,128)(2,1)}, bf16[2,96,1152]{2,1,0:T(8,128)(2,1)S(1)}, u32[]{:S(2)}, u32[]{:S(2)}) collective-permute-start(bf16[2,96,1152]{2,1,0:T(8,128)(2,1)} %get-tuple-element.24), channel_id=1, source_target_pairs={{0,8},{4,12},{8,0},{12,4},{16,24},{20,28},{24,16},{28,20},{1,9},{5... | collective-permute-start | bytes 1327112 | tf_op jit(solution)/shard_map/ppermute | solution.py:324
  99.4 4.9 %copy-start.11 = (f32[1,96,1152]{2,1,0:T(8,128)S(1)}, f32[1,96,1152]{2,1,0:T(8,128)}, u32[]{:S(2)}) copy-start(f32[1,96,1152]{2,1,0:T(8,128)} %get-tuple-element.25) | copy-start | bytes 1327108
  99.4 13.3 %collective-permute-start.11 = (bf16[2,96,1152]{2,1,0:T(8,128)(2,1)}, bf16[2,96,1152]{2,1,0:T(8,128)(2,1)S(1)}, u32[]{:S(2)}, u32[]{:S(2)}) collective-permute-start(bf16[2,96,1152]{2,1,0:T(8,128)(2,1)} %get-tuple-element.21), channel_id=1, source_target_pairs={{0,16},{4,20},{8,24},{12,28},{16,0},{20,4},{24,8},{28,12},{1,17},{... | collective-permute-start | bytes 1327112 | tf_op jit(solution)/shard_map/ppermute | solution.py:324
  99.5 15.3 %collective-permute-start.9 = (bf16[2,96,1152]{2,1,0:T(8,128)(2,1)}, bf16[2,96,1152]{2,1,0:T(8,128)(2,1)S(1)}, u32[]{:S(2)}, u32[]{:S(2)}) collective-permute-start(bf16[2,96,1152]{2,1,0:T(8,128)(2,1)} %get-tuple-element.18), channel_id=1, source_target_pairs={{0,8},{4,12},{8,0},{12,4},{16,24},{20,28},{24,16},{28,20},{1,9},{5... | collective-permute-start | bytes 1327112 | tf_op jit(solution)/shard_map/ppermute | solution.py:324
  101.4 11.3 %copy-start.12 = (f32[1,96,1152]{2,1,0:T(8,128)S(1)}, f32[1,96,1152]{2,1,0:T(8,128)}, u32[]{:S(2)}) copy-start(f32[1,96,1152]{2,1,0:T(8,128)} %get-tuple-element.20) | copy-start | bytes 1327108
  101.4 11.3 %copy-start.13 = (f32[1,96,1152]{2,1,0:T(8,128)S(1)}, f32[1,96,1152]{2,1,0:T(8,128)}, u32[]{:S(2)}) copy-start(f32[1,96,1152]{2,1,0:T(8,128)} %get-tuple-element.22) | copy-start | bytes 1327108
  101.5 17.0 %collective-permute-start.19 = (bf16[1,96,1152]{2,1,0:T(8,128)(2,1)S(1)}, bf16[1,96,1152]{2,1,0:T(8,128)(2,1)S(1)}, u32[]{:S(2)}, u32[]{:S(2)}) collective-permute-start(bf16[1,96,1152]{2,1,0:T(8,128)(2,1)S(1)} %get-tuple-element.29), channel_id=1, source_target_pairs={{0,8},{4,12},{8,0},{12,4},{16,24},{20,28},{24,16},{28,20},{1,9},{5... | collective-permute-start | bytes 663560 | tf_op jit(solution)/shard_map/ppermute | solution.py:324
  101.7 22.7 %collective-permute-start.18 = (f32[1,96,1152]{2,1,0:T(8,128)S(1)}, f32[1,96,1152]{2,1,0:T(8,128)S(1)}, u32[]{:S(2)}, u32[]{:S(2)}) collective-permute-start(f32[1,96,1152]{2,1,0:T(8,128)S(1)} %get-tuple-element.30), channel_id=1, source_target_pairs={{0,4},{4,0},{8,12},{12,8},{16,20},{20,16},{24,28},{28,24},{1,5},{5... | collective-permute-start | bytes 1327112 | tf_op jit(solution)/shard_map/ppermute | solution.py:324
  104.2 8.6 %copy-start.6 = (bf16[2,96,1152]{2,1,0:T(8,128)(2,1)}, bf16[2,96,1152]{2,1,0:T(8,128)(2,1)S(1)}, u32[]{:S(2)}) copy-start(bf16[2,96,1152]{2,1,0:T(8,128)(2,1)S(1)} %collective-permute-done.15.refs_6_) | copy-start | bytes 1327108
  104.3 10.5 %copy-start.10 = (f32[1,96,1152]{2,1,0:T(8,128)S(1)}, f32[1,96,1152]{2,1,0:T(8,128)}, u32[]{:S(2)}) copy-start(f32[1,96,1152]{2,1,0:T(8,128)} %get-tuple-element.19) | copy-start | bytes 1327108
  104.3 15.2 %collective-permute-start.16 = (bf16[1,96,1152]{2,1,0:T(8,128)(2,1)S(1)}, bf16[1,96,1152]{2,1,0:T(8,128)(2,1)S(1)}, u32[]{:S(2)}, u32[]{:S(2)}) collective-permute-start(bf16[1,96,1152]{2,1,0:T(8,128)(2,1)S(1)} %add_convert_fusion.1), channel_id=1, source_target_pairs={{0,16},{4,20},{8,24},{12,28},{16,0},{20,4},{24,8},{28,12},{1,17},{... | collective-permute-start | bytes 663560 | tf_op jit(solution)/shard_map/ppermute | solution.py:324
  112.7 9.6 %copy-start.22 = (pred[96]{0:T(512)(128)(4,1)S(1)}, pred[96]{0:T(512)(128)(4,1)}, u32[]{:S(2)}) copy-start(pred[96]{0:T(512)(128)(4,1)} %constant.119.clone) | copy-start | bytes 292
  112.7 9.6 %copy-start.23 = (pred[96]{0:T(512)(128)(4,1)S(1)}, pred[96]{0:T(512)(128)(4,1)}, u32[]{:S(2)}) copy-start(pred[96]{0:T(512)(128)(4,1)} %constant.120.clone) | copy-start | bytes 292
  112.7 9.6 %copy-start.24 = (f32[96]{0:T(128)S(1)}, f32[96]{0:T(128)}, u32[]{:S(2)}) copy-start(f32[96]{0:T(128)} %constant.127) | copy-start | bytes 1156
  112.7 9.6 %copy-start.25 = (pred[96]{0:T(512)(128)(4,1)S(1)}, pred[96]{0:T(512)(128)(4,1)}, u32[]{:S(2)}) copy-start(pred[96]{0:T(512)(128)(4,1)} %constant.128) | copy-start | bytes 292
  112.8 9.5 %collective-permute-start.13 = (bf16[1,96,1152]{2,1,0:T(8,128)(2,1)S(1)}, bf16[1,96,1152]{2,1,0:T(8,128)(2,1)S(1)}, u32[]{:S(2)}, u32[]{:S(2)}) collective-permute-start(bf16[1,96,1152]{2,1,0:T(8,128)(2,1)S(1)} %get-tuple-element.31), channel_id=1, source_target_pairs={{0,8},{4,12},{8,0},{12,4},{16,24},{20,28},{24,16},{28,20},{1,9},{5... | collective-permute-start | bytes 663560 | tf_op jit(solution)/shard_map/ppermute | solution.py:324
  114.8 9.7 %copy-start.7 = (bf16[2,96,1152]{2,1,0:T(8,128)(2,1)}, bf16[2,96,1152]{2,1,0:T(8,128)(2,1)S(1)}, u32[]{:S(2)}) copy-start(bf16[2,96,1152]{2,1,0:T(8,128)(2,1)S(1)} %collective-permute-done.9.refs_1_) | copy-start | bytes 1327108
  114.8 9.6 %collective-permute-start.12 = (f32[1,96,1152]{2,1,0:T(8,128)S(1)}, f32[1,96,1152]{2,1,0:T(8,128)S(1)}, u32[]{:S(2)}, u32[]{:S(2)}) collective-permute-start(f32[1,96,1152]{2,1,0:T(8,128)S(1)} %get-tuple-element.32), channel_id=1, source_target_pairs={{0,4},{4,0},{8,12},{12,8},{16,20},{20,16},{24,28},{28,24},{1,5},{5... | collective-permute-start | bytes 1327112 | tf_op jit(solution)/shard_map/ppermute | solution.py:324
  118.5 5.9 %collective-permute-start.10 = (bf16[1,96,1152]{2,1,0:T(8,128)(2,1)S(1)}, bf16[1,96,1152]{2,1,0:T(8,128)(2,1)S(1)}, u32[]{:S(2)}, u32[]{:S(2)}) collective-permute-start(bf16[1,96,1152]{2,1,0:T(8,128)(2,1)S(1)} %add_convert_fusion.3), channel_id=1, source_target_pairs={{0,16},{4,20},{8,24},{12,28},{16,0},{20,4},{24,8},{28,12},{1,17},{... | collective-permute-start | bytes 663560 | tf_op jit(solution)/shard_map/ppermute | solution.py:324
  119.5 5.0 %copy-start.16 = (bf16[1,96,1152]{2,1,0:T(8,128)(2,1)}, bf16[1,96,1152]{2,1,0:T(8,128)(2,1)S(1)}, u32[]{:S(2)}) copy-start(bf16[1,96,1152]{2,1,0:T(8,128)(2,1)S(1)} %collective-permute-done.16.refs_7_) | copy-start | bytes 663556
  119.5 4.9 %collective-permute-start.20 = (bf16[1,96,1152]{2,1,0:T(8,128)(2,1)S(1)}, bf16[1,96,1152]{2,1,0:T(8,128)(2,1)S(1)}, u32[]{:S(2)}, u32[]{:S(2)}) collective-permute-start(bf16[1,96,1152]{2,1,0:T(8,128)(2,1)S(1)} %collective-permute-done.19), channel_id=1, source_target_pairs={{0,4},{4,0},{8,12},{12,8},{16,20},{20,16},{24,28},{28,24},{1,5},{5... | collective-permute-start | bytes 663560 | tf_op jit(solution)/shard_map/ppermute | solution.py:324
  122.3 2.1 %collective-permute-start.14 = (bf16[1,96,1152]{2,1,0:T(8,128)(2,1)S(1)}, bf16[1,96,1152]{2,1,0:T(8,128)(2,1)S(1)}, u32[]{:S(2)}, u32[]{:S(2)}) collective-permute-start(bf16[1,96,1152]{2,1,0:T(8,128)(2,1)S(1)} %collective-permute-done.13), channel_id=1, source_target_pairs={{0,4},{4,0},{8,12},{12,8},{16,20},{20,16},{24,28},{28,24},{1,5},{5... | collective-permute-start | bytes 663560 | tf_op jit(solution)/shard_map/ppermute | solution.py:324
  124.4 0.7 copy-start.17
  124.4 0.8 copy-start.18
  124.4 0.9 copy-start.8
  124.4 1.0 copy-start.19
  124.4 1.1 copy-start.9

commit v7 on v6

--- a/solution.py
+++ b/solution.py
@@ -25,8 +25,8 @@
 def project_kernel(part, plan, place, position, *refs):
     groups = sum(len(members) for members, _ in plan)
     tokens = refs[:groups]
-    own_rows, other_rows = refs[groups : groups + 2]
-    outs = refs[groups + 2 : -4]
+    own_rows, other_rows, scaling = refs[groups : groups + 3]
+    outs = refs[groups + 3 : -4]
     weights, picked, sems, weight_sems = refs[-4:]
     core, begin = place[0], place[1]
     depth = own_rows.shape[0]
@@ -100,15 +100,19 @@
             outs[output][index] = result[count * rows : (count + 1) * rows].astype(
                 outs[output].dtype
             )
+    if part == 1:
+        outs[-1][...] = jnp.dot(
+            scaling[...], weights[...], preferred_element_type=jnp.float32
+        )[: outs[-1].shape[0]]
 
 
 def attend_kernel(shape, place, all_lengths, table, *refs):
-    terms, held_count, fresh_len, page, heads = shape
+    terms, held_count, fresh_len, page, heads, depth = shape
     sums = []
     for count in terms:
         sums.append(sum(ref[0].astype(jnp.float32) for ref in refs[:count]))
         refs = refs[count:]
-    bias, cosine, sine_up, sine_down, key_pool, value_pool, *outs = refs[:-3]
+    factors, folded, bias, cosine, sine_up, sine_down, key_pool, value_pool, *outs = refs[:-3]
     keys, values, sems = refs[-3:]
     chunk = CHUNK_PAGES * page
     pairs = heads // 2
@@ -148,10 +152,18 @@
     far = jnp.concatenate(sums[1::2], axis=0)
     core = place[0]
     halves = jnp.where(core == 0, near, far), jnp.where(core == 0, far, near)
-    halves = [
-        half + bias[:, side * half.shape[1] : (side + 1) * half.shape[1]]
-        for side, half in enumerate(halves)
-    ]
+    factors = factors[...].reshape(held_count * fresh_len, depth + 1)
+    devices = folded.shape[0]
+    per = devices // 2 // depth
+    finished = []
+    for side, half in enumerate(halves):
+        half = half * factors[:, 0:1] + bias[:, side * half.shape[1] : (side + 1) * half.shape[1]]
+        for device in range(side, devices, 2):
+            layer = device // 2 // per
+            lines = folded[device]
+            half = half + factors[:, layer + 1 : layer + 2] * lines[0:1] + lines[1:2]
+        finished.append(half)
+    halves = finished
 
     def kind(which):
         pieces = []
@@ -334,19 +346,8 @@
 
     widened = arrivals.reshape(rows, width).astype(jnp.float32)
     middle = jnp.mean(widened, axis=-1)
-    square = jnp.sum(jnp.square(widened - middle[:, None]), axis=-1)
-    local = jnp.stack([middle, square])
-    stats = jnp.broadcast_to(local[None], (wgt_size, 2, rows))
-    stats = lax.all_to_all(stats, "wgt", 0, 0, tiled=True)
-    center = jnp.mean(stats[:, 0], axis=0)
-    square = jnp.sum(stats[:, 1] + width * jnp.square(stats[:, 0] - center[None]), axis=0)
-    scale = lax.rsqrt(square / (width * wgt_size) + EPS)
-    gain, shift = (
-        lax.dynamic_slice_in_dim(value, layer * width, width).astype(jnp.float32)
-        for value in (ln_gain, ln_bias)
-    )
-    tokens = (widened - center[:, None]) * scale[:, None] * gain + shift
-    tokens = tokens.astype(jnp.bfloat16)
+    gain = lax.dynamic_slice_in_dim(ln_gain, layer * width, width).astype(jnp.float32)
+    tokens = ((widened - middle[:, None]) * gain).astype(jnp.bfloat16)
     if per > 1:
         tokens = tokens.reshape(rows, per, block)
 
@@ -366,6 +367,16 @@
 
     received = [route(turn) for turn in range(chips)]
 
+    square = jnp.sum(jnp.square(widened - middle[:, None]), axis=-1)
+    stats = jnp.broadcast_to(jnp.stack([middle, square])[None], (wgt_size, 2, rows))
+    stats = lax.all_to_all(stats, "wgt", 0, 0, tiled=True)
+    center = jnp.mean(stats[:, 0], axis=0)
+    apart = stats[:, 0] - center[None]
+    square = jnp.sum(stats[:, 1] + width * jnp.square(apart), axis=0)
+    scale = lax.rsqrt(square / (width * wgt_size) + EPS)
+    factors = jnp.concatenate([scale[None], apart * scale[None]], axis=0)
+    factors = jnp.broadcast_to(factors[None], (req_size, wgt_size + 1, rows))
+
     square_plane = chips == 4
     if square_plane:
         plan = [([2, 6], jnp.bfloat16), ([5, 7], jnp.bfloat16)]
@@ -387,6 +398,14 @@
     row = (((origin & 1) ^ core) * chips + (origin >> 1)) * req_count + ids % req_count
     position = jnp.sum(jnp.where(row[None, :] == ids[:, None], spot[None, :], 0), axis=1)
 
+    served = me * req_count + jnp.arange(req_count, dtype=jnp.int32)
+    slot_of = group_of * req_count + rank
+    served = jnp.sum(jnp.where(slot_of[None, :] == served[:, None], ids[None, :], 0), axis=1)
+    scaling = jnp.zeros((16, block), jnp.bfloat16)
+    for line, value in enumerate((ln_gain, ln_bias)):
+        value = lax.dynamic_slice_in_dim(value, chip * block, block)
+        scaling = scaling.at[line].set(value)
+
     lane = np.arange(HEAD)
     half_rot = ROT // 2
     inverse = jnp.power(10000.0, -jnp.asarray(lane % half_rot, jnp.float32) * 2.0 / ROT)
@@ -409,7 +428,7 @@
     span = page_table.shape[1]
     pages = span + (req_count - 1) * (span // 2)
 
-    held = after(w_qkv, local)
+    held = w_qkv
     if half_cols % LANES == 0:
         own_rows = w_qkv
     else:
@@ -438,9 +457,10 @@
                 out_shape=[
                     jax.ShapeDtypeStruct((len(members), chunk_rows, half_cols), kind)
                     for members, kind in plan
-                ],
-                in_specs=[SMEM] * 2 + [HBM] * (req_size + 2),
-                out_specs=[VMEM] * len(plan),
+                ]
+                + [jax.ShapeDtypeStruct((8, half_cols), jnp.float32)] * part,
+                in_specs=[SMEM] * 2 + [HBM] * (req_size + 2) + [VMEM],
+                out_specs=[VMEM] * (len(plan) + part),
                 scratch_shapes=[
                     pltpu.VMEM((block, half_cols), jnp.bfloat16),
                     pltpu.VMEM((req_size * half, fresh_len, block), jnp.bfloat16),
@@ -449,20 +469,28 @@
                 ],
                 compiler_params=pltpu.CompilerParams(vmem_limit_bytes=VMEM_LIMIT),
                 name="project",
-            )(place, position, *received, own_rows, other_rows)
-        )
+            )(place, position, *received, own_rows, other_rows, scaling)
+        )
+
+    factors = lax.all_to_all(after(factors, projected[0][0]), "req", 0, 0, tiled=True)
+    factors = factors.reshape(req_size, wgt_size + 1, req_count, fresh_len)
+    factors = factors.transpose(0, 2, 3, 1).reshape(everyone, fresh_len, wgt_size + 1)
+    factors = jnp.take(factors, served, axis=0)
+
+    folded = jnp.broadcast_to(projected[1][-1][None], (req_size, 8, half_cols))
+    folded = lax.all_to_all(folded, "req", 0, 0, tiled=True)
 
     terms, sums = [], []
     for blocks in projected:
-        for side in collect(blocks):
+        for side in collect(blocks[: len(plan)]):
             terms.append(len(side))
             sums += side
     out = jax.ShapeDtypeStruct((req_count, fresh_len, heads * HEAD), jnp.bfloat16)
     return tuple(
         pl.pallas_call(
-            functools.partial(attend_kernel, (terms, req_count, fresh_len, page, heads)),
+            functools.partial(attend_kernel, (terms, req_count, fresh_len, page, heads, wgt_size)),
             out_shape=[out] * 3,
-            in_specs=[SMEM] * 3 + [VMEM] * (len(sums) + 4) + [HBM] * 2,
+            in_specs=[SMEM] * 3 + [VMEM] * (len(sums) + 6) + [HBM] * 2,
             out_specs=[VMEM] * 3,
             scratch_shapes=[
                 pltpu.VMEM((pages, page, heads * HEAD), jnp.bfloat16),
@@ -471,7 +499,7 @@
             ],
             compiler_params=pltpu.CompilerParams(vmem_limit_bytes=VMEM_LIMIT),
             name="attend",
-        )(place, lengths, page_table, *sums, bias, *tables, key_pool, value_pool)
+        )(place, lengths, page_table, *sums, factors, folded, bias, *tables, key_pool, value_pool)
     )
 
 

time: 140 us -> 151 us (1.079); the launches traced: 140 us -> 149 us
  other arithmetic: 6.79 us -> 18.4 us
  waiting for transfers between devices: 51.8 us -> 43.6 us
  local copies, waits for them, and re-layouts: 7.38 us -> 15.4 us
  starting transfers between devices: 41.9 us -> 38.1 us
    ppermute x4, waiting for transfers between devices: 31.7 us -> 7.29 us  [route(): return lax.ppermute(value, ('req', 'wgt'), pairs)]
    all_to_all x1, waiting for transfers between devices: 1.87 us -> 20 us  [per_device(): stats = lax.all_to_all(stats, 'wgt', 0, 0, tiled=True)]
    ppermute x17, starting transfers between devices: 28.1 us -> 14.4 us  [swap(): lax.ppermute(value, 'req', [(device, device ^ distance) for device in ran...]
    all_to_all x0 -> x2, starting transfers between devices: none -> 8.63 us  [the longest x1 5.2 us: per_device(): lax.all_to_all(after(factors, projected[0][0]), 'req', 0, 0, tiled=True)]
    ppermute x4, starting transfers between devices: 7.5 us -> 11.3 us  [route(): return lax.ppermute(value, ('req', 'wgt'), pairs)]
    all_to_all x1, starting transfers between devices: 6.32 us -> 3.74 us  [per_device(): stats = lax.all_to_all(stats, 'wgt', 0, 0, tiled=True)]
    ppermute x17, waiting for transfers between devices: 18.3 us -> 16.1 us  [swap(): lax.ppermute(value, 'req', [(device, device ^ distance) for device in ran...]
    scatter x0 -> x2, local copies, waits for them, and re-layouts: none -> 2 us  [per_device(): scaling = scaling.at[line].set(value)]
  transfers between devices with their start and end apart: 22 -> 24, of which waited for: 10 -> 7; matrix products, arithmetic and copies ran while one was open for 6% -> 18% of each run, Pallas kernels for 6% -> 6%
where the time goes in v7:
time: 151 us; the launch traced here: 149 us
  waiting for transfers between devices  43.6 us (29%)
  starting transfers between devices  38.1 us (25%)
  Pallas kernels  32.1 us (21%)
  other arithmetic  18.4 us (12%)
  local copies, waits for them, and re-layouts  15.4 us (10%)
    all_to_all x1, waiting for transfers between devices, per_device(): stats = lax.all_to_all(stats, 'wgt', 0, 0, tiled=True)  20 us
    pallas_call x2, Pallas kernels, per_device(): pl.pallas_call(functools.partial(project_kernel, part, plan), out_shape=[...  16.7 us
    ppermute x17, waiting for transfers between devices, swap(): lax.ppermute(value, 'req', [(device, device ^ distance) for device in ran...  16.1 us
    pallas_call x1, Pallas kernels, per_device(): pl.pallas_call(functools.partial(attend_kernel, (terms, req_count, fresh_...  15.4 us
    ppermute x17, starting transfers between devices, swap(): lax.ppermute(value, 'req', [(device, device ^ distance) for device in ran...  14.4 us
    ppermute x4, starting transfers between devices, route(): return lax.ppermute(value, ('req', 'wgt'), pairs)  11.3 us
    ppermute x4, waiting for transfers between devices, route(): return lax.ppermute(value, ('req', 'wgt'), pairs)  7.29 us
    all_to_all x1, starting transfers between devices, per_device(): lax.all_to_all(after(factors, projected[0][0]), 'req', 0, 0, tiled=True)  5.2 us
  transfers between devices with their start and end apart: 24, of which 7 were waited for; matrix products, arithmetic and copies ran while one was open for 18% of the time, Pallas kernels for 6%

profile of v7, /device:TPU:0, one launch (start us, length us, event | category | flops | bytes accessed | tf_op | source)
XLA Modules:
  0.0 148.8 jit_solution(14359056126126551631)
XLA Ops:
  0.6 1.2 convert_reduce_fusion
  2.0 0.8 fusion.13
  2.8 2.1 %fusion.1 = bf16[192,1536]{1,0:T(8,128)(2,1)} fusion(bf16[4,48,1536]{2,1,0:T(8,128)(2,1)} %param.19, f32[1536]{0:T(1024)S(1)} %get-tuple-element.60, f32[192]{0:T(256)S(1)} %div.53), kind=kLoop, calls=%fused_computation.4 | loop fusion | flops 1179648 | bytes 1186560 | tf_op jit(solution)/shard_map/convert_element_type | solution.py:350
  4.9 5.0 %collective-permute-start.3 = (bf16[192,1536]{1,0:T(8,128)(2,1)}, bf16[192,1536]{1,0:T(8,128)(2,1)S(1)}, u32[]{:S(2)}, u32[]{:S(2)}) collective-permute-start(bf16[192,1536]{1,0:T(8,128)(2,1)} %fusion.1), channel_id=1, source_target_pairs={{24,0},{16,1},{8,2},{0,3},{28,4},{20,5},{12,6},{4,7},{25,8},{17,9}... | collective-permute-start | bytes 1769480 | tf_op jit(solution)/shard_map/ppermute | solution.py:366
  9.9 1.7 %collective-permute-start = (bf16[192,1536]{1,0:T(8,128)(2,1)}, bf16[192,1536]{1,0:T(8,128)(2,1)S(1)}, u32[]{:S(2)}, u32[]{:S(2)}) collective-permute-start(bf16[192,1536]{1,0:T(8,128)(2,1)} %fusion.1), channel_id=1, source_target_pairs={{0,0},{8,1},{16,2},{24,3},{4,4},{12,5},{20,6},{28,7},{1,8},{9,9},{... | collective-permute-start | bytes 1769480 | tf_op jit(solution)/shard_map/ppermute | solution.py:366
  11.6 2.2 %collective-permute-start.1 = (bf16[192,1536]{1,0:T(8,128)(2,1)}, bf16[192,1536]{1,0:T(8,128)(2,1)S(1)}, u32[]{:S(2)}, u32[]{:S(2)}) collective-permute-start(bf16[192,1536]{1,0:T(8,128)(2,1)} %fusion.1), channel_id=1, source_target_pairs={{8,0},{0,1},{24,2},{16,3},{12,4},{4,5},{28,6},{20,7},{9,8},{1,9},{... | collective-permute-start | bytes 1769480 | tf_op jit(solution)/shard_map/ppermute | solution.py:366
  13.7 2.5 %collective-permute-start.2 = (bf16[192,1536]{1,0:T(8,128)(2,1)}, bf16[192,1536]{1,0:T(8,128)(2,1)}, u32[]{:S(2)}, u32[]{:S(2)}) collective-permute-start(bf16[192,1536]{1,0:T(8,128)(2,1)} %fusion.1), channel_id=1, source_target_pairs={{16,0},{24,1},{0,2},{8,3},{20,4},{28,5},{4,6},{12,7},{17,8},{25,9}... | collective-permute-start | bytes 1769480 | tf_op jit(solution)/shard_map/ppermute | solution.py:366
  16.2 2.9 %constant_dynamic-slice_fusion = bf16[768,1152]{1,0:T(8,128)(2,1)} fusion(bf16[768,2304]{1,0:T(8,128)(2,1)} %refs_8_.3, s32[]{:T(128)S(6)} %select_n.105), kind=kLoop, calls=%fused_computation.60 | loop fusion | bytes 3538948 | tf_op jit(solution)/shard_map/dynamic_slice | solution.py:436
  19.1 0.3 multiply_reduce_fusion
  19.5 0.6 div.54
  20.1 0.6 stack.19
  20.7 0.7 pad_maximum_fusion.1
  21.4 0.6 broadcast_in_dim.110
  22.0 3.7 %all-to-all-start = ((f32[4,2,192]{2,1,0:T(2,128)}), f32[4,2,192]{2,1,0:T(2,128)S(1)}, u32[]{:S(2)}, u32[]{:S(2)}) async-start(f32[4,2,192]{2,1,0:T(2,128)} %broadcast_in_dim.110), calls=%async_computation | async-start | bytes 16384 | tf_op jit(solution)/shard_map/all_to_all | solution.py:372
  25.8 0.9 convert_reduce_fusion.1
  26.7 0.5 copy-done.23
  27.2 1.2 multiply_add_fusion
  28.5 0.8 select_reduce_fusion.1
  29.3 0.5 fusion.12
  29.8 0.5 compare_and_fusion
  30.3 1.3 pad_clamp_fusion.1
  31.6 1.4 gather_fusion
  33.0 0.7 fusion.10
  33.7 0.6 select_reduce_fusion.position
  34.3 0.7 add_convert_fusion.4
  35.0 1.9 %fusion.2 = (f32[4,48,96]{2,1,0:T(8,128)}, f32[4,48,96]{2,1,0:T(8,128)}, f32[4,48,96]{2,1,0:T(8,128)}) fusion(f32[96]{0:T(128)} %constant.199, f32[4,48]{1,0:T(4,128)S(1)} %add_convert_fusion.4, pred[96]{0:T(512)(128)(4,1)} %constant.200, pred[96]{0:T(512)(128)(4,1)} %constant.190.clone, pred[96]{0:T(512)(128)(4,1)} %constant.189.clone), kind=kLoop, calls=%fused_computation.15 | loop fusion | flops 92160 | bytes 222624 | tf_op jit(solution)/shard_map/jit(_where)/select_n | solution.py:420
  36.9 0.6 pad_add_fusion.place
  37.4 0.8 dynamic_slice.15
  38.2 0.6 scatter.6
  38.8 1.4 scatter.9.refs_10_
  40.2 0.2 collective-permute-start.7
  40.5 0.3 collective-permute-start.4
  40.7 0.2 collective-permute-start.5
  41.0 7.3 %collective-permute-done.2 = bf16[192,1536]{1,0:T(8,128)(2,1)} collective-permute-done((bf16[192,1536]{1,0:T(8,128)(2,1)}, bf16[192,1536]{1,0:T(8,128)(2,1)}, u32[]{:S(2)}, u32[]{:S(2)}) %collective-permute-start.2) | collective-permute-done | bytes 589856 | tf_op jit(solution)/shard_map/ppermute | solution.py:366
  48.3 20.0 %all-to-all-done = f32[4,2,192]{2,1,0:T(2,128)S(1)} async-done(((f32[4,2,192]{2,1,0:T(2,128)}), f32[4,2,192]{2,1,0:T(2,128)S(1)}, u32[]{:S(2)}, u32[]{:S(2)}) %all-to-all-start) | async-done | bytes 6176 | tf_op jit(solution)/shard_map/all_to_all | solution.py:372
  68.4 1.2 copy-done.1
  69.6 8.3 %project.3 = (bf16[2,96,1152]{2,1,0:T(8,128)(2,1)}, bf16[2,96,1152]{2,1,0:T(8,128)(2,1)}, f32[1,96,1152]{2,1,0:T(8,128)}, f32[1,96,1152]{2,1,0:T(8,128)}, f32[1,...) custom-call(s32[2]{0:T(128)} %pad_add_fusion.place, s32[32]{0:T(128)} %select_reduce_fusion.position, ...), custom_call_target="tpu_custom_call" | custom-call | tf_op jit(solution)/shard_map/project/pallas_call | solution.py:455
  77.9 1.9 %collective-permute-start.17 = (bf16[2,96,1152]{2,1,0:T(8,128)(2,1)}, bf16[2,96,1152]{2,1,0:T(8,128)(2,1)S(1)}, u32[]{:S(2)}, u32[]{:S(2)}) collective-permute-start(bf16[2,96,1152]{2,1,0:T(8,128)(2,1)} %get-tuple-element.51), channel_id=1, source_target_pairs={{0,16},{4,20},{8,24},{12,28},{16,0},{20,4},{24,8},{28,12},{1,17},{... | collective-permute-start | bytes 1327112 | tf_op jit(solution)/shard_map/ppermute | solution.py:336
  79.9 8.4 %project.2 = (bf16[2,96,1152]{2,1,0:T(8,128)(2,1)}, bf16[2,96,1152]{2,1,0:T(8,128)(2,1)}, f32[1,96,1152]{2,1,0:T(8,128)}, f32[1,96,1152]{2,1,0:T(8,128)}, f32[1,...) custom-call(s32[2]{0:T(128)} %pad_add_fusion.place, s32[32]{0:T(128)} %select_reduce_fusion.position, ...), custom_call_target="tpu_custom_call" | custom-call | tf_op jit(solution)/shard_map/project/pallas_call | solution.py:455
  88.3 0.7 reshape.335
  89.0 5.2 %all-to-all-start.1 = ((f32[8,1,960]{2,1,0:T(1,128)}), f32[8,1,960]{2,1,0:T(1,128)S(1)}, u32[]{:S(2)}, u32[]{:S(2)}) async-start(f32[8,1,960]{2,1,0:T(1,128)} %reshape.335), calls=%async_computation.1 | async-start | bytes 65536 | tf_op jit(solution)/shard_map/all_to_all | solution.py:475
  94.3 0.6 reshape.317.refs_12_
  94.9 2.0 %collective-permute-start.9 = (bf16[2,96,1152]{2,1,0:T(8,128)(2,1)}, bf16[2,96,1152]{2,1,0:T(8,128)(2,1)S(1)}, u32[]{:S(2)}, u32[]{:S(2)}) collective-permute-start(bf16[2,96,1152]{2,1,0:T(8,128)(2,1)} %get-tuple-element.42), channel_id=1, source_target_pairs={{0,8},{4,12},{8,0},{12,4},{16,24},{20,28},{24,16},{28,20},{1,9},{5... | collective-permute-start | bytes 1327112 | tf_op jit(solution)/shard_map/ppermute | solution.py:336
  96.9 2.0 %collective-permute-start.11 = (bf16[2,96,1152]{2,1,0:T(8,128)(2,1)}, bf16[2,96,1152]{2,1,0:T(8,128)(2,1)}, u32[]{:S(2)}, u32[]{:S(2)}) collective-permute-start(bf16[2,96,1152]{2,1,0:T(8,128)(2,1)} %get-tuple-element.45), channel_id=1, source_target_pairs={{0,16},{4,20},{8,24},{12,28},{16,0},{20,4},{24,8},{28,12},{1,17},{... | collective-permute-start | bytes 1327112 | tf_op jit(solution)/shard_map/ppermute | solution.py:336
  98.9 0.2 all-to-all-done.1
  99.1 0.7 broadcast_in_dim.113
  99.8 3.4 %all-to-all-start.2 = ((f32[8,8,1152]{2,1,0:T(8,128)}), f32[8,8,1152]{2,1,0:T(8,128)S(1)}, u32[]{:S(2)}, u32[]{:S(2)}) async-start(f32[8,8,1152]{2,1,0:T(8,128)} %broadcast_in_dim.113), calls=%async_computation.2 | async-start | bytes 589824 | tf_op jit(solution)/shard_map/all_to_all | solution.py:481
  103.2 0.5 broadcast.310
  103.8 0.7 reduce.7
  104.8 0.6 gather_fusion.1
  105.5 0.8 add_convert_fusion
  106.3 1.9 %collective-permute-start.19 = (bf16[1,96,1152]{2,1,0:T(8,128)(2,1)S(1)}, bf16[1,96,1152]{2,1,0:T(8,128)(2,1)S(1)}, u32[]{:S(2)}, u32[]{:S(2)}) collective-permute-start(bf16[1,96,1152]{2,1,0:T(8,128)(2,1)S(1)} %get-tuple-element.55), channel_id=1, source_target_pairs={{0,8},{4,12},{8,0},{12,4},{16,24},{20,28},{24,16},{28,20},{1,9},{5... | collective-permute-start | bytes 663560 | tf_op jit(solution)/shard_map/ppermute | solution.py:336
  108.2 9.3 %collective-permute-done.15.refs_6_ = bf16[2,96,1152]{2,1,0:T(8,128)(2,1)S(1)} collective-permute-done((bf16[2,96,1152]{2,1,0:T(8,128)(2,1)}, bf16[2,96,1152]{2,1,0:T(8,128)(2,1)S(1)}, u32[]{:S(2)}, u32[]{:S(2)}) %collective-permute-start.15) | collective-permute-done | bytes 442400 | tf_op jit(solution)/shard_map/ppermute | solution.py:336
  117.6 2.1 %collective-permute-start.16 = (bf16[1,96,1152]{2,1,0:T(8,128)(2,1)S(1)}, bf16[1,96,1152]{2,1,0:T(8,128)(2,1)S(1)}, u32[]{:S(2)}, u32[]{:S(2)}) collective-permute-start(bf16[1,96,1152]{2,1,0:T(8,128)(2,1)S(1)} %add_convert_fusion.1), channel_id=1, source_target_pairs={{0,16},{4,20},{8,24},{12,28},{16,0},{20,4},{24,8},{28,12},{1,17},{... | collective-permute-start | bytes 663560 | tf_op jit(solution)/shard_map/ppermute | solution.py:336
  119.7 1.1 add_convert_fusion.2
  120.9 1.5 %collective-permute-start.13 = (bf16[1,96,1152]{2,1,0:T(8,128)(2,1)S(1)}, bf16[1,96,1152]{2,1,0:T(8,128)(2,1)}, u32[]{:S(2)}, u32[]{:S(2)}) collective-permute-start(bf16[1,96,1152]{2,1,0:T(8,128)(2,1)S(1)} %get-tuple-element.57), channel_id=1, source_target_pairs={{0,8},{4,12},{8,0},{12,4},{16,24},{20,28},{24,16},{28,20},{1,9},{5... | collective-permute-start | bytes 663560 | tf_op jit(solution)/shard_map/ppermute | solution.py:336
  122.5 3.0 %collective-permute-done.19 = bf16[1,96,1152]{2,1,0:T(8,128)(2,1)S(1)} collective-permute-done((bf16[1,96,1152]{2,1,0:T(8,128)(2,1)S(1)}, bf16[1,96,1152]{2,1,0:T(8,128)(2,1)S(1)}, u32[]{:S(2)}, u32[]{:S(2)}) %collective-permute-start.19) | collective-permute-done | bytes 221216 | tf_op jit(solution)/shard_map/ppermute | solution.py:336
  125.4 2.1 %collective-permute-start.10 = (bf16[1,96,1152]{2,1,0:T(8,128)(2,1)S(1)}, bf16[1,96,1152]{2,1,0:T(8,128)(2,1)S(1)}, u32[]{:S(2)}, u32[]{:S(2)}) collective-permute-start(bf16[1,96,1152]{2,1,0:T(8,128)(2,1)S(1)} %add_convert_fusion.3), channel_id=1, source_target_pairs={{0,16},{4,20},{8,24},{12,28},{16,0},{20,4},{24,8},{28,12},{1,17},{... | collective-permute-start | bytes 663560 | tf_op jit(solution)/shard_map/ppermute | solution.py:336
  127.5 2.4 %collective-permute-done.13 = bf16[1,96,1152]{2,1,0:T(8,128)(2,1)} collective-permute-done((bf16[1,96,1152]{2,1,0:T(8,128)(2,1)S(1)}, bf16[1,96,1152]{2,1,0:T(8,128)(2,1)}, u32[]{:S(2)}, u32[]{:S(2)}) %collective-permute-start.13) | collective-permute-done | bytes 221216 | tf_op jit(solution)/shard_map/ppermute | solution.py:336
  129.9 0.7 broadcast_select_fusion.refs_10_
  130.6 1.5 collective-permute-done.10.refs_2_
  132.2 0.6 copy-done.18
  132.9 0.1 copy-done.9
  133.2 15.4 %attend.1 = (bf16[4,48,768]{2,1,0:T(8,128)(2,1)}, bf16[4,48,768]{2,1,0:T(8,128)(2,1)}, bf16[4,48,768]{2,1,0:T(8,128)(2,1)}) custom-call(s32[2]{0:T(128)} %pad_add_fusion.place, s32[4]{0:T(128)} %all_lengths.1, s32[4,16]{1,0:T(4,128)} %table.1, f32[1,96,1152]{2,1,0:T(8,128)} %get-tuple-element.41.refs_0_, bf16[2,96,1152]{2,1,0:T(8,128)(2,1)} %copy-done.7, ...), custom_call_target="tpu_custom_call" | custom-call | tf_op jit(solution)/shard_map/attend/pallas_call | solution.py:490
  (92 shorter events, 1.1 us)
Async XLA Ops:
  4.9 35.3 %collective-permute-start.3 = (bf16[192,1536]{1,0:T(8,128)(2,1)}, bf16[192,1536]{1,0:T(8,128)(2,1)S(1)}, u32[]{:S(2)}, u32[]{:S(2)}) collective-permute-start(bf16[192,1536]{1,0:T(8,128)(2,1)} %fusion.1), channel_id=1, source_target_pairs={{24,0},{16,1},{8,2},{0,3},{28,4},{20,5},{12,6},{4,7},{25,8},{17,9}... | collective-permute-start | bytes 1769480 | tf_op jit(solution)/shard_map/ppermute | solution.py:366
  9.9 30.6 %collective-permute-start = (bf16[192,1536]{1,0:T(8,128)(2,1)}, bf16[192,1536]{1,0:T(8,128)(2,1)S(1)}, u32[]{:S(2)}, u32[]{:S(2)}) collective-permute-start(bf16[192,1536]{1,0:T(8,128)(2,1)} %fusion.1), channel_id=1, source_target_pairs={{0,0},{8,1},{16,2},{24,3},{4,4},{12,5},{20,6},{28,7},{1,8},{9,9},{... | collective-permute-start | bytes 1769480 | tf_op jit(solution)/shard_map/ppermute | solution.py:366
  11.6 29.2 %collective-permute-start.1 = (bf16[192,1536]{1,0:T(8,128)(2,1)}, bf16[192,1536]{1,0:T(8,128)(2,1)S(1)}, u32[]{:S(2)}, u32[]{:S(2)}) collective-permute-start(bf16[192,1536]{1,0:T(8,128)(2,1)} %fusion.1), channel_id=1, source_target_pairs={{8,0},{0,1},{24,2},{16,3},{12,4},{4,5},{28,6},{20,7},{9,8},{1,9},{... | collective-permute-start | bytes 1769480 | tf_op jit(solution)/shard_map/ppermute | solution.py:366
  13.7 34.5 %collective-permute-start.2 = (bf16[192,1536]{1,0:T(8,128)(2,1)}, bf16[192,1536]{1,0:T(8,128)(2,1)}, u32[]{:S(2)}, u32[]{:S(2)}) collective-permute-start(bf16[192,1536]{1,0:T(8,128)(2,1)} %fusion.1), channel_id=1, source_target_pairs={{16,0},{24,1},{0,2},{8,3},{20,4},{28,5},{4,6},{12,7},{17,8},{25,9}... | collective-permute-start | bytes 1769480 | tf_op jit(solution)/shard_map/ppermute | solution.py:366
  16.2 2.9 %copy-start.2 = (bf16[4,48,1536]{2,1,0:T(8,128)(2,1)S(1)}, bf16[4,48,1536]{2,1,0:T(8,128)(2,1)}, u32[]{:S(2)}) copy-start(bf16[4,48,1536]{2,1,0:T(8,128)(2,1)} %param.19) | copy-start | bytes 1769476
  16.2 15.4 %copy-start = (s32[8]{0:T(128)S(1)}, s32[8]{0:T(128)}, u32[]{:S(2)}) copy-start(s32[8]{0:T(128)} %constant.187.clone) | copy-start | bytes 100
  19.1 49.2 %collective-permute-start.8 = (bf16[768,1152]{1,0:T(8,128)(2,1)}, bf16[768,1152]{1,0:T(8,128)(2,1)S(1)}, u32[]{:S(2)}, u32[]{:S(2)}) collective-permute-start(bf16[768,1152]{1,0:T(8,128)(2,1)} %constant_dynamic-slice_fusion), channel_id=1, source_target_pairs={{0,4},{4,0},{8,12},{12,8},{16,20},{20,16},{24,28},{28,24},{1,5},{5... | collective-permute-start | bytes 5308424 | tf_op jit(solution)/shard_map/ppermute | solution.py:336
  22.0 46.2 %all-to-all-start = ((f32[4,2,192]{2,1,0:T(2,128)}), f32[4,2,192]{2,1,0:T(2,128)S(1)}, u32[]{:S(2)}, u32[]{:S(2)}) async-start(f32[4,2,192]{2,1,0:T(2,128)} %broadcast_in_dim.110), calls=%async_computation | async-start | bytes 16384 | tf_op jit(solution)/shard_map/all_to_all | solution.py:372
  26.7 0.5 copy-start.23
  40.2 28.2 %copy-start.3 = (bf16[192,1536]{1,0:T(8,128)(2,1)}, bf16[192,1536]{1,0:T(8,128)(2,1)S(1)}, u32[]{:S(2)}) copy-start(bf16[192,1536]{1,0:T(8,128)(2,1)S(1)} %collective-permute-done.3) | copy-start | bytes 1769476
  40.2 28.1 %collective-permute-start.7 = (bf16[192,1536]{1,0:T(8,128)(2,1)S(1)}, bf16[192,1536]{1,0:T(8,128)(2,1)}, u32[]{:S(2)}, u32[]{:S(2)}) collective-permute-start(bf16[192,1536]{1,0:T(8,128)(2,1)S(1)} %collective-permute-done.3), channel_id=1, source_target_pairs={{0,4},{4,0},{8,12},{12,8},{16,20},{20,16},{24,28},{28,24},{1,5},{5... | collective-permute-start | bytes 1769480 | tf_op jit(solution)/shard_map/ppermute | solution.py:336
  40.5 27.9 %copy-start.4 = (bf16[192,1536]{1,0:T(8,128)(2,1)}, bf16[192,1536]{1,0:T(8,128)(2,1)S(1)}, u32[]{:S(2)}) copy-start(bf16[192,1536]{1,0:T(8,128)(2,1)S(1)} %collective-permute-done) | copy-start | bytes 1769476
  40.5 27.9 %collective-permute-start.4 = (bf16[192,1536]{1,0:T(8,128)(2,1)S(1)}, bf16[192,1536]{1,0:T(8,128)(2,1)}, u32[]{:S(2)}, u32[]{:S(2)}) collective-permute-start(bf16[192,1536]{1,0:T(8,128)(2,1)S(1)} %collective-permute-done), channel_id=1, source_target_pairs={{0,4},{4,0},{8,12},{12,8},{16,20},{20,16},{24,28},{28,24},{1,5},{5... | collective-permute-start | bytes 1769480 | tf_op jit(solution)/shard_map/ppermute | solution.py:336
  40.7 27.6 %copy-start.5 = (bf16[192,1536]{1,0:T(8,128)(2,1)}, bf16[192,1536]{1,0:T(8,128)(2,1)S(1)}, u32[]{:S(2)}) copy-start(bf16[192,1536]{1,0:T(8,128)(2,1)S(1)} %collective-permute-done.1) | copy-start | bytes 1769476
  40.7 27.6 %collective-permute-start.5 = (bf16[192,1536]{1,0:T(8,128)(2,1)S(1)}, bf16[192,1536]{1,0:T(8,128)(2,1)}, u32[]{:S(2)}, u32[]{:S(2)}) collective-permute-start(bf16[192,1536]{1,0:T(8,128)(2,1)S(1)} %collective-permute-done.1), channel_id=1, source_target_pairs={{0,4},{4,0},{8,12},{12,8},{16,20},{20,16},{24,28},{28,24},{1,5},{5... | collective-permute-start | bytes 1769480 | tf_op jit(solution)/shard_map/ppermute | solution.py:336
  48.3 20.1 %collective-permute-start.6 = (bf16[192,1536]{1,0:T(8,128)(2,1)}, bf16[192,1536]{1,0:T(8,128)(2,1)}, u32[]{:S(2)}, u32[]{:S(2)}) collective-permute-start(bf16[192,1536]{1,0:T(8,128)(2,1)} %collective-permute-done.2), channel_id=1, source_target_pairs={{0,4},{4,0},{8,12},{12,8},{16,20},{20,16},{24,28},{28,24},{1,5},{5... | collective-permute-start | bytes 1769480 | tf_op jit(solution)/shard_map/ppermute | solution.py:336
  68.4 1.2 copy-start.1
  77.9 27.5 %collective-permute-start.17 = (bf16[2,96,1152]{2,1,0:T(8,128)(2,1)}, bf16[2,96,1152]{2,1,0:T(8,128)(2,1)S(1)}, u32[]{:S(2)}, u32[]{:S(2)}) collective-permute-start(bf16[2,96,1152]{2,1,0:T(8,128)(2,1)} %get-tuple-element.51), channel_id=1, source_target_pairs={{0,16},{4,20},{8,24},{12,28},{16,0},{20,4},{24,8},{28,12},{1,17},{... | collective-permute-start | bytes 1327112 | tf_op jit(solution)/shard_map/ppermute | solution.py:336
  79.9 14.3 %copy-start.25 = (s32[4]{0:T(128)S(1)}, s32[4]{0:T(128)}, u32[]{:S(2)}) copy-start(s32[4]{0:T(128)} %fusion.12) | copy-start | bytes 52
  79.9 14.4 %copy-start.22 = (bf16[2304]{0:T(1024)(128)(2,1)S(1)}, bf16[2304]{0:T(1024)(128)(2,1)}, u32[]{:S(2)}) copy-start(bf16[2304]{0:T(1024)(128)(2,1)} %param.26) | copy-start | bytes 13828
  79.9 19.2 %copy-start.21 = (f32[8,1152]{1,0:T(8,128)S(1)}, f32[8,1152]{1,0:T(8,128)}, u32[]{:S(2)}) copy-start(f32[8,1152]{1,0:T(8,128)} %get-tuple-element.54) | copy-start | bytes 110596
  88.3 17.2 %copy-start.15 = (f32[1,96,1152]{2,1,0:T(8,128)S(1)}, f32[1,96,1152]{2,1,0:T(8,128)}, u32[]{:S(2)}) copy-start(f32[1,96,1152]{2,1,0:T(8,128)} %get-tuple-element.50) | copy-start | bytes 1327108
  88.3 17.2 %copy-start.16 = (f32[1,96,1152]{2,1,0:T(8,128)S(1)}, f32[1,96,1152]{2,1,0:T(8,128)}, u32[]{:S(2)}) copy-start(f32[1,96,1152]{2,1,0:T(8,128)} %get-tuple-element.52) | copy-start | bytes 1327108
  89.0 10.0 %all-to-all-start.1 = ((f32[8,1,960]{2,1,0:T(1,128)}), f32[8,1,960]{2,1,0:T(1,128)S(1)}, u32[]{:S(2)}, u32[]{:S(2)}) async-start(f32[8,1,960]{2,1,0:T(1,128)} %reshape.335), calls=%async_computation.1 | async-start | bytes 65536 | tf_op jit(solution)/shard_map/all_to_all | solution.py:475
  94.9 27.5 %collective-permute-start.9 = (bf16[2,96,1152]{2,1,0:T(8,128)(2,1)}, bf16[2,96,1152]{2,1,0:T(8,128)(2,1)S(1)}, u32[]{:S(2)}, u32[]{:S(2)}) collective-permute-start(bf16[2,96,1152]{2,1,0:T(8,128)(2,1)} %get-tuple-element.42), channel_id=1, source_target_pairs={{0,8},{4,12},{8,0},{12,4},{16,24},{20,28},{24,16},{28,20},{1,9},{5... | collective-permute-start | bytes 1327112 | tf_op jit(solution)/shard_map/ppermute | solution.py:336
  96.9 20.6 %collective-permute-start.15 = (bf16[2,96,1152]{2,1,0:T(8,128)(2,1)}, bf16[2,96,1152]{2,1,0:T(8,128)(2,1)S(1)}, u32[]{:S(2)}, u32[]{:S(2)}) collective-permute-start(bf16[2,96,1152]{2,1,0:T(8,128)(2,1)} %get-tuple-element.48), channel_id=1, source_target_pairs={{0,8},{4,12},{8,0},{12,4},{16,24},{20,28},{24,16},{28,20},{1,9},{5... | collective-permute-start | bytes 1327112 | tf_op jit(solution)/shard_map/ppermute | solution.py:336
  96.9 22.8 %collective-permute-start.11 = (bf16[2,96,1152]{2,1,0:T(8,128)(2,1)}, bf16[2,96,1152]{2,1,0:T(8,128)(2,1)}, u32[]{:S(2)}, u32[]{:S(2)}) collective-permute-start(bf16[2,96,1152]{2,1,0:T(8,128)(2,1)} %get-tuple-element.45), channel_id=1, source_target_pairs={{0,16},{4,20},{8,24},{12,28},{16,0},{20,4},{24,8},{28,12},{1,17},{... | collective-permute-start | bytes 1327112 | tf_op jit(solution)/shard_map/ppermute | solution.py:336
  99.8 30.8 %all-to-all-start.2 = ((f32[8,8,1152]{2,1,0:T(8,128)}), f32[8,8,1152]{2,1,0:T(8,128)S(1)}, u32[]{:S(2)}, u32[]{:S(2)}) async-start(f32[8,8,1152]{2,1,0:T(8,128)} %broadcast_in_dim.113), calls=%async_computation.2 | async-start | bytes 589824 | tf_op jit(solution)/shard_map/all_to_all | solution.py:481
  104.8 12.8 %copy-start.12 = (f32[1,96,1152]{2,1,0:T(8,128)S(1)}, f32[1,96,1152]{2,1,0:T(8,128)}, u32[]{:S(2)}) copy-start(f32[1,96,1152]{2,1,0:T(8,128)} %get-tuple-element.49) | copy-start | bytes 1327108
  105.5 14.3 %copy-start.13 = (f32[1,96,1152]{2,1,0:T(8,128)S(1)}, f32[1,96,1152]{2,1,0:T(8,128)}, u32[]{:S(2)}) copy-start(f32[1,96,1152]{2,1,0:T(8,128)} %get-tuple-element.44) | copy-start | bytes 1327108
  105.5 14.2 %copy-start.14 = (f32[1,96,1152]{2,1,0:T(8,128)S(1)}, f32[1,96,1152]{2,1,0:T(8,128)}, u32[]{:S(2)}) copy-start(f32[1,96,1152]{2,1,0:T(8,128)} %get-tuple-element.46) | copy-start | bytes 1327108
  106.3 19.1 %collective-permute-start.19 = (bf16[1,96,1152]{2,1,0:T(8,128)(2,1)S(1)}, bf16[1,96,1152]{2,1,0:T(8,128)(2,1)S(1)}, u32[]{:S(2)}, u32[]{:S(2)}) collective-permute-start(bf16[1,96,1152]{2,1,0:T(8,128)(2,1)S(1)} %get-tuple-element.55), channel_id=1, source_target_pairs={{0,8},{4,12},{8,0},{12,4},{16,24},{20,28},{24,16},{28,20},{1,9},{5... | collective-permute-start | bytes 663560 | tf_op jit(solution)/shard_map/ppermute | solution.py:336
  108.2 23.9 %collective-permute-start.18 = (f32[1,96,1152]{2,1,0:T(8,128)}, f32[1,96,1152]{2,1,0:T(8,128)S(1)}, u32[]{:S(2)}, u32[]{:S(2)}) collective-permute-start(f32[1,96,1152]{2,1,0:T(8,128)} %get-tuple-element.56), channel_id=1, source_target_pairs={{0,4},{4,0},{8,12},{12,8},{16,20},{20,16},{24,28},{28,24},{1,5},{5... | collective-permute-start | bytes 1327112 | tf_op jit(solution)/shard_map/ppermute | solution.py:336
  117.5 3.3 %copy-start.8 = (bf16[2,96,1152]{2,1,0:T(8,128)(2,1)}, bf16[2,96,1152]{2,1,0:T(8,128)(2,1)S(1)}, u32[]{:S(2)}) copy-start(bf16[2,96,1152]{2,1,0:T(8,128)(2,1)S(1)} %collective-permute-done.15.refs_6_) | copy-start | bytes 1327108
  117.6 4.8 %copy-start.11 = (f32[1,96,1152]{2,1,0:T(8,128)S(1)}, f32[1,96,1152]{2,1,0:T(8,128)}, u32[]{:S(2)}) copy-start(f32[1,96,1152]{2,1,0:T(8,128)} %get-tuple-element.43) | copy-start | bytes 1327108
  117.6 9.9 %collective-permute-start.16 = (bf16[1,96,1152]{2,1,0:T(8,128)(2,1)S(1)}, bf16[1,96,1152]{2,1,0:T(8,128)(2,1)S(1)}, u32[]{:S(2)}, u32[]{:S(2)}) collective-permute-start(bf16[1,96,1152]{2,1,0:T(8,128)(2,1)S(1)} %add_convert_fusion.1), channel_id=1, source_target_pairs={{0,16},{4,20},{8,24},{12,28},{16,0},{20,4},{24,8},{28,12},{1,17},{... | collective-permute-start | bytes 663560 | tf_op jit(solution)/shard_map/ppermute | solution.py:336
  119.7 10.2 %copy-start.24 = (pred[4]{0:T(512)(128)(4,1)S(1)}, pred[4]{0:T(512)(128)(4,1)}, u32[]{:S(2)}) copy-start(pred[4]{0:T(512)(128)(4,1)} %compare_and_fusion) | copy-start | bytes 16
  120.9 9.0 %collective-permute-start.13 = (bf16[1,96,1152]{2,1,0:T(8,128)(2,1)S(1)}, bf16[1,96,1152]{2,1,0:T(8,128)(2,1)}, u32[]{:S(2)}, u32[]{:S(2)}) collective-permute-start(bf16[1,96,1152]{2,1,0:T(8,128)(2,1)S(1)} %get-tuple-element.57), channel_id=1, source_target_pairs={{0,8},{4,12},{8,0},{12,4},{16,24},{20,28},{24,16},{28,20},{1,9},{5... | collective-permute-start | bytes 663560 | tf_op jit(solution)/shard_map/ppermute | solution.py:336
  122.4 9.8 %copy-start.7 = (bf16[2,96,1152]{2,1,0:T(8,128)(2,1)}, bf16[2,96,1152]{2,1,0:T(8,128)(2,1)S(1)}, u32[]{:S(2)}) copy-start(bf16[2,96,1152]{2,1,0:T(8,128)(2,1)S(1)} %collective-permute-done.9.refs_1_) | copy-start | bytes 1327108
  122.4 9.7 %collective-permute-start.12 = (f32[1,96,1152]{2,1,0:T(8,128)S(1)}, f32[1,96,1152]{2,1,0:T(8,128)S(1)}, u32[]{:S(2)}, u32[]{:S(2)}) collective-permute-start(f32[1,96,1152]{2,1,0:T(8,128)S(1)} %get-tuple-element.58), channel_id=1, source_target_pairs={{0,4},{4,0},{8,12},{12,8},{16,20},{20,16},{24,28},{28,24},{1,5},{5... | collective-permute-start | bytes 1327112 | tf_op jit(solution)/shard_map/ppermute | solution.py:336
  125.4 6.7 %collective-permute-start.10 = (bf16[1,96,1152]{2,1,0:T(8,128)(2,1)S(1)}, bf16[1,96,1152]{2,1,0:T(8,128)(2,1)S(1)}, u32[]{:S(2)}, u32[]{:S(2)}) collective-permute-start(bf16[1,96,1152]{2,1,0:T(8,128)(2,1)S(1)} %add_convert_fusion.3), channel_id=1, source_target_pairs={{0,16},{4,20},{8,24},{12,28},{16,0},{20,4},{24,8},{28,12},{1,17},{... | collective-permute-start | bytes 663560 | tf_op jit(solution)/shard_map/ppermute | solution.py:336
  127.5 4.7 %copy-start.17 = (bf16[1,96,1152]{2,1,0:T(8,128)(2,1)}, bf16[1,96,1152]{2,1,0:T(8,128)(2,1)S(1)}, u32[]{:S(2)}) copy-start(bf16[1,96,1152]{2,1,0:T(8,128)(2,1)S(1)} %collective-permute-done.16.refs_7_) | copy-start | bytes 663556
  127.5 4.6 %collective-permute-start.20 = (bf16[1,96,1152]{2,1,0:T(8,128)(2,1)S(1)}, bf16[1,96,1152]{2,1,0:T(8,128)(2,1)S(1)}, u32[]{:S(2)}, u32[]{:S(2)}) collective-permute-start(bf16[1,96,1152]{2,1,0:T(8,128)(2,1)S(1)} %collective-permute-done.19), channel_id=1, source_target_pairs={{0,4},{4,0},{8,12},{12,8},{16,20},{20,16},{24,28},{28,24},{1,5},{5... | collective-permute-start | bytes 663560 | tf_op jit(solution)/shard_map/ppermute | solution.py:336
  129.9 2.2 %collective-permute-start.14 = (bf16[1,96,1152]{2,1,0:T(8,128)(2,1)}, bf16[1,96,1152]{2,1,0:T(8,128)(2,1)S(1)}, u32[]{:S(2)}, u32[]{:S(2)}) collective-permute-start(bf16[1,96,1152]{2,1,0:T(8,128)(2,1)} %collective-permute-done.13), channel_id=1, source_target_pairs={{0,4},{4,0},{8,12},{12,8},{16,20},{20,16},{24,28},{28,24},{1,5},{5... | collective-permute-start | bytes 663560 | tf_op jit(solution)/shard_map/ppermute | solution.py:336
  130.6 1.6 %copy-start.6 = (f32[8,8,1152]{2,1,0:T(8,128)}, f32[8,8,1152]{2,1,0:T(8,128)S(1)}, u32[]{:S(2)}) copy-start(f32[8,8,1152]{2,1,0:T(8,128)S(1)} %all-to-all-done.2.refs_11_) | copy-start | bytes 884740
  132.1 0.7 copy-start.18
  132.1 0.8 copy-start.19
  132.1 0.9 copy-start.9
  132.1 1.0 copy-start.20
  132.1 1.1 copy-start.10

commit v8 on v7

--- a/solution.py
+++ b/solution.py
@@ -100,7 +100,7 @@
             outs[output][index] = result[count * rows : (count + 1) * rows].astype(
                 outs[output].dtype
             )
-    if part == 1:
+    if part == 0:
         outs[-1][...] = jnp.dot(
             scaling[...], weights[...], preferred_element_type=jnp.float32
         )[: outs[-1].shape[0]]
@@ -375,7 +375,6 @@
     square = jnp.sum(stats[:, 1] + width * jnp.square(apart), axis=0)
     scale = lax.rsqrt(square / (width * wgt_size) + EPS)
     factors = jnp.concatenate([scale[None], apart * scale[None]], axis=0)
-    factors = jnp.broadcast_to(factors[None], (req_size, wgt_size + 1, rows))
 
     square_plane = chips == 4
     if square_plane:
@@ -442,12 +441,13 @@
         if not square_plane:
             sums = [blocks[0]]
             sums += [swap(block, distance) for distance, block in enumerate(blocks[1:], 1)]
-            return sums[::2], sums[1::2]
+            return sums[::2], sums[1::2], sums[1:]
         along_x, along_y = swap(blocks[0], 2), swap(blocks[1], 4)
         own, own_y, other, other_x = blocks[2:]
         behind_y = swap((own_y + along_x[1:]).astype(jnp.bfloat16), 4)
         behind_x = swap((other_x + along_y[1:]).astype(jnp.bfloat16), 2)
-        return [own, along_x, behind_y], [swap(other + along_y[:1], 1), swap(behind_x, 1)]
+        far = [swap(other + along_y[:1], 1), swap(behind_x, 1)]
+        return [own, along_x, behind_y], far, [along_x, along_y]
 
     projected = []
     for part in range(2):
@@ -458,9 +458,9 @@
                     jax.ShapeDtypeStruct((len(members), chunk_rows, half_cols), kind)
                     for members, kind in plan
                 ]
-                + [jax.ShapeDtypeStruct((8, half_cols), jnp.float32)] * part,
+                + [jax.ShapeDtypeStruct((8, half_cols), jnp.float32)] * (1 - part),
                 in_specs=[SMEM] * 2 + [HBM] * (req_size + 2) + [VMEM],
-                out_specs=[VMEM] * (len(plan) + part),
+                out_specs=[VMEM] * (len(plan) + 1 - part),
                 scratch_shapes=[
                     pltpu.VMEM((block, half_cols), jnp.bfloat16),
                     pltpu.VMEM((req_size * half, fresh_len, block), jnp.bfloat16),
@@ -472,19 +472,23 @@
             )(place, position, *received, own_rows, other_rows, scaling)
         )
 
-    factors = lax.all_to_all(after(factors, projected[0][0]), "req", 0, 0, tiled=True)
-    factors = factors.reshape(req_size, wgt_size + 1, req_count, fresh_len)
-    factors = factors.transpose(0, 2, 3, 1).reshape(everyone, fresh_len, wgt_size + 1)
+    terms, sums, first = [], [], None
+    for blocks in projected:
+        near, far, arrived = collect(blocks[: len(plan)])
+        terms += [len(near), len(far)]
+        sums += near + far
+        first = first or arrived
+
+    count = wgt_size + 1
+    lines = projected[0][-1][:2]
+    message = jnp.zeros((-(-(count + 2) // 8) * 8, half_cols), jnp.float32)
+    message = message.at[:2].set(lines).at[2 : 2 + count, :rows].set(factors)
+    message = jnp.broadcast_to(after(message, first)[None], (req_size, *message.shape))
+    folded = lax.all_to_all(message, "req", 0, 0, tiled=True)
+    factors = folded[:, 2 : 2 + count, :rows].reshape(req_size, count, req_count, fresh_len)
+    factors = factors.transpose(0, 2, 3, 1).reshape(everyone, fresh_len, count)
     factors = jnp.take(factors, served, axis=0)
 
-    folded = jnp.broadcast_to(projected[1][-1][None], (req_size, 8, half_cols))
-    folded = lax.all_to_all(folded, "req", 0, 0, tiled=True)
-
-    terms, sums = [], []
-    for blocks in projected:
-        for side in collect(blocks[: len(plan)]):
-            terms.append(len(side))
-            sums += side
     out = jax.ShapeDtypeStruct((req_count, fresh_len, heads * HEAD), jnp.bfloat16)
     return tuple(
         pl.pallas_call(

time: 151 us -> 144 us (0.954)
  starting transfers between devices: 38.1 us -> 31.8 us
  Pallas kernels: 32.1 us -> 30.1 us
    ppermute x4, waiting for transfers between devices: 7.29 us -> 0.01 us  [route(): return lax.ppermute(value, ('req', 'wgt'), pairs)]
    all_to_all x2 -> x1, waiting for transfers between devices: 0.17 us -> 5.64 us  [per_device(): folded = lax.all_to_all(message, 'req', 0, 0, tiled=True)]
    all_to_all x2 -> x1, starting transfers between devices: 8.63 us -> 3.55 us  [per_device(): folded = lax.all_to_all(message, 'req', 0, 0, tiled=True)]
    all_to_all x1, waiting for transfers between devices: 20 us -> 22.3 us  [per_device(): stats = lax.all_to_all(stats, 'wgt', 0, 0, tiled=True)]
    pallas_call x1, Pallas kernels: 15.4 us -> 13.4 us  [per_device(): pl.pallas_call(functools.partial(attend_kernel, (terms, req_count, fresh_...]
    unnamed x54 -> x56, local copies, waits for them, and re-layouts: 3.65 us -> 3.24 us
  transfers between devices with their start and end apart: 24 -> 23, of which waited for: 7 -> 8; matrix products, arithmetic and copies ran while one was open for 18% -> 19% of each run, Pallas kernels for 6% -> 6%
where the time goes in v8:
time: 144 us; the launch traced here: 143 us
  waiting for transfers between devices  44.7 us (31%)
  starting transfers between devices  31.8 us (22%)
  Pallas kernels  30.1 us (21%)
  other arithmetic  19.2 us (13%)
  local copies, waits for them, and re-layouts  15.6 us (11%)
    all_to_all x1, waiting for transfers between devices, per_device(): stats = lax.all_to_all(stats, 'wgt', 0, 0, tiled=True)  22.3 us
    ppermute x17, waiting for transfers between devices, swap(): lax.ppermute(value, 'req', [(device, device ^ distance) for device in ran...  16.8 us
    pallas_call x2, Pallas kernels, per_device(): pl.pallas_call(functools.partial(project_kernel, part, plan), out_shape=[...  16.7 us
    pallas_call x1, Pallas kernels, per_device(): pl.pallas_call(functools.partial(attend_kernel, (terms, req_count, fresh_...  13.4 us
    ppermute x17, starting transfers between devices, swap(): lax.ppermute(value, 'req', [(device, device ^ distance) for device in ran...  13.3 us
    ppermute x4, starting transfers between devices, route(): return lax.ppermute(value, ('req', 'wgt'), pairs)  11.7 us
    all_to_all x1, waiting for transfers between devices, per_device(): folded = lax.all_to_all(message, 'req', 0, 0, tiled=True)  5.64 us
    all_to_all x1, starting transfers between devices, per_device(): folded = lax.all_to_all(message, 'req', 0, 0, tiled=True)  3.55 us
  transfers between devices with their start and end apart: 23, of which 8 were waited for; matrix products, arithmetic and copies ran while one was open for 19% of the time, Pallas kernels for 6%

profile of v8, /device:TPU:0, one launch (start us, length us, event | category | flops | bytes accessed | tf_op | source)
XLA Modules:
  0.0 142.7 jit_solution(1595737185847295258)
XLA Ops:
  0.6 1.2 convert_reduce_fusion
  2.0 0.8 fusion.14
  2.8 2.1 %fusion.1 = bf16[192,1536]{1,0:T(8,128)(2,1)} fusion(bf16[4,48,1536]{2,1,0:T(8,128)(2,1)} %param.23, f32[1536]{0:T(1024)S(1)} %get-tuple-element.84, f32[192]{0:T(256)S(1)} %div.53), kind=kLoop, calls=%fused_computation.4 | loop fusion | flops 1179648 | bytes 1186560 | tf_op jit(solution)/shard_map/convert_element_type | solution.py:350
  4.9 1.7 %collective-permute-start = (bf16[192,1536]{1,0:T(8,128)(2,1)}, bf16[192,1536]{1,0:T(8,128)(2,1)S(1)}, u32[]{:S(2)}, u32[]{:S(2)}) collective-permute-start(bf16[192,1536]{1,0:T(8,128)(2,1)} %fusion.1), channel_id=1, source_target_pairs={{0,0},{8,1},{16,2},{24,3},{4,4},{12,5},{20,6},{28,7},{1,8},{9,9},{... | collective-permute-start | bytes 1769480 | tf_op jit(solution)/shard_map/ppermute | solution.py:366
  6.6 4.6 %collective-permute-start.1 = (bf16[192,1536]{1,0:T(8,128)(2,1)}, bf16[192,1536]{1,0:T(8,128)(2,1)S(1)}, u32[]{:S(2)}, u32[]{:S(2)}) collective-permute-start(bf16[192,1536]{1,0:T(8,128)(2,1)} %fusion.1), channel_id=1, source_target_pairs={{8,0},{0,1},{24,2},{16,3},{12,4},{4,5},{28,6},{20,7},{9,8},{1,9},{... | collective-permute-start | bytes 1769480 | tf_op jit(solution)/shard_map/ppermute | solution.py:366
  11.2 3.5 %collective-permute-start.2 = (bf16[192,1536]{1,0:T(8,128)(2,1)}, bf16[192,1536]{1,0:T(8,128)(2,1)S(1)}, u32[]{:S(2)}, u32[]{:S(2)}) collective-permute-start(bf16[192,1536]{1,0:T(8,128)(2,1)} %fusion.1), channel_id=1, source_target_pairs={{16,0},{24,1},{0,2},{8,3},{20,4},{28,5},{4,6},{12,7},{17,8},{25,9}... | collective-permute-start | bytes 1769480 | tf_op jit(solution)/shard_map/ppermute | solution.py:366
  14.7 1.9 %collective-permute-start.3 = (bf16[192,1536]{1,0:T(8,128)(2,1)}, bf16[192,1536]{1,0:T(8,128)(2,1)}, u32[]{:S(2)}, u32[]{:S(2)}) collective-permute-start(bf16[192,1536]{1,0:T(8,128)(2,1)} %fusion.1), channel_id=1, source_target_pairs={{24,0},{16,1},{8,2},{0,3},{28,4},{20,5},{12,6},{4,7},{25,8},{17,9}... | collective-permute-start | bytes 1769480 | tf_op jit(solution)/shard_map/ppermute | solution.py:366
  16.6 2.9 %constant_dynamic-slice_fusion = bf16[768,1152]{1,0:T(8,128)(2,1)} fusion(bf16[768,2304]{1,0:T(8,128)(2,1)} %refs_8_.3, s32[]{:T(128)S(6)} %select_n.105), kind=kLoop, calls=%fused_computation.62 | loop fusion | bytes 3538948 | tf_op jit(solution)/shard_map/dynamic_slice | solution.py:435
  19.5 0.3 multiply_reduce_fusion
  19.8 0.6 div.54
  20.4 0.6 stack.19
  21.1 0.7 pad_maximum_fusion.1
  21.8 0.6 broadcast_in_dim.105
  22.4 3.2 %all-to-all-start = ((f32[4,2,192]{2,1,0:T(2,128)}), f32[4,2,192]{2,1,0:T(2,128)S(1)}, u32[]{:S(2)}, u32[]{:S(2)}) async-start(f32[4,2,192]{2,1,0:T(2,128)} %broadcast_in_dim.105), calls=%async_computation | async-start | bytes 16384 | tf_op jit(solution)/shard_map/all_to_all | solution.py:372
  25.7 0.9 convert_reduce_fusion.1
  26.6 0.6 copy-done.25
  27.2 1.2 multiply_add_fusion
  28.3 0.6 pad_clamp_fusion.1
  28.9 1.4 gather_fusion
  30.3 1.2 fusion.11
  31.5 0.8 select_reduce_fusion.1
  32.3 0.7 add_convert_fusion.4
  33.1 1.4 select_reduce_fusion.position
  34.4 0.5 compare_and_fusion
  35.0 1.9 %fusion.2 = (f32[4,48,96]{2,1,0:T(8,128)}, f32[4,48,96]{2,1,0:T(8,128)}, f32[4,48,96]{2,1,0:T(8,128)}) fusion(f32[96]{0:T(128)} %constant.251, f32[4,48]{1,0:T(4,128)S(1)} %add_convert_fusion.4, pred[96]{0:T(512)(128)(4,1)} %constant.252, pred[96]{0:T(512)(128)(4,1)} %constant.242.clone, pred[96]{0:T(512)(128)(4,1)} %constant.241.clone), kind=kLoop, calls=%fused_computation.15 | loop fusion | flops 92160 | bytes 222624 | tf_op jit(solution)/shard_map/jit(_where)/select_n | solution.py:419
  36.8 0.6 pad_clamp_fusion
  37.4 0.6 pad_add_fusion.place
  38.0 0.8 dynamic_slice.15
  38.8 1.3 reshape.370.refs_12_
  40.1 0.6 scatter.14
  40.7 1.4 scatter.15.refs_10_
  42.1 22.3 %all-to-all-done = f32[4,2,192]{2,1,0:T(2,128)S(1)} async-done(((f32[4,2,192]{2,1,0:T(2,128)}), f32[4,2,192]{2,1,0:T(2,128)S(1)}, u32[]{:S(2)}, u32[]{:S(2)}) %all-to-all-start) | async-done | bytes 6176 | tf_op jit(solution)/shard_map/all_to_all | solution.py:372
  64.6 0.5 collective-permute-start.5
  65.1 0.4 collective-permute-start.7
  65.6 0.9 collective-permute-done.4
  66.5 1.7 %collective-permute-done.5 = bf16[192,1536]{1,0:T(8,128)(2,1)S(1)} collective-permute-done((bf16[192,1536]{1,0:T(8,128)(2,1)S(1)}, bf16[192,1536]{1,0:T(8,128)(2,1)S(1)}, u32[]{:S(2)}, u32[]{:S(2)}) %collective-permute-start.5) | collective-permute-done | bytes 589856 | tf_op jit(solution)/shard_map/ppermute | solution.py:336
  68.2 0.8 collective-permute-done.6
  69.1 0.8 copy-done.8
  69.9 0.2 copy-done.9
  70.1 0.5 copy-done.1
  70.6 8.4 %project.2 = (bf16[2,96,1152]{2,1,0:T(8,128)(2,1)}, bf16[2,96,1152]{2,1,0:T(8,128)(2,1)}, f32[1,96,1152]{2,1,0:T(8,128)}, f32[1,96,1152]{2,1,0:T(8,128)}, f32[1,...) custom-call(s32[2]{0:T(128)} %pad_add_fusion.place, s32[32]{0:T(128)} %select_reduce_fusion.position, ...), custom_call_target="tpu_custom_call" | custom-call | tf_op jit(solution)/shard_map/project/pallas_call | solution.py:455
  79.0 1.0 collective-permute-start.9
  80.1 4.4 %collective-permute-start.11 = (bf16[2,96,1152]{2,1,0:T(8,128)(2,1)}, bf16[2,96,1152]{2,1,0:T(8,128)(2,1)S(1)}, u32[]{:S(2)}, u32[]{:S(2)}) collective-permute-start(bf16[2,96,1152]{2,1,0:T(8,128)(2,1)} %get-tuple-element.69), channel_id=1, source_target_pairs={{0,16},{4,20},{8,24},{12,28},{16,0},{20,4},{24,8},{28,12},{1,17},{... | collective-permute-start | bytes 1327112 | tf_op jit(solution)/shard_map/ppermute | solution.py:336
  84.5 8.4 %project.3 = (bf16[2,96,1152]{2,1,0:T(8,128)(2,1)}, bf16[2,96,1152]{2,1,0:T(8,128)(2,1)}, f32[1,96,1152]{2,1,0:T(8,128)}, f32[1,96,1152]{2,1,0:T(8,128)}, f32[1,...) custom-call(s32[2]{0:T(128)} %pad_add_fusion.place, s32[32]{0:T(128)} %select_reduce_fusion.position, ...), custom_call_target="tpu_custom_call" | custom-call | tf_op jit(solution)/shard_map/project/pallas_call | solution.py:455
  92.9 1.5 %collective-permute-start.15 = (bf16[2,96,1152]{2,1,0:T(8,128)(2,1)}, bf16[2,96,1152]{2,1,0:T(8,128)(2,1)S(1)}, u32[]{:S(2)}, u32[]{:S(2)}) collective-permute-start(bf16[2,96,1152]{2,1,0:T(8,128)(2,1)} %get-tuple-element.72), channel_id=1, source_target_pairs={{0,8},{4,12},{8,0},{12,4},{16,24},{20,28},{24,16},{28,20},{1,9},{5... | collective-permute-start | bytes 1327112 | tf_op jit(solution)/shard_map/ppermute | solution.py:336
  94.5 0.4 scatter.19
  94.9 0.8 add_convert_fusion.3
  95.8 2.0 %collective-permute-start.10 = (bf16[1,96,1152]{2,1,0:T(8,128)(2,1)}, bf16[1,96,1152]{2,1,0:T(8,128)(2,1)}, u32[]{:S(2)}, u32[]{:S(2)}) collective-permute-start(bf16[1,96,1152]{2,1,0:T(8,128)(2,1)} %add_convert_fusion.3), channel_id=1, source_target_pairs={{0,16},{4,20},{8,24},{12,28},{16,0},{20,4},{24,8},{28,12},{1,17},{... | collective-permute-start | bytes 663560 | tf_op jit(solution)/shard_map/ppermute | solution.py:336
  97.7 0.8 add_convert_fusion.2
  98.5 0.6 collective-permute-start.13
  99.1 8.6 %collective-permute-done.17 = bf16[2,96,1152]{2,1,0:T(8,128)(2,1)} collective-permute-done((bf16[2,96,1152]{2,1,0:T(8,128)(2,1)}, bf16[2,96,1152]{2,1,0:T(8,128)(2,1)}, u32[]{:S(2)}, u32[]{:S(2)}) %collective-permute-start.17) | collective-permute-done | bytes 442400 | tf_op jit(solution)/shard_map/ppermute | solution.py:336
  107.8 1.2 add_convert_fusion
  109.0 0.7 broadcast_in_dim.106
  109.8 3.6 %all-to-all-start.1 = ((f32[8,8,1152]{2,1,0:T(8,128)}), f32[8,8,1152]{2,1,0:T(8,128)S(1)}, u32[]{:S(2)}, u32[]{:S(2)}) async-start(f32[8,8,1152]{2,1,0:T(8,128)} %broadcast_in_dim.106), calls=%async_computation.1 | async-start | bytes 589824 | tf_op jit(solution)/shard_map/all_to_all | solution.py:487
  113.3 2.0 %collective-permute-start.19 = (bf16[1,96,1152]{2,1,0:T(8,128)(2,1)S(1)}, bf16[1,96,1152]{2,1,0:T(8,128)(2,1)}, u32[]{:S(2)}, u32[]{:S(2)}) collective-permute-start(bf16[1,96,1152]{2,1,0:T(8,128)(2,1)S(1)} %get-tuple-element.79), channel_id=1, source_target_pairs={{0,8},{4,12},{8,0},{12,4},{16,24},{20,28},{24,16},{28,20},{1,9},{5... | collective-permute-start | bytes 663560 | tf_op jit(solution)/shard_map/ppermute | solution.py:336
  115.4 5.6 %all-to-all-done.1.refs_11_ = f32[8,8,1152]{2,1,0:T(8,128)S(1)} async-done(((f32[8,8,1152]{2,1,0:T(8,128)}), f32[8,8,1152]{2,1,0:T(8,128)S(1)}, u32[]{:S(2)}, u32[]{:S(2)}) %all-to-all-start.1) | async-done | bytes 294944 | tf_op jit(solution)/shard_map/all_to_all | solution.py:487
  121.2 0.7 gather_fusion.1
  122.0 0.6 collective-permute-start.16
  122.6 1.8 %collective-permute-done.19 = bf16[1,96,1152]{2,1,0:T(8,128)(2,1)} collective-permute-done((bf16[1,96,1152]{2,1,0:T(8,128)(2,1)S(1)}, bf16[1,96,1152]{2,1,0:T(8,128)(2,1)}, u32[]{:S(2)}, u32[]{:S(2)}) %collective-permute-start.19) | collective-permute-done | bytes 221216 | tf_op jit(solution)/shard_map/ppermute | solution.py:336
  124.5 0.7 broadcast_select_fusion.refs_10_
  125.2 2.8 %collective-permute-done.16.refs_7_ = bf16[1,96,1152]{2,1,0:T(8,128)(2,1)S(1)} collective-permute-done((bf16[1,96,1152]{2,1,0:T(8,128)(2,1)S(1)}, bf16[1,96,1152]{2,1,0:T(8,128)(2,1)S(1)}, u32[]{:S(2)}, u32[]{:S(2)}) %collective-permute-start.16) | collective-permute-done | bytes 221216 | tf_op jit(solution)/shard_map/ppermute | solution.py:336
  128.1 0.6 copy-done.21
  128.7 0.2 copy-done.13
  129.2 13.4 %attend.1 = (bf16[4,48,768]{2,1,0:T(8,128)(2,1)}, bf16[4,48,768]{2,1,0:T(8,128)(2,1)}, bf16[4,48,768]{2,1,0:T(8,128)(2,1)}) custom-call(s32[2]{0:T(128)} %pad_add_fusion.place, s32[4]{0:T(128)} %all_lengths.1, s32[4,16]{1,0:T(4,128)} %table.1, f32[1,96,1152]{2,1,0:T(8,128)} %get-tuple-element.65.refs_0_, bf16[2,96,1152]{2,1,0:T(8,128)(2,1)} %copy-done.11, ...), custom_call_target="tpu_custom_call" | custom-call | tf_op jit(solution)/shard_map/attend/pallas_call | solution.py:494
  (92 shorter events, 1.3 us)
Async XLA Ops:
  4.9 59.5 %collective-permute-start = (bf16[192,1536]{1,0:T(8,128)(2,1)}, bf16[192,1536]{1,0:T(8,128)(2,1)S(1)}, u32[]{:S(2)}, u32[]{:S(2)}) collective-permute-start(bf16[192,1536]{1,0:T(8,128)(2,1)} %fusion.1), channel_id=1, source_target_pairs={{0,0},{8,1},{16,2},{24,3},{4,4},{12,5},{20,6},{28,7},{1,8},{9,9},{... | collective-permute-start | bytes 1769480 | tf_op jit(solution)/shard_map/ppermute | solution.py:366
  6.6 57.9 %collective-permute-start.1 = (bf16[192,1536]{1,0:T(8,128)(2,1)}, bf16[192,1536]{1,0:T(8,128)(2,1)S(1)}, u32[]{:S(2)}, u32[]{:S(2)}) collective-permute-start(bf16[192,1536]{1,0:T(8,128)(2,1)} %fusion.1), channel_id=1, source_target_pairs={{8,0},{0,1},{24,2},{16,3},{12,4},{4,5},{28,6},{20,7},{9,8},{1,9},{... | collective-permute-start | bytes 1769480 | tf_op jit(solution)/shard_map/ppermute | solution.py:366
  11.2 53.8 %collective-permute-start.2 = (bf16[192,1536]{1,0:T(8,128)(2,1)}, bf16[192,1536]{1,0:T(8,128)(2,1)S(1)}, u32[]{:S(2)}, u32[]{:S(2)}) collective-permute-start(bf16[192,1536]{1,0:T(8,128)(2,1)} %fusion.1), channel_id=1, source_target_pairs={{16,0},{24,1},{0,2},{8,3},{20,4},{28,5},{4,6},{12,7},{17,8},{25,9}... | collective-permute-start | bytes 1769480 | tf_op jit(solution)/shard_map/ppermute | solution.py:366
  14.7 50.4 %collective-permute-start.3 = (bf16[192,1536]{1,0:T(8,128)(2,1)}, bf16[192,1536]{1,0:T(8,128)(2,1)}, u32[]{:S(2)}, u32[]{:S(2)}) collective-permute-start(bf16[192,1536]{1,0:T(8,128)(2,1)} %fusion.1), channel_id=1, source_target_pairs={{24,0},{16,1},{8,2},{0,3},{28,4},{20,5},{12,6},{4,7},{25,8},{17,9}... | collective-permute-start | bytes 1769480 | tf_op jit(solution)/shard_map/ppermute | solution.py:366
  16.6 2.9 %copy-start.2 = (bf16[4,48,1536]{2,1,0:T(8,128)(2,1)S(1)}, bf16[4,48,1536]{2,1,0:T(8,128)(2,1)}, u32[]{:S(2)}) copy-start(bf16[4,48,1536]{2,1,0:T(8,128)(2,1)} %param.23) | copy-start | bytes 1769476
  16.6 12.3 %copy-start = (s32[8]{0:T(128)S(1)}, s32[8]{0:T(128)}, u32[]{:S(2)}) copy-start(s32[8]{0:T(128)} %constant.239.clone) | copy-start | bytes 100
  19.5 49.6 %collective-permute-start.8 = (bf16[768,1152]{1,0:T(8,128)(2,1)}, bf16[768,1152]{1,0:T(8,128)(2,1)S(1)}, u32[]{:S(2)}, u32[]{:S(2)}) collective-permute-start(bf16[768,1152]{1,0:T(8,128)(2,1)} %constant_dynamic-slice_fusion), channel_id=1, source_target_pairs={{0,4},{4,0},{8,12},{12,8},{16,20},{20,16},{24,28},{28,24},{1,5},{5... | collective-permute-start | bytes 5308424 | tf_op jit(solution)/shard_map/ppermute | solution.py:336
  22.4 42.0 %all-to-all-start = ((f32[4,2,192]{2,1,0:T(2,128)}), f32[4,2,192]{2,1,0:T(2,128)S(1)}, u32[]{:S(2)}, u32[]{:S(2)}) async-start(f32[4,2,192]{2,1,0:T(2,128)} %broadcast_in_dim.105), calls=%async_computation | async-start | bytes 16384 | tf_op jit(solution)/shard_map/all_to_all | solution.py:372
  26.6 0.6 copy-start.25
  64.4 4.6 %copy-start.3 = (bf16[192,1536]{1,0:T(8,128)(2,1)}, bf16[192,1536]{1,0:T(8,128)(2,1)S(1)}, u32[]{:S(2)}) copy-start(bf16[192,1536]{1,0:T(8,128)(2,1)S(1)} %collective-permute-done) | copy-start | bytes 1769476
  64.5 2.1 %collective-permute-start.4 = (bf16[192,1536]{1,0:T(8,128)(2,1)S(1)}, bf16[192,1536]{1,0:T(8,128)(2,1)S(1)}, u32[]{:S(2)}, u32[]{:S(2)}) collective-permute-start(bf16[192,1536]{1,0:T(8,128)(2,1)S(1)} %collective-permute-done), channel_id=1, source_target_pairs={{0,4},{4,0},{8,12},{12,8},{16,20},{20,16},{24,28},{28,24},{1,5},{5... | collective-permute-start | bytes 1769480 | tf_op jit(solution)/shard_map/ppermute | solution.py:336
  64.5 4.5 %copy-start.4 = (bf16[192,1536]{1,0:T(8,128)(2,1)}, bf16[192,1536]{1,0:T(8,128)(2,1)S(1)}, u32[]{:S(2)}) copy-start(bf16[192,1536]{1,0:T(8,128)(2,1)S(1)} %collective-permute-done.1) | copy-start | bytes 1769476
  64.6 3.7 %collective-permute-start.5 = (bf16[192,1536]{1,0:T(8,128)(2,1)S(1)}, bf16[192,1536]{1,0:T(8,128)(2,1)S(1)}, u32[]{:S(2)}, u32[]{:S(2)}) collective-permute-start(bf16[192,1536]{1,0:T(8,128)(2,1)S(1)} %collective-permute-done.1), channel_id=1, source_target_pairs={{0,4},{4,0},{8,12},{12,8},{16,20},{20,16},{24,28},{28,24},{1,5},{5... | collective-permute-start | bytes 1769480 | tf_op jit(solution)/shard_map/ppermute | solution.py:336
  65.0 4.1 %copy-start.5 = (bf16[192,1536]{1,0:T(8,128)(2,1)}, bf16[192,1536]{1,0:T(8,128)(2,1)S(1)}, u32[]{:S(2)}) copy-start(bf16[192,1536]{1,0:T(8,128)(2,1)S(1)} %collective-permute-done.2) | copy-start | bytes 1769476
  65.0 4.0 %collective-permute-start.6 = (bf16[192,1536]{1,0:T(8,128)(2,1)S(1)}, bf16[192,1536]{1,0:T(8,128)(2,1)S(1)}, u32[]{:S(2)}, u32[]{:S(2)}) collective-permute-start(bf16[192,1536]{1,0:T(8,128)(2,1)S(1)} %collective-permute-done.2), channel_id=1, source_target_pairs={{0,4},{4,0},{8,12},{12,8},{16,20},{20,16},{24,28},{28,24},{1,5},{5... | collective-permute-start | bytes 1769480 | tf_op jit(solution)/shard_map/ppermute | solution.py:336
  65.1 3.9 %collective-permute-start.7 = (bf16[192,1536]{1,0:T(8,128)(2,1)}, bf16[192,1536]{1,0:T(8,128)(2,1)S(1)}, u32[]{:S(2)}, u32[]{:S(2)}) collective-permute-start(bf16[192,1536]{1,0:T(8,128)(2,1)} %collective-permute-done.3), channel_id=1, source_target_pairs={{0,4},{4,0},{8,12},{12,8},{16,20},{20,16},{24,28},{28,24},{1,5},{5... | collective-permute-start | bytes 1769480 | tf_op jit(solution)/shard_map/ppermute | solution.py:336
  66.5 2.6 %copy-start.6 = (bf16[192,1536]{1,0:T(8,128)(2,1)}, bf16[192,1536]{1,0:T(8,128)(2,1)S(1)}, u32[]{:S(2)}) copy-start(bf16[192,1536]{1,0:T(8,128)(2,1)S(1)} %collective-permute-done.4) | copy-start | bytes 1769476
  68.2 0.9 copy-start.7
  69.1 0.8 copy-start.8
  69.1 1.0 copy-start.9
  69.1 1.6 %copy-start.1 = (bf16[768,1152]{1,0:T(8,128)(2,1)}, bf16[768,1152]{1,0:T(8,128)(2,1)S(1)}, u32[]{:S(2)}) copy-start(bf16[768,1152]{1,0:T(8,128)(2,1)S(1)} %collective-permute-done.8.refs_9_) | copy-start | bytes 5308420
  79.0 15.9 %collective-permute-start.9 = (bf16[2,96,1152]{2,1,0:T(8,128)(2,1)}, bf16[2,96,1152]{2,1,0:T(8,128)(2,1)S(1)}, u32[]{:S(2)}, u32[]{:S(2)}) collective-permute-start(bf16[2,96,1152]{2,1,0:T(8,128)(2,1)} %get-tuple-element.66), channel_id=1, source_target_pairs={{0,8},{4,12},{8,0},{12,4},{16,24},{20,28},{24,16},{28,20},{1,9},{5... | collective-permute-start | bytes 1327112 | tf_op jit(solution)/shard_map/ppermute | solution.py:336
  80.1 14.3 %copy-start.24 = (f32[8,1152]{1,0:T(8,128)S(1)}, f32[8,1152]{1,0:T(8,128)}, u32[]{:S(2)}) copy-start(f32[8,1152]{1,0:T(8,128)} %get-tuple-element.77) | copy-start | bytes 110596
  80.1 14.3 %copy-start.26 = (pred[8]{0:T(512)(128)(4,1)S(1)}, pred[8]{0:T(512)(128)(4,1)}, u32[]{:S(2)}) copy-start(pred[8]{0:T(512)(128)(4,1)} %constant.230.clone.1) | copy-start | bytes 28
  80.1 14.9 %copy-start.16 = (f32[1,96,1152]{2,1,0:T(8,128)S(1)}, f32[1,96,1152]{2,1,0:T(8,128)}, u32[]{:S(2)}) copy-start(f32[1,96,1152]{2,1,0:T(8,128)} %get-tuple-element.67) | copy-start | bytes 1327108
  80.1 17.6 %collective-permute-start.11 = (bf16[2,96,1152]{2,1,0:T(8,128)(2,1)}, bf16[2,96,1152]{2,1,0:T(8,128)(2,1)S(1)}, u32[]{:S(2)}, u32[]{:S(2)}) collective-permute-start(bf16[2,96,1152]{2,1,0:T(8,128)(2,1)} %get-tuple-element.69), channel_id=1, source_target_pairs={{0,16},{4,20},{8,24},{12,28},{16,0},{20,4},{24,8},{28,12},{1,17},{... | collective-permute-start | bytes 1327112 | tf_op jit(solution)/shard_map/ppermute | solution.py:336
  92.9 4.9 %copy-start.19 = (f32[1,96,1152]{2,1,0:T(8,128)S(1)}, f32[1,96,1152]{2,1,0:T(8,128)}, u32[]{:S(2)}) copy-start(f32[1,96,1152]{2,1,0:T(8,128)} %get-tuple-element.68) | copy-start | bytes 1327108
  92.9 4.8 %copy-start.20 = (f32[1,96,1152]{2,1,0:T(8,128)S(1)}, f32[1,96,1152]{2,1,0:T(8,128)}, u32[]{:S(2)}) copy-start(f32[1,96,1152]{2,1,0:T(8,128)} %get-tuple-element.70) | copy-start | bytes 1327108
  92.9 20.4 %collective-permute-start.15 = (bf16[2,96,1152]{2,1,0:T(8,128)(2,1)}, bf16[2,96,1152]{2,1,0:T(8,128)(2,1)S(1)}, u32[]{:S(2)}, u32[]{:S(2)}) collective-permute-start(bf16[2,96,1152]{2,1,0:T(8,128)(2,1)} %get-tuple-element.72), channel_id=1, source_target_pairs={{0,8},{4,12},{8,0},{12,4},{16,24},{20,28},{24,16},{28,20},{1,9},{5... | collective-permute-start | bytes 1327112 | tf_op jit(solution)/shard_map/ppermute | solution.py:336
  94.3 13.4 %collective-permute-start.17 = (bf16[2,96,1152]{2,1,0:T(8,128)(2,1)}, bf16[2,96,1152]{2,1,0:T(8,128)(2,1)}, u32[]{:S(2)}, u32[]{:S(2)}) collective-permute-start(bf16[2,96,1152]{2,1,0:T(8,128)(2,1)} %get-tuple-element.75), channel_id=1, source_target_pairs={{0,16},{4,20},{8,24},{12,28},{16,0},{20,4},{24,8},{28,12},{1,17},{... | collective-permute-start | bytes 1327112 | tf_op jit(solution)/shard_map/ppermute | solution.py:336
  94.9 3.6 %copy-start.11 = (bf16[2,96,1152]{2,1,0:T(8,128)(2,1)}, bf16[2,96,1152]{2,1,0:T(8,128)(2,1)S(1)}, u32[]{:S(2)}) copy-start(bf16[2,96,1152]{2,1,0:T(8,128)(2,1)S(1)} %collective-permute-done.9.refs_1_) | copy-start | bytes 1327108
  95.7 12.0 %copy-start.17 = (f32[1,96,1152]{2,1,0:T(8,128)S(1)}, f32[1,96,1152]{2,1,0:T(8,128)}, u32[]{:S(2)}) copy-start(f32[1,96,1152]{2,1,0:T(8,128)} %get-tuple-element.74) | copy-start | bytes 1327108
  95.8 12.0 %copy-start.18 = (f32[1,96,1152]{2,1,0:T(8,128)S(1)}, f32[1,96,1152]{2,1,0:T(8,128)}, u32[]{:S(2)}) copy-start(f32[1,96,1152]{2,1,0:T(8,128)} %get-tuple-element.76) | copy-start | bytes 1327108
  95.8 26.3 %collective-permute-start.10 = (bf16[1,96,1152]{2,1,0:T(8,128)(2,1)}, bf16[1,96,1152]{2,1,0:T(8,128)(2,1)}, u32[]{:S(2)}, u32[]{:S(2)}) collective-permute-start(bf16[1,96,1152]{2,1,0:T(8,128)(2,1)} %add_convert_fusion.3), channel_id=1, source_target_pairs={{0,16},{4,20},{8,24},{12,28},{16,0},{20,4},{24,8},{28,12},{1,17},{... | collective-permute-start | bytes 663560 | tf_op jit(solution)/shard_map/ppermute | solution.py:336
  98.5 29.5 %collective-permute-start.12 = (f32[1,96,1152]{2,1,0:T(8,128)S(1)}, f32[1,96,1152]{2,1,0:T(8,128)S(1)}, u32[]{:S(2)}, u32[]{:S(2)}) collective-permute-start(f32[1,96,1152]{2,1,0:T(8,128)S(1)} %get-tuple-element.82), channel_id=1, source_target_pairs={{0,4},{4,0},{8,12},{12,8},{16,20},{20,16},{24,28},{28,24},{1,5},{5... | collective-permute-start | bytes 1327112 | tf_op jit(solution)/shard_map/ppermute | solution.py:336
  98.5 24.1 %collective-permute-start.13 = (bf16[1,96,1152]{2,1,0:T(8,128)(2,1)}, bf16[1,96,1152]{2,1,0:T(8,128)(2,1)}, u32[]{:S(2)}, u32[]{:S(2)}) collective-permute-start(bf16[1,96,1152]{2,1,0:T(8,128)(2,1)} %get-tuple-element.81), channel_id=1, source_target_pairs={{0,8},{4,12},{8,0},{12,4},{16,24},{20,28},{24,16},{28,20},{1,9},{5... | collective-permute-start | bytes 663560 | tf_op jit(solution)/shard_map/ppermute | solution.py:336
  107.8 7.6 %copy-start.15 = (f32[1,96,1152]{2,1,0:T(8,128)S(1)}, f32[1,96,1152]{2,1,0:T(8,128)}, u32[]{:S(2)}) copy-start(f32[1,96,1152]{2,1,0:T(8,128)} %get-tuple-element.73) | copy-start | bytes 1327108
  108.9 19.1 %collective-permute-start.18 = (f32[1,96,1152]{2,1,0:T(8,128)S(1)}, f32[1,96,1152]{2,1,0:T(8,128)S(1)}, u32[]{:S(2)}, u32[]{:S(2)}) collective-permute-start(f32[1,96,1152]{2,1,0:T(8,128)S(1)} %get-tuple-element.80), channel_id=1, source_target_pairs={{0,4},{4,0},{8,12},{12,8},{16,20},{20,16},{24,28},{28,24},{1,5},{5... | collective-permute-start | bytes 1327112 | tf_op jit(solution)/shard_map/ppermute | solution.py:336
  109.8 14.7 %copy-start.27 = (pred[4]{0:T(512)(128)(4,1)S(1)}, pred[4]{0:T(512)(128)(4,1)}, u32[]{:S(2)}) copy-start(pred[4]{0:T(512)(128)(4,1)} %compare_and_fusion) | copy-start | bytes 16
  109.8 11.3 %all-to-all-start.1 = ((f32[8,8,1152]{2,1,0:T(8,128)}), f32[8,8,1152]{2,1,0:T(8,128)S(1)}, u32[]{:S(2)}, u32[]{:S(2)}) async-start(f32[8,8,1152]{2,1,0:T(8,128)} %broadcast_in_dim.106), calls=%async_computation.1 | async-start | bytes 589824 | tf_op jit(solution)/shard_map/all_to_all | solution.py:487
  113.3 14.8 %copy-start.12 = (bf16[2,96,1152]{2,1,0:T(8,128)(2,1)}, bf16[2,96,1152]{2,1,0:T(8,128)(2,1)S(1)}, u32[]{:S(2)}) copy-start(bf16[2,96,1152]{2,1,0:T(8,128)(2,1)S(1)} %collective-permute-done.15.refs_6_) | copy-start | bytes 1327108
  113.3 11.1 %collective-permute-start.19 = (bf16[1,96,1152]{2,1,0:T(8,128)(2,1)S(1)}, bf16[1,96,1152]{2,1,0:T(8,128)(2,1)}, u32[]{:S(2)}, u32[]{:S(2)}) collective-permute-start(bf16[1,96,1152]{2,1,0:T(8,128)(2,1)S(1)} %get-tuple-element.79), channel_id=1, source_target_pairs={{0,8},{4,12},{8,0},{12,4},{16,24},{20,28},{24,16},{28,20},{1,9},{5... | collective-permute-start | bytes 663560 | tf_op jit(solution)/shard_map/ppermute | solution.py:336
  121.0 7.1 %copy-start.10 = (f32[8,8,1152]{2,1,0:T(8,128)}, f32[8,8,1152]{2,1,0:T(8,128)S(1)}, u32[]{:S(2)}) copy-start(f32[8,8,1152]{2,1,0:T(8,128)S(1)} %all-to-all-done.1.refs_11_) | copy-start | bytes 884740
  122.0 6.0 %collective-permute-start.16 = (bf16[1,96,1152]{2,1,0:T(8,128)(2,1)S(1)}, bf16[1,96,1152]{2,1,0:T(8,128)(2,1)S(1)}, u32[]{:S(2)}, u32[]{:S(2)}) collective-permute-start(bf16[1,96,1152]{2,1,0:T(8,128)(2,1)S(1)} %add_convert_fusion.1), channel_id=1, source_target_pairs={{0,16},{4,20},{8,24},{12,28},{16,0},{20,4},{24,8},{28,12},{1,17},{... | collective-permute-start | bytes 663560 | tf_op jit(solution)/shard_map/ppermute | solution.py:336
  122.6 5.4 %collective-permute-start.14 = (bf16[1,96,1152]{2,1,0:T(8,128)(2,1)}, bf16[1,96,1152]{2,1,0:T(8,128)(2,1)S(1)}, u32[]{:S(2)}, u32[]{:S(2)}) collective-permute-start(bf16[1,96,1152]{2,1,0:T(8,128)(2,1)} %collective-permute-done.13), channel_id=1, source_target_pairs={{0,4},{4,0},{8,12},{12,8},{16,20},{20,16},{24,28},{28,24},{1,5},{5... | collective-permute-start | bytes 663560 | tf_op jit(solution)/shard_map/ppermute | solution.py:336
  124.5 3.6 %collective-permute-start.20 = (bf16[1,96,1152]{2,1,0:T(8,128)(2,1)}, bf16[1,96,1152]{2,1,0:T(8,128)(2,1)S(1)}, u32[]{:S(2)}, u32[]{:S(2)}) collective-permute-start(bf16[1,96,1152]{2,1,0:T(8,128)(2,1)} %collective-permute-done.19), channel_id=1, source_target_pairs={{0,4},{4,0},{8,12},{12,8},{16,20},{20,16},{24,28},{28,24},{1,5},{5... | collective-permute-start | bytes 663560 | tf_op jit(solution)/shard_map/ppermute | solution.py:336
  128.0 0.7 copy-start.21
  128.0 0.8 copy-start.13
  128.0 0.9 copy-start.22
  128.0 1.0 copy-start.14
  128.1 1.1 copy-start.23

commit v9 on v6

--- a/solution.py
+++ b/solution.py
@@ -16,6 +16,7 @@
 WINDOW = 2 * LANES
 CHUNK_PAGES = 4
 VMEM_LIMIT = 58 * 1024 * 1024
+PROJECT_LIMIT = 20 * 1024 * 1024
 
 SMEM = pl.BlockSpec(memory_space=pltpu.SMEM)
 VMEM = pl.BlockSpec(memory_space=pltpu.VMEM)
@@ -447,7 +448,7 @@
                     pltpu.SemaphoreType.DMA((everyone,)),
                     pltpu.SemaphoreType.DMA((2,)),
                 ],
-                compiler_params=pltpu.CompilerParams(vmem_limit_bytes=VMEM_LIMIT),
+                compiler_params=pltpu.CompilerParams(vmem_limit_bytes=PROJECT_LIMIT),
                 name="project",
             )(place, position, *received, own_rows, other_rows)
         )

time: 140 us -> 139 us (level)
  Pallas kernels: 31.2 us -> 25.6 us
  waiting for transfers between devices: 51.8 us -> 55 us
  other arithmetic: 6.79 us -> 8.2 us
    pallas_call x2, Pallas kernels: 16.7 us -> 12.9 us  [per_device(): pl.pallas_call(functools.partial(project_kernel, part, plan), out_shape=[...]
    ppermute x17, waiting for transfers between devices: 18.3 us -> 22 us  [swap(): lax.ppermute(value, 'req', [(device, device ^ distance) for device in ran...]
    pallas_call x1, Pallas kernels: 14.5 us -> 12.7 us  [per_device(): pl.pallas_call(functools.partial(attend_kernel, (terms, req_count, fresh_...]
  transfers between devices with their start and end apart: 22 -> 22, of which waited for: 10 -> 12; matrix products, arithmetic and copies ran while one was open for 6% -> 7% of each run, Pallas kernels for 6% -> 5%
where the time goes in v9:
time: 139 us; the launch traced here: 138 us
  waiting for transfers between devices  55 us (40%)
  starting transfers between devices  41.4 us (30%)
  Pallas kernels  25.6 us (18%)
  other arithmetic  8.2 us (6%)
  local copies, waits for them, and re-layouts  6.9 us (5%)
    ppermute x4, waiting for transfers between devices, route(): return lax.ppermute(value, ('req', 'wgt'), pairs)  31.7 us
    ppermute x17, starting transfers between devices, swap(): lax.ppermute(value, 'req', [(device, device ^ distance) for device in ran...  27.1 us
    ppermute x17, waiting for transfers between devices, swap(): lax.ppermute(value, 'req', [(device, device ^ distance) for device in ran...  22 us
    pallas_call x2, Pallas kernels, per_device(): pl.pallas_call(functools.partial(project_kernel, part, plan), out_shape=[...  12.9 us
    pallas_call x1, Pallas kernels, per_device(): pl.pallas_call(functools.partial(attend_kernel, (terms, req_count, fresh_...  12.7 us
    ppermute x4, starting transfers between devices, route(): return lax.ppermute(value, ('req', 'wgt'), pairs)  8.06 us
    all_to_all x1, starting transfers between devices, per_device(): stats = lax.all_to_all(stats, 'wgt', 0, 0, tiled=True)  6.32 us
    dynamic_slice x1, local copies, waits for them, and re-layouts, per_device(): lax.dynamic_slice_in_dim(held, (1 - core) * half_cols, half_cols, 1)  2.96 us
  transfers between devices with their start and end apart: 22, of which 12 were waited for; matrix products, arithmetic and copies ran while one was open for 7% of the time, Pallas kernels for 5%

profile of v9, /device:TPU:0, one launch (start us, length us, event | category | flops | bytes accessed | tf_op | source)
XLA Modules:
  0.0 138.1 jit_solution(3700283720519871516)
XLA Ops:
  0.6 1.2 convert_reduce_fusion
  1.9 1.4 multiply_reduce_fusion
  3.2 0.1 div.51
  3.3 0.1 stack.19
  3.4 0.6 broadcast_in_dim.69
  4.0 6.3 %all-to-all-start = ((f32[4,2,192]{2,1,0:T(2,128)}), f32[4,2,192]{2,1,0:T(2,128)}, u32[]{:S(2)}, u32[]{:S(2)}) async-start(f32[4,2,192]{2,1,0:T(2,128)} %broadcast_in_dim.69), calls=%async_computation | async-start | bytes 16384 | tf_op jit(solution)/shard_map/all_to_all | solution.py:341
  10.3 3.0 %constant_dynamic-slice_fusion = bf16[768,1152]{1,0:T(8,128)(2,1)} fusion(bf16[768,2304]{1,0:T(8,128)(2,1)} %refs_8_.3, s32[]{:T(128)S(6)} %select_n.78), kind=kLoop, calls=%fused_computation.53 | loop fusion | bytes 3538948 | tf_op jit(solution)/shard_map/dynamic_slice | solution.py:418
  13.3 0.0 collective-permute-start.8
  13.3 1.4 %dynamic-slice_convert_fusion = (f32[1536]{0:T(1024)S(1)}, f32[1536]{0:T(1024)}) fusion(bf16[6144]{0:T(1024)(128)(2,1)} %param.20, s32[]{:T(128)S(6)} %select_n.77, bf16[6144]{0:T(1024)(128)(2,1)} %param.19), kind=kLoop, calls=%fused_computation.32 | loop fusion | flops 3072 | bytes 18436 | tf_op jit(solution)/shard_map/convert_element_type | solution.py:346
  14.7 1.3 all-to-all-done
  16.0 0.8 slice_reduce_fusion
  16.9 1.5 %fusion.3 = bf16[192,1536]{1,0:T(8,128)(2,1)S(1)} fusion(bf16[4,48,1536]{2,1,0:T(8,128)(2,1)} %param.15, f32[1536]{0:T(1024)S(1)} %get-tuple-element.41, f32[1536]{0:T(1024)} %get-tuple-element.42, f32[192]{0:T(256)S(1)} %add_rsqrt_fusion, f32[192]{0:T(256)S(1)} %broadcast_multiply_fusion.1), kind=kLoop, calls=%fused_computation.5 | loop fusion | flops 1769472 | bytes 1193472 | tf_op jit(solution)/shard_map/convert_element_type | solution.py:350
  18.4 1.7 %collective-permute-start.2 = (bf16[192,1536]{1,0:T(8,128)(2,1)S(1)}, bf16[192,1536]{1,0:T(8,128)(2,1)}, u32[]{:S(2)}, u32[]{:S(2)}) collective-permute-start(bf16[192,1536]{1,0:T(8,128)(2,1)S(1)} %fusion.3), channel_id=1, source_target_pairs={{16,0},{24,1},{0,2},{8,3},{20,4},{28,5},{4,6},{12,7},{17,8},{25,9}... | collective-permute-start | bytes 1769480 | tf_op jit(solution)/shard_map/ppermute | solution.py:366
  20.0 3.3 %collective-permute-start.3 = (bf16[192,1536]{1,0:T(8,128)(2,1)S(1)}, bf16[192,1536]{1,0:T(8,128)(2,1)}, u32[]{:S(2)}, u32[]{:S(2)}) collective-permute-start(bf16[192,1536]{1,0:T(8,128)(2,1)S(1)} %fusion.3), channel_id=1, source_target_pairs={{24,0},{16,1},{8,2},{0,3},{28,4},{20,5},{12,6},{4,7},{25,8},{17,9}... | collective-permute-start | bytes 1769480 | tf_op jit(solution)/shard_map/ppermute | solution.py:366
  23.4 1.5 %collective-permute-start = (bf16[192,1536]{1,0:T(8,128)(2,1)S(1)}, bf16[192,1536]{1,0:T(8,128)(2,1)}, u32[]{:S(2)}, u32[]{:S(2)}) collective-permute-start(bf16[192,1536]{1,0:T(8,128)(2,1)S(1)} %fusion.3), channel_id=1, source_target_pairs={{0,0},{8,1},{16,2},{24,3},{4,4},{12,5},{20,6},{28,7},{1,8},{9,9},{... | collective-permute-start | bytes 1769480 | tf_op jit(solution)/shard_map/ppermute | solution.py:366
  24.8 1.6 %collective-permute-start.1 = (bf16[192,1536]{1,0:T(8,128)(2,1)S(1)}, bf16[192,1536]{1,0:T(8,128)(2,1)}, u32[]{:S(2)}, u32[]{:S(2)}) collective-permute-start(bf16[192,1536]{1,0:T(8,128)(2,1)S(1)} %fusion.3), channel_id=1, source_target_pairs={{8,0},{0,1},{24,2},{16,3},{12,4},{4,5},{28,6},{20,7},{9,8},{1,9},{... | collective-permute-start | bytes 1769480 | tf_op jit(solution)/shard_map/ppermute | solution.py:366
  26.4 19.1 %collective-permute-done.2 = bf16[192,1536]{1,0:T(8,128)(2,1)} collective-permute-done((bf16[192,1536]{1,0:T(8,128)(2,1)S(1)}, bf16[192,1536]{1,0:T(8,128)(2,1)}, u32[]{:S(2)}, u32[]{:S(2)}) %collective-permute-start.2) | collective-permute-done | bytes 589856 | tf_op jit(solution)/shard_map/ppermute | solution.py:366
  45.6 0.8 collective-permute-done.3
  46.4 0.5 collective-permute-start.4
  46.9 11.7 %collective-permute-done.1 = bf16[192,1536]{1,0:T(8,128)(2,1)} collective-permute-done((bf16[192,1536]{1,0:T(8,128)(2,1)S(1)}, bf16[192,1536]{1,0:T(8,128)(2,1)}, u32[]{:S(2)}, u32[]{:S(2)}) %collective-permute-start.1) | collective-permute-done | bytes 589856 | tf_op jit(solution)/shard_map/ppermute | solution.py:366
  58.6 0.0 collective-permute-start.5
  58.6 0.7 gather_fusion
  59.3 0.1 pad_add_fusion.place
  59.4 0.2 convert_reduce_fusion.1
  59.6 0.1 select_reduce_fusion.position
  59.7 0.0 collective-permute-done.6
  59.8 0.0 collective-permute-done.7
  59.8 1.2 collective-permute-done.5
  61.0 0.0 collective-permute-done.8.refs_9_
  61.0 0.0 copy-start.14
  61.0 6.5 %project.3 = (bf16[2,96,1152]{2,1,0:T(8,128)(2,1)S(1)}, bf16[2,96,1152]{2,1,0:T(8,128)(2,1)S(1)}, f32[1,96,1152]{2,1,0:T(8,128)S(1)}, f32[1,96,1152]{2,1,0:T(8,1...) custom-call(s32[2]{0:T(128)S(1)} %pad_add_fusion.place, s32[32]{0:T(128)S(1)} %select_reduce_fusion.position, ...), custom_call_target="tpu_custom_call" | custom-call | tf_op jit(solution)/shard_map/project/pallas_call | solution.py:437
  67.5 0.8 copy-done.1
  68.2 22.1 %collective-permute-start.17 = (bf16[2,96,1152]{2,1,0:T(8,128)(2,1)S(1)}, bf16[2,96,1152]{2,1,0:T(8,128)(2,1)S(1)}, u32[]{:S(2)}, u32[]{:S(2)}) collective-permute-start(bf16[2,96,1152]{2,1,0:T(8,128)(2,1)S(1)} %get-tuple-element.27), channel_id=1, source_target_pairs={{0,16},{4,20},{8,24},{12,28},{16,0},{20,4},{24,8},{28,12},{1,17},{... | collective-permute-start | bytes 1327112 | tf_op jit(solution)/shard_map/ppermute | solution.py:325
  90.4 0.6 reshape.218.refs_10_
  91.0 0.1 add_convert_fusion.4
  91.1 0.0 collective-permute-start.15
  91.1 6.4 %project.2 = (bf16[2,96,1152]{2,1,0:T(8,128)(2,1)S(1)}, bf16[2,96,1152]{2,1,0:T(8,128)(2,1)S(1)}, f32[1,96,1152]{2,1,0:T(8,128)S(1)}, f32[1,96,1152]{2,1,0:T(8,1...) custom-call(s32[2]{0:T(128)S(1)} %pad_add_fusion.place, s32[32]{0:T(128)S(1)} %select_reduce_fusion.position, ...), custom_call_target="tpu_custom_call" | custom-call | tf_op jit(solution)/shard_map/project/pallas_call | solution.py:437
  97.5 0.1 collective-permute-start.11
  97.6 2.1 %collective-permute-start.9 = (bf16[2,96,1152]{2,1,0:T(8,128)(2,1)S(1)}, bf16[2,96,1152]{2,1,0:T(8,128)(2,1)S(1)}, u32[]{:S(2)}, u32[]{:S(2)}) collective-permute-start(bf16[2,96,1152]{2,1,0:T(8,128)(2,1)S(1)} %get-tuple-element.18), channel_id=1, source_target_pairs={{0,8},{4,12},{8,0},{12,4},{16,24},{20,28},{24,16},{28,20},{1,9},{5... | collective-permute-start | bytes 1327112 | tf_op jit(solution)/shard_map/ppermute | solution.py:325
  99.7 1.7 %collective-permute-done.17 = bf16[2,96,1152]{2,1,0:T(8,128)(2,1)S(1)} collective-permute-done((bf16[2,96,1152]{2,1,0:T(8,128)(2,1)S(1)}, bf16[2,96,1152]{2,1,0:T(8,128)(2,1)S(1)}, u32[]{:S(2)}, u32[]{:S(2)}) %collective-permute-start.17) | collective-permute-done | bytes 442400 | tf_op jit(solution)/shard_map/ppermute | solution.py:325
  101.3 0.1 add_convert_fusion
  101.4 0.1 collective-permute-start.19
  101.5 0.1 collective-permute-start.18
  101.6 2.5 %collective-permute-done.15.refs_6_ = bf16[2,96,1152]{2,1,0:T(8,128)(2,1)S(1)} collective-permute-done((bf16[2,96,1152]{2,1,0:T(8,128)(2,1)S(1)}, bf16[2,96,1152]{2,1,0:T(8,128)(2,1)S(1)}, u32[]{:S(2)}, u32[]{:S(2)}) %collective-permute-start.15) | collective-permute-done | bytes 442400 | tf_op jit(solution)/shard_map/ppermute | solution.py:325
  104.2 0.1 collective-permute-start.16
  104.3 6.6 %collective-permute-done.11 = bf16[2,96,1152]{2,1,0:T(8,128)(2,1)S(1)} collective-permute-done((bf16[2,96,1152]{2,1,0:T(8,128)(2,1)S(1)}, bf16[2,96,1152]{2,1,0:T(8,128)(2,1)S(1)}, u32[]{:S(2)}, u32[]{:S(2)}) %collective-permute-start.11) | collective-permute-done | bytes 442400 | tf_op jit(solution)/shard_map/ppermute | solution.py:325
  110.8 0.1 add_convert_fusion.2
  110.9 1.9 %collective-permute-start.13 = (bf16[1,96,1152]{2,1,0:T(8,128)(2,1)S(1)}, bf16[1,96,1152]{2,1,0:T(8,128)(2,1)S(1)}, u32[]{:S(2)}, u32[]{:S(2)}) collective-permute-start(bf16[1,96,1152]{2,1,0:T(8,128)(2,1)S(1)} %get-tuple-element.31), channel_id=1, source_target_pairs={{0,8},{4,12},{8,0},{12,4},{16,24},{20,28},{24,16},{28,20},{1,9},{5... | collective-permute-start | bytes 663560 | tf_op jit(solution)/shard_map/ppermute | solution.py:325
  112.9 0.7 collective-permute-done.9.refs_1_
  113.6 0.0 collective-permute-start.12
  113.7 4.7 %collective-permute-done.19 = bf16[1,96,1152]{2,1,0:T(8,128)(2,1)S(1)} collective-permute-done((bf16[1,96,1152]{2,1,0:T(8,128)(2,1)S(1)}, bf16[1,96,1152]{2,1,0:T(8,128)(2,1)S(1)}, u32[]{:S(2)}, u32[]{:S(2)}) %collective-permute-start.19) | collective-permute-done | bytes 221216 | tf_op jit(solution)/shard_map/ppermute | solution.py:325
  118.3 0.0 collective-permute-start.10
  118.4 0.0 collective-permute-done.16.refs_7_
  118.4 0.1 collective-permute-start.20
  118.4 3.5 %collective-permute-done.13 = bf16[1,96,1152]{2,1,0:T(8,128)(2,1)S(1)} collective-permute-done((bf16[1,96,1152]{2,1,0:T(8,128)(2,1)S(1)}, bf16[1,96,1152]{2,1,0:T(8,128)(2,1)S(1)}, u32[]{:S(2)}, u32[]{:S(2)}) %collective-permute-start.13) | collective-permute-done | bytes 221216 | tf_op jit(solution)/shard_map/ppermute | solution.py:325
  121.9 0.0 collective-permute-start.14
  122.0 1.1 fusion.4
  123.1 1.2 collective-permute-done.10.refs_2_
  124.4 0.6 copy-done.10
  125.0 0.1 copy-done.11
  125.1 0.2 copy-done.7
  125.2 0.1 copy-done.12
  125.3 0.1 copy-done.8
  125.4 12.7 %attend.1 = (bf16[4,48,768]{2,1,0:T(8,128)(2,1)}, bf16[4,48,768]{2,1,0:T(8,128)(2,1)}, bf16[4,48,768]{2,1,0:T(8,128)(2,1)}) custom-call(s32[2]{0:T(128)} %copy-done.3, s32[4]{0:T(128)} %all_lengths.1, s32[4,16]{1,0:T(4,128)} %table.1, f32[1,96,1152]{2,1,0:T(8,128)} %copy-done.2, bf16[2,96,1152]{2,1,0:T(8,128)(2,1)} %copy-done.6, ...), custom_call_target="tpu_custom_call" | custom-call | tf_op jit(solution)/shard_map/attend/pallas_call | solution.py:463
  (51 shorter events, 0.3 us)
Async XLA Ops:
  4.0 12.0 %all-to-all-start = ((f32[4,2,192]{2,1,0:T(2,128)}), f32[4,2,192]{2,1,0:T(2,128)}, u32[]{:S(2)}, u32[]{:S(2)}) async-start(f32[4,2,192]{2,1,0:T(2,128)} %broadcast_in_dim.69), calls=%async_computation | async-start | bytes 16384 | tf_op jit(solution)/shard_map/all_to_all | solution.py:341
  10.3 50.6 %copy-start = (bf16[768,2304]{1,0:T(8,128)(2,1)S(1)}, bf16[768,2304]{1,0:T(8,128)(2,1)}, u32[]{:S(2)}) copy-start(bf16[768,2304]{1,0:T(8,128)(2,1)} %refs_8_.3) | copy-start | bytes 10616836
  13.3 13.1 %copy-start.19 = (s32[32]{0:T(128)S(1)}, s32[32]{0:T(128)}, u32[]{:S(2)}) copy-start(s32[32]{0:T(128)} %param.16) | copy-start | bytes 388
  13.3 45.3 %copy-start.4 = (s32[8]{0:T(128)S(1)}, s32[8]{0:T(128)}, u32[]{:S(2)}) copy-start(s32[8]{0:T(128)} %constant.117.clone) | copy-start | bytes 100
  13.3 47.7 %collective-permute-start.8 = (bf16[768,1152]{1,0:T(8,128)(2,1)}, bf16[768,1152]{1,0:T(8,128)(2,1)}, u32[]{:S(2)}, u32[]{:S(2)}) collective-permute-start(bf16[768,1152]{1,0:T(8,128)(2,1)} %constant_dynamic-slice_fusion), channel_id=1, source_target_pairs={{0,4},{4,0},{8,12},{12,8},{16,20},{20,16},{24,28},{28,24},{1,5},{5... | collective-permute-start | bytes 5308424 | tf_op jit(solution)/shard_map/ppermute | solution.py:325
  18.4 27.2 %collective-permute-start.2 = (bf16[192,1536]{1,0:T(8,128)(2,1)S(1)}, bf16[192,1536]{1,0:T(8,128)(2,1)}, u32[]{:S(2)}, u32[]{:S(2)}) collective-permute-start(bf16[192,1536]{1,0:T(8,128)(2,1)S(1)} %fusion.3), channel_id=1, source_target_pairs={{16,0},{24,1},{0,2},{8,3},{20,4},{28,5},{4,6},{12,7},{17,8},{25,9}... | collective-permute-start | bytes 1769480 | tf_op jit(solution)/shard_map/ppermute | solution.py:366
  20.0 26.4 %collective-permute-start.3 = (bf16[192,1536]{1,0:T(8,128)(2,1)S(1)}, bf16[192,1536]{1,0:T(8,128)(2,1)}, u32[]{:S(2)}, u32[]{:S(2)}) collective-permute-start(bf16[192,1536]{1,0:T(8,128)(2,1)S(1)} %fusion.3), channel_id=1, source_target_pairs={{24,0},{16,1},{8,2},{0,3},{28,4},{20,5},{12,6},{4,7},{25,8},{17,9}... | collective-permute-start | bytes 1769480 | tf_op jit(solution)/shard_map/ppermute | solution.py:366
  23.4 23.0 %collective-permute-start = (bf16[192,1536]{1,0:T(8,128)(2,1)S(1)}, bf16[192,1536]{1,0:T(8,128)(2,1)}, u32[]{:S(2)}, u32[]{:S(2)}) collective-permute-start(bf16[192,1536]{1,0:T(8,128)(2,1)S(1)} %fusion.3), channel_id=1, source_target_pairs={{0,0},{8,1},{16,2},{24,3},{4,4},{12,5},{20,6},{28,7},{1,8},{9,9},{... | collective-permute-start | bytes 1769480 | tf_op jit(solution)/shard_map/ppermute | solution.py:366
  24.8 33.8 %collective-permute-start.1 = (bf16[192,1536]{1,0:T(8,128)(2,1)S(1)}, bf16[192,1536]{1,0:T(8,128)(2,1)}, u32[]{:S(2)}, u32[]{:S(2)}) collective-permute-start(bf16[192,1536]{1,0:T(8,128)(2,1)S(1)} %fusion.3), channel_id=1, source_target_pairs={{8,0},{0,1},{24,2},{16,3},{12,4},{4,5},{28,6},{20,7},{9,8},{1,9},{... | collective-permute-start | bytes 1769480 | tf_op jit(solution)/shard_map/ppermute | solution.py:366
  45.6 14.2 %collective-permute-start.6 = (bf16[192,1536]{1,0:T(8,128)(2,1)}, bf16[192,1536]{1,0:T(8,128)(2,1)}, u32[]{:S(2)}, u32[]{:S(2)}) collective-permute-start(bf16[192,1536]{1,0:T(8,128)(2,1)} %collective-permute-done.2), channel_id=1, source_target_pairs={{0,4},{4,0},{8,12},{12,8},{16,20},{20,16},{24,28},{28,24},{1,5},{5... | collective-permute-start | bytes 1769480 | tf_op jit(solution)/shard_map/ppermute | solution.py:325
  46.4 13.4 %collective-permute-start.7 = (bf16[192,1536]{1,0:T(8,128)(2,1)}, bf16[192,1536]{1,0:T(8,128)(2,1)}, u32[]{:S(2)}, u32[]{:S(2)}) collective-permute-start(bf16[192,1536]{1,0:T(8,128)(2,1)} %collective-permute-done.3), channel_id=1, source_target_pairs={{0,4},{4,0},{8,12},{12,8},{16,20},{20,16},{24,28},{28,24},{1,5},{5... | collective-permute-start | bytes 1769480 | tf_op jit(solution)/shard_map/ppermute | solution.py:325
  46.4 13.4 %collective-permute-start.4 = (bf16[192,1536]{1,0:T(8,128)(2,1)}, bf16[192,1536]{1,0:T(8,128)(2,1)}, u32[]{:S(2)}, u32[]{:S(2)}) collective-permute-start(bf16[192,1536]{1,0:T(8,128)(2,1)} %collective-permute-done), channel_id=1, source_target_pairs={{0,4},{4,0},{8,12},{12,8},{16,20},{20,16},{24,28},{28,24},{1,5},{5... | collective-permute-start | bytes 1769480 | tf_op jit(solution)/shard_map/ppermute | solution.py:325
  58.6 2.3 %collective-permute-start.5 = (bf16[192,1536]{1,0:T(8,128)(2,1)}, bf16[192,1536]{1,0:T(8,128)(2,1)}, u32[]{:S(2)}, u32[]{:S(2)}) collective-permute-start(bf16[192,1536]{1,0:T(8,128)(2,1)} %collective-permute-done.1), channel_id=1, source_target_pairs={{0,4},{4,0},{8,12},{12,8},{16,20},{20,16},{24,28},{28,24},{1,5},{5... | collective-permute-start | bytes 1769480 | tf_op jit(solution)/shard_map/ppermute | solution.py:325
  59.4 31.7 %copy-start.3 = (s32[2]{0:T(128)}, s32[2]{0:T(128)S(1)}, u32[]{:S(2)}) copy-start(s32[2]{0:T(128)S(1)} %pad_add_fusion.place) | copy-start | bytes 28
  61.0 29.4 %copy-start.13 = (bf16[2304]{0:T(1024)(128)(2,1)S(1)}, bf16[2304]{0:T(1024)(128)(2,1)}, u32[]{:S(2)}) copy-start(bf16[2304]{0:T(1024)(128)(2,1)} %param.22) | copy-start | bytes 13828
  61.0 30.0 %copy-start.14 = (s32[4]{0:T(128)S(1)}, s32[4]{0:T(128)}, u32[]{:S(2)}) copy-start(s32[4]{0:T(128)} %all_lengths.1) | copy-start | bytes 52
  67.5 0.8 copy-start.1
  68.2 33.1 %collective-permute-start.17 = (bf16[2,96,1152]{2,1,0:T(8,128)(2,1)S(1)}, bf16[2,96,1152]{2,1,0:T(8,128)(2,1)S(1)}, u32[]{:S(2)}, u32[]{:S(2)}) collective-permute-start(bf16[2,96,1152]{2,1,0:T(8,128)(2,1)S(1)} %get-tuple-element.27), channel_id=1, source_target_pairs={{0,16},{4,20},{8,24},{12,28},{16,0},{20,4},{24,8},{28,12},{1,17},{... | collective-permute-start | bytes 1327112 | tf_op jit(solution)/shard_map/ppermute | solution.py:325
  91.1 13.1 %collective-permute-start.15 = (bf16[2,96,1152]{2,1,0:T(8,128)(2,1)S(1)}, bf16[2,96,1152]{2,1,0:T(8,128)(2,1)S(1)}, u32[]{:S(2)}, u32[]{:S(2)}) collective-permute-start(bf16[2,96,1152]{2,1,0:T(8,128)(2,1)S(1)} %get-tuple-element.24), channel_id=1, source_target_pairs={{0,8},{4,12},{8,0},{12,4},{16,24},{20,28},{24,16},{28,20},{1,9},{5... | collective-permute-start | bytes 1327112 | tf_op jit(solution)/shard_map/ppermute | solution.py:325
  97.5 6.7 %copy-start.2 = (f32[1,96,1152]{2,1,0:T(8,128)}, f32[1,96,1152]{2,1,0:T(8,128)S(1)}, u32[]{:S(2)}) copy-start(f32[1,96,1152]{2,1,0:T(8,128)S(1)} %get-tuple-element.17.refs_0_) | copy-start | bytes 1327108
  97.5 13.3 %collective-permute-start.11 = (bf16[2,96,1152]{2,1,0:T(8,128)(2,1)S(1)}, bf16[2,96,1152]{2,1,0:T(8,128)(2,1)S(1)}, u32[]{:S(2)}, u32[]{:S(2)}) collective-permute-start(bf16[2,96,1152]{2,1,0:T(8,128)(2,1)S(1)} %get-tuple-element.21), channel_id=1, source_target_pairs={{0,16},{4,20},{8,24},{12,28},{16,0},{20,4},{24,8},{28,12},{1,17},{... | collective-permute-start | bytes 1327112 | tf_op jit(solution)/shard_map/ppermute | solution.py:325
  97.6 16.0 %collective-permute-start.9 = (bf16[2,96,1152]{2,1,0:T(8,128)(2,1)S(1)}, bf16[2,96,1152]{2,1,0:T(8,128)(2,1)S(1)}, u32[]{:S(2)}, u32[]{:S(2)}) collective-permute-start(bf16[2,96,1152]{2,1,0:T(8,128)(2,1)S(1)} %get-tuple-element.18), channel_id=1, source_target_pairs={{0,8},{4,12},{8,0},{12,4},{16,24},{20,28},{24,16},{28,20},{1,9},{5... | collective-permute-start | bytes 1327112 | tf_op jit(solution)/shard_map/ppermute | solution.py:325
  101.4 16.9 %collective-permute-start.19 = (bf16[1,96,1152]{2,1,0:T(8,128)(2,1)S(1)}, bf16[1,96,1152]{2,1,0:T(8,128)(2,1)S(1)}, u32[]{:S(2)}, u32[]{:S(2)}) collective-permute-start(bf16[1,96,1152]{2,1,0:T(8,128)(2,1)S(1)} %get-tuple-element.29), channel_id=1, source_target_pairs={{0,8},{4,12},{8,0},{12,4},{16,24},{20,28},{24,16},{28,20},{1,9},{5... | collective-permute-start | bytes 663560 | tf_op jit(solution)/shard_map/ppermute | solution.py:325
  101.5 22.8 %collective-permute-start.18 = (f32[1,96,1152]{2,1,0:T(8,128)S(1)}, f32[1,96,1152]{2,1,0:T(8,128)S(1)}, u32[]{:S(2)}, u32[]{:S(2)}) collective-permute-start(f32[1,96,1152]{2,1,0:T(8,128)S(1)} %get-tuple-element.30), channel_id=1, source_target_pairs={{0,4},{4,0},{8,12},{12,8},{16,20},{20,16},{24,28},{28,24},{1,5},{5... | collective-permute-start | bytes 1327112 | tf_op jit(solution)/shard_map/ppermute | solution.py:325
  104.1 6.8 %copy-start.5 = (bf16[2,96,1152]{2,1,0:T(8,128)(2,1)}, bf16[2,96,1152]{2,1,0:T(8,128)(2,1)S(1)}, u32[]{:S(2)}) copy-start(bf16[2,96,1152]{2,1,0:T(8,128)(2,1)S(1)} %collective-permute-done.15.refs_6_) | copy-start | bytes 1327108
  104.2 14.2 %collective-permute-start.16 = (bf16[1,96,1152]{2,1,0:T(8,128)(2,1)S(1)}, bf16[1,96,1152]{2,1,0:T(8,128)(2,1)S(1)}, u32[]{:S(2)}, u32[]{:S(2)}) collective-permute-start(bf16[1,96,1152]{2,1,0:T(8,128)(2,1)S(1)} %add_convert_fusion.1), channel_id=1, source_target_pairs={{0,16},{4,20},{8,24},{12,28},{16,0},{20,4},{24,8},{28,12},{1,17},{... | collective-permute-start | bytes 663560 | tf_op jit(solution)/shard_map/ppermute | solution.py:325
  110.8 11.1 %copy-start.15 = (pred[96]{0:T(512)(128)(4,1)S(1)}, pred[96]{0:T(512)(128)(4,1)}, u32[]{:S(2)}) copy-start(pred[96]{0:T(512)(128)(4,1)} %constant.119.clone) | copy-start | bytes 292
  110.8 11.1 %copy-start.16 = (pred[96]{0:T(512)(128)(4,1)S(1)}, pred[96]{0:T(512)(128)(4,1)}, u32[]{:S(2)}) copy-start(pred[96]{0:T(512)(128)(4,1)} %constant.120.clone) | copy-start | bytes 292
  110.8 11.1 %copy-start.17 = (f32[96]{0:T(128)S(1)}, f32[96]{0:T(128)}, u32[]{:S(2)}) copy-start(f32[96]{0:T(128)} %constant.127) | copy-start | bytes 1156
  110.8 11.1 %copy-start.18 = (pred[96]{0:T(512)(128)(4,1)S(1)}, pred[96]{0:T(512)(128)(4,1)}, u32[]{:S(2)}) copy-start(pred[96]{0:T(512)(128)(4,1)} %constant.128) | copy-start | bytes 292
  110.9 11.0 %collective-permute-start.13 = (bf16[1,96,1152]{2,1,0:T(8,128)(2,1)S(1)}, bf16[1,96,1152]{2,1,0:T(8,128)(2,1)S(1)}, u32[]{:S(2)}, u32[]{:S(2)}) collective-permute-start(bf16[1,96,1152]{2,1,0:T(8,128)(2,1)S(1)} %get-tuple-element.31), channel_id=1, source_target_pairs={{0,8},{4,12},{8,0},{12,4},{16,24},{20,28},{24,16},{28,20},{1,9},{5... | collective-permute-start | bytes 663560 | tf_op jit(solution)/shard_map/ppermute | solution.py:325
  113.6 10.7 %copy-start.6 = (bf16[2,96,1152]{2,1,0:T(8,128)(2,1)}, bf16[2,96,1152]{2,1,0:T(8,128)(2,1)S(1)}, u32[]{:S(2)}) copy-start(bf16[2,96,1152]{2,1,0:T(8,128)(2,1)S(1)} %collective-permute-done.9.refs_1_) | copy-start | bytes 1327108
  113.6 10.7 %collective-permute-start.12 = (f32[1,96,1152]{2,1,0:T(8,128)S(1)}, f32[1,96,1152]{2,1,0:T(8,128)S(1)}, u32[]{:S(2)}, u32[]{:S(2)}) collective-permute-start(f32[1,96,1152]{2,1,0:T(8,128)S(1)} %get-tuple-element.32), channel_id=1, source_target_pairs={{0,4},{4,0},{8,12},{12,8},{16,20},{20,16},{24,28},{28,24},{1,5},{5... | collective-permute-start | bytes 1327112 | tf_op jit(solution)/shard_map/ppermute | solution.py:325
  118.3 5.9 %collective-permute-start.10 = (bf16[1,96,1152]{2,1,0:T(8,128)(2,1)S(1)}, bf16[1,96,1152]{2,1,0:T(8,128)(2,1)S(1)}, u32[]{:S(2)}, u32[]{:S(2)}) collective-permute-start(bf16[1,96,1152]{2,1,0:T(8,128)(2,1)S(1)} %add_convert_fusion.3), channel_id=1, source_target_pairs={{0,16},{4,20},{8,24},{12,28},{16,0},{20,4},{24,8},{28,12},{1,17},{... | collective-permute-start | bytes 663560 | tf_op jit(solution)/shard_map/ppermute | solution.py:325
  118.4 6.0 %copy-start.9 = (bf16[1,96,1152]{2,1,0:T(8,128)(2,1)}, bf16[1,96,1152]{2,1,0:T(8,128)(2,1)S(1)}, u32[]{:S(2)}) copy-start(bf16[1,96,1152]{2,1,0:T(8,128)(2,1)S(1)} %collective-permute-done.16.refs_7_) | copy-start | bytes 663556
  118.4 5.9 %collective-permute-start.20 = (bf16[1,96,1152]{2,1,0:T(8,128)(2,1)S(1)}, bf16[1,96,1152]{2,1,0:T(8,128)(2,1)S(1)}, u32[]{:S(2)}, u32[]{:S(2)}) collective-permute-start(bf16[1,96,1152]{2,1,0:T(8,128)(2,1)S(1)} %collective-permute-done.19), channel_id=1, source_target_pairs={{0,4},{4,0},{8,12},{12,8},{16,20},{20,16},{24,28},{28,24},{1,5},{5... | collective-permute-start | bytes 663560 | tf_op jit(solution)/shard_map/ppermute | solution.py:325
  121.9 2.4 %collective-permute-start.14 = (bf16[1,96,1152]{2,1,0:T(8,128)(2,1)S(1)}, bf16[1,96,1152]{2,1,0:T(8,128)(2,1)S(1)}, u32[]{:S(2)}, u32[]{:S(2)}) collective-permute-start(bf16[1,96,1152]{2,1,0:T(8,128)(2,1)S(1)} %collective-permute-done.13), channel_id=1, source_target_pairs={{0,4},{4,0},{8,12},{12,8},{16,20},{20,16},{24,28},{28,24},{1,5},{5... | collective-permute-start | bytes 663560 | tf_op jit(solution)/shard_map/ppermute | solution.py:325
  124.3 0.7 copy-start.10
  124.3 0.8 copy-start.11
  124.3 0.9 copy-start.7
  124.3 1.0 copy-start.12
  124.3 1.1 copy-start.8
